TPU v7x, 32 devices: a whole 2x2x4 slice. The times are simulated.
32 devices in a mesh: seq: 2 (over core), mp: 4 (over y, x), dp: 4 (over z).
Axes of the slice: x: 2, y: 2, z: 4, core: 2. Of those that a mesh axis runs over, the one named last changes fastest.
Arguments:
- tokens: bfloat16 [2048, 8, 1024], P('seq', 'dp'), may hold values from -6 to 6
- lengths: int32 [8], P('dp'), may hold values from 512 to 2048, as said below
- mixer_gain: bfloat16 [1024], replicated, may hold values from 0.099609375 to 1.8984375
- project_weight: bfloat16 [1024, 4, 512], P(None, 'mp'), may hold values from -0.1875 to 0.1875
- filter_weight: bfloat16 [4, 4, 512], P(None, 'mp'), may hold values from -3 to 3
- rank_down: bfloat16 [1024, 16], replicated, may hold values from -0.1875 to 0.1875
- rank_up: bfloat16 [16, 4, 128], P(None, 'mp'), may hold values from -1.5 to 1.5
- decay_bias: float32 [4, 128], P('mp'), may hold values from -1 to 6
- gate_weight: bfloat16 [1024, 1024], P(None, 'mp'), may hold values from -0.1875 to 0.1875
- head_gain: bfloat16 [256], replicated, may hold values from 0.099609375 to 1.8984375
- output_weight: bfloat16 [1024, 1024], P('mp'), may hold values from -0.1875 to 0.1875
- channel_gain: bfloat16 [1024], replicated, may hold values from 0.099609375 to 1.8984375
- hidden_gate: bfloat16 [1024, 2816], P(None, 'mp'), may hold values from -0.1875 to 0.1875
- hidden_up: bfloat16 [1024, 2816], P(None, 'mp'), may hold values from -0.1875 to 0.1875
- hidden_down: bfloat16 [2816, 1024], P('mp'), may hold values from -0.109375 to 0.109375
- cotangent: bfloat16 [2048, 8, 1024], P('seq', 'dp'), may hold values from -6 to 6
Outputs:
- output: bfloat16 [2048, 8, 1024], P(('seq', 'mp'), 'dp')
- tokens_grad: float32 [2048, 8, 1024], P(('seq', 'mp'), 'dp')
- mixer_gain_grad: float32 [1024], replicated
- project_grad: float32 [1024, 4, 512], P(('seq', 'dp'), 'mp')
- filter_grad: float32 [4, 4, 512], P(None, 'mp', ('seq', 'dp'))
- rank_down_grad: float32 [1024, 16], replicated
- rank_up_grad: float32 [16, 4, 128], P(None, 'mp', ('seq', 'dp'))
- decay_bias_grad: float32 [4, 128], P('mp', ('seq', 'dp'))
- gate_grad: float32 [1024, 1024], P(('seq', 'dp'), 'mp')
- head_gain_grad: float32 [256], replicated
- output_weight_grad: float32 [1024, 1024], P('mp', ('seq', 'dp'))
- channel_gain_grad: float32 [1024], replicated
- hidden_gate_grad: float32 [1024, 2816], P(('seq', 'dp'), 'mp')
- hidden_up_grad: float32 [1024, 2816], P(('seq', 'dp'), 'mp')
- hidden_down_grad: float32 [2816, 1024], P('mp', ('seq', 'dp'))
Inputs may be any that keep to these rules, and one draw needn't show every extreme that they name: Sequence s holds its valid positions 0 .. lengths[s] - 1 first; among each 2 consecutive sequences (those of one index of dp) one has all 2048 positions valid.
All inputs are finite; a program needn't handle non-finite values.
Results may differ from a plain program's by a relative error of at most 0.038.
Values may be sent and summed in bfloat16 or wider, within the bound.
A program may use at most 192 MiB of HBM per device.

v0:
```python
import jax
import jax.numpy as jnp
from jax import lax
from jax.sharding import PartitionSpec as P

CONV = 4
BLOCK = 64


EPS_NORM = 1e-06
EPS_HEAD = 1e-05
GATE_NORMALIZER = 16.0
HIGHEST = lax.Precision.HIGHEST


def prefix(value, axis, join, neutral, backward):
    count, mine = (lax.axis_size(axis), lax.axis_index(axis))
    pieces = jax.tree.map(lambda part: lax.all_gather(part, axis), value)
    if backward:
        pieces = jax.tree.map(lambda part: part[::-1], pieces)
        mine = count - 1 - mine
    subtotal = jax.tree.map(
        lambda part, zero: jnp.full_like(part, 0) + jnp.asarray(zero, part.dtype), value, neutral
    )

    def hop(position, subtotal):
        longer = join(subtotal, jax.tree.map(lambda part: part[position], pieces))
        return jax.tree.map(lambda new, old: jnp.where(position < mine, new, old), longer, subtotal)

    return lax.fori_loop(0, count - 1, hop, subtotal)


def passed_along(block, axis, distance):
    devices = range(lax.axis_size(axis))
    route = [(i - distance, i) for i in devices if i - distance in devices]
    return lax.ppermute(block, axis, route)


def quick(form, left, right):
    return jnp.einsum(form, left, right, preferred_element_type=jnp.float32)


def precise(form, left, right):
    return jnp.einsum(form, left, right, precision=HIGHEST, preferred_element_type=jnp.float32)


def normalize(values, gain, epsilon):
    return values * lax.rsqrt(jnp.mean(values * values, axis=-1, keepdims=True) + epsilon) * gain


def normalize_back(values, gain, upstream, epsilon):
    inverse = lax.rsqrt(jnp.mean(values * values, axis=-1, keepdims=True) + epsilon)
    unit_rows = values * inverse
    scaled = upstream * gain
    through = inverse * (scaled - unit_rows * jnp.mean(scaled * unit_rows, axis=-1, keepdims=True))
    gain_grad = jnp.sum(upstream * unit_rows, axis=tuple(range(values.ndim - 1)))
    return (through, gain_grad)


def swish_slope(values):
    sigmoid_rows = jax.nn.sigmoid(values)
    return sigmoid_rows * (1.0 + values * (1.0 - sigmoid_rows))


def filter_apply(extended, taps):
    length_here = extended.shape[0] - taps.shape[0] + 1
    filtered = taps[0] * extended[0:length_here]
    for offset in range(1, taps.shape[0]):
        filtered = filtered + taps[offset] * extended[offset : offset + length_here]
    return jax.nn.silu(filtered)


def mix_local(queries, key_rows, value_rows, decay_rows):
    length_here, sequence_count, key_width = queries.shape
    block_count = length_here // BLOCK

    def in_blocks(values):
        return values.reshape(block_count, BLOCK, sequence_count, values.shape[-1])

    cumulative = jnp.cumsum(in_blocks(decay_rows), axis=1)
    block_totals = cumulative[:, -1]
    preceding = jnp.cumsum(block_totals, axis=0) - block_totals
    causal = lax.broadcasted_iota(jnp.int32, (BLOCK, BLOCK), 0) >= lax.broadcasted_iota(
        jnp.int32, (BLOCK, BLOCK), 1
    )

    def advance(memory, pieces):
        block_queries, block_keys, block_values, block_decay = pieces
        lifted = block_queries * jnp.exp(block_decay)
        lowered = block_keys * jnp.exp(-block_decay)
        scores = jnp.where(causal[None], precise("ibk,jbk->bij", lifted, lowered), 0.0)
        mixed = precise("bij,jbv->ibv", scores, block_values) + precise(
            "ibk,bkv->ibv", lifted, memory
        )
        last_row = block_decay[-1]
        tails = block_keys * jnp.exp(last_row[None] - block_decay)
        carried = jnp.exp(last_row)[:, :, None] * memory + precise(
            "ibk,ibv->bkv", tails, block_values
        )
        return (carried, mixed)

    start_memory = jnp.zeros((sequence_count, key_width, value_rows.shape[-1]), jnp.float32)
    local_state, mixed = lax.scan(
        advance,
        start_memory,
        (in_blocks(queries), in_blocks(key_rows), in_blocks(value_rows), cumulative),
    )
    profile = jnp.exp(cumulative + preceding[:, None]).reshape(
        length_here, sequence_count, key_width
    )
    return (
        mixed.reshape(length_here, sequence_count, -1),
        local_state,
        jnp.sum(block_totals, axis=0),
        profile,
    )


def mix_full(queries, key_rows, value_rows, decay_rows, entering):
    mixed, local_state, decay_sum, profile = mix_local(queries, key_rows, value_rows, decay_rows)
    head_out = (mixed + precise("pbk,bkv->pbv", queries * profile, entering)) * queries.shape[
        -1
    ] ** (-0.5)
    leaving = jnp.exp(decay_sum)[:, :, None] * entering + local_state
    return (head_out, leaving)


def combine_forward(earlier, later):
    return (earlier[0] + later[0], jnp.exp(later[0])[..., None] * earlier[1] + later[1])


def combine_backward(earlier, later):
    return (earlier[0] + later[0], later[1] + jnp.exp(later[0])[..., None] * earlier[1])


def chain_states(decay_sum, block_state, combine, reverse):
    empty = (jnp.zeros_like(decay_sum), jnp.zeros_like(block_state))
    result = prefix((decay_sum, block_state), "seq", combine, empty, reverse)
    return result[1]


def on_device(
    tokens,
    lengths,
    mixer_gain,
    project_weight,
    filter_weight,
    rank_down,
    rank_up,
    decay_bias,
    gate_weight,
    head_gain,
    output_weight,
    channel_gain,
    hidden_gate,
    hidden_up,
    hidden_down,
    cotangent,
):
    length_here, sequence_count, width_here = tokens.shape
    own_rows = length_here // lax.axis_size("mp")
    first_row = lax.axis_index("mp") * own_rows
    key_width = rank_up.shape[2]
    project_local = project_weight[:, 0]
    filter_local = filter_weight[:, 0].astype(jnp.float32)
    rank_up_local = rank_up[:, 0].astype(jnp.float32)
    bias_local = decay_bias[0]
    mixer_gain_f = mixer_gain.astype(jnp.float32)
    channel_gain_f = channel_gain.astype(jnp.float32)
    head_gain_f = head_gain.astype(jnp.float32)
    edge_count = CONV - 1
    positions = lax.axis_index("seq") * length_here + lax.broadcasted_iota(
        jnp.int32, (length_here, sequence_count), 0
    )
    valid = positions < lengths[None, :]
    valid_rows = lax.dynamic_slice_in_dim(valid, first_row, own_rows, 0)
    tokens_f = tokens.astype(jnp.float32)
    token_rows = lax.dynamic_slice_in_dim(tokens_f, first_row, own_rows, 0)
    normed = normalize(tokens_f, mixer_gain_f, EPS_NORM).astype(jnp.bfloat16)
    projected = quick("pbd,dc->pbc", normed, project_local).astype(jnp.bfloat16)
    edge_rows = passed_along(projected[length_here - edge_count :], "seq", 1)
    extended = jnp.concatenate([edge_rows, projected], axis=0).astype(jnp.float32)
    convolved = filter_apply(extended, filter_local).astype(jnp.bfloat16).astype(jnp.float32)
    queries = convolved[..., :key_width]
    key_rows = convolved[..., key_width : 2 * key_width]
    value_rows = convolved[..., 2 * key_width :]
    low_rank = quick("pbd,dr->pbr", normed, rank_down).astype(jnp.bfloat16).astype(jnp.float32)
    logit = precise("pbr,rk->pbk", low_rank, rank_up_local) + bias_local
    log_decay = jax.nn.log_sigmoid(logit) / GATE_NORMALIZER
    mixed, local_state, decay_sum, profile = mix_local(queries, key_rows, value_rows, log_decay)
    entering = chain_states(decay_sum, local_state, combine_forward, False)
    head_out = (mixed + precise("pbk,bkv->pbv", queries * profile, entering)) * key_width ** (-0.5)
    head_normed = normalize(head_out, head_gain_f, EPS_HEAD)
    out_gate = quick("pbd,dv->pbv", normed, gate_weight)
    gated = (head_normed * jax.nn.silu(out_gate)).astype(jnp.bfloat16)
    mixer_out = lax.psum_scatter(
        quick("pbv,vd->pbd", gated, output_weight), "mp", scatter_dimension=0, tiled=True
    )
    residual = token_rows + mixer_out
    ffn_rows_normed = normalize(residual, channel_gain_f, EPS_NORM).astype(jnp.bfloat16)
    ffn_normed = lax.all_gather(ffn_rows_normed, "mp", axis=0, tiled=True)
    gate_rows = quick("pbd,df->pbf", ffn_normed, hidden_gate)
    up_rows = quick("pbd,df->pbf", ffn_normed, hidden_up)
    hidden = (jax.nn.silu(gate_rows) * up_rows).astype(jnp.bfloat16)
    ffn_out = lax.psum_scatter(
        quick("pbf,fd->pbd", hidden, hidden_down), "mp", scatter_dimension=0, tiled=True
    )
    output = jnp.where(valid_rows[..., None], residual + ffn_out, 0.0).astype(jnp.bfloat16)
    grad_full = jnp.where(valid[..., None], cotangent.astype(jnp.float32), 0.0)
    grad_result = grad_full.astype(jnp.bfloat16)
    grad_result_rows = lax.dynamic_slice_in_dim(grad_full, first_row, own_rows, 0)
    hidden_down_grad = quick("pbf,pbd->fd", hidden, grad_result)
    grad_hidden = quick("pbd,fd->pbf", grad_result, hidden_down)
    grad_gate = (grad_hidden * up_rows * swish_slope(gate_rows)).astype(jnp.bfloat16)
    grad_up = (grad_hidden * jax.nn.silu(gate_rows)).astype(jnp.bfloat16)
    hidden_gate_grad = quick("pbd,pbf->df", ffn_normed, grad_gate)
    hidden_up_grad = quick("pbd,pbf->df", ffn_normed, grad_up)
    gate_part = grad_gate
    grad_ffn_normed = lax.psum_scatter(
        quick("pbf,df->pbd", gate_part, hidden_gate) + quick("pbf,df->pbd", grad_up, hidden_up),
        "mp",
        scatter_dimension=0,
        tiled=True,
    )
    through_ffn, channel_gain_grad = normalize_back(
        residual, channel_gain_f, grad_ffn_normed, EPS_NORM
    )
    grad_residual = grad_result_rows + through_ffn
    grad_mixer = lax.all_gather(grad_residual.astype(jnp.bfloat16), "mp", axis=0, tiled=True)
    output_weight_grad = quick("pbv,pbd->vd", gated, grad_mixer)
    grad_gated = quick("pbd,vd->pbv", grad_mixer, output_weight)
    grad_out_gate = (grad_gated * head_normed * swish_slope(out_gate)).astype(jnp.bfloat16)
    gate_grad = quick("pbd,pbv->dv", normed, grad_out_gate)
    grad_head_normed = grad_gated * jax.nn.silu(out_gate)
    grad_head_out, head_gain_grad = normalize_back(
        head_out, head_gain_f, grad_head_normed, EPS_HEAD
    )
    state_grad = precise("pbk,pbv->bkv", queries * profile, grad_head_out) * key_width ** (-0.5)
    leaving_grad = chain_states(decay_sum, state_grad, combine_backward, True)

    def mix_here(queries_in, keys_in, values_in, decay_in):
        return mix_full(queries_in, keys_in, values_in, decay_in, entering)

    _, mix_pull = jax.vjp(mix_here, queries, key_rows, value_rows, log_decay)
    grad_queries, grad_keys, grad_values, grad_log_decay = mix_pull((grad_head_out, leaving_grad))
    grad_logit = grad_log_decay / GATE_NORMALIZER * jax.nn.sigmoid(-logit)
    rank_up_grad = precise("pbr,pbk->rk", low_rank, grad_logit)
    decay_bias_grad = jnp.sum(grad_logit, axis=(0, 1))
    grad_low_rank = precise("pbk,rk->pbr", grad_logit, rank_up_local)
    rank_down_partial = precise("pbd,pbr->dr", normed, grad_low_rank)
    grad_convolved = jnp.concatenate([grad_queries, grad_keys, grad_values], axis=-1)
    _, filter_pull = jax.vjp(filter_apply, extended, filter_local)
    grad_extended, filter_grad = filter_pull(grad_convolved)
    edge_grad = passed_along(grad_extended[:edge_count], "seq", -1)
    grad_projected = grad_extended[edge_count:] + jnp.pad(
        edge_grad, ((length_here - edge_count, 0), (0, 0), (0, 0))
    )
    grad_projected = grad_projected.astype(jnp.bfloat16)
    project_grad = quick("pbd,pbc->dc", normed, grad_projected)
    gate_part = grad_out_gate
    grad_normed = lax.psum_scatter(
        quick("pbc,dc->pbd", grad_projected, project_local)
        + quick("pbv,dv->pbd", gate_part, gate_weight)
        + precise("pbr,dr->pbd", grad_low_rank, rank_down),
        "mp",
        scatter_dimension=0,
        tiled=True,
    )
    through_mixer, mixer_gain_grad = normalize_back(token_rows, mixer_gain_f, grad_normed, EPS_NORM)
    tokens_grad = grad_residual + through_mixer
    small = lax.psum(
        (mixer_gain_grad, channel_gain_grad, head_gain_grad, rank_down_partial), ("seq", "mp", "dp")
    )
    reduced = (
        lax.psum_scatter(project_grad[:, None], ("seq", "dp"), scatter_dimension=0, tiled=True),
        lax.psum_scatter(filter_grad[:, None], ("seq", "dp"), scatter_dimension=2, tiled=True),
        lax.psum_scatter(rank_up_grad[:, None], ("seq", "dp"), scatter_dimension=2, tiled=True),
        lax.psum_scatter(decay_bias_grad[None], ("seq", "dp"), scatter_dimension=1, tiled=True),
        lax.psum_scatter(gate_grad, ("seq", "dp"), scatter_dimension=0, tiled=True),
        lax.psum_scatter(output_weight_grad, ("seq", "dp"), scatter_dimension=1, tiled=True),
        lax.psum_scatter(hidden_gate_grad, ("seq", "dp"), scatter_dimension=0, tiled=True),
        lax.psum_scatter(hidden_up_grad, ("seq", "dp"), scatter_dimension=0, tiled=True),
        lax.psum_scatter(hidden_down_grad, ("seq", "dp"), scatter_dimension=1, tiled=True),
    )
    return (
        output,
        tokens_grad,
        small[0],
        reduced[0],
        reduced[1],
        small[3],
        reduced[2],
        reduced[3],
        reduced[4],
        small[2],
        reduced[5],
        small[1],
        reduced[6],
        reduced[7],
        reduced[8],
    )


def solution(mesh):
    in_specs = (
        P("seq", "dp", None),
        P("dp"),
        P(),
        P(None, "mp", None),
        P(None, "mp", None),
        P(),
        P(None, "mp", None),
        P("mp", None),
        P(None, "mp"),
        P(),
        P("mp", None),
        P(),
        P(None, "mp"),
        P(None, "mp"),
        P("mp", None),
        P("seq", "dp", None),
    )
    out_specs = (
        P(("seq", "mp"), "dp", None),
        P(("seq", "mp"), "dp", None),
        P(),
        P(("seq", "dp"), "mp", None),
        P(None, "mp", ("seq", "dp")),
        P(),
        P(None, "mp", ("seq", "dp")),
        P("mp", ("seq", "dp")),
        P(("seq", "dp"), "mp"),
        P(),
        P("mp", ("seq", "dp")),
        P(),
        P(("seq", "dp"), "mp"),
        P(("seq", "dp"), "mp"),
        P("mp", ("seq", "dp")),
    )
    return jax.shard_map(
        on_device, mesh=mesh, in_specs=in_specs, out_specs=out_specs, check_vma=False
    )
```

profile of v0, /device:TPU:0, one launch (start us, length us, event | category | flops | bytes accessed | tf_op | source)
XLA Modules:
  0.0 1615.8 jit_solution(18306343462580552908)
XLA Ops:
  8.1 3.7 multiply_reduce_fusion
  11.8 4.0 convolution_convert_fusion
  31.9 3.8 fusion.107
  44.2 88.5 %while.79 = (s32[]{:T(128)}, f32[2,128,256]{2,1,0:T(8,128)S(1)}, f32[16,64,2,256]{3,1,0,2:T(8,128)}, f32[16,64,2,128]{3,1,2,0:T(8,128)S(1)}, f32[16,64,2,128]{3,...) while((s32[]{:T(128)}, f32[2,128,256]{2,1,0:T(8,128)S(1)}, ...), condition=%wide.region_3.4_spmd.clone, body=%wide.region_2.3_spmd.clone.sunk | while | flops 138817536 | bytes 2053764 | solution.py:103
  135.1 3.1 copy.150
  138.2 4.2 multiply_reduce_fusion.13
  142.5 3.5 multiply_convert_fusion.7
  147.1 4.6 fusion.143
  152.3 7.0 copy_convert_fusion
  159.4 80.9 %reduce-scatter.20.cloned.1.call-done = f32[256,2,1024]{2,0,1:T(8,128)} async-done(((f32[1024,2,1024]{2,0,1:T(8,128)}), f32[256,2,1024]{2,0,1:T(8,128)}) %reduce-scatter.20.cloned.1.call-update) | async-done | bytes 2097168 | tf_op jit(solution)/shard_map/reduce_scatter | solution.py:196
  240.3 3.2 multiply_reduce_fusion.12
  246.0 51.6 %all-gather.7.cloned.1.call-done = bf16[1024,2,1024]{2,0,1:T(8,128)(2,1)} async-done(((bf16[256,2,1024]{2,0,1:T(8,128)(2,1)}), bf16[1024,2,1024]{2,0,1:T(8,128)(2,1)}) %all-gather.7.cloned.1.call-update) | async-done | bytes 4194320 | tf_op jit(solution)/shard_map/all_gather | solution.py:201
  297.7 5.6 fusion.122
  303.3 5.0 fusion.126
  308.3 9.2 multiply_convert_fusion.1
  317.5 6.5 fusion.124
  324.0 6.0 convolution_add_fusion.4
  330.1 7.7 fusion.119
  338.2 5.9 convert_select_fusion
  344.1 72.5 %reduce-scatter.24.cloned.1.call-done = f32[256,2,1024]{2,0,1:T(8,128)} async-done(((f32[1024,2,1024]{2,0,1:T(8,128)}), f32[256,2,1024]{2,0,1:T(8,128)}) %reduce-scatter.24.cloned.1.call-update) | async-done | bytes 2097168 | tf_op jit(solution)/shard_map/reduce_scatter | solution.py:219
  419.4 86.5 %reduce-scatter.22.cloned.1.call-done = f32[256,2,1024]{2,0,1:T(8,128)} async-done(((f32[1024,2,1024]{2,0,1:T(8,128)}), f32[256,2,1024]{2,0,1:T(8,128)}) %reduce-scatter.22.cloned.1.call-update) | async-done | bytes 2097168 | tf_op jit(solution)/shard_map/reduce_scatter | solution.py:205
  506.0 5.5 fusion.192
  511.6 119.5 %while.80 = (s32[]{:T(128)}, f32[2,128,256]{2,1,0:T(8,128)S(1)}, f32[16,64,2,128]{3,1,2,0:T(8,128)}, f32[16,64,2,128]{3,1,2,0:T(8,128)}, f32[16,64,2,128]{3,1,2,...) while((s32[]{:T(128)}, f32[2,128,256]{2,1,0:T(8,128)S(1)}, ...), condition=%wide.region_15.16_spmd.clone, body=%wide.region_14.15_spmd.clone.sunk | while | flops 63348740 | bytes 2249428 | solution.py:103
  631.1 6.7 multiply_reduce_fusion.6
  639.7 3.4 convolution_multiply_fusion
  643.1 3.1 copy.163
  653.4 291.1 %while.78 = (s32[]{:T(128)}, f32[2,128,256]{2,1,0:T(8,128)S(1)}, f32[16,64,2,128]{3,1,0,2:T(8,128)}, f32[16,64,2,128]{3,1,0,2:T(8,128)}, f32[16,64,2,256]{3,1,0,...) while((s32[]{:T(128)}, f32[2,128,256]{2,1,0:T(8,128)S(1)}, ...), condition=%wide.region_19.20_spmd.clone, body=%wide.region_16.19_spmd.clone.sunk | while | flops 277438464 | bytes 5037817 | solution.py:103
  664.3 2.8 dynamic_update_slice.137
  682.4 2.8 dynamic_update_slice.137
  700.6 2.8 dynamic_update_slice.137
  718.8 2.8 dynamic_update_slice.137
  736.9 2.8 dynamic_update_slice.137
  755.1 2.8 dynamic_update_slice.137
  773.3 2.8 dynamic_update_slice.137
  791.4 2.8 dynamic_update_slice.137
  809.6 2.8 dynamic_update_slice.137
  845.9 2.8 dynamic_update_slice.137
  882.2 2.8 dynamic_update_slice.137
  900.3 2.8 dynamic_update_slice.137
  944.5 6.2 bitcast_add_fusion.1
  950.9 6.6 multiply_reduce_fusion.4
  959.4 9.4 broadcast_multiply_fusion
  972.8 10.3 pad_add_fusion
  987.2 8.4 convolution_bitcast_fusion.8
  996.3 3.5 fusion.165
  1001.2 6.0 add_add_fusion
  1007.2 7.7 convolution_bitcast_fusion.7
  1015.1 7.8 convolution_bitcast_fusion.6
  1023.2 8.2 fusion.115
  1031.5 6.5 convolution_bitcast_fusion.12
  1038.0 4.5 convolution_bitcast_fusion.9
  1042.6 5.3 convolution_bitcast_fusion.10
  1052.9 15.0 reduce-scatter.42.cloned.1.call-done
  1069.3 49.4 %reduce-scatter.28.cloned.1.call-done = f32[128,1,512]{2,0,1:T(8,128)} async-done(((f32[1024,1,512]{2,0,1:T(8,128)}), f32[128,1,512]{2,0,1:T(8,128)}) %reduce-scatter.28.cloned.1.call-update) | async-done | bytes 262160 | tf_op jit(solution)/shard_map/reduce_scatter | solution.py:275
  1120.6 86.5 %reduce-scatter.26.cloned.1.call-done = f32[256,2,1024]{2,0,1:T(8,128)} async-done(((f32[1024,2,1024]{2,0,1:T(8,128)}), f32[256,2,1024]{2,0,1:T(8,128)}) %reduce-scatter.26.cloned.1.call-update) | async-done | bytes 2097168 | tf_op jit(solution)/shard_map/reduce_scatter | solution.py:261
  1207.1 2.9 multiply_reduce_fusion.7
  1212.3 2.9 copy.185
  1215.2 42.9 %all-reduce.11 = (f32[1024]{0:T(1024)}, f32[256]{0:T(256)}, f32[1024]{0:T(1024)}) all-reduce(f32[1024]{0:T(1024)S(1)} %get-tuple-element.980, f32[256]{0:T(256)S(1)} %copy-done.81, f32[1024]{0:T(1024)S(1)} %copy-done.68), channel_id=1, replica_groups=mesh['seq'=2,'mp'=4,'dp'=4] {'seq','mp','dp'}, use_global_device_ids=true, to_apply=%region_27.28 | all-reduce | flops 2304 | bytes 18432 | tf_op jit(solution)/shard_map/psum | solution.py:271
  1258.1 16.8 %reduce-scatter.34.cloned.1.call-done = f32[128,704]{0,1:T(8,128)} async-done(((f32[1024,704]{0,1:T(8,128)}), f32[128,704]{0,1:T(8,128)}) %reduce-scatter.34.cloned.1.call-update) | async-done | bytes 360464 | tf_op jit(solution)/shard_map/reduce_scatter | solution.py:281
  1274.9 66.0 %reduce-scatter.36.cloned.1.call-done = f32[128,704]{0,1:T(8,128)} async-done(((f32[1024,704]{0,1:T(8,128)}), f32[128,704]{0,1:T(8,128)}) %reduce-scatter.36.cloned.1.call-update) | async-done | bytes 360464 | tf_op jit(solution)/shard_map/reduce_scatter | solution.py:282
  1340.9 66.1 %reduce-scatter.38.cloned.1.call-done = f32[704,128]{1,0:T(8,128)} async-done(((f32[704,1024]{1,0:T(8,128)}), f32[704,128]{1,0:T(8,128)}) %reduce-scatter.38.cloned.1.call-update) | async-done | bytes 360464 | tf_op jit(solution)/shard_map/reduce_scatter | solution.py:283
  1406.9 123.8 %all-reduce.14.cloned.1.call-done = f32[1024,16]{0,1:T(8,128)} async-done(((f32[1024,16]{0,1:T(8,128)}), f32[1024,16]{0,1:T(8,128)}) %all-reduce.14.cloned.1.call-update) | async-done | bytes 65552 | tf_op jit(solution)/shard_map/psum | solution.py:271
  1530.8 39.2 %reduce-scatter.32.cloned.1.call-done = f32[256,128]{1,0:T(8,128)} async-done(((f32[256,1024]{1,0:T(8,128)}), f32[256,128]{1,0:T(8,128)}) %reduce-scatter.32.cloned.1.call-update) | async-done | bytes 131088 | tf_op jit(solution)/shard_map/reduce_scatter | solution.py:280
  1570.0 37.5 %reduce-scatter.30.cloned.1.call-done = f32[128,256]{1,0:T(8,128)} async-done(((f32[1024,256]{1,0:T(8,128)}), f32[128,256]{1,0:T(8,128)}) %reduce-scatter.30.cloned.1.call-update) | async-done | bytes 131088 | tf_op jit(solution)/shard_map/reduce_scatter | solution.py:279
  (757 shorter events, 531.7 us)
Async XLA Ops:
  7.2 301.1 %copy-start = (bf16[704,1024]{1,0:T(8,128)(2,1)S(1)}, bf16[704,1024]{1,0:T(8,128)(2,1)}, u32[]{:S(2)}) copy-start(bf16[704,1024]{1,0:T(8,128)(2,1)} %param.36) | copy-start | bytes 4325380
  7.2 233.1 %reduce-scatter.20.cloned.1.call-start = ((), (), s32[]{:S(2)}) async-start(), calls=%async_computation.13 | async-start | bytes 10485760 | tf_op jit(solution)/shard_map/reduce_scatter | solution.py:196
  8.1 134.4 %copy-start.49 = (f32[1024]{0:T(1024)}, f32[1024]{0:T(1024)S(1)}, u32[]{:S(2)}) copy-start(f32[1024]{0:T(1024)S(1)} %convert_element_type.72) | copy-start | bytes 12292
  11.8 130.7 %copy-start.73 = (f32[1024,2]{0,1:T(2,128)}, f32[1024,2]{0,1:T(2,128)S(1)}, u32[]{:S(2)}) copy-start(f32[1024,2]{0,1:T(2,128)S(1)} %add_rsqrt_fusion.1) | copy-start | bytes 24580
  15.9 13.8 collective-permute-start
  22.2 7.4 copy-start.86
  22.9 8.9 copy-start.70
  24.3 7.6 copy-start.57
  24.3 7.6 copy-start.59
  24.3 7.6 copy-start.61
  24.3 7.6 copy-start.63
  26.7 111.5 %copy-start.65 = (f32[2,128]{1,0:T(2,128)}, f32[2,128]{1,0:T(2,128)S(1)}, u32[]{:S(2)}) copy-start(f32[2,128]{1,0:T(2,128)S(1)} %get-tuple-element.1133) | copy-start | bytes 3076
  29.6 112.9 %copy-start.78 = (f32[256]{0:T(256)}, f32[256]{0:T(256)S(1)}, u32[]{:S(2)}) copy-start(f32[256]{0:T(256)S(1)} %convert_element_type.80) | copy-start | bytes 3076
  132.7 9.7 copy-start.14
  135.1 7.3 copy-start.27
  151.7 146.0 %all-gather.7.cloned.1.call-start = ((), (), s32[]{:S(2)}) async-start(), calls=%async_computation.14 | async-start | bytes 5242880 | tf_op jit(solution)/shard_map/all_gather | solution.py:201
  152.3 91.2 %copy-start.45 = (f32[1024]{0:T(1024)}, f32[1024]{0:T(1024)S(1)}, u32[]{:S(2)}) copy-start(f32[1024]{0:T(1024)S(1)} %convert_element_type.82) | copy-start | bytes 12292
  243.6 59.7 %copy-start.51 = (f32[256,2]{0,1:T(2,128)}, f32[256,2]{0,1:T(2,128)S(1)}, u32[]{:S(2)}) copy-start(f32[256,2]{0,1:T(2,128)S(1)} %add_rsqrt_fusion.3) | copy-start | bytes 6148
  244.8 171.8 %reduce-scatter.24.cloned.1.call-start = ((), (), s32[]{:S(2)}) async-start(), calls=%async_computation.16 | async-start | bytes 10485760 | tf_op jit(solution)/shard_map/reduce_scatter | solution.py:219
  246.0 92.2 %copy-start.55 = (pred[1024,2]{0,1:T(4,128)(4,1)}, pred[1024,2]{0,1:T(4,128)(4,1)S(1)}, u32[]{:S(2)}) copy-start(pred[1024,2]{0,1:T(4,128)(4,1)S(1)} %broadcast_compare_fusion) | copy-start | bytes 6148
  330.1 175.9 %reduce-scatter.22.cloned.1.call-start = ((), (), s32[]{:S(2)}) async-start(), calls=%async_computation.15 | async-start | bytes 10485760 | tf_op jit(solution)/shard_map/reduce_scatter | solution.py:205
  337.8 293.3 %all-gather.9.cloned.1.call-start = ((), (), s32[]{:S(2)}) async-start(), calls=%async_computation.17 | async-start | bytes 5242880 | tf_op jit(solution)/shard_map/all_gather | solution.py:229
  338.2 78.4 %copy-start.46 = (f32[1024]{0:T(1024)S(1)}, f32[1024]{0:T(1024)}, u32[]{:S(2)}) copy-start(f32[1024]{0:T(1024)} %copy-done.45) | copy-start | bytes 12292
  338.2 78.4 %copy-start.52 = (f32[256,2]{0,1:T(2,128)S(1)}, f32[256,2]{0,1:T(2,128)}, u32[]{:S(2)}) copy-start(f32[256,2]{0,1:T(2,128)} %copy-done.51) | copy-start | bytes 6148
  511.5 119.6 %copy-start.38 = (bf16[256,1024]{1,0:T(8,128)(2,1)S(1)}, bf16[256,1024]{1,0:T(8,128)(2,1)}, u32[]{:S(2)}) copy-start(bf16[256,1024]{1,0:T(8,128)(2,1)} %param.32) | copy-start | bytes 1572868
  511.5 538.5 %reduce-scatter.44.cloned.1.call-start = ((), (), s32[]{:S(2)}) async-start(), calls=%async_computation.28 | async-start | bytes 73728
  511.5 119.6 %copy-start.8 = (f32[1024,2,256]{0,2,1:T(8,128)S(1)}, f32[1024,2,256]{0,2,1:T(8,128)}, u32[]{:S(2)}) copy-start(f32[1024,2,256]{0,2,1:T(8,128)} %copy-done.7) | copy-start | bytes 6291460
  511.6 119.5 %copy-start.44 = (f32[1024,2]{0,1:T(2,128)S(1)}, f32[1024,2]{0,1:T(2,128)}, u32[]{:S(2)}) copy-start(f32[1024,2]{0,1:T(2,128)} %copy-done.43) | copy-start | bytes 24580
  511.6 119.5 %copy-start.79 = (f32[256]{0:T(256)S(1)}, f32[256]{0:T(256)}, u32[]{:S(2)}) copy-start(f32[256]{0:T(256)} %copy-done.78) | copy-start | bytes 3076
  639.7 8.6 copy-start.66
  639.7 8.6 copy-start.77
  653.4 291.1 %copy-start.9 = (f32[1024,2,256]{0,2,1:T(8,128)S(1)}, f32[1024,2,256]{0,2,1:T(8,128)}, u32[]{:S(2)}) copy-start(f32[1024,2,256]{0,2,1:T(8,128)} %broadcast_multiply_fusion.4) | copy-start | bytes 6291460
  653.4 291.1 %copy-start.18 = (f32[16,64,2,128]{3,1,0,2:T(8,128)S(1)}, f32[16,64,2,128]{3,1,0,2:T(8,128)}, u32[]{:S(2)}) copy-start(f32[16,64,2,128]{3,1,0,2:T(8,128)} %copy.148) | copy-start | bytes 3145732
  653.4 291.1 %copy-start.67 = (f32[2,128]{1,0:T(2,128)S(1)}, f32[2,128]{1,0:T(2,128)}, u32[]{:S(2)}) copy-start(f32[2,128]{1,0:T(2,128)} %copy-done.65) | copy-start | bytes 3076
  950.8 8.5 copy-start.58
  950.8 8.5 copy-start.60
  950.8 8.5 copy-start.62
  950.8 8.5 copy-start.64
  959.3 9.5 copy-start.11
  959.3 9.5 copy-start.19
  959.3 9.4 copy-start.42
  959.3 10.1 copy-start.71
  959.3 10.2 copy-start.15
  959.3 10.2 copy-start.26
  972.6 78.7 %reduce-scatter.40.cloned.1.call-start = ((), (), s32[]{:S(2)}) async-start(), calls=%async_computation.26 | async-start | bytes 294912
  972.8 10.4 copy-start.3
  972.8 10.4 copy-start.4
  972.8 10.4 copy-start.5
  984.0 3.1 collective-permute-start.1
  985.4 82.5 %reduce-scatter.42.cloned.1.call-start = ((), (), s32[]{:S(2)}) async-start(), calls=%async_computation.27 | async-start | bytes 73728
  987.1 8.6 copy-start.76
  987.1 9.2 copy-start.54
  987.1 131.6 %reduce-scatter.28.cloned.1.call-start = ((), (), s32[]{:S(2)}) async-start(), calls=%async_computation.19 | async-start | bytes 2359296 | tf_op jit(solution)/shard_map/reduce_scatter | solution.py:275
  995.6 211.5 %reduce-scatter.26.cloned.1.call-start = ((), (), s32[]{:S(2)}) async-start(), calls=%async_computation.18 | async-start | bytes 10485760 | tf_op jit(solution)/shard_map/reduce_scatter | solution.py:261
  1007.2 267.7 %reduce-scatter.34.cloned.1.call-start = ((), (), s32[]{:S(2)}) async-start(), calls=%async_computation.23 | async-start | bytes 3244032 | tf_op jit(solution)/shard_map/reduce_scatter | solution.py:281
  1015.0 8.2 copy-start.56
  1015.0 325.9 %reduce-scatter.36.cloned.1.call-start = ((), (), s32[]{:S(2)}) async-start(), calls=%async_computation.24 | async-start | bytes 3244032 | tf_op jit(solution)/shard_map/reduce_scatter | solution.py:282
  1022.9 384.0 %reduce-scatter.38.cloned.1.call-start = ((), (), s32[]{:S(2)}) async-start(), calls=%async_computation.25 | async-start | bytes 3244032 | tf_op jit(solution)/shard_map/reduce_scatter | solution.py:283
  1031.4 6.6 copy-start.32
  1031.4 499.3 %all-reduce.14.cloned.1.call-start = ((), (), s32[]{:S(2)}) async-start(), calls=%async_computation.20 | async-start | bytes 131072 | tf_op jit(solution)/shard_map/psum | solution.py:271
  1038.0 532.0 %reduce-scatter.32.cloned.1.call-start = ((), (), s32[]{:S(2)}) async-start(), calls=%async_computation.22 | async-start | bytes 1179648 | tf_op jit(solution)/shard_map/reduce_scatter | solution.py:280
  1042.6 564.9 %reduce-scatter.30.cloned.1.call-start = ((), (), s32[]{:S(2)}) async-start(), calls=%async_computation.21 | async-start | bytes 1179648 | tf_op jit(solution)/shard_map/reduce_scatter | solution.py:279
  1047.9 162.1 %copy-start.21 = (f32[256,2,1024]{2,0,1:T(8,128)S(1)}, f32[256,2,1024]{2,0,1:T(8,128)}, u32[]{:S(2)}) copy-start(f32[256,2,1024]{2,0,1:T(8,128)} %get-tuple-element.1092) | copy-start | bytes 6291460
  1210.1 398.9 %copy-start.1 = (bf16[704,1024]{1,0:T(8,128)(2,1)S(1)}, bf16[704,1024]{1,0:T(8,128)(2,1)}, u32[]{:S(2)}) copy-start(bf16[704,1024]{1,0:T(8,128)(2,1)} %param.36) | copy-start | bytes 4325380
  (46 other events, 190.1 us)
Sparse Core Ops, SparseCore 0:
  151.8 88.4 reduce-scatter.19
  244.9 52.6 all-gather.6
  330.2 86.4 reduce-scatter.23
  419.6 86.3 reduce-scatter.21
  511.6 52.6 all-gather.8
  972.7 30.4 reduce-scatter.43
  1006.0 30.3 reduce-scatter.39
  1038.7 29.1 reduce-scatter.41
  1070.8 47.8 reduce-scatter.27
  1121.6 85.4 reduce-scatter.25
  1210.1 64.7 reduce-scatter.33
  1277.8 63.0 reduce-scatter.35
  1343.9 63.0 reduce-scatter.37
  1413.9 116.8 all-reduce.13
  1533.6 36.3 reduce-scatter.31
  1572.8 34.6 reduce-scatter.29
where the time goes:
time: 1630 us; the launch traced here: 1620 us
  waiting for transfers between devices  792 us (49%)
  matrix products  467 us (29%)
  other arithmetic  149 us (9%)
  local copies, waits for them, and re-layouts  135 us (8%)
  blocking collectives  49.2 us (3%)
    dot_general x232, matrix products, precise(): jnp.einsum(form, left, right, precision=HIGHEST, preferred_element_type=j...  357 us
    psum x1, waiting for transfers between devices, on_device(): lax.psum((mixer_gain_grad, channel_gain_grad, head_gain_grad, rank_down_p...  124 us
    dot_general x19, matrix products, quick(): return jnp.einsum(form, left, right, preferred_element_type=jnp.float32)  110 us
    reduce_scatter x1, waiting for transfers between devices, on_device(): lax.psum_scatter(quick('pbf,fd->pbd', hidden, hidden_down), 'mp', scatter...  86.5 us
    reduce_scatter x1, waiting for transfers between devices, on_device(): lax.psum_scatter(quick('pbc,dc->pbd', grad_projected, project_local) + qu...  86.5 us
    reduce_scatter x1, waiting for transfers between devices, on_device(): lax.psum_scatter(quick('pbv,vd->pbd', gated, output_weight), 'mp', scatte...  80.9 us
    reduce_scatter x1, waiting for transfers between devices, on_device(): lax.psum_scatter(quick('pbf,df->pbd', gate_part, hidden_gate) + quick('pb...  72.5 us
    reduce_scatter x1, waiting for transfers between devices, on_device(): lax.psum_scatter(hidden_down_grad, ('seq', 'dp'), scatter_dimension=1, ti...  66.1 us
  transfers between devices with their start and end apart: 18, of which 13 were waited for; matrix products, arithmetic and copies ran while one was open for 15% of the time, Pallas kernels for 0%

commit v1 on v0

v1 whole, which is shorter than its diff:
```python
import functools

import jax
import jax.numpy as jnp
from jax import lax
from jax.experimental import pallas as pl
from jax.experimental.pallas import tpu as pltpu
from jax.sharding import PartitionSpec as P

CONV = 4
EDGE = CONV - 1
CHUNK = 128
STEP = 256
EPS_NORM = 1e-06
EPS_HEAD = 1e-05
GATE_NORMALIZER = 16.0
HIGHEST = lax.Precision.HIGHEST
BF16 = jnp.bfloat16
F32 = jnp.float32
VMEM_LIMIT = 56 * 2**20


def mm(left, right):
    return lax.dot_general(left, right, (((1,), (0,)), ((), ())), preferred_element_type=F32)


def mm_nt(left, right):
    return lax.dot_general(left, right, (((1,), (1,)), ((), ())), preferred_element_type=F32)


def mm_tn(left, right):
    return lax.dot_general(left, right, (((0,), (0,)), ((), ())), preferred_element_type=F32)


def sigmoid(values):
    return 1.0 / (1.0 + jnp.exp(-values))


def whole(shape):
    return pl.BlockSpec(shape, lambda *_: (0,) * len(shape))


def rows_of(size, width):
    return pl.BlockSpec((size, width), lambda i, *_: (i, 0))


def call(body, grid, in_specs, out_specs, out_shape, scratch, flops, moved, prefetch=0):
    return pl.pallas_call(
        body,
        grid_spec=pltpu.PrefetchScalarGridSpec(
            num_scalar_prefetch=prefetch,
            grid=grid,
            in_specs=in_specs,
            out_specs=out_specs,
            scratch_shapes=scratch,
        ),
        out_shape=out_shape,
        compiler_params=pltpu.CompilerParams(
            dimension_semantics=("arbitrary",), vmem_limit_bytes=VMEM_LIMIT
        ),
        cost_estimate=pl.CostEstimate(flops=flops, bytes_accessed=moved, transcendentals=0),
    )


def shape_of(shape, dtype):
    return jax.ShapeDtypeStruct(shape, dtype)


def project_body(tok, gain, w_proj, w_gate, w_rank, normed, projected, out_gate, low_rank):
    rows = tok[...].astype(F32)
    inverse = lax.rsqrt(jnp.mean(rows * rows, axis=-1, keepdims=True) + EPS_NORM)
    rounded = (rows * inverse * gain[...]).astype(BF16)
    normed[...] = rounded
    projected[...] = mm(rounded, w_proj[...]).astype(BF16)
    out_gate[...] = mm(rounded, w_gate[...]).astype(BF16)
    low_rank[...] = mm(rounded, w_rank[...]).astype(BF16)


def project(tok, gain, w_proj, w_gate, w_rank):
    length, width = tok.shape
    c3, dv, rank = w_proj.shape[1], w_gate.shape[1], w_rank.shape[1]
    return call(
        project_body,
        (length // STEP,),
        [
            rows_of(STEP, width),
            whole((1, width)),
            whole((width, c3)),
            whole((width, dv)),
            whole((width, rank)),
        ],
        [rows_of(STEP, width), rows_of(STEP, c3), rows_of(STEP, dv), rows_of(STEP, rank)],
        [
            shape_of((length, width), BF16),
            shape_of((length, c3), BF16),
            shape_of((length, dv), BF16),
            shape_of((length, rank), BF16),
        ],
        [],
        2 * length * width * (c3 + dv + rank),
        length * (2 * width + c3 + dv) * 2 + width * (c3 + dv) * 2,
    )(tok, gain, w_proj, w_gate, w_rank)


def triangle(lower):
    row = lax.broadcasted_iota(jnp.int32, (CHUNK, CHUNK), 0)
    column = lax.broadcasted_iota(jnp.int32, (CHUNK, CHUNK), 1)
    return row >= column if lower else row <= column


def running_sum(values, lower):
    ones = triangle(lower).astype(F32)
    return lax.dot_general(
        ones, values, (((1,), (0,)), ((), ())), precision=HIGHEST, preferred_element_type=F32
    )


def filter_rows(buffer, taps, count):
    total = taps[0:1, :] * buffer[pl.ds(8 - EDGE, count), :]
    for offset in range(1, CONV):
        total = total + taps[offset : offset + 1, :] * buffer[pl.ds(8 - EDGE + offset, count), :]
    return total


def forward_body(
    projected, halo, low_rank, taps_in, rank_up, bias,
    head_local, query_profile, cumulative, states, before, end_state, total_decay,
    extended, memory, preceding,
):
    step = pl.program_id(0)

    @pl.when(step == 0)
    def _():
        extended[0:8, :] = halo[...]
        memory[...] = jnp.zeros_like(memory)
        preceding[...] = jnp.zeros_like(preceding)

    @pl.when(step > 0)
    def _():
        extended[0:8, :] = extended[STEP : STEP + 8, :]

    extended[8 : 8 + STEP, :] = projected[...].astype(F32)
    filtered = filter_rows(extended, taps_in[...], STEP)
    convolved = (filtered * sigmoid(filtered)).astype(BF16)
    logit = mm(low_rank[...], rank_up[...]) + bias[...]
    decay = (jnp.minimum(logit, 0.0) - jnp.log1p(jnp.exp(-jnp.abs(logit)))) / GATE_NORMALIZER
    width = rank_up.shape[1]
    causal = triangle(True)
    for part in range(STEP // CHUNK):
        rows = slice(part * CHUNK, (part + 1) * CHUNK)
        queries = convolved[rows, :width].astype(F32)
        keys = convolved[rows, width : 2 * width].astype(F32)
        values = convolved[rows, 2 * width :]
        total = running_sum(decay[rows], True)
        middle, last = total[CHUNK // 2 - 1 : CHUNK // 2], total[CHUNK - 1 : CHUNK]
        lifted = (queries * jnp.exp(total - middle)).astype(BF16)
        lowered = (keys * jnp.exp(middle - total)).astype(BF16)
        scores = jnp.where(causal, mm_nt(lifted, lowered), 0.0).astype(BF16)
        entry = memory[...]
        entry_low = entry.astype(BF16)
        states[part] = entry_low
        profile = queries * jnp.exp(total)
        head_local[rows, :] = mm(scores, values) + mm_nt(profile.astype(BF16), entry_low)
        query_profile[rows, :] = (profile * jnp.exp(preceding[...])).astype(BF16)
        cumulative[rows, :] = total
        tails = (keys * jnp.exp(last - total)).astype(BF16)
        memory[...] = entry * jnp.exp(last) + mm_tn(values, tails)
        before[pl.ds(step * (STEP // CHUNK) + part, 1), :] = preceding[...]
        preceding[...] = preceding[...] + last
    end_state[...] = memory[...]
    total_decay[...] = preceding[...]


def forward_mix(projected, halo, low_rank, taps, rank_up, bias, dv):
    length, c3 = projected.shape
    rank, dk = rank_up.shape
    chunks = length // CHUNK
    per_step = STEP // CHUNK
    return call(
        forward_body,
        (length // STEP,),
        [
            rows_of(STEP, c3),
            whole((8, c3)),
            rows_of(STEP, rank),
            whole(taps.shape),
            whole((rank, dk)),
            whole((1, dk)),
        ],
        [
            rows_of(STEP, dv),
            rows_of(STEP, dk),
            rows_of(STEP, dk),
            pl.BlockSpec((per_step, dv, dk), lambda i: (i, 0, 0)),
            whole((chunks, dk)),
            whole((dv, dk)),
            whole((1, dk)),
        ],
        [
            shape_of((length, dv), F32),
            shape_of((length, dk), BF16),
            shape_of((length, dk), F32),
            shape_of((chunks, dv, dk), BF16),
            shape_of((chunks, dk), F32),
            shape_of((dv, dk), F32),
            shape_of((1, dk), F32),
        ],
        [
            pltpu.VMEM((STEP + 8, c3), F32),
            pltpu.VMEM((dv, dk), F32),
            pltpu.VMEM((1, dk), F32),
        ],
        2 * length * (4 * dk * dv + dk * dk) * 8,
        length * (c3 * 2 + dv * 4 + dk * 6) + chunks * dv * dk * 2,
    )(projected, halo, low_rank, taps, rank_up, bias)


def head_rows(head_local, query_profile, entering, scale):
    return (head_local + mm_nt(query_profile, entering.astype(BF16))) * scale


def gate_body(head_local, query_profile, entering, out_gate, gain, gated):
    scale = query_profile.shape[1] ** (-0.5)
    head = head_rows(head_local[...], query_profile[...], entering[...], scale)
    inverse = lax.rsqrt(jnp.mean(head * head, axis=-1, keepdims=True) + EPS_HEAD)
    logits = out_gate[...].astype(F32)
    gated[...] = (head * inverse * gain[...] * (logits * sigmoid(logits))).astype(BF16)


def gate(head_local, query_profile, entering, out_gate, gain):
    length, dv = head_local.shape
    dk = query_profile.shape[1]
    return call(
        gate_body,
        (length // STEP,),
        [
            rows_of(STEP, dv),
            rows_of(STEP, dk),
            whole((dv, dk)),
            rows_of(STEP, dv),
            whole((1, dv)),
        ],
        rows_of(STEP, dv),
        shape_of((length, dv), BF16),
        [],
        2 * length * dk * dv * 4,
        length * (dv * 8 + dk * 2),
    )(head_local, query_profile, entering, out_gate, gain)


def ffn_body(
    mine, g0, g1, g2, g3, w0, w1, w2, w3, tok, gain, w_gate, w_up, w_down, upstream,
    normed, hidden, grad_gate, grad_up, out_part, grad_part, own_residual, gain_grad,
):
    del mine
    step = pl.program_id(0)
    mixed = mm(g0[...], w0[...]) + mm(g1[...], w1[...])
    mixed = mixed + mm(g2[...], w2[...]) + mm(g3[...], w3[...])
    residual = tok[...].astype(F32) + mixed

    @pl.when(step == 0)
    def _():
        own_residual[...] = residual
        gain_grad[...] = jnp.zeros_like(gain_grad)

    inverse = lax.rsqrt(jnp.mean(residual * residual, axis=-1, keepdims=True) + EPS_NORM)
    unit = residual * inverse
    rounded = (unit * gain[...]).astype(BF16)
    normed[...] = rounded
    gate_rows = mm(rounded, w_gate[...])
    up_rows = mm(rounded, w_up[...])
    share = sigmoid(gate_rows)
    swished = gate_rows * share
    hidden_rows = (swished * up_rows).astype(BF16)
    hidden[...] = hidden_rows
    out_part[0] = mm(hidden_rows, w_down[...]).astype(BF16)
    grad_hidden = mm_nt(upstream[...], w_down[...])
    slope = share * (1.0 + gate_rows * (1.0 - share))
    grad_gate_rows = (grad_hidden * up_rows * slope).astype(BF16)
    grad_up_rows = (grad_hidden * swished).astype(BF16)
    grad_gate[...] = grad_gate_rows
    grad_up[...] = grad_up_rows
    grad_rows = mm_nt(grad_gate_rows, w_gate[...]) + mm_nt(grad_up_rows, w_up[...])
    grad_part[0] = grad_rows.astype(BF16)
    gain_grad[...] += jnp.sum(grad_rows * unit, axis=0, keepdims=True)


def feed_forward(mine, gathered, weights, tok, gain, w_gate, w_up, w_down, upstream):
    length, width = tok.shape
    dv, units = gathered[0].shape[1], w_gate.shape[1]
    quarter = length // 4

    def natural(size, columns):
        return pl.BlockSpec((size, columns), lambda i, m: (i ^ m[0], 0))

    slot = pl.BlockSpec((1, quarter, width), lambda i, m: (i, 0, 0))
    return call(
        ffn_body,
        (4,),
        [natural(quarter, dv)] * 4
        + [whole((dv, width))] * 4
        + [
            natural(quarter, width),
            whole((1, width)),
            whole((width, units)),
            whole((width, units)),
            whole((units, width)),
            natural(quarter, width),
        ],
        [
            natural(quarter, width),
            natural(quarter, units),
            natural(quarter, units),
            natural(quarter, units),
            slot,
            slot,
            whole((quarter, width)),
            whole((1, width)),
        ],
        [
            shape_of((length, width), BF16),
            shape_of((length, units), BF16),
            shape_of((length, units), BF16),
            shape_of((length, units), BF16),
            shape_of((4, quarter, width), BF16),
            shape_of((4, quarter, width), BF16),
            shape_of((quarter, width), F32),
            shape_of((1, width), F32),
        ],
        [],
        2 * length * width * (4 * dv + 6 * units),
        length * (6 * width + 3 * units) * 2 + 3 * units * width * 2 + 4 * dv * width * 2,
        prefetch=1,
    )(mine, *gathered, *weights, tok, gain, w_gate, w_up, w_down, upstream)


def ungate_body(
    mine, r0, r1, r2, r3, head_local, query_profile, entering, out_gate, gain,
    grad_out_gate, grad_head, state_grad, gain_grad,
):
    step = pl.program_id(0)

    @pl.when(step == 0)
    def _():
        state_grad[...] = jnp.zeros_like(state_grad)
        gain_grad[...] = jnp.zeros_like(gain_grad)

    source = step ^ mine[0]
    grad_gated = jnp.where(
        source < 2,
        jnp.where(source == 0, r0[...], r1[...]),
        jnp.where(source == 2, r2[...], r3[...]),
    ).astype(F32)
    scale = query_profile.shape[1] ** (-0.5)
    head = head_rows(head_local[...], query_profile[...], entering[...], scale)
    inverse = lax.rsqrt(jnp.mean(head * head, axis=-1, keepdims=True) + EPS_HEAD)
    unit = head * inverse
    logits = out_gate[...].astype(F32)
    share = sigmoid(logits)
    slope = share * (1.0 + logits * (1.0 - share))
    grad_out_gate[...] = (grad_gated * unit * gain[...] * slope).astype(BF16)
    grad_normed = grad_gated * (logits * share)
    gain_grad[...] += jnp.sum(grad_normed * unit, axis=0, keepdims=True)
    scaled = grad_normed * gain[...]
    through = inverse * (scaled - unit * jnp.mean(scaled * unit, axis=-1, keepdims=True))
    rounded = (through * scale).astype(BF16)
    grad_head[...] = rounded
    state_grad[...] += mm_tn(rounded, query_profile[...])


def ungate(mine, received, head_local, query_profile, entering, out_gate, gain):
    length, dv = head_local.shape
    dk = query_profile.shape[1]
    quarter = length // 4
    return call(
        ungate_body,
        (4,),
        [whole((quarter, dv))] * 4
        + [
            rows_of(quarter, dv),
            rows_of(quarter, dk),
            whole((dv, dk)),
            rows_of(quarter, dv),
            whole((1, dv)),
        ],
        [rows_of(quarter, dv), rows_of(quarter, dv), whole((dv, dk)), whole((1, dv))],
        [
            shape_of((length, dv), BF16),
            shape_of((length, dv), BF16),
            shape_of((dv, dk), F32),
            shape_of((1, dv), F32),
        ],
        [],
        2 * length * dk * dv * 8,
        length * (dv * 12 + dk * 2),
        prefetch=1,
    )(mine, *received, head_local, query_profile, entering, out_gate, gain)


def backward_body(
    projected, earlier, halo, low_rank, taps_in, rank_up, bias, cumulative, states, before,
    entering, leaving, grad_head,
    grad_projected, grad_low_rank, first_rows, filter_grad, rank_up_grad, bias_grad,
    extended, grad_extended, upstream,
):
    back = pl.program_id(0)
    step = pl.num_programs(0) - 1 - back
    per_step = STEP // CHUNK

    @pl.when(back == 0)
    def _():
        upstream[...] = leaving[...]
        grad_extended[STEP : STEP + 8, :] = jnp.zeros_like(grad_extended[STEP : STEP + 8, :])
        filter_grad[...] = jnp.zeros_like(filter_grad)
        rank_up_grad[...] = jnp.zeros_like(rank_up_grad)
        bias_grad[...] = jnp.zeros_like(bias_grad)

    @pl.when(back > 0)
    def _():
        grad_extended[STEP : STEP + 8, :] = grad_extended[0:8, :]

    @pl.when(step == 0)
    def _():
        extended[0:8, :] = halo[...]

    @pl.when(step > 0)
    def _():
        extended[0:8, :] = earlier[...].astype(F32)[8:16, :]

    extended[8 : 8 + STEP, :] = projected[...].astype(F32)
    taps = taps_in[...]
    filtered = filter_rows(extended, taps, STEP)
    share = sigmoid(filtered)
    convolved = (filtered * share).astype(BF16)
    slope = share * (1.0 + filtered * (1.0 - share))
    logit = mm(low_rank[...], rank_up[...]) + bias[...]
    width = rank_up.shape[1]
    causal = triangle(True)
    logit_grads = [None] * per_step
    for part in reversed(range(per_step)):
        rows = slice(part * CHUNK, (part + 1) * CHUNK)
        queries = convolved[rows, :width].astype(F32)
        keys = convolved[rows, width : 2 * width].astype(F32)
        values = convolved[rows, 2 * width :]
        grad_rows = grad_head[rows, :]
        total = cumulative[rows, :]
        middle, last = total[CHUNK // 2 - 1 : CHUNK // 2], total[CHUNK - 1 : CHUNK]
        lift, lower = jnp.exp(total - middle), jnp.exp(middle - total)
        inner, outer, whole_decay = jnp.exp(total), jnp.exp(last - total), jnp.exp(last)
        lifted, lowered = (queries * lift).astype(BF16), (keys * lower).astype(BF16)
        profile, tails = (queries * inner).astype(BF16), (keys * outer).astype(BF16)
        previous = before[pl.ds(step * per_step + part, 1), :]
        state = states[part].astype(F32) + entering[...] * jnp.exp(previous)
        scores = jnp.where(causal, mm_nt(lifted, lowered), 0.0).astype(BF16)
        grad_scores = jnp.where(causal, mm_nt(grad_rows, values), 0.0).astype(BF16)
        later = upstream[...]
        later_low = later.astype(BF16)
        grad_values = mm_tn(scores, grad_rows) + mm_nt(tails, later_low)
        grad_lifted = mm(grad_scores, lowered)
        grad_lowered = mm_tn(grad_scores, lifted)
        grad_profile = mm(grad_rows, state.astype(BF16))
        grad_tails = mm(values, later_low)
        upstream[...] = later * whole_decay + mm_tn(grad_rows, profile)
        tail_terms = tails.astype(F32) * grad_tails
        grad_total = (
            lifted.astype(F32) * grad_lifted
            - lowered.astype(F32) * grad_lowered
            + profile.astype(F32) * grad_profile
            - tail_terms
        )
        grad_last = jnp.sum(tail_terms, axis=0, keepdims=True) + whole_decay * jnp.sum(
            later * state, axis=0, keepdims=True
        )
        grad_decay = running_sum(grad_total, False) + grad_last
        logit_grads[part] = grad_decay / GATE_NORMALIZER * sigmoid(-logit[rows])
        grad_extended[rows, :width] = (grad_lifted * lift + grad_profile * inner) * slope[rows, :width]
        grad_extended[rows, width : 2 * width] = (
            grad_lowered * lower + grad_tails * outer
        ) * slope[rows, width : 2 * width]
        grad_extended[rows, 2 * width :] = grad_values * slope[rows, 2 * width :]
    logit_grad = jnp.concatenate(logit_grads, axis=0)
    logit_low = logit_grad.astype(BF16)
    bias_grad[...] += jnp.sum(logit_grad, axis=0, keepdims=True)
    rank_up_grad[...] += mm_tn(low_rank[...], logit_low)
    grad_low_rank[...] = mm_nt(logit_low, rank_up[...]).astype(BF16)
    total_rows = taps[EDGE : EDGE + 1, :] * grad_extended[0:STEP, :]
    for offset in range(EDGE):
        total_rows = total_rows + taps[offset : offset + 1, :] * grad_extended[
            pl.ds(EDGE - offset, STEP), :
        ]
    grad_projected[...] = total_rows.astype(BF16)
    grad_filtered = grad_extended[0:STEP, :]
    for offset in range(CONV):
        filter_grad[offset : offset + 1, :] += jnp.sum(
            grad_filtered * extended[pl.ds(8 - EDGE + offset, STEP), :], axis=0, keepdims=True
        )
    first_rows[...] = grad_extended[0:8, :]


def backward_mix(
    projected, halo, low_rank, taps, rank_up, bias, cumulative, states, before, entering,
    leaving, grad_head,
):
    length, c3 = projected.shape
    rank, dk = rank_up.shape
    dv = grad_head.shape[1]
    chunks, per_step, steps = length // CHUNK, STEP // CHUNK, length // STEP

    def reverse(size, width):
        return pl.BlockSpec((size, width), lambda i: (steps - 1 - i, 0))

    return call(
        backward_body,
        (steps,),
        [
            reverse(STEP, c3),
            pl.BlockSpec(
                (16, c3), lambda i: (jnp.maximum((steps - 1 - i) * (STEP // 16) - 1, 0), 0)
            ),
            whole((8, c3)),
            reverse(STEP, rank),
            whole(taps.shape),
            whole((rank, dk)),
            whole((1, dk)),
            reverse(STEP, dk),
            pl.BlockSpec((per_step, dv, dk), lambda i: (steps - 1 - i, 0, 0)),
            whole((chunks, dk)),
            whole((dv, dk)),
            whole((dv, dk)),
            reverse(STEP, dv),
        ],
        [
            reverse(STEP, c3),
            reverse(STEP, rank),
            whole((8, c3)),
            whole(taps.shape),
            whole((rank, dk)),
            whole((1, dk)),
        ],
        [
            shape_of((length, c3), BF16),
            shape_of((length, rank), BF16),
            shape_of((8, c3), F32),
            shape_of(taps.shape, F32),
            shape_of((rank, dk), F32),
            shape_of((1, dk), F32),
        ],
        [
            pltpu.VMEM((STEP + 8, c3), F32),
            pltpu.VMEM((STEP + 8, c3), F32),
            pltpu.VMEM((dv, dk), F32),
        ],
        2 * length * (12 * dk * dv) * 8,
        length * (c3 * 4 + dk * 4 + dv * 2) + chunks * dv * dk * 2,
    )(
        projected, projected, halo, low_rank, taps, rank_up, bias, cumulative, states, before,
        entering, leaving, grad_head,
    )


def input_grad_body(
    mine, grad_projected, grad_out_gate, grad_low_rank, w_proj, w_gate, w_rank, normed,
    parts, gain_grad,
):
    del mine

    @pl.when(pl.program_id(0) == 0)
    def _():
        gain_grad[...] = jnp.zeros_like(gain_grad)

    total = mm_nt(grad_projected[...], w_proj[...]) + mm_nt(grad_out_gate[...], w_gate[...])
    total = total + mm_nt(grad_low_rank[...], w_rank[...])
    parts[0] = total.astype(BF16)
    gain_grad[...] += jnp.sum(total * normed[...].astype(F32), axis=0, keepdims=True)


def input_grad(mine, grad_projected, grad_out_gate, grad_low_rank, w_proj, w_gate, w_rank, normed):
    length, width = normed.shape
    c3, dv, rank = w_proj.shape[1], w_gate.shape[1], w_rank.shape[1]
    quarter = length // 4

    def natural(columns):
        return pl.BlockSpec((quarter, columns), lambda i, m: (i ^ m[0], 0))

    return call(
        input_grad_body,
        (4,),
        [
            natural(c3),
            natural(dv),
            natural(rank),
            whole((width, c3)),
            whole((width, dv)),
            whole((width, rank)),
            natural(width),
        ],
        [pl.BlockSpec((1, quarter, width), lambda i, m: (i, 0, 0)), whole((1, width))],
        [shape_of((4, quarter, width), BF16), shape_of((1, width), F32)],
        [],
        2 * length * width * (c3 + dv + rank),
        length * (2 * width + c3 + dv) * 2 + width * (c3 + dv) * 2,
        prefetch=1,
    )(mine, grad_projected, grad_out_gate, grad_low_rank, w_proj, w_gate, w_rank, normed)


ACROSS = [(i, i ^ 1) for i in range(4)]
DOWN = [(i, i ^ 2) for i in range(4)]
OPPOSITE = [(i, i ^ 3) for i in range(4)]


def gather_relative(block):
    half = block.shape[0] // 2
    across = lax.ppermute(block, "mp", ACROSS)
    down = lax.ppermute(block, "mp", DOWN)
    first = lax.ppermute(across[:half], "mp", DOWN)
    second = lax.ppermute(down[half:], "mp", ACROSS)
    return [block, across, down, jnp.concatenate([first, second], axis=0)]


def scatter_relative(parts):
    half = parts.shape[1] // 2
    via_across = lax.ppermute(parts[3, :half], "mp", ACROSS)
    via_down = lax.ppermute(parts[3, half:], "mp", DOWN)
    across_a = lax.ppermute(parts[1, :half], "mp", ACROSS)
    down_b = lax.ppermute(parts[2, half:], "mp", DOWN)
    across_b = lax.ppermute(parts[1, half:] + via_down, "mp", ACROSS)
    down_a = lax.ppermute(parts[2, :half] + via_across, "mp", DOWN)
    across = jnp.concatenate([across_a, across_b], axis=0).astype(F32)
    down = jnp.concatenate([down_a, down_b], axis=0).astype(F32)
    return parts[0].astype(F32) + across + down


def passed_along(block, axis, distance):
    devices = range(lax.axis_size(axis))
    route = [(i - distance, i) for i in devices if i - distance in devices]
    return lax.ppermute(block, axis, route)


def chain_states(decay, state, backward):
    count, mine = lax.axis_size("seq"), lax.axis_index("seq")
    if count == 2:
        return passed_along(state, "seq", -1 if backward else 1)
    decays, states = lax.all_gather(decay, "seq"), lax.all_gather(state, "seq")
    if backward:
        decays, states, mine = decays[::-1], states[::-1], count - 1 - mine

    def hop(position, subtotal):
        longer = subtotal * jnp.exp(decays[position]) + states[position]
        return jnp.where(position < mine, longer, subtotal)

    return lax.fori_loop(0, count - 1, hop, jnp.zeros_like(state))


def sum_shards(grad):
    if lax.axis_size("seq") != 2 or lax.axis_size("dp") != 4:
        total = lax.psum_scatter(grad, ("seq", "dp"), scatter_dimension=0, tiled=True)
        return total[0].astype(F32)
    side, place = lax.axis_index("seq"), lax.axis_index("dp")
    other = lax.dynamic_slice_in_dim(grad, (1 - side) * 4, 4, 0)
    kept = lax.dynamic_slice_in_dim(grad, side * 4, 4, 0)
    kept = kept + lax.ppermute(other, "seq", [(0, 1), (1, 0)])
    upward, downward = None, None
    for turn in range(1, 4):
        above = lax.dynamic_index_in_dim(kept, jnp.minimum(place + 4 - turn, 3), 0, False)
        below = lax.dynamic_index_in_dim(kept, jnp.maximum(place - 4 + turn, 0), 0, False)
        if turn > 1:
            above, below = above + upward, below + downward
        upward = lax.ppermute(above, "dp", [(i, i + 1) for i in range(turn)])
        downward = lax.ppermute(below, "dp", [(3 - i, 2 - i) for i in range(turn)])
    mine = lax.dynamic_index_in_dim(kept, place, 0, False)
    return mine.astype(F32) + upward.astype(F32) + downward.astype(F32)


def sum_over(values, axes):
    for axis in axes:
        count = lax.axis_size(axis)
        if count & (count - 1) or count > 4:
            values = lax.psum(values, axis)
            continue
        distance = 1
        while distance < count:
            values = values + lax.ppermute(values, axis, [(i, i ^ distance) for i in range(count)])
            distance *= 2
    return values


def on_device(
    tokens, lengths, mixer_gain, project_weight, filter_weight, rank_down, rank_up, decay_bias,
    gate_weight, head_gain, output_weight, channel_gain, hidden_gate, hidden_up, hidden_down,
    cotangent,
):
    length, sequences, width = tokens.shape
    shards = lax.axis_size("seq") * lax.axis_size("dp")
    shard = lax.axis_index("seq") * lax.axis_size("dp") + lax.axis_index("dp")
    me = lax.axis_index("mp")
    mine = me.astype(jnp.int32).reshape(1)
    own_rows = length // lax.axis_size("mp")
    w_proj = project_weight[:, 0]
    taps = filter_weight[:, 0].astype(F32)
    rank_up_here = rank_up[:, 0]
    bias = decay_bias.astype(F32)
    mixer_gain_f = mixer_gain.astype(F32)[None]
    channel_gain_f = channel_gain.astype(F32)[None]
    head_gain_f = head_gain.astype(F32)[None]
    dv = gate_weight.shape[1]
    positions = lax.axis_index("seq") * length + lax.broadcasted_iota(jnp.int32, (length, 1), 0)

    edge_tokens = passed_along(tokens[length - EDGE :], "seq", 1)
    edge_f = edge_tokens.astype(F32)
    edge_inverse = lax.rsqrt(jnp.mean(edge_f * edge_f, axis=-1, keepdims=True) + EPS_NORM)
    edge_normed = (edge_f * edge_inverse * mixer_gain_f).astype(BF16)
    edge_projected = jnp.einsum(
        "psd,dc->psc", edge_normed, w_proj, preferred_element_type=F32
    ).astype(BF16)
    halos = jnp.pad(edge_projected.astype(F32), ((8 - EDGE, 0), (0, 0), (0, 0)))

    output_weights = gather_relative(output_weight)
    turns = range(sequences)
    toks = [tokens[:, s] for s in turns]
    masks = [positions < lengths[s] for s in turns]
    upstreams = [jnp.where(masks[s], cotangent[:, s], jnp.zeros((), BF16)) for s in turns]
    fronts = [project(toks[s], mixer_gain_f, w_proj, gate_weight, rank_down) for s in turns]
    mixes = []
    for s in turns:
        _, projected, _, low_rank = fronts[s]
        mixes.append(forward_mix(projected, halos[:, s], low_rank, taps, rank_up_here, bias, dv))
    enterings = [chain_states(mixes[s][6], mixes[s][5], False) for s in turns]
    gateds, gathered = [], []
    for s in turns:
        gateds.append(gate(mixes[s][0], mixes[s][1], enterings[s], fronts[s][2], head_gain_f))
        gathered.append(gather_relative(gateds[s]))
    ffns = [
        feed_forward(
            mine, gathered[s], output_weights, toks[s], channel_gain_f, hidden_gate, hidden_up,
            hidden_down, upstreams[s],
        )
        for s in turns
    ]

    grad_residuals, grad_mixers, backs = [], [], []
    for s in turns:
        residual = ffns[s][6]
        grad_normed = scatter_relative(ffns[s][5])
        inverse = lax.rsqrt(jnp.mean(residual * residual, axis=-1, keepdims=True) + EPS_NORM)
        unit = residual * inverse
        scaled = grad_normed * channel_gain_f
        through = inverse * (scaled - unit * jnp.mean(scaled * unit, axis=-1, keepdims=True))
        own_upstream = lax.dynamic_slice_in_dim(upstreams[s], me * own_rows, own_rows, 0)
        grad_residual = own_upstream.astype(F32) + through
        grad_mixer = grad_residual.astype(BF16)
        grad_residuals.append(grad_residual)
        grad_mixers.append(grad_mixer)
        pieces = [mm_nt(grad_mixer, weight).astype(BF16) for weight in output_weights]
        received = [
            pieces[0],
            lax.ppermute(pieces[1], "mp", ACROSS),
            lax.ppermute(pieces[2], "mp", DOWN),
            lax.ppermute(pieces[3], "mp", OPPOSITE),
        ]
        grad_out_gate, grad_head, state_grad, head_gain_part = ungate(
            mine, received, mixes[s][0], mixes[s][1], enterings[s], fronts[s][2], head_gain_f
        )
        leaving = chain_states(mixes[s][6], state_grad, True)
        grads = backward_mix(
            fronts[s][1], halos[:, s], fronts[s][3], taps, rank_up_here, bias, mixes[s][2],
            mixes[s][3], mixes[s][4], enterings[s], leaving, grad_head,
        )
        first = grads[2]
        edge = jnp.concatenate(
            [
                sum(taps[j : j + 1] * first[i - j : i - j + 1] for j in range(i + 1))
                for i in range(EDGE)
            ],
            axis=0,
        )
        edge = passed_along(edge, "seq", -1)
        grad_projected = grads[0]
        tail = grad_projected[length - 16 :].astype(F32) + jnp.pad(edge, ((16 - EDGE, 0), (0, 0)))
        grad_projected = lax.dynamic_update_slice_in_dim(
            grad_projected, tail.astype(BF16), length - 16, 0
        )
        parts, mixer_gain_part = input_grad(
            mine, grad_projected, grad_out_gate, grads[1], w_proj, gate_weight, rank_down,
            fronts[s][0],
        )
        backs.append((grad_projected, grad_out_gate, grads, head_gain_part, parts, mixer_gain_part))

    def weight_grad(lefts, rights):
        return sum(mm_tn(left, right) for left, right in zip(lefts, rights))

    def in_shards(grad):
        return grad.astype(BF16).reshape(shards, width // shards, grad.shape[-1])

    hidden_grads = jnp.stack(
        [
            in_shards(weight_grad([f[0] for f in ffns], [f[2] for f in ffns])),
            in_shards(weight_grad([f[0] for f in ffns], [f[3] for f in ffns])),
            in_shards(weight_grad(upstreams, [f[1] for f in ffns])),
        ],
        axis=1,
    )
    hidden_grads = sum_shards(hidden_grads)

    output_parts = []
    for slot in range(4):
        own_gated = [
            lax.dynamic_slice_in_dim(gathered[s][slot], me * own_rows, own_rows, 0) for s in turns
        ]
        output_parts.append(weight_grad(grad_mixers, own_gated).astype(BF16))
    output_grad = scatter_relative(jnp.stack(output_parts))
    normed_rows = [front[0] for front in fronts]
    mixer_grads = jnp.concatenate(
        [
            in_shards(weight_grad(normed_rows, [b[0] for b in backs])),
            in_shards(weight_grad(normed_rows, [b[1] for b in backs])),
            in_shards(output_grad),
        ],
        axis=-1,
    )
    mixer_grads = sum_shards(mixer_grads)
    c3 = w_proj.shape[1]

    rank_down_part = weight_grad(normed_rows, [b[2][1] for b in backs])
    shared = [
        sum(b[5] for b in backs)[0] / mixer_gain_f[0],
        sum(f[7] for f in ffns)[0],
        sum(b[3] for b in backs)[0],
        rank_down_part.reshape(-1),
    ]
    local = [
        sum(b[2][3] for b in backs).reshape(-1),
        sum(b[2][4] for b in backs).reshape(-1),
        sum(b[2][5] for b in backs).reshape(-1),
    ]
    shared_size = sum(part.shape[0] for part in shared)
    small = sum_over(jnp.concatenate(shared + local), ("seq", "dp"))
    shared_sum = sum_over(small[:shared_size], ("mp",))

    def take(values, start, shape):
        count = 1
        for size in shape:
            count *= size
        return lax.slice_in_dim(values, start, start + count).reshape(shape)

    def own(values):
        share = values.shape[-1] // shards
        return lax.dynamic_slice_in_dim(values, shard * share, share, values.ndim - 1)

    mixer_gain_grad = take(shared_sum, 0, (width,))
    channel_gain_grad = take(shared_sum, width, (width,))
    head_gain_grad = take(shared_sum, 2 * width, (dv,))
    rank_down_grad = take(shared_sum, 2 * width + dv, rank_down.shape)
    filter_grad = own(take(small, shared_size, filter_weight.shape))
    start = shared_size + filter_weight.size
    rank_up_grad = own(take(small, start, rank_up.shape))
    decay_bias_grad = own(take(small, start + rank_up.size, decay_bias.shape))

    outputs, token_grads = [], []
    for s in turns:
        ffn_out = scatter_relative(ffns[s][4])
        own_mask = lax.dynamic_slice_in_dim(masks[s], me * own_rows, own_rows, 0)
        outputs.append(jnp.where(own_mask, ffns[s][6] + ffn_out, 0.0).astype(BF16))
        grad_normed = scatter_relative(backs[s][4])
        rows = lax.dynamic_slice_in_dim(toks[s], me * own_rows, own_rows, 0).astype(F32)
        inverse = lax.rsqrt(jnp.mean(rows * rows, axis=-1, keepdims=True) + EPS_NORM)
        unit = rows * inverse
        scaled = grad_normed * mixer_gain_f
        through = inverse * (scaled - unit * jnp.mean(scaled * unit, axis=-1, keepdims=True))
        token_grads.append(grad_residuals[s] + through)
    return (
        jnp.stack(outputs, axis=1),
        jnp.stack(token_grads, axis=1),
        mixer_gain_grad,
        mixer_grads[:, None, :c3],
        filter_grad,
        rank_down_grad,
        rank_up_grad,
        decay_bias_grad,
        mixer_grads[:, c3 : c3 + dv],
        head_gain_grad,
        mixer_grads[:, c3 + dv :].T,
        channel_gain_grad,
        hidden_grads[0],
        hidden_grads[1],
        hidden_grads[2].T,
    )


def solution(mesh):
    in_specs = (
        P("seq", "dp", None),
        P("dp"),
        P(),
        P(None, "mp", None),
        P(None, "mp", None),
        P(),
        P(None, "mp", None),
        P("mp", None),
        P(None, "mp"),
        P(),
        P("mp", None),
        P(),
        P(None, "mp"),
        P(None, "mp"),
        P("mp", None),
        P("seq", "dp", None),
    )
    out_specs = (
        P(("seq", "mp"), "dp", None),
        P(("seq", "mp"), "dp", None),
        P(),
        P(("seq", "dp"), "mp", None),
        P(None, "mp", ("seq", "dp")),
        P(),
        P(None, "mp", ("seq", "dp")),
        P("mp", ("seq", "dp")),
        P(("seq", "dp"), "mp"),
        P(),
        P("mp", ("seq", "dp")),
        P(),
        P(("seq", "dp"), "mp"),
        P(("seq", "dp"), "mp"),
        P("mp", ("seq", "dp")),
    )
    return jax.shard_map(
        on_device, mesh=mesh, in_specs=in_specs, out_specs=out_specs, check_vma=False
    )
```

time: 1630 us -> 487 us (0.30)
  waiting for transfers between devices: 792 us -> 68.2 us
  matrix products: 467 us -> 42.1 us
  Pallas kernels: 0 us -> 124 us
  starting transfers between devices: 5.4 us -> 121 us
  other arithmetic: 149 us -> 37.8 us
  local copies, waits for them, and re-layouts: 135 us -> 81.6 us
  blocking collectives: 49.2 us -> 0 us
    reduce_scatter x10 -> x0, waiting for transfers between devices: 601 us -> none  [the longest x1 86.5 us: on_device(): lax.psum_scatter(quick('pbf,fd->pbd', hidden, hidden_down), 'mp', scatter...]
    dot_general x251 -> x29, matrix products: 467 us -> 42.1 us  [the longest x20 36.6 us: mm_tn(): lax.dot_general(left, right, (((0,), (0,)), ((), ())), preferred_element_...]
    pallas_call x0 -> x14, Pallas kernels: none -> 124 us  [the longest x2 44.4 us: feed_forward(): call(ffn_body, (4,), [natural(quarter, dv)] * 4 + [whole((dv, width))] *...]
    psum x1 -> x0, waiting for transfers between devices: 124 us -> none  [on_device(): lax.psum((mixer_gain_grad, channel_gain_grad, head_gain_grad, rank_down_p...]
    ppermute x0 -> x79, starting transfers between devices: none -> 112 us  [the longest x6 24.3 us: sum_shards(): upward = lax.ppermute(above, 'dp', [(i, i + 1) for i in range(turn)])]
    ppermute x0 -> x79, waiting for transfers between devices: none -> 67.8 us  [the longest x6 15.2 us: sum_shards(): upward = lax.ppermute(above, 'dp', [(i, i + 1) for i in range(turn)])]
    dynamic_update_slice x48 -> x0, local copies, waits for them, and re-layouts: 63 us -> none  [mix_local(): lax.scan(advance, start_memory, (in_blocks(queries), in_blocks(key_rows),...]
    all_gather x2 -> x0, waiting for transfers between devices: 51.6 us -> none  [the longest x1 51.6 us: on_device(): ffn_normed = lax.all_gather(ffn_rows_normed, 'mp', axis=0, tiled=True)]
  transfers between devices with their start and end apart: 18 -> 86, of which waited for: 13 -> 32; matrix products, arithmetic and copies ran while one was open for 15% -> 30% of each run, Pallas kernels for 0% -> 26%
where the time goes in v1:
time: 487 us; the launch traced here: 478 us
  Pallas kernels  124 us (25%)
  starting transfers between devices  121 us (25%)
  local copies, waits for them, and re-layouts  81.6 us (17%)
  waiting for transfers between devices  68.2 us (14%)
  matrix products  42.1 us (9%)
  other arithmetic  37.8 us (8%)
    pallas_call x2, Pallas kernels, feed_forward(): call(ffn_body, (4,), [natural(quarter, dv)] * 4 + [whole((dv, width))] *...  44.4 us
    dot_general x20, matrix products, mm_tn(): lax.dot_general(left, right, (((0,), (0,)), ((), ())), preferred_element_...  36.6 us
    unnamed x193, local copies, waits for them, and re-layouts  35.2 us
    ppermute x6, starting transfers between devices, sum_shards(): upward = lax.ppermute(above, 'dp', [(i, i + 1) for i in range(turn)])  24.3 us
    pallas_call x2, Pallas kernels, backward_mix(): call(backward_body, (steps,), [reverse(STEP, c3), pl.BlockSpec((16, c3),...  20.8 us
    ppermute x6, waiting for transfers between devices, sum_shards(): upward = lax.ppermute(above, 'dp', [(i, i + 1) for i in range(turn)])  15.2 us
    pallas_call x2, Pallas kernels, forward_mix(): call(forward_body, (length // STEP,), [rows_of(STEP, c3), whole((8, c3)),...  14.7 us
    pallas_call x2, Pallas kernels, input_grad(): call(input_grad_body, (4,), [natural(c3), natural(dv), natural(rank), who...  13.2 us
  transfers between devices with their start and end apart: 86, of which 32 were waited for; matrix products, arithmetic and copies ran while one was open for 30% of the time, Pallas kernels for 26%

profile of v1, /device:TPU:0, one launch (start us, length us, event | category | flops | bytes accessed | tf_op | source)
XLA Modules:
  0.0 477.9 jit_solution(90115174729112903)
XLA Ops:
  0.6 3.0 collective-permute-start.7
  7.2 10.1 %fusion.87 = (bf16[1024,1,1024]{2,1,0:T(2,128)(2,1)}, bf16[1024,1,1024]{2,1,0:T(2,128)(2,1)}) fusion(bf16[1024,2,1024]{2,1,0:T(2,128)(2,1)} %param.16), kind=kLoop, calls=%fused_computation.254 | loop fusion | bytes 8388608 | tf_op jit(solution)/shard_map/slice | solution.py:719
  20.1 10.2 %fusion.86 = (bf16[1024,1,1024]{2,1,0:T(2,128)(2,1)}, bf16[1024,1,1024]{2,1,0:T(2,128)(2,1)}) fusion(bf16[1024,2,1024]{2,1,0:T(2,128)(2,1)} %param.31), kind=kLoop, calls=%fused_computation.253 | loop fusion | bytes 8388608 | tf_op jit(solution)/shard_map/slice | solution.py:721
  30.3 2.1 copy.97
  33.2 2.1 copy.96
  36.0 4.3 fusion.1.upstream
  40.3 6.0 %shard_map.275 = (bf16[1024,1024]{1,0:T(8,128)(2,1)}, bf16[1024,512]{1,0:T(8,128)(2,1)}, bf16[1024,256]{1,0:T(8,128)(2,1)}, bf16[1024,16]{1,0:T(8,128)(2,1)}) custom-call(bf16[1024,1024]{1,0:T(8,128)(2,1)} %bitcast.325, f32[1,1024]{1,0:T(1,128)} %bitcast.336, bf16[1024,512]{1,0:T(8,128)(2,1)} %bitcast.329, bf16[1024,256]{1,0:T(8,128)(2,1)} %w_gate.9, ...), custom_call_target="tpu_custom_call" | custom-call | flops 1644167168 | bytes 7340032 | tf_op jit(solution)/shard_map/pallas_call | solution.py:82
  46.3 6.1 %shard_map.271 = (bf16[1024,1024]{1,0:T(8,128)(2,1)}, bf16[1024,512]{1,0:T(8,128)(2,1)}, bf16[1024,256]{1,0:T(8,128)(2,1)}, bf16[1024,16]{1,0:T(8,128)(2,1)}) custom-call(bf16[1024,1024]{1,0:T(8,128)(2,1)} %bitcast.327, f32[1,1024]{1,0:T(1,128)} %bitcast.337, bf16[1024,512]{1,0:T(8,128)(2,1)} %bitcast.330, bf16[1024,256]{1,0:T(8,128)(2,1)} %w_gate.9, ...), custom_call_target="tpu_custom_call" | custom-call | flops 1644167168 | bytes 7340032 | tf_op jit(solution)/shard_map/pallas_call | solution.py:82
  54.0 7.3 %shard_map.276 = (f32[1024,256]{1,0:T(8,128)}, bf16[1024,128]{1,0:T(8,128)(2,1)}, f32[1024,128]{1,0:T(8,128)}, bf16[8,256,128]{2,1,0:T(8,128)(2,1)}, f32[8,128]{...) custom-call(bf16[1024,512]{1,0:T(8,128)(2,1)} %get-tuple-element.83.projected.earlier, ...), custom_call_target="tpu_custom_call" | custom-call | flops 2415919104 | bytes 3407872 | tf_op jit(solution)/shard_map/pallas_call | solution.py:179
  62.7 7.3 %shard_map.272 = (f32[1024,256]{1,0:T(8,128)}, bf16[1024,128]{1,0:T(8,128)(2,1)}, f32[1024,128]{1,0:T(8,128)}, bf16[8,256,128]{2,1,0:T(8,128)(2,1)}, f32[8,128]{...) custom-call(bf16[1024,512]{1,0:T(8,128)(2,1)} %get-tuple-element.75.projected.earlier, ...), custom_call_target="tpu_custom_call" | custom-call | flops 2415919104 | bytes 3407872 | tf_op jit(solution)/shard_map/pallas_call | solution.py:179
  72.9 4.3 shard_map.277.g0
  78.4 4.1 shard_map.273.g0
  82.8 2.1 fusion.upstream
  85.7 2.2 copy.75
  102.6 2.6 copy.57.w_gate
  105.1 2.6 copy.58.w_up
  117.7 1.8 collective-permute-done.4
  120.5 3.1 collective-permute-done.5
  124.4 22.0 %shard_map.274 = (bf16[1024,1024]{1,0:T(8,128)(2,1)}, bf16[1024,704]{1,0:T(8,128)(2,1)}, bf16[1024,704]{1,0:T(8,128)(2,1)}, bf16[1024,704]{1,0:T(8,128)(2,1)}, b...) custom-call(s32[1]{0:T(128)} %bitcast.1.mine, ...), custom_call_target="tpu_custom_call" | custom-call | flops 11005853696 | bytes 23330816 | tf_op jit(solution)/shard_map/pallas_call | solution.py:297
  146.4 2.3 slice_bitcast_fusion.31
  154.7 22.4 %shard_map.278 = (bf16[1024,1024]{1,0:T(8,128)(2,1)}, bf16[1024,704]{1,0:T(8,128)(2,1)}, bf16[1024,704]{1,0:T(8,128)(2,1)}, bf16[1024,704]{1,0:T(8,128)(2,1)}, b...) custom-call(s32[1]{0:T(128)} %bitcast.1.mine, ...), custom_call_target="tpu_custom_call" | custom-call | flops 11005853696 | bytes 23330816 | tf_op jit(solution)/shard_map/pallas_call | solution.py:297
  180.4 3.3 fusion.97
  206.3 2.0 collective-permute-start.44
  211.9 2.0 collective-permute-start.29
  213.9 2.0 collective-permute-done.24
  217.5 2.0 collective-permute-start.46
  219.5 2.0 collective-permute-done.44
  223.1 1.9 collective-permute-start.15
  228.7 2.0 collective-permute-start.21
  234.4 2.0 collective-permute-start.23
  237.1 8.5 %collective-permute-done.26 = bf16[128,1024]{1,0:T(8,128)(2,1)S(1)} collective-permute-done((bf16[128,1024]{1,0:T(8,128)(2,1)S(1)}, bf16[128,1024]{1,0:T(8,128)(2,1)S(1)}, u32[]{:S(2)}, u32[]{:S(2)}) %collective-permute-start.26) | collective-permute-done | bytes 262176 | tf_op jit(solution)/shard_map/ppermute | solution.py:625
  245.6 2.0 collective-permute-start.10
  249.1 2.1 collective-permute-done.25
  261.9 2.3 fusion.65
  267.4 1.9 collective-permute-start.34
  270.5 2.8 collective-permute-start.35
  282.0 2.0 copy.70
  284.0 1.9 collective-permute-start.71
  288.2 5.3 %shard_map.279 = (bf16[1024,256]{1,0:T(8,128)(2,1)}, bf16[1024,256]{1,0:T(8,128)(2,1)}, f32[256,128]{1,0:T(8,128)}, f32[1,256]{1,0:T(1,128)}) custom-call(s32[1]{0:T(128)} %bitcast.1.mine, bf16[256,256]{1,0:T(8,128)(2,1)} %convolution_convert_fusion.7.r0, bf16[256,256]{1,0:T(8,128)(2,1)} %copy-done.47, bf16[256,256]{1,0:T(8,128)(2,1)} %copy-done.49, ...), custom_call_target="tpu_custom_call" | custom-call | flops 536870912 | bytes 3407872 | tf_op jit(solution)/shard_map/pallas_call | solution.py:375
  296.1 5.5 %shard_map.282 = (bf16[1024,256]{1,0:T(8,128)(2,1)}, bf16[1024,256]{1,0:T(8,128)(2,1)}, f32[256,128]{1,0:T(8,128)}, f32[1,256]{1,0:T(1,128)}) custom-call(s32[1]{0:T(128)} %bitcast.1.mine, bf16[256,256]{1,0:T(8,128)(2,1)} %convolution_convert_fusion.3.r0, bf16[256,256]{1,0:T(8,128)(2,1)} %copy-done.45, bf16[256,256]{1,0:T(8,128)(2,1)} %copy-done.46, ...), custom_call_target="tpu_custom_call" | custom-call | flops 536870912 | bytes 3407872 | tf_op jit(solution)/shard_map/pallas_call | solution.py:375
  301.6 1.9 fusion.94
  306.5 10.4 %shard_map.280 = (bf16[1024,512]{1,0:T(8,128)(2,1)}, bf16[1024,16]{1,0:T(8,128)(2,1)}, f32[8,512]{1,0:T(8,128)}, f32[4,512]{1,0:T(4,128)}, f32[16,128]{1,0:T(8,128)}, /*index=5*/f32[1,128]{1,0:T(1,128)}) custom-call(bf16[1024,512]{1,0:T(8,128)(2,1)} %get-tuple-element.75.projected.earlier, bf16[1024,512]{1,0:T(8,128)(2,1)} %get-tuple-element.75.projected.earlier, ...), custom_call_target="tpu_custom_call" | custom-call | flops 6442450944 | bytes 3670016 | tf_op jit(solution)/shard_map/pallas_call | solution.py:512
  319.1 10.4 %shard_map.283 = (bf16[1024,512]{1,0:T(8,128)(2,1)}, bf16[1024,16]{1,0:T(8,128)(2,1)}, f32[8,512]{1,0:T(8,128)}, f32[4,512]{1,0:T(4,128)}, f32[16,128]{1,0:T(8,128)}, /*index=5*/f32[1,128]{1,0:T(1,128)}) custom-call(bf16[1024,512]{1,0:T(8,128)(2,1)} %get-tuple-element.83.projected.earlier, bf16[1024,512]{1,0:T(8,128)(2,1)} %get-tuple-element.83.projected.earlier, ...), custom_call_target="tpu_custom_call" | custom-call | flops 6442450944 | bytes 3670016 | tf_op jit(solution)/shard_map/pallas_call | solution.py:512
  338.7 4.5 fusion.93
  343.1 6.6 %shard_map.284 = (bf16[4,256,1024]{2,1,0:T(8,128)(2,1)}, f32[1,1024]{1,0:T(1,128)}) custom-call(s32[1]{0:T(128)} %bitcast.1.mine, bf16[1024,512]{1,0:T(8,128)(2,1)} %fusion.72.grad_projected, bf16[1024,256]{1,0:T(8,128)(2,1)} %get-tuple-element.111.grad_out_gate, bf16[1024,16]{1,0:T(8,128)(2,1)} %get-tuple-element.112.grad_low_rank, ...), custom_call_target="tpu_custom_call" | custom-call | flops 1644167168 | bytes 7340032 | tf_op jit(solution)/shard_map/pallas_call | solution.py:585
  351.1 6.5 %shard_map.281 = (bf16[4,256,1024]{2,1,0:T(8,128)(2,1)}, f32[1,1024]{1,0:T(1,128)}) custom-call(s32[1]{0:T(128)} %bitcast.1.mine, bf16[1024,512]{1,0:T(8,128)(2,1)} %fusion.71.grad_projected, bf16[1024,256]{1,0:T(8,128)(2,1)} %get-tuple-element.99.grad_out_gate, bf16[1024,16]{1,0:T(8,128)(2,1)} %get-tuple-element.100.grad_low_rank, ...), custom_call_target="tpu_custom_call" | custom-call | flops 1644167168 | bytes 7340032 | tf_op jit(solution)/shard_map/pallas_call | solution.py:585
  357.7 3.0 add_convert_fusion.3
  365.4 2.5 collective-permute-done.62
  379.3 3.4 collective-permute-done.58
  382.7 2.6 collective-permute-start.63
  386.2 3.4 collective-permute-done.63
  391.6 2.4 collective-permute-done.64
  395.5 3.1 collective-permute-done.65
  409.5 2.6 dynamic-slice_add_fusion
  412.3 3.2 collective-permute-start.73
  422.2 4.4 collective-permute-start.74
  426.6 7.1 %collective-permute-done.80 = bf16[3,128,704]{1,2,0:T(8,128)(2,1)S(1)} collective-permute-done((bf16[3,128,704]{1,2,0:T(8,128)(2,1)S(1)}, bf16[3,128,704]{1,2,0:T(8,128)(2,1)S(1)}, u32[]{:S(2)}, u32[]{:S(2)}) %collective-permute-start.80) | collective-permute-done | bytes 540704 | tf_op jit(solution)/shard_map/ppermute | solution.py:668
  433.9 4.4 collective-permute-start.81
  440.5 4.6 collective-permute-done.81
  448.1 5.0 %collective-permute-start.75 = (bf16[128,1024]{1,0:T(8,128)(2,1)S(1)}, bf16[128,1024]{1,0:T(8,128)(2,1)S(1)}, u32[]{:S(2)}, u32[]{:S(2)}) collective-permute-start(bf16[128,1024]{1,0:T(8,128)(2,1)S(1)} %get-tuple-element.222), channel_id=1, source_target_pairs={{0,1},{1,2},{2,3},{4,5},{5,6},{6,7},{8,9},{9,10},{10,11},{12,13},{... | collective-permute-start | bytes 786440 | tf_op jit(solution)/shard_map/ppermute | solution.py:668
  454.6 2.9 copy.71
  457.6 5.9 %collective-permute-start.82 = (bf16[3,128,704]{1,2,0:T(8,128)(2,1)}, bf16[3,128,704]{1,2,0:T(8,128)(2,1)}, u32[]{:S(2)}, u32[]{:S(2)}) collective-permute-start(bf16[3,128,704]{1,2,0:T(8,128)(2,1)} %get-tuple-element.179), channel_id=1, source_target_pairs={{0,1},{1,2},{2,3},{4,5},{5,6},{6,7},{8,9},{9,10},{10,11},{12,13},{... | collective-permute-start | bytes 1622024 | tf_op jit(solution)/shard_map/ppermute | solution.py:668
  467.5 2.5 collective-permute-done.82
  469.9 5.1 %collective-permute-done.85 = bf16[3,128,704]{1,2,0:T(8,128)(2,1)} collective-permute-done((bf16[3,128,704]{1,2,0:T(8,128)(2,1)S(1)}, bf16[3,128,704]{1,2,0:T(8,128)(2,1)}, u32[]{:S(2)}, u32[]{:S(2)}) %collective-permute-start.85) | collective-permute-done | bytes 540704 | tf_op jit(solution)/shard_map/ppermute | solution.py:669
  (457 shorter events, 184.9 us)
Async XLA Ops:
  0.6 92.5 %collective-permute-start.7 = (bf16[256,1024]{1,0:T(8,128)(2,1)}, bf16[256,1024]{1,0:T(8,128)(2,1)S(1)}, u32[]{:S(2)}, u32[]{:S(2)}) collective-permute-start(bf16[256,1024]{1,0:T(8,128)(2,1)} %w0.3), channel_id=1, source_target_pairs={{0,8},{4,12},{8,0},{12,4},{1,9},{5,13},{9,1},{13,5},{2,10},{6,14},... | collective-permute-start | bytes 1572872 | tf_op jit(solution)/shard_map/ppermute | solution.py:614
  3.7 91.6 %collective-permute-start.6 = (bf16[256,1024]{1,0:T(8,128)(2,1)}, bf16[256,1024]{1,0:T(8,128)(2,1)S(1)}, u32[]{:S(2)}, u32[]{:S(2)}) collective-permute-start(bf16[256,1024]{1,0:T(8,128)(2,1)} %w0.3), channel_id=1, source_target_pairs={{0,4},{4,0},{8,12},{12,8},{1,5},{5,1},{9,13},{13,9},{2,6},{6,2},{1... | collective-permute-start | bytes 1572872 | tf_op jit(solution)/shard_map/ppermute | solution.py:613
  5.9 47.0 %collective-permute-start = (bf16[3,2,1024]{2,1,0:T(2,128)(2,1)S(1)}, bf16[3,2,1024]{2,1,0:T(2,128)(2,1)S(1)}, u32[]{:S(2)}, u32[]{:S(2)}) collective-permute-start(bf16[3,2,1024]{2,1,0:T(2,128)(2,1)S(1)} %slice.312), channel_id=1, source_target_pairs={{0,16},{1,17},{2,18},{3,19},{4,20},{5,21},{6,22},{7,23},{8,24},{9,... | collective-permute-start | bytes 36872 | tf_op jit(solution)/shard_map/ppermute | solution.py:636
  61.4 10.9 %collective-permute-start.16 = (f32[256,128]{1,0:T(8,128)}, f32[256,128]{1,0:T(8,128)S(1)}, u32[]{:S(2)}, u32[]{:S(2)}) collective-permute-start(f32[256,128]{1,0:T(8,128)} %get-tuple-element.87), channel_id=1, source_target_pairs={{0,16},{1,17},{2,18},{3,19},{4,20},{5,21},{6,22},{7,23},{8,24},{9,... | collective-permute-start | bytes 393224 | tf_op jit(solution)/shard_map/ppermute | solution.py:636
  77.2 24.2 %collective-permute-start.18 = (bf16[1024,256]{1,0:T(8,128)(2,1)}, bf16[1024,256]{1,0:T(8,128)(2,1)}, u32[]{:S(2)}, u32[]{:S(2)}) collective-permute-start(bf16[1024,256]{1,0:T(8,128)(2,1)} %shard_map.277.g0), channel_id=1, source_target_pairs={{0,8},{4,12},{8,0},{12,4},{1,9},{5,13},{9,1},{13,5},{2,10},{6,14},... | collective-permute-start | bytes 1572872 | tf_op jit(solution)/shard_map/ppermute | solution.py:614
  82.5 15.2 %collective-permute-start.2 = (bf16[1024,256]{1,0:T(8,128)(2,1)}, bf16[1024,256]{1,0:T(8,128)(2,1)}, u32[]{:S(2)}, u32[]{:S(2)}) collective-permute-start(bf16[1024,256]{1,0:T(8,128)(2,1)} %shard_map.273.g0), channel_id=1, source_target_pairs={{0,4},{4,0},{8,12},{12,8},{1,5},{5,1},{9,13},{13,9},{2,6},{6,2},{1... | collective-permute-start | bytes 1572872 | tf_op jit(solution)/shard_map/ppermute | solution.py:613
  91.3 18.7 %collective-permute-start.17 = (bf16[1024,256]{1,0:T(8,128)(2,1)}, bf16[1024,256]{1,0:T(8,128)(2,1)}, u32[]{:S(2)}, u32[]{:S(2)}) collective-permute-start(bf16[1024,256]{1,0:T(8,128)(2,1)} %shard_map.277.g0), channel_id=1, source_target_pairs={{0,4},{4,0},{8,12},{12,8},{1,5},{5,1},{9,13},{13,9},{2,6},{6,2},{1... | collective-permute-start | bytes 1572872 | tf_op jit(solution)/shard_map/ppermute | solution.py:613
  93.1 18.4 %collective-permute-start.3 = (bf16[1024,256]{1,0:T(8,128)(2,1)}, bf16[1024,256]{1,0:T(8,128)(2,1)}, u32[]{:S(2)}, u32[]{:S(2)}) collective-permute-start(bf16[1024,256]{1,0:T(8,128)(2,1)} %shard_map.273.g0), channel_id=1, source_target_pairs={{0,8},{4,12},{8,0},{12,4},{1,9},{5,13},{9,1},{13,5},{2,10},{6,14},... | collective-permute-start | bytes 1572872 | tf_op jit(solution)/shard_map/ppermute | solution.py:614
  95.3 21.4 %collective-permute-start.9 = (bf16[128,1024]{1,0:T(8,128)(2,1)S(1)}, bf16[128,1024]{1,0:T(8,128)(2,1)}, u32[]{:S(2)}, u32[]{:S(2)}) collective-permute-start(bf16[128,1024]{1,0:T(8,128)(2,1)S(1)} %slice.407), channel_id=1, source_target_pairs={{0,4},{4,0},{8,12},{12,8},{1,5},{5,1},{9,13},{13,9},{2,6},{6,2},{1... | collective-permute-start | bytes 786440 | tf_op jit(solution)/shard_map/ppermute | solution.py:616
  97.7 16.3 %collective-permute-start.8 = (bf16[128,1024]{1,0:T(8,128)(2,1)}, bf16[128,1024]{1,0:T(8,128)(2,1)}, u32[]{:S(2)}, u32[]{:S(2)}) collective-permute-start(bf16[128,1024]{1,0:T(8,128)(2,1)} %slice.406), channel_id=1, source_target_pairs={{0,8},{4,12},{8,0},{12,4},{1,9},{5,13},{9,1},{13,5},{2,10},{6,14},... | collective-permute-start | bytes 786440 | tf_op jit(solution)/shard_map/ppermute | solution.py:615
  101.4 18.1 %collective-permute-start.4 = (bf16[512,256]{1,0:T(8,128)(2,1)}, bf16[512,256]{1,0:T(8,128)(2,1)}, u32[]{:S(2)}, u32[]{:S(2)}) collective-permute-start(bf16[512,256]{1,0:T(8,128)(2,1)} %slice.404), channel_id=1, source_target_pairs={{0,8},{4,12},{8,0},{12,4},{1,9},{5,13},{9,1},{13,5},{2,10},{6,14},... | collective-permute-start | bytes 786440 | tf_op jit(solution)/shard_map/ppermute | solution.py:615
  110.1 43.8 %collective-permute-start.20 = (bf16[512,256]{1,0:T(8,128)(2,1)S(1)}, bf16[512,256]{1,0:T(8,128)(2,1)S(1)}, u32[]{:S(2)}, u32[]{:S(2)}) collective-permute-start(bf16[512,256]{1,0:T(8,128)(2,1)S(1)} %slice.410), channel_id=1, source_target_pairs={{0,4},{4,0},{8,12},{12,8},{1,5},{5,1},{9,13},{13,9},{2,6},{6,2},{1... | collective-permute-start | bytes 786440 | tf_op jit(solution)/shard_map/ppermute | solution.py:616
  111.6 41.7 %collective-permute-start.19 = (bf16[512,256]{1,0:T(8,128)(2,1)S(1)}, bf16[512,256]{1,0:T(8,128)(2,1)S(1)}, u32[]{:S(2)}, u32[]{:S(2)}) collective-permute-start(bf16[512,256]{1,0:T(8,128)(2,1)S(1)} %slice.409), channel_id=1, source_target_pairs={{0,8},{4,12},{8,0},{12,4},{1,9},{5,13},{9,1},{13,5},{2,10},{6,14},... | collective-permute-start | bytes 786440 | tf_op jit(solution)/shard_map/ppermute | solution.py:615
  148.7 48.6 %collective-permute-start.13 = (bf16[128,1024]{1,0:T(8,128)(2,1)S(1)}, bf16[128,1024]{1,0:T(8,128)(2,1)S(1)}, u32[]{:S(2)}, u32[]{:S(2)}) collective-permute-start(bf16[128,1024]{1,0:T(8,128)(2,1)S(1)} %get-tuple-element.209), channel_id=1, source_target_pairs={{0,4},{4,0},{8,12},{12,8},{1,5},{5,1},{9,13},{13,9},{2,6},{6,2},{1... | collective-permute-start | bytes 786440 | tf_op jit(solution)/shard_map/ppermute | solution.py:622
  149.1 51.8 %collective-permute-start.11 = (bf16[128,1024]{1,0:T(8,128)(2,1)}, bf16[128,1024]{1,0:T(8,128)(2,1)S(1)}, u32[]{:S(2)}, u32[]{:S(2)}) collective-permute-start(bf16[128,1024]{1,0:T(8,128)(2,1)} %get-tuple-element.211), channel_id=1, source_target_pairs={{0,8},{4,12},{8,0},{12,4},{1,9},{5,13},{9,1},{13,5},{2,10},{6,14},... | collective-permute-start | bytes 786440 | tf_op jit(solution)/shard_map/ppermute | solution.py:623
  151.7 50.8 %collective-permute-start.30 = (bf16[128,1024]{1,0:T(8,128)(2,1)}, bf16[128,1024]{1,0:T(8,128)(2,1)S(1)}, u32[]{:S(2)}, u32[]{:S(2)}) collective-permute-start(bf16[128,1024]{1,0:T(8,128)(2,1)} %get-tuple-element.203), channel_id=1, source_target_pairs={{0,4},{4,0},{8,12},{12,8},{1,5},{5,1},{9,13},{13,9},{2,6},{6,2},{1... | collective-permute-start | bytes 786440 | tf_op jit(solution)/shard_map/ppermute | solution.py:622
  153.3 50.6 %collective-permute-start.28 = (bf16[128,1024]{1,0:T(8,128)(2,1)}, bf16[128,1024]{1,0:T(8,128)(2,1)S(1)}, u32[]{:S(2)}, u32[]{:S(2)}) collective-permute-start(bf16[128,1024]{1,0:T(8,128)(2,1)} %get-tuple-element.204), channel_id=1, source_target_pairs={{0,8},{4,12},{8,0},{12,4},{1,9},{5,13},{9,1},{13,5},{2,10},{6,14},... | collective-permute-start | bytes 786440 | tf_op jit(solution)/shard_map/ppermute | solution.py:623
  179.9 24.5 %collective-permute-start.47 = (bf16[128,1024]{1,0:T(8,128)(2,1)S(1)}, bf16[128,1024]{1,0:T(8,128)(2,1)S(1)}, u32[]{:S(2)}, u32[]{:S(2)}) collective-permute-start(bf16[128,1024]{1,0:T(8,128)(2,1)S(1)} %get-tuple-element.197), channel_id=1, source_target_pairs={{0,4},{4,0},{8,12},{12,8},{1,5},{5,1},{9,13},{13,9},{2,6},{6,2},{1... | collective-permute-start | bytes 786440 | tf_op jit(solution)/shard_map/ppermute | solution.py:622
  203.8 12.0 %collective-permute-start.24 = (bf16[128,1024]{1,0:T(8,128)(2,1)S(1)}, bf16[128,1024]{1,0:T(8,128)(2,1)S(1)}, u32[]{:S(2)}, u32[]{:S(2)}) collective-permute-start(bf16[128,1024]{1,0:T(8,128)(2,1)S(1)} %get-tuple-element.215), channel_id=1, source_target_pairs={{0,4},{4,0},{8,12},{12,8},{1,5},{5,1},{9,13},{13,9},{2,6},{6,2},{1... | collective-permute-start | bytes 786440 | tf_op jit(solution)/shard_map/ppermute | solution.py:622
  204.4 13.1 %collective-permute-start.22 = (bf16[128,1024]{1,0:T(8,128)(2,1)S(1)}, bf16[128,1024]{1,0:T(8,128)(2,1)S(1)}, u32[]{:S(2)}, u32[]{:S(2)}) collective-permute-start(bf16[128,1024]{1,0:T(8,128)(2,1)S(1)} %get-tuple-element.217), channel_id=1, source_target_pairs={{0,8},{4,12},{8,0},{12,4},{1,9},{5,13},{9,1},{13,5},{2,10},{6,14},... | collective-permute-start | bytes 786440 | tf_op jit(solution)/shard_map/ppermute | solution.py:623
  206.3 15.2 %collective-permute-start.44 = (bf16[128,1024]{1,0:T(8,128)(2,1)S(1)}, bf16[128,1024]{1,0:T(8,128)(2,1)S(1)}, u32[]{:S(2)}, u32[]{:S(2)}) collective-permute-start(bf16[128,1024]{1,0:T(8,128)(2,1)S(1)} %get-tuple-element.195), channel_id=1, source_target_pairs={{0,4},{4,0},{8,12},{12,8},{1,5},{5,1},{9,13},{13,9},{2,6},{6,2},{1... | collective-permute-start | bytes 786440 | tf_op jit(solution)/shard_map/ppermute | solution.py:624
  210.2 12.9 %collective-permute-start.49 = (bf16[128,1024]{1,0:T(8,128)(2,1)S(1)}, bf16[128,1024]{1,0:T(8,128)(2,1)S(1)}, u32[]{:S(2)}, u32[]{:S(2)}) collective-permute-start(bf16[128,1024]{1,0:T(8,128)(2,1)S(1)} %get-tuple-element.196), channel_id=1, source_target_pairs={{0,8},{4,12},{8,0},{12,4},{1,9},{5,13},{9,1},{13,5},{2,10},{6,14},... | collective-permute-start | bytes 786440 | tf_op jit(solution)/shard_map/ppermute | solution.py:625
  211.9 14.0 %collective-permute-start.29 = (bf16[128,1024]{1,0:T(8,128)(2,1)S(1)}, bf16[128,1024]{1,0:T(8,128)(2,1)S(1)}, u32[]{:S(2)}, u32[]{:S(2)}) collective-permute-start(bf16[128,1024]{1,0:T(8,128)(2,1)S(1)} %get-tuple-element.205), channel_id=1, source_target_pairs={{0,4},{4,0},{8,12},{12,8},{1,5},{5,1},{9,13},{13,9},{2,6},{6,2},{1... | collective-permute-start | bytes 786440 | tf_op jit(solution)/shard_map/ppermute | solution.py:626
  215.8 12.9 %collective-permute-start.31 = (bf16[128,1024]{1,0:T(8,128)(2,1)S(1)}, bf16[128,1024]{1,0:T(8,128)(2,1)S(1)}, u32[]{:S(2)}, u32[]{:S(2)}) collective-permute-start(bf16[128,1024]{1,0:T(8,128)(2,1)S(1)} %get-tuple-element.206), channel_id=1, source_target_pairs={{0,8},{4,12},{8,0},{12,4},{1,9},{5,13},{9,1},{13,5},{2,10},{6,14},... | collective-permute-start | bytes 786440 | tf_op jit(solution)/shard_map/ppermute | solution.py:627
  217.5 13.4 %collective-permute-start.46 = (bf16[128,1024]{1,0:T(8,128)(2,1)S(1)}, bf16[128,1024]{1,0:T(8,128)(2,1)S(1)}, u32[]{:S(2)}, u32[]{:S(2)}) collective-permute-start(bf16[128,1024]{1,0:T(8,128)(2,1)S(1)} %get-tuple-element.199), channel_id=1, source_target_pairs={{0,4},{4,0},{8,12},{12,8},{1,5},{5,1},{9,13},{13,9},{2,6},{6,2},{1... | collective-permute-start | bytes 786440 | tf_op jit(solution)/shard_map/ppermute | solution.py:626
  221.5 12.9 %collective-permute-start.48 = (bf16[128,1024]{1,0:T(8,128)(2,1)S(1)}, bf16[128,1024]{1,0:T(8,128)(2,1)S(1)}, u32[]{:S(2)}, u32[]{:S(2)}) collective-permute-start(bf16[128,1024]{1,0:T(8,128)(2,1)S(1)} %get-tuple-element.200), channel_id=1, source_target_pairs={{0,8},{4,12},{8,0},{12,4},{1,9},{5,13},{9,1},{13,5},{2,10},{6,14},... | collective-permute-start | bytes 786440 | tf_op jit(solution)/shard_map/ppermute | solution.py:627
  223.1 32.9 %collective-permute-start.15 = (bf16[128,1024]{1,0:T(8,128)(2,1)}, bf16[128,1024]{1,0:T(8,128)(2,1)S(1)}, u32[]{:S(2)}, u32[]{:S(2)}) collective-permute-start(bf16[128,1024]{1,0:T(8,128)(2,1)} %get-tuple-element.210), channel_id=1, source_target_pairs={{0,8},{4,12},{8,0},{12,4},{1,9},{5,13},{9,1},{13,5},{2,10},{6,14},... | collective-permute-start | bytes 786440 | tf_op jit(solution)/shard_map/ppermute | solution.py:625
  225.9 19.7 %collective-permute-start.26 = (bf16[128,1024]{1,0:T(8,128)(2,1)S(1)}, bf16[128,1024]{1,0:T(8,128)(2,1)S(1)}, u32[]{:S(2)}, u32[]{:S(2)}) collective-permute-start(bf16[128,1024]{1,0:T(8,128)(2,1)S(1)} %get-tuple-element.216), channel_id=1, source_target_pairs={{0,8},{4,12},{8,0},{12,4},{1,9},{5,13},{9,1},{13,5},{2,10},{6,14},... | collective-permute-start | bytes 786440 | tf_op jit(solution)/shard_map/ppermute | solution.py:625
  228.7 18.8 %collective-permute-start.21 = (bf16[128,1024]{1,0:T(8,128)(2,1)S(1)}, bf16[128,1024]{1,0:T(8,128)(2,1)S(1)}, u32[]{:S(2)}, u32[]{:S(2)}) collective-permute-start(bf16[128,1024]{1,0:T(8,128)(2,1)S(1)} %get-tuple-element.218), channel_id=1, source_target_pairs={{0,4},{4,0},{8,12},{12,8},{1,5},{5,1},{9,13},{13,9},{2,6},{6,2},{1... | collective-permute-start | bytes 786440 | tf_op jit(solution)/shard_map/ppermute | solution.py:624
  230.9 20.3 %collective-permute-start.25 = (bf16[128,1024]{1,0:T(8,128)(2,1)S(1)}, bf16[128,1024]{1,0:T(8,128)(2,1)S(1)}, u32[]{:S(2)}, u32[]{:S(2)}) collective-permute-start(bf16[128,1024]{1,0:T(8,128)(2,1)S(1)} %get-tuple-element.213), channel_id=1, source_target_pairs={{0,8},{4,12},{8,0},{12,4},{1,9},{5,13},{9,1},{13,5},{2,10},{6,14},... | collective-permute-start | bytes 786440 | tf_op jit(solution)/shard_map/ppermute | solution.py:627
  234.4 18.6 %collective-permute-start.23 = (bf16[128,1024]{1,0:T(8,128)(2,1)S(1)}, bf16[128,1024]{1,0:T(8,128)(2,1)S(1)}, u32[]{:S(2)}, u32[]{:S(2)}) collective-permute-start(bf16[128,1024]{1,0:T(8,128)(2,1)S(1)} %get-tuple-element.214), channel_id=1, source_target_pairs={{0,4},{4,0},{8,12},{12,8},{1,5},{5,1},{9,13},{13,9},{2,6},{6,2},{1... | collective-permute-start | bytes 786440 | tf_op jit(solution)/shard_map/ppermute | solution.py:626
  245.6 10.4 %collective-permute-start.10 = (bf16[128,1024]{1,0:T(8,128)(2,1)S(1)}, bf16[128,1024]{1,0:T(8,128)(2,1)S(1)}, u32[]{:S(2)}, u32[]{:S(2)}) collective-permute-start(bf16[128,1024]{1,0:T(8,128)(2,1)S(1)} %get-tuple-element.212), channel_id=1, source_target_pairs={{0,4},{4,0},{8,12},{12,8},{1,5},{5,1},{9,13},{13,9},{2,6},{6,2},{1... | collective-permute-start | bytes 786440 | tf_op jit(solution)/shard_map/ppermute | solution.py:624
  264.5 17.3 %collective-permute-start.33 = (bf16[256,256]{1,0:T(8,128)(2,1)S(1)}, bf16[256,256]{1,0:T(8,128)(2,1)S(1)}, u32[]{:S(2)}, u32[]{:S(2)}) collective-permute-start(bf16[256,256]{1,0:T(8,128)(2,1)S(1)} %convolution_convert_fusion.6), channel_id=1, source_target_pairs={{0,4},{4,0},{8,12},{12,8},{1,5},{5,1},{9,13},{13,9},{2,6},{6,2},{1... | collective-permute-start | bytes 393224 | tf_op jit(solution)/shard_map/ppermute | solution.py:756
  266.7 26.8 %collective-permute-start.50 = (bf16[256,256]{1,0:T(8,128)(2,1)S(1)}, bf16[256,256]{1,0:T(8,128)(2,1)S(1)}, u32[]{:S(2)}, u32[]{:S(2)}) collective-permute-start(bf16[256,256]{1,0:T(8,128)(2,1)S(1)} %convolution_convert_fusion.2), channel_id=1, source_target_pairs={{0,4},{4,0},{8,12},{12,8},{1,5},{5,1},{9,13},{13,9},{2,6},{6,2},{1... | collective-permute-start | bytes 393224 | tf_op jit(solution)/shard_map/ppermute | solution.py:756
  267.4 16.7 %collective-permute-start.34 = (bf16[256,256]{1,0:T(8,128)(2,1)S(1)}, bf16[256,256]{1,0:T(8,128)(2,1)S(1)}, u32[]{:S(2)}, u32[]{:S(2)}) collective-permute-start(bf16[256,256]{1,0:T(8,128)(2,1)S(1)} %convolution_convert_fusion.5), channel_id=1, source_target_pairs={{0,8},{4,12},{8,0},{12,4},{1,9},{5,13},{9,1},{13,5},{2,10},{6,14},... | collective-permute-start | bytes 393224 | tf_op jit(solution)/shard_map/ppermute | solution.py:757
  270.3 23.8 %collective-permute-start.51 = (bf16[256,256]{1,0:T(8,128)(2,1)}, bf16[256,256]{1,0:T(8,128)(2,1)S(1)}, u32[]{:S(2)}, u32[]{:S(2)}) collective-permute-start(bf16[256,256]{1,0:T(8,128)(2,1)} %convolution_convert_fusion.1), channel_id=1, source_target_pairs={{0,8},{4,12},{8,0},{12,4},{1,9},{5,13},{9,1},{13,5},{2,10},{6,14},... | collective-permute-start | bytes 393224 | tf_op jit(solution)/shard_map/ppermute | solution.py:757
  270.5 15.5 %collective-permute-start.35 = (bf16[256,256]{1,0:T(8,128)(2,1)S(1)}, bf16[256,256]{1,0:T(8,128)(2,1)S(1)}, u32[]{:S(2)}, u32[]{:S(2)}) collective-permute-start(bf16[256,256]{1,0:T(8,128)(2,1)S(1)} %convolution_convert_fusion.4), channel_id=1, source_target_pairs={{0,12},{4,8},{8,4},{12,0},{1,13},{5,9},{9,5},{13,1},{2,14},{6,10},... | collective-permute-start | bytes 393224 | tf_op jit(solution)/shard_map/ppermute | solution.py:758
  281.8 12.9 %collective-permute-start.52 = (bf16[256,256]{1,0:T(8,128)(2,1)}, bf16[256,256]{1,0:T(8,128)(2,1)S(1)}, u32[]{:S(2)}, u32[]{:S(2)}) collective-permute-start(bf16[256,256]{1,0:T(8,128)(2,1)} %convolution_convert_fusion), channel_id=1, source_target_pairs={{0,12},{4,8},{8,4},{12,0},{1,13},{5,9},{9,5},{13,1},{2,14},{6,10},... | collective-permute-start | bytes 393224 | tf_op jit(solution)/shard_map/ppermute | solution.py:758
  284.0 83.9 %collective-permute-start.71 = (bf16[512,256]{1,0:T(8,128)(2,1)}, bf16[512,256]{1,0:T(8,128)(2,1)}, u32[]{:S(2)}, u32[]{:S(2)}) collective-permute-start(bf16[512,256]{1,0:T(8,128)(2,1)} %slice_bitcast_fusion.4), channel_id=1, source_target_pairs={{0,8},{4,12},{8,0},{12,4},{1,9},{5,13},{9,1},{13,5},{2,10},{6,14},... | collective-permute-start | bytes 786440 | tf_op jit(solution)/shard_map/ppermute | solution.py:625
  286.6 45.6 %collective-permute-start.69 = (bf16[512,256]{1,0:T(8,128)(2,1)S(1)}, bf16[512,256]{1,0:T(8,128)(2,1)S(1)}, u32[]{:S(2)}, u32[]{:S(2)}) collective-permute-start(bf16[512,256]{1,0:T(8,128)(2,1)S(1)} %get-tuple-element.230), channel_id=1, source_target_pairs={{0,4},{4,0},{8,12},{12,8},{1,5},{5,1},{9,13},{13,9},{2,6},{6,2},{1... | collective-permute-start | bytes 786440 | tf_op jit(solution)/shard_map/ppermute | solution.py:622
  293.5 40.1 %collective-permute-start.67 = (bf16[512,256]{1,0:T(8,128)(2,1)}, bf16[512,256]{1,0:T(8,128)(2,1)S(1)}, u32[]{:S(2)}, u32[]{:S(2)}) collective-permute-start(bf16[512,256]{1,0:T(8,128)(2,1)} %get-tuple-element.231), channel_id=1, source_target_pairs={{0,8},{4,12},{8,0},{12,4},{1,9},{5,13},{9,1},{13,5},{2,10},{6,14},... | collective-permute-start | bytes 786440 | tf_op jit(solution)/shard_map/ppermute | solution.py:623
  294.1 74.5 %collective-permute-start.66 = (bf16[512,256]{1,0:T(8,128)(2,1)}, bf16[512,256]{1,0:T(8,128)(2,1)}, u32[]{:S(2)}, u32[]{:S(2)}) collective-permute-start(bf16[512,256]{1,0:T(8,128)(2,1)} %slice_bitcast_fusion.9), channel_id=1, source_target_pairs={{0,4},{4,0},{8,12},{12,8},{1,5},{5,1},{9,13},{13,9},{2,6},{6,2},{1... | collective-permute-start | bytes 786440 | tf_op jit(solution)/shard_map/ppermute | solution.py:624
  294.7 10.4 %collective-permute-start.36 = (f32[256,128]{1,0:T(8,128)}, f32[256,128]{1,0:T(8,128)}, u32[]{:S(2)}, u32[]{:S(2)}) collective-permute-start(f32[256,128]{1,0:T(8,128)} %get-tuple-element.95), channel_id=1, source_target_pairs={{16,0},{17,1},{18,2},{19,3},{20,4},{21,5},{22,6},{23,7},{24,8},{25... | collective-permute-start | bytes 393224 | tf_op jit(solution)/shard_map/ppermute | solution.py:636
  305.2 12.6 %collective-permute-start.53 = (f32[256,128]{1,0:T(8,128)}, f32[256,128]{1,0:T(8,128)S(1)}, u32[]{:S(2)}, u32[]{:S(2)}) collective-permute-start(f32[256,128]{1,0:T(8,128)} %get-tuple-element.107), channel_id=1, source_target_pairs={{16,0},{17,1},{18,2},{19,3},{20,4},{21,5},{22,6},{23,7},{24,8},{25... | collective-permute-start | bytes 393224 | tf_op jit(solution)/shard_map/ppermute | solution.py:636
  317.8 32.0 %collective-permute-start.37 = (f32[3,512]{1,0:T(4,128)S(1)}, f32[3,512]{1,0:T(4,128)S(1)}, u32[]{:S(2)}, u32[]{:S(2)}) collective-permute-start(f32[3,512]{1,0:T(4,128)S(1)} %pad_maximum_fusion.11), channel_id=1, source_target_pairs={{16,0},{17,1},{18,2},{19,3},{20,4},{21,5},{22,6},{23,7},{24,8},{25... | collective-permute-start | bytes 18440 | tf_op jit(solution)/shard_map/ppermute | solution.py:636
  333.6 35.7 %collective-permute-start.70 = (bf16[512,256]{1,0:T(8,128)(2,1)S(1)}, bf16[512,256]{1,0:T(8,128)(2,1)}, u32[]{:S(2)}, u32[]{:S(2)}) collective-permute-start(bf16[512,256]{1,0:T(8,128)(2,1)S(1)} %fusion.54), channel_id=1, source_target_pairs={{0,8},{4,12},{8,0},{12,4},{1,9},{5,13},{9,1},{13,5},{2,10},{6,14},... | collective-permute-start | bytes 786440 | tf_op jit(solution)/shard_map/ppermute | solution.py:627
  335.9 34.8 %collective-permute-start.68 = (bf16[512,256]{1,0:T(8,128)(2,1)S(1)}, bf16[512,256]{1,0:T(8,128)(2,1)S(1)}, u32[]{:S(2)}, u32[]{:S(2)}) collective-permute-start(bf16[512,256]{1,0:T(8,128)(2,1)S(1)} %fusion.55), channel_id=1, source_target_pairs={{0,4},{4,0},{8,12},{12,8},{1,5},{5,1},{9,13},{13,9},{2,6},{6,2},{1... | collective-permute-start | bytes 786440 | tf_op jit(solution)/shard_map/ppermute | solution.py:626
  367.9 40.9 %collective-permute-start.79 = (bf16[4,3,128,704]{2,3,1,0:T(8,128)(2,1)}, bf16[4,3,128,704]{2,3,1,0:T(8,128)(2,1)}, u32[]{:S(2)}, u32[]{:S(2)}) collective-permute-start(bf16[4,3,128,704]{2,3,1,0:T(8,128)(2,1)} %constant_dynamic-slice_fusion), channel_id=1, source_target_pairs={{0,16},{16,0},{1,17},{17,1},{2,18},{18,2},{3,19},{19,3},{4,20},{20... | collective-permute-start | bytes 6488072 | tf_op jit(solution)/shard_map/ppermute | solution.py:661
  369.3 13.4 %collective-permute-start.58 = (bf16[128,1024]{1,0:T(8,128)(2,1)S(1)}, bf16[128,1024]{1,0:T(8,128)(2,1)S(1)}, u32[]{:S(2)}, u32[]{:S(2)}) collective-permute-start(bf16[128,1024]{1,0:T(8,128)(2,1)S(1)} %get-tuple-element.185), channel_id=1, source_target_pairs={{0,4},{4,0},{8,12},{12,8},{1,5},{5,1},{9,13},{13,9},{2,6},{6,2},{1... | collective-permute-start | bytes 786440 | tf_op jit(solution)/shard_map/ppermute | solution.py:622
  371.4 13.9 %collective-permute-start.56 = (bf16[128,1024]{1,0:T(8,128)(2,1)S(1)}, bf16[128,1024]{1,0:T(8,128)(2,1)S(1)}, u32[]{:S(2)}, u32[]{:S(2)}) collective-permute-start(bf16[128,1024]{1,0:T(8,128)(2,1)S(1)} %get-tuple-element.186), channel_id=1, source_target_pairs={{0,8},{4,12},{8,0},{12,4},{1,9},{5,13},{9,1},{13,5},{2,10},{6,14},... | collective-permute-start | bytes 786440 | tf_op jit(solution)/shard_map/ppermute | solution.py:623
  377.1 28.3 %collective-permute-start.38 = (bf16[128,1024]{1,0:T(8,128)(2,1)}, bf16[128,1024]{1,0:T(8,128)(2,1)S(1)}, u32[]{:S(2)}, u32[]{:S(2)}) collective-permute-start(bf16[128,1024]{1,0:T(8,128)(2,1)} %get-tuple-element.189), channel_id=1, source_target_pairs={{0,4},{4,0},{8,12},{12,8},{1,5},{5,1},{9,13},{13,9},{2,6},{6,2},{1... | collective-permute-start | bytes 786440 | tf_op jit(solution)/shard_map/ppermute | solution.py:624
  377.8 29.1 %collective-permute-start.43 = (bf16[128,1024]{1,0:T(8,128)(2,1)}, bf16[128,1024]{1,0:T(8,128)(2,1)}, u32[]{:S(2)}, u32[]{:S(2)}) collective-permute-start(bf16[128,1024]{1,0:T(8,128)(2,1)} %get-tuple-element.190), channel_id=1, source_target_pairs={{0,8},{4,12},{8,0},{12,4},{1,9},{5,13},{9,1},{13,5},{2,10},{6,14},... | collective-permute-start | bytes 786440 | tf_op jit(solution)/shard_map/ppermute | solution.py:625
  385.3 17.9 %collective-permute-start.72 = (bf16[4,128,1024]{2,1,0:T(8,128)(2,1)}, bf16[4,128,1024]{2,1,0:T(8,128)(2,1)}, u32[]{:S(2)}, u32[]{:S(2)}) collective-permute-start(bf16[4,128,1024]{2,1,0:T(8,128)(2,1)} %constant_dynamic-slice_fusion.3), channel_id=1, source_target_pairs={{0,16},{16,0},{1,17},{17,1},{2,18},{18,2},{3,19},{19,3},{4,20},{20... | collective-permute-start | bytes 3145736 | tf_op jit(solution)/shard_map/ppermute | solution.py:661
  415.5 18.3 %collective-permute-start.80 = (bf16[3,128,704]{1,2,0:T(8,128)(2,1)S(1)}, bf16[3,128,704]{1,2,0:T(8,128)(2,1)S(1)}, u32[]{:S(2)}, u32[]{:S(2)}) collective-permute-start(bf16[3,128,704]{1,2,0:T(8,128)(2,1)S(1)} %get-tuple-element.181), channel_id=1, source_target_pairs={{0,1},{4,5},{8,9},{12,13},{16,17},{20,21},{24,25},{28,29}} | collective-permute-start | bytes 1622024 | tf_op jit(solution)/shard_map/ppermute | solution.py:668
  419.7 20.0 %collective-permute-start.76 = (bf16[128,1024]{1,0:T(8,128)(2,1)S(1)}, bf16[128,1024]{1,0:T(8,128)(2,1)S(1)}, u32[]{:S(2)}, u32[]{:S(2)}) collective-permute-start(bf16[128,1024]{1,0:T(8,128)(2,1)S(1)} %get-tuple-element.225), channel_id=1, source_target_pairs={{3,2},{7,6},{11,10},{15,14},{19,18},{23,22},{27,26},{31,30}} | collective-permute-start | bytes 786440 | tf_op jit(solution)/shard_map/ppermute | solution.py:669
  420.5 20.0 %collective-permute-start.83 = (bf16[3,128,704]{1,2,0:T(8,128)(2,1)S(1)}, bf16[3,128,704]{1,2,0:T(8,128)(2,1)S(1)}, u32[]{:S(2)}, u32[]{:S(2)}) collective-permute-start(bf16[3,128,704]{1,2,0:T(8,128)(2,1)S(1)} %get-tuple-element.182), channel_id=1, source_target_pairs={{3,2},{7,6},{11,10},{15,14},{19,18},{23,22},{27,26},{31,30}} | collective-permute-start | bytes 1622024 | tf_op jit(solution)/shard_map/ppermute | solution.py:669
  422.2 17.5 %collective-permute-start.74 = (bf16[128,1024]{1,0:T(8,128)(2,1)S(1)}, bf16[128,1024]{1,0:T(8,128)(2,1)S(1)}, u32[]{:S(2)}, u32[]{:S(2)}) collective-permute-start(bf16[128,1024]{1,0:T(8,128)(2,1)S(1)} %bitcast_add_fusion.6), channel_id=1, source_target_pairs={{0,1},{1,2},{4,5},{5,6},{8,9},{9,10},{12,13},{13,14},{16,17},{17,1... | collective-permute-start | bytes 786440 | tf_op jit(solution)/shard_map/ppermute | solution.py:668
  433.9 11.3 %collective-permute-start.81 = (bf16[3,128,704]{1,2,0:T(8,128)(2,1)S(1)}, bf16[3,128,704]{1,2,0:T(8,128)(2,1)S(1)}, u32[]{:S(2)}, u32[]{:S(2)}) collective-permute-start(bf16[3,128,704]{1,2,0:T(8,128)(2,1)S(1)} %bitcast_add_fusion.2), channel_id=1, source_target_pairs={{0,1},{1,2},{4,5},{5,6},{8,9},{9,10},{12,13},{13,14},{16,17},{17,1... | collective-permute-start | bytes 1622024 | tf_op jit(solution)/shard_map/ppermute | solution.py:668
  439.8 13.4 %collective-permute-start.77 = (bf16[128,1024]{1,0:T(8,128)(2,1)S(1)}, bf16[128,1024]{1,0:T(8,128)(2,1)S(1)}, u32[]{:S(2)}, u32[]{:S(2)}) collective-permute-start(bf16[128,1024]{1,0:T(8,128)(2,1)S(1)} %get-tuple-element.223), channel_id=1, source_target_pairs={{3,2},{2,1},{7,6},{6,5},{11,10},{10,9},{15,14},{14,13},{19,18},{18... | collective-permute-start | bytes 786440 | tf_op jit(solution)/shard_map/ppermute | solution.py:669
  446.1 17.5 %collective-permute-start.84 = (bf16[3,128,704]{1,2,0:T(8,128)(2,1)S(1)}, bf16[3,128,704]{1,2,0:T(8,128)(2,1)S(1)}, u32[]{:S(2)}, u32[]{:S(2)}) collective-permute-start(bf16[3,128,704]{1,2,0:T(8,128)(2,1)S(1)} %get-tuple-element.180), channel_id=1, source_target_pairs={{3,2},{2,1},{7,6},{6,5},{11,10},{10,9},{15,14},{14,13},{19,18},{18... | collective-permute-start | bytes 1622024 | tf_op jit(solution)/shard_map/ppermute | solution.py:669
  448.1 16.8 %collective-permute-start.75 = (bf16[128,1024]{1,0:T(8,128)(2,1)S(1)}, bf16[128,1024]{1,0:T(8,128)(2,1)S(1)}, u32[]{:S(2)}, u32[]{:S(2)}) collective-permute-start(bf16[128,1024]{1,0:T(8,128)(2,1)S(1)} %get-tuple-element.222), channel_id=1, source_target_pairs={{0,1},{1,2},{2,3},{4,5},{5,6},{6,7},{8,9},{9,10},{10,11},{12,13},{... | collective-permute-start | bytes 786440 | tf_op jit(solution)/shard_map/ppermute | solution.py:668
  453.2 11.7 %collective-permute-start.78 = (bf16[128,1024]{1,0:T(8,128)(2,1)S(1)}, bf16[128,1024]{1,0:T(8,128)(2,1)S(1)}, u32[]{:S(2)}, u32[]{:S(2)}) collective-permute-start(bf16[128,1024]{1,0:T(8,128)(2,1)S(1)} %bitcast_add_fusion.5), channel_id=1, source_target_pairs={{3,2},{2,1},{1,0},{7,6},{6,5},{5,4},{11,10},{10,9},{9,8},{15,14},{... | collective-permute-start | bytes 786440 | tf_op jit(solution)/shard_map/ppermute | solution.py:669
  457.6 12.3 %collective-permute-start.82 = (bf16[3,128,704]{1,2,0:T(8,128)(2,1)}, bf16[3,128,704]{1,2,0:T(8,128)(2,1)}, u32[]{:S(2)}, u32[]{:S(2)}) collective-permute-start(bf16[3,128,704]{1,2,0:T(8,128)(2,1)} %get-tuple-element.179), channel_id=1, source_target_pairs={{0,1},{1,2},{2,3},{4,5},{5,6},{6,7},{8,9},{9,10},{10,11},{12,13},{... | collective-permute-start | bytes 1622024 | tf_op jit(solution)/shard_map/ppermute | solution.py:668
  463.6 11.4 %collective-permute-start.85 = (bf16[3,128,704]{1,2,0:T(8,128)(2,1)S(1)}, bf16[3,128,704]{1,2,0:T(8,128)(2,1)}, u32[]{:S(2)}, u32[]{:S(2)}) collective-permute-start(bf16[3,128,704]{1,2,0:T(8,128)(2,1)S(1)} %bitcast_add_fusion.1), channel_id=1, source_target_pairs={{3,2},{2,1},{1,0},{7,6},{6,5},{5,4},{11,10},{10,9},{9,8},{15,14},{... | collective-permute-start | bytes 1622024 | tf_op jit(solution)/shard_map/ppermute | solution.py:669
  (106 other events, 652.4 us)

commit v2 on v1

v2 whole, which is shorter than its diff:
```python
import functools

import jax
import jax.numpy as jnp
from jax import lax
from jax.experimental import pallas as pl
from jax.experimental.pallas import tpu as pltpu
from jax.sharding import PartitionSpec as P

CONV = 4
EDGE = CONV - 1
CHUNK = 128
STEP = 256
EPS_NORM = 1e-06
EPS_HEAD = 1e-05
GATE_NORMALIZER = 16.0
HIGHEST = lax.Precision.HIGHEST
BF16 = jnp.bfloat16
F32 = jnp.float32
VMEM_LIMIT = 56 * 2**20


def mm(left, right):
    return lax.dot_general(left, right, (((1,), (0,)), ((), ())), preferred_element_type=F32)


def mm_nt(left, right):
    return lax.dot_general(left, right, (((1,), (1,)), ((), ())), preferred_element_type=F32)


def mm_tn(left, right):
    return lax.dot_general(left, right, (((0,), (0,)), ((), ())), preferred_element_type=F32)


def sigmoid(values):
    return 1.0 / (1.0 + jnp.exp(-values))


def whole(shape):
    return pl.BlockSpec(shape, lambda *_: (0,) * len(shape))


def rows_of(size, width):
    return pl.BlockSpec((size, width), lambda i, *_: (i, 0))


def call(body, grid, in_specs, out_specs, out_shape, scratch, flops, moved, prefetch=0):
    return pl.pallas_call(
        body,
        grid_spec=pltpu.PrefetchScalarGridSpec(
            num_scalar_prefetch=prefetch,
            grid=grid,
            in_specs=in_specs,
            out_specs=out_specs,
            scratch_shapes=scratch,
        ),
        out_shape=out_shape,
        compiler_params=pltpu.CompilerParams(
            dimension_semantics=("arbitrary",), vmem_limit_bytes=VMEM_LIMIT
        ),
        cost_estimate=pl.CostEstimate(flops=flops, bytes_accessed=moved, transcendentals=0),
    )


def shape_of(shape, dtype):
    return jax.ShapeDtypeStruct(shape, dtype)


def project_body(
    places, tok_in, cot_in, gain, w_proj, w_gate, w_rank,
    tok, upstream, normed, projected, out_gate, low_rank,
):
    step = pl.program_id(0)
    sequences, count, _ = tok.shape
    total = sequences * count
    row = lax.broadcasted_iota(jnp.int32, (total, total), 0)
    column = lax.broadcasted_iota(jnp.int32, (total, total), 1)
    source = (row % count) * sequences + row // count
    order = jnp.where(column == source, 1.0, 0.0).astype(BF16)
    rows = mm(order, tok_in[...])
    grads = mm(order, cot_in[...])
    first = places[sequences] + step * count
    position = first + lax.broadcasted_iota(jnp.int32, (count, 1), 0)
    inverse = lax.rsqrt(jnp.mean(rows * rows, axis=-1, keepdims=True) + EPS_NORM)
    rounded = (rows * inverse * gain[...]).astype(BF16)
    projected_rows = mm(rounded, w_proj[...]).astype(BF16)
    gate_rows = mm(rounded, w_gate[...]).astype(BF16)
    rank_rows = mm(rounded, w_rank[...]).astype(BF16)
    for s in range(sequences):
        part = slice(s * count, (s + 1) * count)
        tok[s] = rows[part].astype(BF16)
        upstream[s] = jnp.where(position < places[s], grads[part], 0.0).astype(BF16)
        normed[s] = rounded[part]
        projected[s] = projected_rows[part]
        out_gate[s] = gate_rows[part]
        low_rank[s] = rank_rows[part]


def rows3(sequences, size, width):
    return pl.BlockSpec((sequences, size, width), lambda i, *_: (0, i, 0))


def project(places, tok, cot, sequences, gain, w_proj, w_gate, w_rank):
    length, width = tok.shape[0] // sequences, tok.shape[1]
    c3, dv, rank = w_proj.shape[1], w_gate.shape[1], w_rank.shape[1]
    widths = (width, width, width, c3, dv, rank)
    return call(
        project_body,
        (length // CHUNK,),
        [
            rows_of(CHUNK * sequences, width),
            rows_of(CHUNK * sequences, width),
            whole((1, width)),
            whole((width, c3)),
            whole((width, dv)),
            whole((width, rank)),
        ],
        [rows3(sequences, CHUNK, w) for w in widths],
        [shape_of((sequences, length, w), BF16) for w in widths],
        [],
        2 * sequences * length * width * (c3 + dv + rank + 512),
        sequences * length * (5 * width + c3 + dv) * 2 + width * (c3 + dv) * 2,
        prefetch=1,
    )(places, tok, cot, gain, w_proj, w_gate, w_rank)


def triangle(lower):
    row = lax.broadcasted_iota(jnp.int32, (CHUNK, CHUNK), 0)
    column = lax.broadcasted_iota(jnp.int32, (CHUNK, CHUNK), 1)
    return row >= column if lower else row <= column


def running_sum(values, lower):
    ones = triangle(lower).astype(F32)
    return lax.dot_general(
        ones, values, (((1,), (0,)), ((), ())), precision=HIGHEST, preferred_element_type=F32
    )


def filter_rows(buffer, taps, count):
    total = taps[0:1, :] * buffer[pl.ds(8 - EDGE, count), :]
    for offset in range(1, CONV):
        total = total + taps[offset : offset + 1, :] * buffer[pl.ds(8 - EDGE + offset, count), :]
    return total


def forward_body(
    projected, halo, low_rank, taps_in, rank_up, bias,
    head_local, query_profile, cumulative, states, before, end_state, total_decay,
    extended, memory, preceding,
):
    step = pl.program_id(0)
    sequences = projected.shape[0]

    @pl.when(step == 0)
    def _():
        extended[:, 0:8, :] = halo[...]
        memory[...] = jnp.zeros_like(memory)
        preceding[...] = jnp.zeros_like(preceding)

    @pl.when(step > 0)
    def _():
        extended[:, 0:8, :] = extended[:, STEP : STEP + 8, :]

    width = rank_up.shape[1]
    causal = triangle(True)
    for s in range(sequences):
        extended[s, 8 : 8 + STEP, :] = projected[s].astype(F32)
        filtered = filter_rows(extended.at[s], taps_in[...], STEP)
        convolved = (filtered * sigmoid(filtered)).astype(BF16)
        logit = mm(low_rank[s], rank_up[...]) + bias[...]
        decay = (jnp.minimum(logit, 0.0) - jnp.log1p(jnp.exp(-jnp.abs(logit)))) / GATE_NORMALIZER
        for part in range(STEP // CHUNK):
            rows = slice(part * CHUNK, (part + 1) * CHUNK)
            queries = convolved[rows, :width].astype(F32)
            keys = convolved[rows, width : 2 * width].astype(F32)
            values = convolved[rows, 2 * width :]
            total = running_sum(decay[rows], True)
            middle, last = total[CHUNK // 2 - 1 : CHUNK // 2], total[CHUNK - 1 : CHUNK]
            lifted = (queries * jnp.exp(total - middle)).astype(BF16)
            lowered = (keys * jnp.exp(middle - total)).astype(BF16)
            scores = jnp.where(causal, mm_nt(lifted, lowered), 0.0).astype(BF16)
            entry = memory[s]
            entry_low = entry.astype(BF16)
            states[s, part] = entry_low
            profile = queries * jnp.exp(total)
            head_local[s, rows, :] = mm(scores, values) + mm_nt(profile.astype(BF16), entry_low)
            gone = preceding[s]
            query_profile[s, rows, :] = (profile * jnp.exp(gone)).astype(BF16)
            cumulative[s, rows, :] = total
            tails = (keys * jnp.exp(last - total)).astype(BF16)
            memory[s] = entry * jnp.exp(last) + mm_tn(values, tails)
            before[s, pl.ds(step * (STEP // CHUNK) + part, 1), :] = gone
            preceding[s] = gone + last
    end_state[...] = memory[...]
    total_decay[...] = preceding[...]


def forward_mix(projected, halo, low_rank, taps, rank_up, bias, dv):
    sequences, length, c3 = projected.shape
    rank, dk = rank_up.shape
    chunks = length // CHUNK
    per_step = STEP // CHUNK
    return call(
        forward_body,
        (length // STEP,),
        [
            rows3(sequences, STEP, c3),
            whole((sequences, 8, c3)),
            rows3(sequences, STEP, rank),
            whole(taps.shape),
            whole((rank, dk)),
            whole((1, dk)),
        ],
        [
            rows3(sequences, STEP, dv),
            rows3(sequences, STEP, dk),
            rows3(sequences, STEP, dk),
            pl.BlockSpec((sequences, per_step, dv, dk), lambda i: (0, i, 0, 0)),
            whole((sequences, chunks, dk)),
            whole((sequences, dv, dk)),
            whole((sequences, 1, dk)),
        ],
        [
            shape_of((sequences, length, dv), F32),
            shape_of((sequences, length, dk), BF16),
            shape_of((sequences, length, dk), F32),
            shape_of((sequences, chunks, dv, dk), BF16),
            shape_of((sequences, chunks, dk), F32),
            shape_of((sequences, dv, dk), F32),
            shape_of((sequences, 1, dk), F32),
        ],
        [
            pltpu.VMEM((sequences, STEP + 8, c3), F32),
            pltpu.VMEM((sequences, dv, dk), F32),
            pltpu.VMEM((sequences, 1, dk), F32),
        ],
        2 * sequences * length * (4 * dk * dv + dk * dk) * 8,
        sequences * (length * (c3 * 2 + dv * 4 + dk * 6) + chunks * dv * dk * 2),
    )(projected, halo, low_rank, taps, rank_up, bias)


def head_rows(head_local, query_profile, entering, scale):
    return (head_local + mm_nt(query_profile, entering.astype(BF16))) * scale


def gate_body(head_local, query_profile, entering, out_gate, gain, gated):
    scale = query_profile.shape[-1] ** (-0.5)
    for s in range(head_local.shape[0]):
        head = head_rows(head_local[s], query_profile[s], entering[s], scale)
        inverse = lax.rsqrt(jnp.mean(head * head, axis=-1, keepdims=True) + EPS_HEAD)
        logits = out_gate[s].astype(F32)
        gated[s] = (head * inverse * gain[...] * (logits * sigmoid(logits))).astype(BF16)


def gate(head_local, query_profile, entering, out_gate, gain):
    sequences, length, dv = head_local.shape
    dk = query_profile.shape[-1]
    return call(
        gate_body,
        (length // STEP,),
        [
            rows3(sequences, STEP, dv),
            rows3(sequences, STEP, dk),
            whole((sequences, dv, dk)),
            rows3(sequences, STEP, dv),
            whole((1, dv)),
        ],
        rows3(sequences, STEP, dv),
        shape_of((sequences, length, dv), BF16),
        [],
        2 * sequences * length * dk * dv * 4,
        sequences * length * (dv * 8 + dk * 2),
    )(head_local, query_profile, entering, out_gate, gain)


PIECE = 128
HALF = PIECE // 2


def ffn_body(
    gated, w_own, w_across, w_down_hop, w_far, tok, gain, w_gate, w_up, w_down, upstream,
    out_part, weight_grads, output_grads, grad_gated, own_residual, own_grad, gain_grad,
    g_across, g_down, g_far, tok_here, up_here, wg, wu, wd, normed, hidden, grad_gate, grad_up,
    out_stage, part, via_across, via_down, from_across, from_down, residual_here, grad_here,
    mixer_here, pieces, received, weight_stage, output_stage,
    load_sem, row_sem, ag_send, ag_recv, rs_send, rs_recv, back_send, back_recv, store_sem,
    stage_sem, last_sem,
):
    turns = up_here.shape[0]
    halves = 2
    width = tok_here.shape[-1]
    me = lax.axis_index("mp")
    across = me + 1 - 2 * (me % 2)
    down = (me + 2) % 4
    far = 3 - me
    MESH = pl.DeviceIdType.MESH

    def remote(source, target, send, recv, device):
        return pltpu.make_async_remote_copy(
            src_ref=source,
            dst_ref=target,
            send_sem=send,
            recv_sem=recv,
            device_id={"mp": device},
            device_id_type=MESH,
        )

    def load(index, source, target):
        return pltpu.make_async_copy(source, target, load_sem.at[index])

    def load_tok(turn):
        return pltpu.make_async_copy(
            tok.at[turn // halves, :, turn % halves], tok_here.at[turn % 2], row_sem.at[0, turn]
        )

    def load_up(turn):
        return pltpu.make_async_copy(
            upstream.at[turn // halves, :, turn % halves], up_here.at[turn], row_sem.at[1, turn]
        )

    def direct(turn, side):
        return remote(
            gated.at[turn // halves, :, turn % halves],
            (g_across, g_down)[side].at[turn],
            ag_send.at[side, turn],
            ag_recv.at[side, turn],
            (across, down)[side],
        )

    def relay(turn, side):
        cut = pl.ds(2 * side, 2)
        return remote(
            (g_across, g_down)[side].at[turn, cut],
            g_far.at[turn, cut],
            ag_send.at[2 + side, turn],
            ag_recv.at[2 + side, turn],
            (down, across)[side],
        )

    first, second = pl.ds(0, HALF), pl.ds(HALF, HALF)

    def scatter(turn, index):
        source, target, device = (
            (part.at[turn, far, first], via_across.at[turn], across),
            (part.at[turn, far, second], via_down.at[turn], down),
            (part.at[turn, across, first], from_across.at[turn, first], across),
            (part.at[turn, down, second], from_down.at[turn, second], down),
            (part.at[turn, across, second], from_across.at[turn, second], across),
            (part.at[turn, down, first], from_down.at[turn, first], down),
        )[index]
        return remote(source, target, rs_send.at[index, turn], rs_recv.at[index, turn], device)

    def give_back(turn, slot):
        return remote(
            pieces.at[turn, slot],
            received.at[turn, slot],
            back_send.at[slot, turn],
            back_recv.at[slot, turn],
            (me, across, down, far)[slot],
        )

    def store_out(turn):
        return pltpu.make_async_copy(
            out_stage.at[turn % 2],
            out_part.at[turn // halves, :, turn % halves],
            store_sem.at[turn],
        )

    barrier = pltpu.get_barrier_semaphore()
    loads = [load(0, w_gate, wg), load(1, w_up, wu), load(2, w_down, wd)]
    for copy in loads:
        copy.start()
    for turn in range(turns):
        if turn < 2:
            load_tok(turn).start()
        load_up(turn).start()
    for device in (across, down, far):
        pl.semaphore_signal(barrier, inc=1, device_id={"mp": device}, device_id_type=MESH)
    pl.semaphore_wait(barrier, 3)
    for side in range(2):
        direct(0, side).start()
    for side in range(2):
        direct(1, side).start()
    gain_grad[...] = jnp.zeros_like(gain_grad)
    for side in range(2):
        direct(0, side).wait_recv()
        relay(0, side).start()
    for copy in loads:
        copy.wait()

    def forward_and_back(turn):
        for side in range(2):

            @pl.when(turn + 1 < turns)
            def _():
                direct(turn + 1, side).wait_recv()
                relay(turn + 1, side).start()

            @pl.when(turn + 2 < turns)
            def _():
                direct(turn + 2, side).start()

        load_tok(turn).wait()
        load_up(turn).wait()
        for side in range(2):
            relay(turn, side).wait_recv()
        rows = 4 * PIECE

        def flat(values):
            return values.reshape(rows, values.shape[-1])

        mixed = mm(flat(gated[turn // halves, :, turn % halves]), w_own[...])
        mixed = mixed + mm(flat(g_across[turn]), w_across[...])
        mixed = mixed + mm(flat(g_down[turn]), w_down_hop[...])
        mixed = mixed + mm(flat(g_far[turn]), w_far[...])
        residual = flat(tok_here[turn % 2]).astype(F32) + mixed
        for quarter in range(4):

            @pl.when(me == quarter)
            def _():
                residual_here[turn] = residual[quarter * PIECE : (quarter + 1) * PIECE]

        inverse = lax.rsqrt(jnp.mean(residual * residual, axis=-1, keepdims=True) + EPS_NORM)
        unit = residual * inverse
        rounded = (unit * gain[...]).astype(BF16)
        normed[turn] = rounded
        gate_rows = mm(rounded, wg[...])
        up_rows = mm(rounded, wu[...])
        share = sigmoid(gate_rows)
        swished = gate_rows * share
        hidden_rows = (swished * up_rows).astype(BF16)
        hidden[turn] = hidden_rows
        grad_hidden = mm_nt(flat(up_here[turn]), wd[...])
        slope = share * (1.0 + gate_rows * (1.0 - share))
        grad_gate_rows = (grad_hidden * up_rows * slope).astype(BF16)
        grad_up_rows = (grad_hidden * swished).astype(BF16)
        grad_gate[turn] = grad_gate_rows
        grad_up[turn] = grad_up_rows
        grad_rows = mm_nt(grad_gate_rows, wg[...]) + mm_nt(grad_up_rows, wu[...])
        part[turn] = grad_rows.astype(BF16).reshape(4, PIECE, width)
        for index in range(4):
            scatter(turn, index).start()
        gain_grad[...] += jnp.sum(grad_rows * unit, axis=0, keepdims=True)

        @pl.when(turn >= 2)
        def _():
            store_out(turn - 2).wait()

        out_stage[turn % 2] = mm(hidden_rows, wd[...]).astype(BF16).reshape(4, PIECE, width)
        store_out(turn).start()

        @pl.when(turn + 2 < turns)
        def _():
            load_tok(turn + 2).start()

    def pass_on(turn):
        scatter(turn, 0).wait_recv()
        part[turn, down, 0:HALF] = part[turn, down, 0:HALF] + via_across[turn]
        scatter(turn, 5).start()
        scatter(turn, 1).wait_recv()
        part[turn, across, HALF:PIECE] = part[turn, across, HALF:PIECE] + via_down[turn]
        scatter(turn, 4).start()

    def collect(turn):
        for index in range(2, 6):
            scatter(turn, index).wait_recv()
        grad_normed = part[turn, me].astype(F32) + from_across[turn].astype(F32)
        grad_normed = grad_normed + from_down[turn].astype(F32)
        residual = residual_here[turn]
        inverse = lax.rsqrt(jnp.mean(residual * residual, axis=-1, keepdims=True) + EPS_NORM)
        unit = residual * inverse
        scaled = grad_normed * gain[...]
        through = inverse * (scaled - unit * jnp.mean(scaled * unit, axis=-1, keepdims=True))
        grad_residual = up_here[turn, me].astype(F32) + through
        grad_here[turn] = grad_residual
        grad_mixer = grad_residual.astype(BF16)
        mixer_here[turn] = grad_mixer
        for slot, weight in enumerate((w_own, w_across, w_down_hop, w_far)):
            piece = mm_nt(grad_mixer, weight[...]).astype(BF16)
            if slot == 0:
                received[turn, 0] = piece
            else:
                pieces[turn, slot] = piece
                give_back(turn, slot).start()

    def round_of(index, carry):
        @pl.when(index < turns)
        def _():
            forward_and_back(index)

        @pl.when(jnp.logical_and(index >= 1, index <= turns))
        def _():
            pass_on(index - 1)

        @pl.when(index >= 2)
        def _():
            collect(index - 2)

        return carry

    lax.fori_loop(0, turns + 2, round_of, 0)

    tile = weight_stage.shape[2]
    tiles = width // tile

    def store_weight(kind, index, slot):
        return pltpu.make_async_copy(
            weight_stage.at[slot, kind],
            weight_grads.at[kind, pl.ds(index * tile, tile)],
            stage_sem.at[slot, kind],
        )

    all_rows = turns * 4 * PIECE

    def weight_tile(index, carry):
        slot = index % 2
        columns = pl.ds(pl.multiple_of(index * tile, tile), tile)

        @pl.when(index >= 2)
        def _():
            for kind in range(3):
                store_weight(kind, index - 2, slot).wait()

        left = normed[:, :, columns].reshape(all_rows, tile)
        upper = up_here[:, :, :, columns].reshape(all_rows, tile)
        units = hidden.shape[-1]
        for kind, (one, other) in enumerate(
            ((left, grad_gate), (left, grad_up), (upper, hidden))
        ):
            weight_stage[slot, kind] = mm_tn(one, other[...].reshape(all_rows, units)).astype(BF16)
            store_weight(kind, index, slot).start()
        return carry

    lax.fori_loop(0, tiles, weight_tile, 0)
    mixer_rows = mixer_here[...].reshape(turns * PIECE, width)
    dv = gated.shape[-1]
    for slot in range(4):
        if slot == 0:
            blocks = [gated[t // halves, me, t % halves] for t in range(turns)]
        else:
            source = (None, g_across, g_down, g_far)[slot]
            blocks = [source[t, me] for t in range(turns)]
        rows = jnp.concatenate(blocks, axis=0)
        output_stage[slot] = mm_tn(mixer_rows, rows).astype(BF16)

    last = [
        pltpu.make_async_copy(residual_here, own_residual, last_sem.at[0]),
        pltpu.make_async_copy(grad_here, own_grad, last_sem.at[1]),
        pltpu.make_async_copy(output_stage, output_grads, last_sem.at[2]),
    ]
    for copy in last:
        copy.start()
    for turn in range(turns):
        for slot in range(1, 4):
            give_back(turn, slot).wait_recv()
        for slot in range(4):
            source = (me, across, down, far)[slot]
            pltpu.make_async_copy(
                received.at[turn, slot],
                grad_gated.at[turn // halves, source, turn % halves],
                last_sem.at[3 + turn * 4 + slot],
            ).start()
    for turn in range(turns):
        for slot in range(4):
            source = (me, across, down, far)[slot]
            pltpu.make_async_copy(
                received.at[turn, slot],
                grad_gated.at[turn // halves, source, turn % halves],
                last_sem.at[3 + turn * 4 + slot],
            ).wait()
        if turn >= turns - 2:
            store_out(turn).wait()
        for side in range(2):
            direct(turn, side).wait_send()
            relay(turn, side).wait_send()
        for index in range(6):
            scatter(turn, index).wait_send()
        for slot in range(1, 4):
            give_back(turn, slot).wait_send()
    for index in range(max(tiles - 2, 0), tiles):
        for kind in range(3):
            store_weight(kind, index, index % 2).wait()
    for copy in last:
        copy.wait()


def feed_forward(gated, weights, tok, gain, w_gate, w_up, w_down, upstream):
    sequences, length, width = tok.shape
    dv, units = gated.shape[-1], w_gate.shape[1]
    halves = length // 4 // PIECE
    turns = sequences * halves

    def pieces_of(values):
        return values.reshape(sequences, 4, halves, PIECE, values.shape[-1])

    anywhere = pl.BlockSpec(memory_space=pl.ANY)
    vmem = pl.BlockSpec(memory_space=pltpu.VMEM)
    dma = pltpu.SemaphoreType.DMA
    rows = 4 * PIECE
    outs = pl.pallas_call(
        ffn_body,
        in_specs=[vmem] * 5 + [anywhere, vmem] + [anywhere] * 4,
        out_specs=[anywhere] * 6 + [vmem],
        out_shape=[
            shape_of((sequences, 4, halves, PIECE, width), BF16),
            shape_of((3, width, units), BF16),
            shape_of((4, width, dv), BF16),
            shape_of((sequences, 4, halves, PIECE, dv), BF16),
            shape_of((turns, PIECE, width), F32),
            shape_of((turns, PIECE, width), F32),
            shape_of((1, width), F32),
        ],
        scratch_shapes=[
            pltpu.VMEM((turns, 4, PIECE, dv), BF16),
            pltpu.VMEM((turns, 4, PIECE, dv), BF16),
            pltpu.VMEM((turns, 4, PIECE, dv), BF16),
            pltpu.VMEM((2, 4, PIECE, width), BF16),
            pltpu.VMEM((turns, 4, PIECE, width), BF16),
            pltpu.VMEM((width, units), BF16),
            pltpu.VMEM((width, units), BF16),
            pltpu.VMEM((units, width), BF16),
            pltpu.VMEM((turns, rows, width), BF16),
            pltpu.VMEM((turns, rows, units), BF16),
            pltpu.VMEM((turns, rows, units), BF16),
            pltpu.VMEM((turns, rows, units), BF16),
            pltpu.VMEM((2, 4, PIECE, width), BF16),
            pltpu.VMEM((turns, 4, PIECE, width), BF16),
            pltpu.VMEM((turns, HALF, width), BF16),
            pltpu.VMEM((turns, HALF, width), BF16),
            pltpu.VMEM((turns, PIECE, width), BF16),
            pltpu.VMEM((turns, PIECE, width), BF16),
            pltpu.VMEM((turns, PIECE, width), F32),
            pltpu.VMEM((turns, PIECE, width), F32),
            pltpu.VMEM((turns, PIECE, width), BF16),
            pltpu.VMEM((turns, 4, PIECE, dv), BF16),
            pltpu.VMEM((turns, 4, PIECE, dv), BF16),
            pltpu.VMEM((2, 3, 256, units), BF16),
            pltpu.VMEM((4, width, dv), BF16),
            dma((3,)),
            dma((2, turns)),
            dma((4, turns)),
            dma((4, turns)),
            dma((6, turns)),
            dma((6, turns)),
            dma((4, turns)),
            dma((4, turns)),
            dma((turns,)),
            dma((2, 3)),
            dma((3 + 4 * turns,)),
        ],
        compiler_params=pltpu.CompilerParams(
            collective_id=0, has_side_effects=True, vmem_limit_bytes=64 * 2**20
        ),
        cost_estimate=pl.CostEstimate(
            flops=2 * sequences * length * width * (4 * dv + 9 * units),
            bytes_accessed=sequences * length * width * 8,
            transcendentals=0,
        ),
        name="feed_forward",
    )(pieces_of(gated), *weights, pieces_of(tok), gain, w_gate, w_up, w_down, pieces_of(upstream))
    out_part, weight_grads, output_grads, grad_gated, own_residual, own_grad, gain_grad = outs
    return (
        out_part.reshape(sequences, 4, length // 4, width),
        weight_grads,
        output_grads,
        grad_gated.reshape(sequences, length, dv),
        own_residual.reshape(sequences, length // 4, width),
        own_grad.reshape(sequences, length // 4, width),
        gain_grad,
    )


def ungate_body(
    grad_gated, head_local, query_profile, entering, out_gate, gain,
    grad_out_gate, grad_head, state_grad, gain_grad,
):
    step = pl.program_id(0)

    @pl.when(step == 0)
    def _():
        state_grad[...] = jnp.zeros_like(state_grad)
        gain_grad[...] = jnp.zeros_like(gain_grad)

    scale = query_profile.shape[-1] ** (-0.5)
    for s in range(head_local.shape[0]):
        upper = grad_gated[s].astype(F32)
        head = head_rows(head_local[s], query_profile[s], entering[s], scale)
        inverse = lax.rsqrt(jnp.mean(head * head, axis=-1, keepdims=True) + EPS_HEAD)
        unit = head * inverse
        logits = out_gate[s].astype(F32)
        share = sigmoid(logits)
        slope = share * (1.0 + logits * (1.0 - share))
        grad_out_gate[s] = (upper * unit * gain[...] * slope).astype(BF16)
        grad_normed = upper * (logits * share)
        gain_grad[...] += jnp.sum(grad_normed * unit, axis=0, keepdims=True)
        scaled = grad_normed * gain[...]
        through = inverse * (scaled - unit * jnp.mean(scaled * unit, axis=-1, keepdims=True))
        rounded = (through * scale).astype(BF16)
        grad_head[s] = rounded
        state_grad[s] += mm_tn(rounded, query_profile[s])


def ungate(grad_gated, head_local, query_profile, entering, out_gate, gain):
    sequences, length, dv = head_local.shape
    dk = query_profile.shape[-1]
    return call(
        ungate_body,
        (length // STEP,),
        [
            rows3(sequences, STEP, dv),
            rows3(sequences, STEP, dv),
            rows3(sequences, STEP, dk),
            whole((sequences, dv, dk)),
            rows3(sequences, STEP, dv),
            whole((1, dv)),
        ],
        [
            rows3(sequences, STEP, dv),
            rows3(sequences, STEP, dv),
            whole((sequences, dv, dk)),
            whole((1, dv)),
        ],
        [
            shape_of((sequences, length, dv), BF16),
            shape_of((sequences, length, dv), BF16),
            shape_of((sequences, dv, dk), F32),
            shape_of((1, dv), F32),
        ],
        [],
        2 * sequences * length * dk * dv * 8,
        sequences * length * (dv * 12 + dk * 2),
    )(grad_gated, head_local, query_profile, entering, out_gate, gain)


def backward_body(
    projected, earlier, halo, low_rank, taps_in, rank_up, bias, cumulative, states, before,
    entering, leaving, grad_head,
    grad_projected, grad_low_rank, first_rows, filter_grad, rank_up_grad, bias_grad,
    extended, grad_extended, upstream,
):
    back = pl.program_id(0)
    step = pl.num_programs(0) - 1 - back
    per_step = STEP // CHUNK
    sequences = projected.shape[0]

    @pl.when(back == 0)
    def _():
        upstream[...] = leaving[...]
        grad_extended[:, STEP : STEP + 8, :] = jnp.zeros_like(grad_extended[:, STEP : STEP + 8, :])
        filter_grad[...] = jnp.zeros_like(filter_grad)
        rank_up_grad[...] = jnp.zeros_like(rank_up_grad)
        bias_grad[...] = jnp.zeros_like(bias_grad)

    @pl.when(back > 0)
    def _():
        grad_extended[:, STEP : STEP + 8, :] = grad_extended[:, 0:8, :]

    @pl.when(step == 0)
    def _():
        extended[:, 0:8, :] = halo[...]

    @pl.when(step > 0)
    def _():
        extended[:, 0:8, :] = earlier[...].astype(F32)[:, 8:16, :]

    taps = taps_in[...]
    width = rank_up.shape[1]
    causal = triangle(True)
    for s in range(sequences):
        extended[s, 8 : 8 + STEP, :] = projected[s].astype(F32)
        filtered = filter_rows(extended.at[s], taps, STEP)
        share = sigmoid(filtered)
        convolved = (filtered * share).astype(BF16)
        slope = share * (1.0 + filtered * (1.0 - share))
        logit = mm(low_rank[s], rank_up[...]) + bias[...]
        logit_grads = [None] * per_step
        for part in reversed(range(per_step)):
            rows = slice(part * CHUNK, (part + 1) * CHUNK)
            queries = convolved[rows, :width].astype(F32)
            keys = convolved[rows, width : 2 * width].astype(F32)
            values = convolved[rows, 2 * width :]
            grad_rows = grad_head[s, rows, :]
            total = cumulative[s, rows, :]
            middle, last = total[CHUNK // 2 - 1 : CHUNK // 2], total[CHUNK - 1 : CHUNK]
            lift, lower = jnp.exp(total - middle), jnp.exp(middle - total)
            inner, outer, whole_decay = jnp.exp(total), jnp.exp(last - total), jnp.exp(last)
            lifted, lowered = (queries * lift).astype(BF16), (keys * lower).astype(BF16)
            profile, tails = (queries * inner).astype(BF16), (keys * outer).astype(BF16)
            previous = before[s, pl.ds(step * per_step + part, 1), :]
            state = states[s, part].astype(F32) + entering[s] * jnp.exp(previous)
            scores = jnp.where(causal, mm_nt(lifted, lowered), 0.0).astype(BF16)
            grad_scores = jnp.where(causal, mm_nt(grad_rows, values), 0.0).astype(BF16)
            later = upstream[s]
            later_low = later.astype(BF16)
            grad_values = mm_tn(scores, grad_rows) + mm_nt(tails, later_low)
            grad_lifted = mm(grad_scores, lowered)
            grad_lowered = mm_tn(grad_scores, lifted)
            grad_profile = mm(grad_rows, state.astype(BF16))
            grad_tails = mm(values, later_low)
            upstream[s] = later * whole_decay + mm_tn(grad_rows, profile)
            tail_terms = tails.astype(F32) * grad_tails
            grad_total = (
                lifted.astype(F32) * grad_lifted
                - lowered.astype(F32) * grad_lowered
                + profile.astype(F32) * grad_profile
                - tail_terms
            )
            grad_last = jnp.sum(tail_terms, axis=0, keepdims=True) + whole_decay * jnp.sum(
                later * state, axis=0, keepdims=True
            )
            grad_decay = running_sum(grad_total, False) + grad_last
            logit_grads[part] = grad_decay / GATE_NORMALIZER * sigmoid(-logit[rows])
            grad_extended[s, rows, :width] = (
                grad_lifted * lift + grad_profile * inner
            ) * slope[rows, :width]
            grad_extended[s, rows, width : 2 * width] = (
                grad_lowered * lower + grad_tails * outer
            ) * slope[rows, width : 2 * width]
            grad_extended[s, rows, 2 * width :] = grad_values * slope[rows, 2 * width :]
        logit_grad = jnp.concatenate(logit_grads, axis=0)
        logit_low = logit_grad.astype(BF16)
        bias_grad[...] += jnp.sum(logit_grad, axis=0, keepdims=True)
        rank_up_grad[...] += mm_tn(low_rank[s], logit_low)
        grad_low_rank[s] = mm_nt(logit_low, rank_up[...]).astype(BF16)
        total_rows = taps[EDGE : EDGE + 1, :] * grad_extended[s, 0:STEP, :]
        for offset in range(EDGE):
            total_rows = total_rows + taps[offset : offset + 1, :] * grad_extended[
                s, pl.ds(EDGE - offset, STEP), :
            ]
        grad_projected[s] = total_rows.astype(BF16)
        grad_filtered = grad_extended[s, 0:STEP, :]
        for offset in range(CONV):
            filter_grad[offset : offset + 1, :] += jnp.sum(
                grad_filtered * extended[s, pl.ds(8 - EDGE + offset, STEP), :],
                axis=0,
                keepdims=True,
            )
        first_rows[s] = grad_extended[s, 0:8, :]


def backward_mix(
    projected, halo, low_rank, taps, rank_up, bias, cumulative, states, before, entering,
    leaving, grad_head,
):
    sequences, length, c3 = projected.shape
    rank, dk = rank_up.shape
    dv = grad_head.shape[-1]
    chunks, per_step, steps = length // CHUNK, STEP // CHUNK, length // STEP

    def reverse(size, width):
        return pl.BlockSpec((sequences, size, width), lambda i: (0, steps - 1 - i, 0))

    return call(
        backward_body,
        (steps,),
        [
            reverse(STEP, c3),
            pl.BlockSpec(
                (sequences, 16, c3),
                lambda i: (0, jnp.maximum((steps - 1 - i) * (STEP // 16) - 1, 0), 0),
            ),
            whole((sequences, 8, c3)),
            reverse(STEP, rank),
            whole(taps.shape),
            whole((rank, dk)),
            whole((1, dk)),
            reverse(STEP, dk),
            pl.BlockSpec((sequences, per_step, dv, dk), lambda i: (0, steps - 1 - i, 0, 0)),
            whole((sequences, chunks, dk)),
            whole((sequences, dv, dk)),
            whole((sequences, dv, dk)),
            reverse(STEP, dv),
        ],
        [
            reverse(STEP, c3),
            reverse(STEP, rank),
            whole((sequences, 8, c3)),
            whole(taps.shape),
            whole((rank, dk)),
            whole((1, dk)),
        ],
        [
            shape_of((sequences, length, c3), BF16),
            shape_of((sequences, length, rank), BF16),
            shape_of((sequences, 8, c3), F32),
            shape_of(taps.shape, F32),
            shape_of((rank, dk), F32),
            shape_of((1, dk), F32),
        ],
        [
            pltpu.VMEM((sequences, STEP + 8, c3), F32),
            pltpu.VMEM((sequences, STEP + 8, c3), F32),
            pltpu.VMEM((sequences, dv, dk), F32),
        ],
        2 * sequences * length * (12 * dk * dv) * 8,
        sequences * (length * (c3 * 4 + dk * 4 + dv * 2) + chunks * dv * dk * 2),
    )(
        projected, projected, halo, low_rank, taps, rank_up, bias, cumulative, states, before,
        entering, leaving, grad_head,
    )


def input_grad_body(
    grad_projected, grad_out_gate, grad_low_rank, w_proj, w_gate, w_rank, normed,
    parts, gain_grad,
):
    @pl.when(pl.program_id(0) == 0)
    def _():
        gain_grad[...] = jnp.zeros_like(gain_grad)

    for s in range(normed.shape[0]):
        total = mm_nt(grad_projected[s], w_proj[...]) + mm_nt(grad_out_gate[s], w_gate[...])
        total = total + mm_nt(grad_low_rank[s], w_rank[...])
        parts[s] = total.astype(BF16)
        gain_grad[...] += jnp.sum(total * normed[s].astype(F32), axis=0, keepdims=True)


def input_grad(grad_projected, grad_out_gate, grad_low_rank, w_proj, w_gate, w_rank, normed):
    sequences, length, width = normed.shape
    c3, dv, rank = w_proj.shape[1], w_gate.shape[1], w_rank.shape[1]
    return call(
        input_grad_body,
        (length // STEP,),
        [
            rows3(sequences, STEP, c3),
            rows3(sequences, STEP, dv),
            rows3(sequences, STEP, rank),
            whole((width, c3)),
            whole((width, dv)),
            whole((width, rank)),
            rows3(sequences, STEP, width),
        ],
        [rows3(sequences, STEP, width), whole((1, width))],
        [shape_of((sequences, length, width), BF16), shape_of((1, width), F32)],
        [],
        2 * sequences * length * width * (c3 + dv + rank),
        sequences * length * (2 * width + c3 + dv) * 2 + width * (c3 + dv) * 2,
    )(grad_projected, grad_out_gate, grad_low_rank, w_proj, w_gate, w_rank, normed)


ACROSS = [(i, i ^ 1) for i in range(4)]
DOWN = [(i, i ^ 2) for i in range(4)]
OPPOSITE = [(i, i ^ 3) for i in range(4)]


def gather_relative(block):
    half = block.shape[0] // 2
    across = lax.ppermute(block, "mp", ACROSS)
    down = lax.ppermute(block, "mp", DOWN)
    first = lax.ppermute(across[:half], "mp", DOWN)
    second = lax.ppermute(down[half:], "mp", ACROSS)
    return [block, across, down, jnp.concatenate([first, second], axis=0)]


def scatter_rows(first, across, down, far):
    via_across = lax.ppermute(far[:1], "mp", ACROSS)
    via_down = lax.ppermute(far[1:], "mp", DOWN)
    across_a = lax.ppermute(across[:1], "mp", ACROSS)
    down_b = lax.ppermute(down[1:], "mp", DOWN)
    across_b = lax.ppermute(across[1:] + via_down, "mp", ACROSS)
    down_a = lax.ppermute(down[:1] + via_across, "mp", DOWN)
    across = jnp.concatenate([across_a, across_b], axis=0).astype(F32)
    down = jnp.concatenate([down_a, down_b], axis=0).astype(F32)
    return first.astype(F32) + across + down


def scatter_quarters(parts, me):
    return scatter_rows(
        *[lax.dynamic_index_in_dim(parts, me ^ slot, 1, False) for slot in range(4)]
    )


def passed_along(block, axis, distance):
    devices = range(lax.axis_size(axis))
    route = [(i - distance, i) for i in devices if i - distance in devices]
    return lax.ppermute(block, axis, route)


def chain_states(decay, state, backward):
    count, mine = lax.axis_size("seq"), lax.axis_index("seq")
    if count == 2:
        return passed_along(state, "seq", -1 if backward else 1)
    decays, states = lax.all_gather(decay, "seq"), lax.all_gather(state, "seq")
    if backward:
        decays, states, mine = decays[::-1], states[::-1], count - 1 - mine

    def hop(position, subtotal):
        longer = subtotal * jnp.exp(decays[position]) + states[position]
        return jnp.where(position < mine, longer, subtotal)

    return lax.fori_loop(0, count - 1, hop, jnp.zeros_like(state))


def sum_shards(grad):
    if lax.axis_size("seq") != 2 or lax.axis_size("dp") != 4:
        total = lax.psum_scatter(grad, ("seq", "dp"), scatter_dimension=0, tiled=True)
        return total[0].astype(F32)
    side, place = lax.axis_index("seq"), lax.axis_index("dp")
    other = lax.dynamic_slice_in_dim(grad, (1 - side) * 4, 4, 0)
    kept = lax.dynamic_slice_in_dim(grad, side * 4, 4, 0)
    kept = kept + lax.ppermute(other, "seq", [(0, 1), (1, 0)])
    upward, downward = None, None
    for turn in range(1, 4):
        above = lax.dynamic_index_in_dim(kept, jnp.minimum(place + 4 - turn, 3), 0, False)
        below = lax.dynamic_index_in_dim(kept, jnp.maximum(place - 4 + turn, 0), 0, False)
        if turn > 1:
            above, below = above + upward, below + downward
        upward = lax.ppermute(above, "dp", [(i, i + 1) for i in range(turn)])
        downward = lax.ppermute(below, "dp", [(3 - i, 2 - i) for i in range(turn)])
    mine = lax.dynamic_index_in_dim(kept, place, 0, False)
    return mine.astype(F32) + upward.astype(F32) + downward.astype(F32)


def sum_over(values, axes):
    for axis in axes:
        count = lax.axis_size(axis)
        if count & (count - 1) or count > 4:
            values = lax.psum(values, axis)
            continue
        distance = 1
        while distance < count:
            values = values + lax.ppermute(values, axis, [(i, i ^ distance) for i in range(count)])
            distance *= 2
    return values


def on_device(
    tokens, lengths, mixer_gain, project_weight, filter_weight, rank_down, rank_up, decay_bias,
    gate_weight, head_gain, output_weight, channel_gain, hidden_gate, hidden_up, hidden_down,
    cotangent,
):
    length, sequences, width = tokens.shape
    shards = lax.axis_size("seq") * lax.axis_size("dp")
    shard = lax.axis_index("seq") * lax.axis_size("dp") + lax.axis_index("dp")
    me = lax.axis_index("mp")
    own_rows = length // lax.axis_size("mp")
    w_proj = project_weight[:, 0]
    taps = filter_weight[:, 0].astype(F32)
    rank_up_here = rank_up[:, 0]
    bias = decay_bias.astype(F32)
    mixer_gain_f = mixer_gain.astype(F32)[None]
    channel_gain_f = channel_gain.astype(F32)[None]
    head_gain_f = head_gain.astype(F32)[None]
    dv = gate_weight.shape[1]
    places = jnp.concatenate(
        [lengths.astype(jnp.int32), (lax.axis_index("seq") * length).astype(jnp.int32).reshape(1)]
    )

    edge_tokens = passed_along(tokens[length - EDGE :], "seq", 1)
    edge_f = edge_tokens.astype(F32)
    edge_inverse = lax.rsqrt(jnp.mean(edge_f * edge_f, axis=-1, keepdims=True) + EPS_NORM)
    edge_normed = (edge_f * edge_inverse * mixer_gain_f).astype(BF16)
    edge_projected = jnp.einsum(
        "psd,dc->spc", edge_normed, w_proj, preferred_element_type=F32
    ).astype(BF16)
    halo = jnp.pad(edge_projected.astype(F32), ((0, 0), (8 - EDGE, 0), (0, 0)))

    output_weights = gather_relative(output_weight)
    tok, upstream, normed, projected, out_gate, low_rank = project(
        places,
        tokens.reshape(length * sequences, width),
        cotangent.reshape(length * sequences, width),
        sequences,
        mixer_gain_f,
        w_proj,
        gate_weight,
        rank_down,
    )
    head_local, query_profile, cumulative, states, before, end_state, total_decay = forward_mix(
        projected, halo, low_rank, taps, rank_up_here, bias, dv
    )
    entering = chain_states(total_decay, end_state, False)
    gated = gate(head_local, query_profile, entering, out_gate, head_gain_f)
    (
        out_part, hidden_grads, output_parts, grad_gated, residual, grad_residual,
        channel_gain_part,
    ) = feed_forward(
        gated, output_weights, tok, channel_gain_f, hidden_gate, hidden_up, hidden_down, upstream
    )
    grad_out_gate, grad_head, state_grad, head_gain_part = ungate(
        grad_gated, head_local, query_profile, entering, out_gate, head_gain_f
    )
    leaving = chain_states(total_decay, state_grad, True)
    (
        grad_projected, grad_low_rank, first_rows, filter_part, rank_up_part, bias_part,
    ) = backward_mix(
        projected, halo, low_rank, taps, rank_up_here, bias, cumulative, states, before,
        entering, leaving, grad_head,
    )
    edge = jnp.concatenate(
        [
            sum(taps[j : j + 1] * first_rows[:, i - j : i - j + 1] for j in range(i + 1))
            for i in range(EDGE)
        ],
        axis=1,
    )
    edge = passed_along(edge, "seq", -1)
    tail = grad_projected[:, length - 16 :].astype(F32)
    tail = tail + jnp.pad(edge, ((0, 0), (16 - EDGE, 0), (0, 0)))
    grad_projected = lax.dynamic_update_slice_in_dim(
        grad_projected, tail.astype(BF16), length - 16, 1
    )
    normed_parts, mixer_gain_part = input_grad(
        grad_projected, grad_out_gate, grad_low_rank, w_proj, gate_weight, rank_down, normed
    )

    def flat(values):
        return values.reshape(sequences * length, values.shape[-1])

    def in_shards(grad):
        return grad.astype(BF16).reshape(shards, width // shards, grad.shape[-1])

    hidden_grads = hidden_grads.reshape(3, shards, width // shards, hidden_grads.shape[-1])
    hidden_grads = sum_shards(hidden_grads.swapaxes(0, 1))
    halved = output_parts.reshape(4, 2, width // 2, dv)
    output_grad = scatter_rows(*[halved[slot] for slot in range(4)])
    mixer_grads = jnp.concatenate(
        [
            in_shards(mm_tn(flat(normed), flat(grad_projected))),
            in_shards(mm_tn(flat(normed), flat(grad_out_gate))),
            in_shards(output_grad.reshape(width, dv)),
        ],
        axis=-1,
    )
    mixer_grads = sum_shards(mixer_grads)
    c3 = w_proj.shape[1]

    shared = [
        mixer_gain_part[0] / mixer_gain_f[0],
        channel_gain_part[0],
        head_gain_part[0],
        mm_tn(flat(normed), flat(grad_low_rank)).reshape(-1),
    ]
    local = [filter_part.reshape(-1), rank_up_part.reshape(-1), bias_part.reshape(-1)]
    shared_size = sum(part.shape[0] for part in shared)
    small = sum_over(jnp.concatenate(shared + local), ("seq", "dp"))
    shared_sum = sum_over(small[:shared_size], ("mp",))

    def take(values, start, shape):
        count = 1
        for size in shape:
            count *= size
        return lax.slice_in_dim(values, start, start + count).reshape(shape)

    def own(values):
        share = values.shape[-1] // shards
        return lax.dynamic_slice_in_dim(values, shard * share, share, values.ndim - 1)

    mixer_gain_grad = take(shared_sum, 0, (width,))
    channel_gain_grad = take(shared_sum, width, (width,))
    head_gain_grad = take(shared_sum, 2 * width, (dv,))
    rank_down_grad = take(shared_sum, 2 * width + dv, rank_down.shape)
    filter_grad = own(take(small, shared_size, filter_weight.shape))
    start = shared_size + filter_weight.size
    rank_up_grad = own(take(small, start, rank_up.shape))
    decay_bias_grad = own(take(small, start + rank_up.size, decay_bias.shape))

    own_shape = (sequences, 4, own_rows, width)
    ffn_out = scatter_quarters(out_part, me)
    own_positions = lax.axis_index("seq") * length + me * own_rows
    own_positions = own_positions + lax.broadcasted_iota(jnp.int32, (1, own_rows, 1), 1)
    own_mask = own_positions < lengths[:, None, None]
    outputs = jnp.where(own_mask, residual + ffn_out, 0.0).astype(BF16)
    grad_normed = scatter_quarters(normed_parts.reshape(own_shape), me)
    rows = lax.dynamic_index_in_dim(tok.reshape(own_shape), me, 1, False).astype(F32)
    inverse = lax.rsqrt(jnp.mean(rows * rows, axis=-1, keepdims=True) + EPS_NORM)
    unit = rows * inverse
    scaled = grad_normed * mixer_gain_f
    through = inverse * (scaled - unit * jnp.mean(scaled * unit, axis=-1, keepdims=True))
    token_grads = grad_residual + through
    return (
        outputs.swapaxes(0, 1),
        token_grads.swapaxes(0, 1),
        mixer_gain_grad,
        mixer_grads[:, None, :c3],
        filter_grad,
        rank_down_grad,
        rank_up_grad,
        decay_bias_grad,
        mixer_grads[:, c3 : c3 + dv],
        head_gain_grad,
        mixer_grads[:, c3 + dv :].T,
        channel_gain_grad,
        hidden_grads[0],
        hidden_grads[1],
        hidden_grads[2].T,
    )


def solution(mesh):
    in_specs = (
        P("seq", "dp", None),
        P("dp"),
        P(),
        P(None, "mp", None),
        P(None, "mp", None),
        P(),
        P(None, "mp", None),
        P("mp", None),
        P(None, "mp"),
        P(),
        P("mp", None),
        P(),
        P(None, "mp"),
        P(None, "mp"),
        P("mp", None),
        P("seq", "dp", None),
    )
    out_specs = (
        P(("seq", "mp"), "dp", None),
        P(("seq", "mp"), "dp", None),
        P(),
        P(("seq", "dp"), "mp", None),
        P(None, "mp", ("seq", "dp")),
        P(),
        P(None, "mp", ("seq", "dp")),
        P("mp", ("seq", "dp")),
        P(("seq", "dp"), "mp"),
        P(),
        P("mp", ("seq", "dp")),
        P(),
        P(("seq", "dp"), "mp"),
        P(("seq", "dp"), "mp"),
        P("mp", ("seq", "dp")),
    )
    return jax.shard_map(
        on_device, mesh=mesh, in_specs=in_specs, out_specs=out_specs, check_vma=False
    )
```

time: 487 us -> 385 us (0.79)
  starting transfers between devices: 121 us -> 68.3 us
  Pallas kernels: 124 us -> 166 us
  matrix products: 42.1 us -> 8.15 us
  local copies, waits for them, and re-layouts: 81.6 us -> 53.2 us
  other arithmetic: 37.8 us -> 25.3 us
  waiting for transfers between devices: 68.2 us -> 56.4 us
    ppermute x48 -> x18, starting transfers between devices: 60.7 us -> 18.5 us  [the longest x3 4.49 us: scatter_rows(): via_down = lax.ppermute(far[1:], 'mp', DOWN)]
    pallas_call x14 -> x7, Pallas kernels: 124 us -> 166 us  [the longest x1 97.2 us: feed_forward(): pl.pallas_call(ffn_body, in_specs=[vmem] * 5 + [anywhere, vmem] + [anywhe...]
    dot_general x20 -> x3, matrix products: 36.6 us -> 7.89 us  [mm_tn(): lax.dot_general(left, right, (((0,), (0,)), ((), ())), preferred_element_...]
    unnamed x193 -> x90, local copies, waits for them, and re-layouts: 35.2 us -> 20 us
    reshape x1 -> x3, local copies, waits for them, and re-layouts: 0.19 us -> 14.6 us  [the longest x1 7.23 us: on_device(): cotangent.reshape(length * sequences, width)]
    slice x3 -> x5, local copies, waits for them, and re-layouts: 21 us -> 8.07 us  [the longest x2 3.54 us: scatter_rows(): across_a = lax.ppermute(across[:1], 'mp', ACROSS)]
    squeeze x10 -> x0, local copies, waits for them, and re-layouts: 9.01 us -> none  [the longest x5 4.6 us: scatter_relative(): across_a = lax.ppermute(parts[1, :half], 'mp', ACROSS)]
    ppermute x48 -> x18, waiting for transfers between devices: 29.6 us -> 20.7 us  [the longest x3 9.16 us: scatter_rows(): via_down = lax.ppermute(far[1:], 'mp', DOWN)]
  transfers between devices with their start and end apart: 86 -> 45, of which waited for: 32 -> 15; matrix products, arithmetic and copies ran while one was open for 30% -> 22% of each run, Pallas kernels for 26% -> 16%
where the time goes in v2:
time: 385 us; the launch traced here: 379 us
  Pallas kernels  166 us (43%)
  starting transfers between devices  68.3 us (18%)
  waiting for transfers between devices  56.4 us (15%)
  local copies, waits for them, and re-layouts  53.2 us (14%)
  other arithmetic  25.3 us (7%)
  matrix products  8.15 us (2%)
    pallas_call x1, Pallas kernels, feed_forward(): pl.pallas_call(ffn_body, in_specs=[vmem] * 5 + [anywhere, vmem] + [anywhe...  97.2 us
    ppermute x6, starting transfers between devices, sum_shards(): upward = lax.ppermute(above, 'dp', [(i, i + 1) for i in range(turn)])  26.2 us
    unnamed x90, local copies, waits for them, and re-layouts  20 us
    pallas_call x1, Pallas kernels, backward_mix(): call(backward_body, (steps,), [reverse(STEP, c3), pl.BlockSpec((sequences...  18.6 us
    pallas_call x1, Pallas kernels, project(): call(project_body, (length // CHUNK,), [rows_of(CHUNK * sequences, width)...  15.1 us
    ppermute x6, waiting for transfers between devices, sum_shards(): upward = lax.ppermute(above, 'dp', [(i, i + 1) for i in range(turn)])  13.7 us
    pallas_call x1, Pallas kernels, forward_mix(): call(forward_body, (length // STEP,), [rows3(sequences, STEP, c3), whole(...  13 us
    ppermute x5, waiting for transfers between devices, sum_over(): lax.ppermute(values, axis, [(i, i ^ distance) for i in range(count)])  11 us
  transfers between devices with their start and end apart: 45, of which 15 were waited for; matrix products, arithmetic and copies ran while one was open for 22% of the time, Pallas kernels for 16%

profile of v2, /device:TPU:0, one launch (start us, length us, event | category | flops | bytes accessed | tf_op | source)
XLA Modules:
  0.0 379.2 jit_solution(12359910289836147205)
XLA Ops:
  0.6 3.0 collective-permute-start.2
  3.6 1.5 collective-permute-start.3
  7.2 7.2 %reshape.243.tok_in = bf16[2048,1024]{1,0:T(8,128)(2,1)} reshape(bf16[1024,2,1024]{2,1,0:T(2,128)(2,1)} %param.16) | data formatting | bytes 8388608 | tf_op jit(solution)/shard_map/reshape | solution.py:1062
  17.1 7.2 %reshape.244.cot_in = bf16[2048,1024]{1,0:T(8,128)(2,1)} reshape(bf16[1024,2,1024]{2,1,0:T(2,128)(2,1)} %param.31) | data formatting | bytes 8388608 | tf_op jit(solution)/shard_map/reshape | solution.py:1063
  24.9 15.1 %shard_map.271 = (bf16[2,1024,1024]{2,1,0:T(8,128)(2,1)}, bf16[2,1024,1024]{2,1,0:T(8,128)(2,1)}, bf16[2,1024,1024]{2,1,0:T(8,128)(2,1)}, bf16[2,1024,512]{2,1,0...) custom-call(s32[3]{0:T(128)} %pad_add_fusion.places, bf16[2048,1024]{1,0:T(8,128)(2,1)} %reshape.243.tok_in, ...), custom_call_target="tpu_custom_call" | custom-call | flops 5435817984 | bytes 25690112 | tf_op jit(solution)/shard_map/pallas_call | solution.py:107
  40.0 1.5 fusion.7
  43.2 13.0 %shard_map.272 = (f32[2,1024,256]{2,1,0:T(8,128)}, bf16[2,1024,128]{2,1,0:T(8,128)(2,1)}, f32[2,1024,128]{2,1,0:T(8,128)}, bf16[2,8,256,128]{3,2,1,0:T(8,128)(2,...) custom-call(bf16[2,1024,512]{2,1,0:T(8,128)(2,1)} %get-tuple-element.46.projected.earlier, ...), custom_call_target="tpu_custom_call" | custom-call | flops 4831838208 | bytes 6815744 | tf_op jit(solution)/shard_map/pallas_call | solution.py:204
  56.2 1.6 collective-permute-start.1
  58.5 1.6 copy.58.w_gate
  60.1 1.6 copy.59.w_up
  66.5 4.8 %shard_map.273 = bf16[2,1024,256]{2,1,0:T(8,128)(2,1)} custom-call(f32[2,1024,256]{2,1,0:T(8,128)} %get-tuple-element.48.head_local, bf16[2,1024,128]{2,1,0:T(8,128)(2,1)} %get-tuple-element.49.query_profile, f32[2,256,128]{2,1,0:T(8,128)} %copy-done.12, bf16[2,1024,256]{2,1,0:T(8,128)(2,1)} %get-tuple-element.51.out_gate, f32[1,256]{1,0:T(1,128)} %bitcast.198), custom_call_target="tpu_custom_call" | custom-call | flops 536870912 | bytes 4718592 | tf_op jit(solution)/shard_map/pallas_call | solution.py:259
  72.9 97.2 %feed_forward.1 = (bf16[2,4,2,128,1024]{4,3,2,1,0:T(8,128)(2,1)}, bf16[3,1024,704]{2,1,0:T(8,128)(2,1)}, bf16[4,1024,256]{2,1,0:T(8,128)(2,1)}, bf16[2,4,2,128,2...) custom-call(bf16[2,4,2,128,256]{4,3,2,1,0:T(8,128)(2,1)} %bitcast.184, ...), custom_call_target="tpu_custom_call" | custom-call | flops 30870077440 | bytes 16777216 | tf_op jit(solution)/shard_map/feed_forward/pallas_call | solution.py:601
  170.0 7.7 %shard_map.274 = (bf16[2,1024,256]{2,1,0:T(8,128)(2,1)}, bf16[2,1024,256]{2,1,0:T(8,128)(2,1)}, f32[2,256,128]{2,1,0:T(8,128)}, f32[1,256]{1,0:T(1,128)}) custom-call(bf16[2,1024,256]{2,1,0:T(8,128)(2,1)} %bitcast.185, f32[2,1024,256]{2,1,0:T(8,128)} %get-tuple-element.48.head_local, bf16[2,1024,128]{2,1,0:T(8,128)(2,1)} %get-tuple-element.49.query_profile, ...), custom_call_target="tpu_custom_call" | custom-call | flops 1073741824 | bytes 6815744 | tf_op jit(solution)/shard_map/pallas_call | solution.py:707
  177.7 1.4 collective-permute-start.12
  179.2 2.2 fusion.30
  183.6 1.7 constant_dynamic-slice_fusion.1
  186.4 4.2 %copy.80 = bf16[3,4,128,704]{2,3,0,1:T(8,128)(2,1)} copy(bf16[3,4,128,704]{3,2,1,0:T(8,128)(2,1)} %get-tuple-element.108) | data formatting | bytes 4325376
  190.6 2.4 copy.79
  193.0 1.4 collective-permute-start.26
  195.0 1.5 collective-permute-start.25
  197.1 2.9 dynamic-slice_bitcast_fusion.9
  200.0 18.6 %shard_map.275 = (bf16[2,1024,512]{2,1,0:T(8,128)(2,1)}, bf16[2,1024,16]{2,1,0:T(8,128)(2,1)}, f32[2,8,512]{2,1,0:T(8,128)}, f32[4,512]{1,0:T(4,128)}, f32[16,128]{1,0:T(8,128)}, /*index=5*/f32[1,128]{1,0:T(1,128)}) custom-call(bf16[2,1024,512]{2,1,0:T(8,128)(2,1)} %get-tuple-element.46.projected.earlier, ...), custom_call_target="tpu_custom_call" | custom-call | flops 12884901888 | bytes 7340032 | tf_op jit(solution)/shard_map/pallas_call | solution.py:854
  220.9 1.8 slice_add_fusion.1
  222.7 1.4 collective-permute-start.27
  224.7 2.3 convolution_bitcast_fusion.1
  227.3 1.4 fusion.25.grad_projected
  228.7 9.7 %shard_map.276 = (bf16[2,1024,1024]{2,1,0:T(8,128)(2,1)}, f32[1,1024]{1,0:T(1,128)}) custom-call(bf16[2,1024,512]{2,1,0:T(8,128)(2,1)} %fusion.25.grad_projected, bf16[2,1024,256]{2,1,0:T(8,128)(2,1)} %get-tuple-element.65.grad_out_gate, bf16[2,1024,16]{2,1,0:T(8,128)(2,1)} %get-tuple-element.66.grad_low_rank, bf16[1024,512]{1,0:T(8,128)(2,1)} %bitcast.182, ...), custom_call_target="tpu_custom_call" | custom-call | flops 3288334336 | bytes 13107200 | tf_op jit(solution)/shard_map/pallas_call | solution.py:922
  239.8 4.3 %bitcast_convert_fusion = bf16[1024,512]{1,0:T(8,128)(2,1)S(1)} fusion(bf16[2,1024,1024]{2,1,0:T(8,128)(2,1)S(1)} %copy-done.5, bf16[2,1024,512]{2,1,0:T(8,128)(2,1)} %fusion.25.grad_projected), kind=kOutput, calls=%fused_computation.20 | convolution fusion | flops 2148007936 | bytes 7340032 | tf_op jit(solution)/shard_map/dot_general | solution.py:32
  244.1 1.6 collective-permute-start.21
  247.1 1.6 collective-permute-done.21
  248.8 1.5 collective-permute-start.7
  250.9 1.5 collective-permute-start.15
  254.6 9.2 %collective-permute-done.7 = bf16[1,256,1024]{2,1,0:T(8,128)(2,1)S(1)} collective-permute-done((bf16[1,256,1024]{2,1,0:T(8,128)(2,1)}, bf16[1,256,1024]{2,1,0:T(8,128)(2,1)S(1)}, u32[]{:S(2)}, u32[]{:S(2)}) %collective-permute-start.7) | collective-permute-done | bytes 524320 | tf_op jit(solution)/shard_map/ppermute | solution.py:958
  263.8 2.6 collective-permute-start.22
  266.3 2.1 fusion.22
  268.4 2.2 collective-permute-done.22
  270.7 1.5 collective-permute-start.23
  273.5 3.9 %collective-permute-done.23 = f32[18688]{0:T(1024)S(1)} collective-permute-done((f32[18688]{0:T(1024)S(1)}, f32[18688]{0:T(1024)S(1)}, u32[]{:S(2)}, u32[]{:S(2)}) %collective-permute-start.23) | collective-permute-done | bytes 74784 | tf_op jit(solution)/shard_map/ppermute | solution.py:1023
  278.7 3.3 collective-permute-done.24
  284.7 1.5 collective-permute-start.6
  286.7 1.6 fusion.21
  288.4 1.5 collective-permute-start.8
  291.3 3.5 collective-permute-start.32
  294.8 1.9 bitcast_add_fusion
  297.7 2.1 collective-permute-done.6
  299.8 1.5 collective-permute-start.19
  301.2 7.0 %collective-permute-done.10 = bf16[1,256,1024]{2,1,0:T(8,128)(2,1)S(1)} collective-permute-done((bf16[1,256,1024]{2,1,0:T(8,128)(2,1)}, bf16[1,256,1024]{2,1,0:T(8,128)(2,1)S(1)}, u32[]{:S(2)}, u32[]{:S(2)}) %collective-permute-start.10) | collective-permute-done | bytes 524320 | tf_op jit(solution)/shard_map/ppermute | solution.py:962
  308.8 2.2 collective-permute-done.8
  311.0 1.5 collective-permute-start.18
  312.5 3.5 collective-permute-start.39
  316.0 2.1 fusion.17
  318.1 2.0 copy.68
  320.2 4.4 %collective-permute-done.39 = bf16[3,128,704]{1,2,0:T(8,128)(2,1)S(1)} collective-permute-done((bf16[3,128,704]{1,2,0:T(8,128)(2,1)S(1)}, bf16[3,128,704]{1,2,0:T(8,128)(2,1)S(1)}, u32[]{:S(2)}, u32[]{:S(2)}) %collective-permute-start.39) | collective-permute-done | bytes 540704 | tf_op jit(solution)/shard_map/ppermute | solution.py:1009
  325.4 4.4 %collective-permute-start.33 = (bf16[128,1024]{1,0:T(8,128)(2,1)S(1)}, bf16[128,1024]{1,0:T(8,128)(2,1)S(1)}, u32[]{:S(2)}, u32[]{:S(2)}) collective-permute-start(bf16[128,1024]{1,0:T(8,128)(2,1)S(1)} %bitcast_add_fusion.7), channel_id=1, source_target_pairs={{0,1},{1,2},{4,5},{5,6},{8,9},{9,10},{12,13},{13,14},{16,17},{17,1... | collective-permute-start | bytes 786440 | tf_op jit(solution)/shard_map/ppermute | solution.py:1009
  330.5 3.4 collective-permute-start.40
  334.8 1.5 collective-permute-done.33
  337.1 5.0 %collective-permute-start.34 = (bf16[128,1024]{1,0:T(8,128)(2,1)S(1)}, bf16[128,1024]{1,0:T(8,128)(2,1)S(1)}, u32[]{:S(2)}, u32[]{:S(2)}) collective-permute-start(bf16[128,1024]{1,0:T(8,128)(2,1)S(1)} %get-tuple-element.134), channel_id=1, source_target_pairs={{0,1},{1,2},{2,3},{4,5},{5,6},{6,7},{8,9},{9,10},{10,11},{12,13},{... | collective-permute-start | bytes 786440 | tf_op jit(solution)/shard_map/ppermute | solution.py:1009
  342.2 5.7 %collective-permute-done.40 = bf16[3,128,704]{1,2,0:T(8,128)(2,1)S(1)} collective-permute-done((bf16[3,128,704]{1,2,0:T(8,128)(2,1)S(1)}, bf16[3,128,704]{1,2,0:T(8,128)(2,1)S(1)}, u32[]{:S(2)}, u32[]{:S(2)}) %collective-permute-start.40) | collective-permute-done | bytes 540704 | tf_op jit(solution)/shard_map/ppermute | solution.py:1009
  348.7 1.5 collective-permute-start.37
  351.0 2.9 copy.69
  354.0 6.4 %collective-permute-start.41 = (bf16[3,128,704]{1,2,0:T(8,128)(2,1)S(1)}, bf16[3,128,704]{1,2,0:T(8,128)(2,1)}, u32[]{:S(2)}, u32[]{:S(2)}) collective-permute-start(bf16[3,128,704]{1,2,0:T(8,128)(2,1)S(1)} %get-tuple-element.121), channel_id=1, source_target_pairs={{0,1},{1,2},{2,3},{4,5},{5,6},{6,7},{8,9},{9,10},{10,11},{12,13},{... | collective-permute-start | bytes 1622024 | tf_op jit(solution)/shard_map/ppermute | solution.py:1009
  364.3 2.1 collective-permute-done.41
  366.4 10.2 %collective-permute-done.44 = bf16[3,128,704]{1,2,0:T(8,128)(2,1)} collective-permute-done((bf16[3,128,704]{1,2,0:T(8,128)(2,1)S(1)}, bf16[3,128,704]{1,2,0:T(8,128)(2,1)}, u32[]{:S(2)}, u32[]{:S(2)}) %collective-permute-start.44) | collective-permute-done | bytes 540704 | tf_op jit(solution)/shard_map/ppermute | solution.py:1010
  376.6 1.4 fusion.16
  (201 shorter events, 45.5 us)
Async XLA Ops:
  0.6 61.6 %collective-permute-start.2 = (bf16[256,1024]{1,0:T(8,128)(2,1)}, bf16[256,1024]{1,0:T(8,128)(2,1)}, u32[]{:S(2)}, u32[]{:S(2)}) collective-permute-start(bf16[256,1024]{1,0:T(8,128)(2,1)} %w_own.1), channel_id=1, source_target_pairs={{0,4},{4,0},{8,12},{12,8},{1,5},{5,1},{9,13},{13,9},{2,6},{6,2},{1... | collective-permute-start | bytes 1572872 | tf_op jit(solution)/shard_map/ppermute | solution.py:949
  3.6 60.1 %collective-permute-start.3 = (bf16[256,1024]{1,0:T(8,128)(2,1)}, bf16[256,1024]{1,0:T(8,128)(2,1)}, u32[]{:S(2)}, u32[]{:S(2)}) collective-permute-start(bf16[256,1024]{1,0:T(8,128)(2,1)} %w_own.1), channel_id=1, source_target_pairs={{0,8},{4,12},{8,0},{12,4},{1,9},{5,13},{9,1},{13,5},{2,10},{6,14},... | collective-permute-start | bytes 1572872 | tf_op jit(solution)/shard_map/ppermute | solution.py:950
  5.9 36.2 %collective-permute-start = (bf16[3,2,1024]{2,1,0:T(2,128)(2,1)S(1)}, bf16[3,2,1024]{2,1,0:T(2,128)(2,1)S(1)}, u32[]{:S(2)}, u32[]{:S(2)}) collective-permute-start(bf16[3,2,1024]{2,1,0:T(2,128)(2,1)S(1)} %slice.213), channel_id=1, source_target_pairs={{0,16},{1,17},{2,18},{3,19},{4,20},{5,21},{6,22},{7,23},{8,24},{9,... | collective-permute-start | bytes 36872 | tf_op jit(solution)/shard_map/ppermute | solution.py:977
  24.9 17.3 %copy-start.15 = (f32[1024]{0:T(1024)S(1)}, f32[1024]{0:T(1024)}, u32[]{:S(2)}) copy-start(f32[1024]{0:T(1024)} %convert_element_type.125) | copy-start | bytes 12292
  24.9 17.4 %copy-start.11 = (bf16[1024,1,512]{2,0,1:T(8,128)(2,1)S(1)}, bf16[1024,1,512]{2,0,1:T(8,128)(2,1)}, u32[]{:S(2)}) copy-start(bf16[1024,1,512]{2,0,1:T(8,128)(2,1)} %param.19) | copy-start | bytes 3145732
  43.2 14.7 %copy-start.33 = (bf16[256]{0:T(256)(128)(2,1)S(1)}, bf16[256]{0:T(256)(128)(2,1)}, u32[]{:S(2)}) copy-start(bf16[256]{0:T(256)(128)(2,1)} %param.25) | copy-start | bytes 1540
  43.2 15.3 %copy-start.9 = (bf16[1024,704]{0,1:T(8,128)(2,1)S(1)}, bf16[1024,704]{0,1:T(8,128)(2,1)}, u32[]{:S(2)}) copy-start(bf16[1024,704]{0,1:T(8,128)(2,1)} %param.28) | copy-start | bytes 4325380
  56.2 9.5 %collective-permute-start.1 = (f32[2,256,128]{2,1,0:T(8,128)}, f32[2,256,128]{2,1,0:T(8,128)S(1)}, u32[]{:S(2)}, u32[]{:S(2)}) collective-permute-start(f32[2,256,128]{2,1,0:T(8,128)} %get-tuple-element.50), channel_id=1, source_target_pairs={{0,16},{1,17},{2,18},{3,19},{4,20},{5,21},{6,22},{7,23},{8,24},{9,... | collective-permute-start | bytes 786440 | tf_op jit(solution)/shard_map/ppermute | solution.py:977
  63.2 8.0 %collective-permute-start.4 = (bf16[128,1024]{1,0:T(8,128)(2,1)S(1)}, bf16[128,1024]{1,0:T(8,128)(2,1)S(1)}, u32[]{:S(2)}, u32[]{:S(2)}) collective-permute-start(bf16[128,1024]{1,0:T(8,128)(2,1)S(1)} %slice.270), channel_id=1, source_target_pairs={{0,8},{4,12},{8,0},{12,4},{1,9},{5,13},{9,1},{13,5},{2,10},{6,14},... | collective-permute-start | bytes 786440 | tf_op jit(solution)/shard_map/ppermute | solution.py:951
  64.8 7.3 %collective-permute-start.5 = (bf16[128,1024]{1,0:T(8,128)(2,1)S(1)}, bf16[128,1024]{1,0:T(8,128)(2,1)S(1)}, u32[]{:S(2)}, u32[]{:S(2)}) collective-permute-start(bf16[128,1024]{1,0:T(8,128)(2,1)S(1)} %slice.271), channel_id=1, source_target_pairs={{0,4},{4,0},{8,12},{12,8},{1,5},{5,1},{9,13},{13,9},{2,6},{6,2},{1... | collective-permute-start | bytes 786440 | tf_op jit(solution)/shard_map/ppermute | solution.py:952
  170.0 11.3 %copy-start.3 = (bf16[2,1024,1024]{2,1,0:T(8,128)(2,1)S(1)}, bf16[2,1024,1024]{2,1,0:T(8,128)(2,1)}, u32[]{:S(2)}) copy-start(bf16[2,1024,1024]{2,1,0:T(8,128)(2,1)} %get-tuple-element.67.normed) | copy-start | bytes 12582916
  177.7 22.2 %collective-permute-start.12 = (f32[2,256,128]{2,1,0:T(8,128)}, f32[2,256,128]{2,1,0:T(8,128)}, u32[]{:S(2)}, u32[]{:S(2)}) collective-permute-start(f32[2,256,128]{2,1,0:T(8,128)} %get-tuple-element.61), channel_id=1, source_target_pairs={{16,0},{17,1},{18,2},{19,3},{20,4},{21,5},{22,6},{23,7},{24,8},{25... | collective-permute-start | bytes 786440 | tf_op jit(solution)/shard_map/ppermute | solution.py:977
  193.0 27.9 %collective-permute-start.26 = (bf16[1,512,256]{2,1,0:T(8,128)(2,1)}, bf16[1,512,256]{2,1,0:T(8,128)(2,1)S(1)}, u32[]{:S(2)}, u32[]{:S(2)}) collective-permute-start(bf16[1,512,256]{2,1,0:T(8,128)(2,1)} %get-tuple-element.128), channel_id=1, source_target_pairs={{0,8},{4,12},{8,0},{12,4},{1,9},{5,13},{9,1},{13,5},{2,10},{6,14},... | collective-permute-start | bytes 786440 | tf_op jit(solution)/shard_map/ppermute | solution.py:958
  194.5 26.4 %collective-permute-start.28 = (bf16[1,512,256]{2,1,0:T(8,128)(2,1)}, bf16[1,512,256]{2,1,0:T(8,128)(2,1)S(1)}, u32[]{:S(2)}, u32[]{:S(2)}) collective-permute-start(bf16[1,512,256]{2,1,0:T(8,128)(2,1)} %get-tuple-element.127), channel_id=1, source_target_pairs={{0,4},{4,0},{8,12},{12,8},{1,5},{5,1},{9,13},{13,9},{2,6},{6,2},{1... | collective-permute-start | bytes 786440 | tf_op jit(solution)/shard_map/ppermute | solution.py:957
  195.0 53.7 %collective-permute-start.25 = (bf16[1,512,256]{2,1,0:T(8,128)(2,1)}, bf16[1,512,256]{2,1,0:T(8,128)(2,1)S(1)}, u32[]{:S(2)}, u32[]{:S(2)}) collective-permute-start(bf16[1,512,256]{2,1,0:T(8,128)(2,1)} %get-tuple-element.125), channel_id=1, source_target_pairs={{0,4},{4,0},{8,12},{12,8},{1,5},{5,1},{9,13},{13,9},{2,6},{6,2},{1... | collective-permute-start | bytes 786440 | tf_op jit(solution)/shard_map/ppermute | solution.py:959
  196.5 54.4 %collective-permute-start.30 = (bf16[1,512,256]{2,1,0:T(8,128)(2,1)}, bf16[1,512,256]{2,1,0:T(8,128)(2,1)S(1)}, u32[]{:S(2)}, u32[]{:S(2)}) collective-permute-start(bf16[1,512,256]{2,1,0:T(8,128)(2,1)} %get-tuple-element.126), channel_id=1, source_target_pairs={{0,8},{4,12},{8,0},{12,4},{1,9},{5,13},{9,1},{13,5},{2,10},{6,14},... | collective-permute-start | bytes 786440 | tf_op jit(solution)/shard_map/ppermute | solution.py:960
  199.9 18.7 %copy-start.24 = (f32[1,1,512]{2,0,1:T(1,128)S(1)}, f32[1,1,512]{2,0,1:T(1,128)}, u32[]{:S(2)}) copy-start(f32[1,1,512]{2,0,1:T(1,128)} %get-tuple-element.147) | copy-start | bytes 6148
  199.9 18.7 %copy-start.25 = (f32[1,1,512]{2,0,1:T(1,128)S(1)}, f32[1,1,512]{2,0,1:T(1,128)}, u32[]{:S(2)}) copy-start(f32[1,1,512]{2,0,1:T(1,128)} %get-tuple-element.148) | copy-start | bytes 6148
  199.9 18.7 %copy-start.26 = (f32[1,1,512]{2,0,1:T(1,128)S(1)}, f32[1,1,512]{2,0,1:T(1,128)}, u32[]{:S(2)}) copy-start(f32[1,1,512]{2,0,1:T(1,128)} %get-tuple-element.149) | copy-start | bytes 6148
  200.0 24.7 %copy-start.4 = (bf16[2,1024,1024]{2,1,0:T(8,128)(2,1)S(1)}, bf16[2,1024,1024]{2,1,0:T(8,128)(2,1)}, u32[]{:S(2)}) copy-start(bf16[2,1024,1024]{2,1,0:T(8,128)(2,1)} %get-tuple-element.67.normed) | copy-start | bytes 12582916
  219.6 7.7 %collective-permute-start.13 = (f32[2,3,512]{2,1,0:T(4,128)S(1)}, f32[2,3,512]{2,1,0:T(4,128)S(1)}, u32[]{:S(2)}, u32[]{:S(2)}) collective-permute-start(f32[2,3,512]{2,1,0:T(4,128)S(1)} %pad_maximum_fusion.6), channel_id=1, source_target_pairs={{16,0},{17,1},{18,2},{19,3},{20,4},{21,5},{22,6},{23,7},{24,8},{25... | collective-permute-start | bytes 36872 | tf_op jit(solution)/shard_map/ppermute | solution.py:977
  222.7 27.6 %collective-permute-start.27 = (bf16[1,512,256]{2,1,0:T(8,128)(2,1)}, bf16[1,512,256]{2,1,0:T(8,128)(2,1)S(1)}, u32[]{:S(2)}, u32[]{:S(2)}) collective-permute-start(bf16[1,512,256]{2,1,0:T(8,128)(2,1)} %get-tuple-element.129), channel_id=1, source_target_pairs={{0,4},{4,0},{8,12},{12,8},{1,5},{5,1},{9,13},{13,9},{2,6},{6,2},{1... | collective-permute-start | bytes 786440 | tf_op jit(solution)/shard_map/ppermute | solution.py:961
  224.1 28.3 %collective-permute-start.29 = (bf16[1,512,256]{2,1,0:T(8,128)(2,1)S(1)}, bf16[1,512,256]{2,1,0:T(8,128)(2,1)S(1)}, u32[]{:S(2)}, u32[]{:S(2)}) collective-permute-start(bf16[1,512,256]{2,1,0:T(8,128)(2,1)S(1)} %get-tuple-element.130), channel_id=1, source_target_pairs={{0,8},{4,12},{8,0},{12,4},{1,9},{5,13},{9,1},{13,5},{2,10},{6,14},... | collective-permute-start | bytes 786440 | tf_op jit(solution)/shard_map/ppermute | solution.py:962
  228.7 10.4 %copy-start.22 = (f32[16,128]{1,0:T(8,128)S(1)}, f32[16,128]{1,0:T(8,128)}, u32[]{:S(2)}) copy-start(f32[16,128]{1,0:T(8,128)} %get-tuple-element.73) | copy-start | bytes 24580
  228.7 10.5 %copy-start.34 = (f32[1,128]{1,0:T(1,128)S(1)}, f32[1,128]{1,0:T(1,128)}, u32[]{:S(2)}) copy-start(f32[1,128]{1,0:T(1,128)} %get-tuple-element.74) | copy-start | bytes 1540
  228.7 11.1 %copy-start.5 = (bf16[2,1024,1024]{2,1,0:T(8,128)(2,1)S(1)}, bf16[2,1024,1024]{2,1,0:T(8,128)(2,1)}, u32[]{:S(2)}) copy-start(bf16[2,1024,1024]{2,1,0:T(8,128)(2,1)} %get-tuple-element.67.normed) | copy-start | bytes 12582916
  239.2 4.9 %collective-permute-start.20 = (f32[22912]{0:T(1024)S(1)}, f32[22912]{0:T(1024)S(1)}, u32[]{:S(2)}, u32[]{:S(2)}) collective-permute-start(f32[22912]{0:T(1024)S(1)} %constant_dynamic-update-slice_fusion), channel_id=1, source_target_pairs={{0,16},{16,0},{1,17},{17,1},{2,18},{18,2},{3,19},{19,3},{4,20},{20... | collective-permute-start | bytes 274952 | tf_op jit(solution)/shard_map/ppermute | solution.py:1023
  244.1 4.6 %collective-permute-start.21 = (f32[22912]{0:T(1024)S(1)}, f32[22912]{0:T(1024)S(1)}, u32[]{:S(2)}, u32[]{:S(2)}) collective-permute-start(f32[22912]{0:T(1024)S(1)} %add.270), channel_id=1, source_target_pairs={{0,1},{1,0},{2,3},{3,2},{4,5},{5,4},{6,7},{7,6},{8,9},{9,8},{10,11... | collective-permute-start | bytes 274952 | tf_op jit(solution)/shard_map/ppermute | solution.py:1023
  248.7 42.6 %collective-permute-start.38 = (bf16[4,3,128,704]{2,3,1,0:T(8,128)(2,1)}, bf16[4,3,128,704]{2,3,1,0:T(8,128)(2,1)}, u32[]{:S(2)}, u32[]{:S(2)}) collective-permute-start(bf16[4,3,128,704]{2,3,1,0:T(8,128)(2,1)} %bitcast.66), channel_id=1, source_target_pairs={{0,16},{16,0},{1,17},{17,1},{2,18},{18,2},{3,19},{19,3},{4,20},{20... | collective-permute-start | bytes 6488072 | tf_op jit(solution)/shard_map/ppermute | solution.py:1002
  248.8 15.0 %collective-permute-start.7 = (bf16[1,256,1024]{2,1,0:T(8,128)(2,1)}, bf16[1,256,1024]{2,1,0:T(8,128)(2,1)S(1)}, u32[]{:S(2)}, u32[]{:S(2)}) collective-permute-start(bf16[1,256,1024]{2,1,0:T(8,128)(2,1)} %get-tuple-element.118), channel_id=1, source_target_pairs={{0,8},{4,12},{8,0},{12,4},{1,9},{5,13},{9,1},{13,5},{2,10},{6,14},... | collective-permute-start | bytes 1572872 | tf_op jit(solution)/shard_map/ppermute | solution.py:958
  250.3 16.1 %collective-permute-start.9 = (bf16[1,256,1024]{2,1,0:T(8,128)(2,1)}, bf16[1,256,1024]{2,1,0:T(8,128)(2,1)S(1)}, u32[]{:S(2)}, u32[]{:S(2)}) collective-permute-start(bf16[1,256,1024]{2,1,0:T(8,128)(2,1)} %get-tuple-element.117), channel_id=1, source_target_pairs={{0,4},{4,0},{8,12},{12,8},{1,5},{5,1},{9,13},{13,9},{2,6},{6,2},{1... | collective-permute-start | bytes 1572872 | tf_op jit(solution)/shard_map/ppermute | solution.py:957
  250.9 33.7 %collective-permute-start.15 = (bf16[1,256,1024]{2,1,0:T(8,128)(2,1)}, bf16[1,256,1024]{2,1,0:T(8,128)(2,1)}, u32[]{:S(2)}, u32[]{:S(2)}) collective-permute-start(bf16[1,256,1024]{2,1,0:T(8,128)(2,1)} %get-tuple-element.110), channel_id=1, source_target_pairs={{0,8},{4,12},{8,0},{12,4},{1,9},{5,13},{9,1},{13,5},{2,10},{6,14},... | collective-permute-start | bytes 1572872 | tf_op jit(solution)/shard_map/ppermute | solution.py:958
  252.4 33.7 %collective-permute-start.17 = (bf16[1,256,1024]{2,1,0:T(8,128)(2,1)}, bf16[1,256,1024]{2,1,0:T(8,128)(2,1)}, u32[]{:S(2)}, u32[]{:S(2)}) collective-permute-start(bf16[1,256,1024]{2,1,0:T(8,128)(2,1)} %get-tuple-element.112), channel_id=1, source_target_pairs={{0,4},{4,0},{8,12},{12,8},{1,5},{5,1},{9,13},{13,9},{2,6},{6,2},{1... | collective-permute-start | bytes 1572872 | tf_op jit(solution)/shard_map/ppermute | solution.py:957
  263.8 6.9 %collective-permute-start.22 = (f32[22912]{0:T(1024)S(1)}, f32[22912]{0:T(1024)S(1)}, u32[]{:S(2)}, u32[]{:S(2)}) collective-permute-start(f32[22912]{0:T(1024)S(1)} %add.271), channel_id=1, source_target_pairs={{0,2},{1,3},{2,0},{3,1},{4,6},{5,7},{6,4},{7,5},{8,10},{9,11},{10,... | collective-permute-start | bytes 274952 | tf_op jit(solution)/shard_map/ppermute | solution.py:1023
  266.3 22.0 %collective-permute-start.31 = (bf16[4,128,1024]{2,1,0:T(8,128)(2,1)}, bf16[4,128,1024]{2,1,0:T(8,128)(2,1)}, u32[]{:S(2)}, u32[]{:S(2)}) collective-permute-start(bf16[4,128,1024]{2,1,0:T(8,128)(2,1)} %constant_dynamic-slice_fusion.4), channel_id=1, source_target_pairs={{0,16},{16,0},{1,17},{17,1},{2,18},{18,2},{3,19},{19,3},{4,20},{20... | collective-permute-start | bytes 3145736 | tf_op jit(solution)/shard_map/ppermute | solution.py:1002
  270.7 6.8 %collective-permute-start.23 = (f32[18688]{0:T(1024)S(1)}, f32[18688]{0:T(1024)S(1)}, u32[]{:S(2)}, u32[]{:S(2)}) collective-permute-start(f32[18688]{0:T(1024)S(1)} %slice.275), channel_id=1, source_target_pairs={{0,4},{4,0},{8,12},{12,8},{1,5},{5,1},{9,13},{13,9},{2,6},{6,2},{1... | collective-permute-start | bytes 224264 | tf_op jit(solution)/shard_map/ppermute | solution.py:1023
  277.5 4.5 %collective-permute-start.24 = (f32[18688]{0:T(1024)S(1)}, f32[18688]{0:T(1024)S(1)}, u32[]{:S(2)}, u32[]{:S(2)}) collective-permute-start(f32[18688]{0:T(1024)S(1)} %slice_add_fusion.2), channel_id=1, source_target_pairs={{0,8},{4,12},{8,0},{12,4},{1,9},{5,13},{9,1},{13,5},{2,10},{6,14},... | collective-permute-start | bytes 224264 | tf_op jit(solution)/shard_map/ppermute | solution.py:1023
  281.9 15.2 %collective-permute-start.11 = (bf16[1,256,1024]{2,1,0:T(8,128)(2,1)}, bf16[1,256,1024]{2,1,0:T(8,128)(2,1)}, u32[]{:S(2)}, u32[]{:S(2)}) collective-permute-start(bf16[1,256,1024]{2,1,0:T(8,128)(2,1)} %get-tuple-element.120), channel_id=1, source_target_pairs={{0,8},{4,12},{8,0},{12,4},{1,9},{5,13},{9,1},{13,5},{2,10},{6,14},... | collective-permute-start | bytes 1572872 | tf_op jit(solution)/shard_map/ppermute | solution.py:960
  284.7 15.1 %collective-permute-start.6 = (bf16[1,256,1024]{2,1,0:T(8,128)(2,1)}, bf16[1,256,1024]{2,1,0:T(8,128)(2,1)S(1)}, u32[]{:S(2)}, u32[]{:S(2)}) collective-permute-start(bf16[1,256,1024]{2,1,0:T(8,128)(2,1)} %get-tuple-element.119), channel_id=1, source_target_pairs={{0,4},{4,0},{8,12},{12,8},{1,5},{5,1},{9,13},{13,9},{2,6},{6,2},{1... | collective-permute-start | bytes 1572872 | tf_op jit(solution)/shard_map/ppermute | solution.py:959
  286.2 22.1 %collective-permute-start.10 = (bf16[1,256,1024]{2,1,0:T(8,128)(2,1)}, bf16[1,256,1024]{2,1,0:T(8,128)(2,1)S(1)}, u32[]{:S(2)}, u32[]{:S(2)}) collective-permute-start(bf16[1,256,1024]{2,1,0:T(8,128)(2,1)} %get-tuple-element.115), channel_id=1, source_target_pairs={{0,8},{4,12},{8,0},{12,4},{1,9},{5,13},{9,1},{13,5},{2,10},{6,14},... | collective-permute-start | bytes 1572872 | tf_op jit(solution)/shard_map/ppermute | solution.py:962
  288.4 22.6 %collective-permute-start.8 = (bf16[1,256,1024]{2,1,0:T(8,128)(2,1)S(1)}, bf16[1,256,1024]{2,1,0:T(8,128)(2,1)S(1)}, u32[]{:S(2)}, u32[]{:S(2)}) collective-permute-start(bf16[1,256,1024]{2,1,0:T(8,128)(2,1)S(1)} %get-tuple-element.116), channel_id=1, source_target_pairs={{0,4},{4,0},{8,12},{12,8},{1,5},{5,1},{9,13},{13,9},{2,6},{6,2},{1... | collective-permute-start | bytes 1572872 | tf_op jit(solution)/shard_map/ppermute | solution.py:961
  291.3 21.2 %collective-permute-start.32 = (bf16[128,1024]{1,0:T(8,128)(2,1)S(1)}, bf16[128,1024]{1,0:T(8,128)(2,1)S(1)}, u32[]{:S(2)}, u32[]{:S(2)}) collective-permute-start(bf16[128,1024]{1,0:T(8,128)(2,1)S(1)} %get-tuple-element.136), channel_id=1, source_target_pairs={{0,1},{4,5},{8,9},{12,13},{16,17},{20,21},{24,25},{28,29}} | collective-permute-start | bytes 786440 | tf_op jit(solution)/shard_map/ppermute | solution.py:1009
  296.7 19.2 %copy-start.8 = (f32[4,128,1024]{2,1,0:T(8,128)S(1)}, f32[4,128,1024]{2,1,0:T(8,128)}, u32[]{:S(2)}) copy-start(f32[4,128,1024]{2,1,0:T(8,128)} %get-tuple-element.54) | copy-start | bytes 6291460
  296.7 19.2 %copy-start.28 = (pred[2,256]{1,0:T(4,128)(4,1)S(1)}, pred[2,256]{1,0:T(4,128)(4,1)}, u32[]{:S(2)}) copy-start(pred[2,256]{1,0:T(4,128)(4,1)} %broadcast_compare_fusion) | copy-start | bytes 1540
  297.1 28.3 %collective-permute-start.14 = (bf16[1,256,1024]{2,1,0:T(8,128)(2,1)S(1)}, bf16[1,256,1024]{2,1,0:T(8,128)(2,1)S(1)}, u32[]{:S(2)}, u32[]{:S(2)}) collective-permute-start(bf16[1,256,1024]{2,1,0:T(8,128)(2,1)S(1)} %copy-done.14), channel_id=1, source_target_pairs={{0,4},{4,0},{8,12},{12,8},{1,5},{5,1},{9,13},{13,9},{2,6},{6,2},{1... | collective-permute-start | bytes 1572872 | tf_op jit(solution)/shard_map/ppermute | solution.py:959
  299.8 30.0 %collective-permute-start.19 = (bf16[1,256,1024]{2,1,0:T(8,128)(2,1)S(1)}, bf16[1,256,1024]{2,1,0:T(8,128)(2,1)S(1)}, u32[]{:S(2)}, u32[]{:S(2)}) collective-permute-start(bf16[1,256,1024]{2,1,0:T(8,128)(2,1)S(1)} %copy-done.13), channel_id=1, source_target_pairs={{0,8},{4,12},{8,0},{12,4},{1,9},{5,13},{9,1},{13,5},{2,10},{6,14},... | collective-permute-start | bytes 1572872 | tf_op jit(solution)/shard_map/ppermute | solution.py:960
  308.2 22.3 %collective-permute-start.16 = (bf16[1,256,1024]{2,1,0:T(8,128)(2,1)S(1)}, bf16[1,256,1024]{2,1,0:T(8,128)(2,1)S(1)}, u32[]{:S(2)}, u32[]{:S(2)}) collective-permute-start(bf16[1,256,1024]{2,1,0:T(8,128)(2,1)S(1)} %get-tuple-element.113), channel_id=1, source_target_pairs={{0,4},{4,0},{8,12},{12,8},{1,5},{5,1},{9,13},{13,9},{2,6},{6,2},{1... | collective-permute-start | bytes 1572872 | tf_op jit(solution)/shard_map/ppermute | solution.py:961
  311.0 22.9 %collective-permute-start.18 = (bf16[1,256,1024]{2,1,0:T(8,128)(2,1)S(1)}, bf16[1,256,1024]{2,1,0:T(8,128)(2,1)S(1)}, u32[]{:S(2)}, u32[]{:S(2)}) collective-permute-start(bf16[1,256,1024]{2,1,0:T(8,128)(2,1)S(1)} %get-tuple-element.114), channel_id=1, source_target_pairs={{0,8},{4,12},{8,0},{12,4},{1,9},{5,13},{9,1},{13,5},{2,10},{6,14},... | collective-permute-start | bytes 1572872 | tf_op jit(solution)/shard_map/ppermute | solution.py:962
  312.5 12.2 %collective-permute-start.39 = (bf16[3,128,704]{1,2,0:T(8,128)(2,1)S(1)}, bf16[3,128,704]{1,2,0:T(8,128)(2,1)S(1)}, u32[]{:S(2)}, u32[]{:S(2)}) collective-permute-start(bf16[3,128,704]{1,2,0:T(8,128)(2,1)S(1)} %get-tuple-element.123), channel_id=1, source_target_pairs={{0,1},{4,5},{8,9},{12,13},{16,17},{20,21},{24,25},{28,29}} | collective-permute-start | bytes 1622024 | tf_op jit(solution)/shard_map/ppermute | solution.py:1009
  316.0 17.9 %copy-start.6 = (bf16[2,1024,1024]{2,1,0:T(8,128)(2,1)S(1)}, bf16[2,1024,1024]{2,1,0:T(8,128)(2,1)}, u32[]{:S(2)}) copy-start(bf16[2,1024,1024]{2,1,0:T(8,128)(2,1)} %get-tuple-element.52) | copy-start | bytes 12582916
  318.1 15.9 %copy-start.2 = (bf16[2,1024,1024]{2,1,0:T(8,128)(2,1)S(1)}, bf16[2,1024,1024]{2,1,0:T(8,128)(2,1)}, u32[]{:S(2)}) copy-start(bf16[2,1024,1024]{2,1,0:T(8,128)(2,1)} %get-tuple-element.68) | copy-start | bytes 12582916
  318.1 15.9 %copy-start.16 = (f32[1024]{0:T(1024)S(1)}, f32[1024]{0:T(1024)}, u32[]{:S(2)}) copy-start(f32[1024]{0:T(1024)} %convert_element_type.125) | copy-start | bytes 12292
  318.1 15.9 %copy-start.19 = (f32[2,256]{1,0:T(2,128)S(1)}, f32[2,256]{1,0:T(2,128)}, u32[]{:S(2)}) copy-start(f32[2,256]{1,0:T(2,128)} %add_rsqrt_fusion) | copy-start | bytes 6148
  324.6 10.1 %collective-permute-start.35 = (bf16[128,1024]{1,0:T(8,128)(2,1)S(1)}, bf16[128,1024]{1,0:T(8,128)(2,1)S(1)}, u32[]{:S(2)}, u32[]{:S(2)}) collective-permute-start(bf16[128,1024]{1,0:T(8,128)(2,1)S(1)} %get-tuple-element.137), channel_id=1, source_target_pairs={{3,2},{7,6},{11,10},{15,14},{19,18},{23,22},{27,26},{31,30}} | collective-permute-start | bytes 786440 | tf_op jit(solution)/shard_map/ppermute | solution.py:1010
  325.4 10.9 %collective-permute-start.33 = (bf16[128,1024]{1,0:T(8,128)(2,1)S(1)}, bf16[128,1024]{1,0:T(8,128)(2,1)S(1)}, u32[]{:S(2)}, u32[]{:S(2)}) collective-permute-start(bf16[128,1024]{1,0:T(8,128)(2,1)S(1)} %bitcast_add_fusion.7), channel_id=1, source_target_pairs={{0,1},{1,2},{4,5},{5,6},{8,9},{9,10},{12,13},{13,14},{16,17},{17,1... | collective-permute-start | bytes 786440 | tf_op jit(solution)/shard_map/ppermute | solution.py:1009
  329.8 12.4 %collective-permute-start.42 = (bf16[3,128,704]{1,2,0:T(8,128)(2,1)S(1)}, bf16[3,128,704]{1,2,0:T(8,128)(2,1)S(1)}, u32[]{:S(2)}, u32[]{:S(2)}) collective-permute-start(bf16[3,128,704]{1,2,0:T(8,128)(2,1)S(1)} %get-tuple-element.124), channel_id=1, source_target_pairs={{3,2},{7,6},{11,10},{15,14},{19,18},{23,22},{27,26},{31,30}} | collective-permute-start | bytes 1622024 | tf_op jit(solution)/shard_map/ppermute | solution.py:1010
  330.5 17.3 %collective-permute-start.40 = (bf16[3,128,704]{1,2,0:T(8,128)(2,1)S(1)}, bf16[3,128,704]{1,2,0:T(8,128)(2,1)S(1)}, u32[]{:S(2)}, u32[]{:S(2)}) collective-permute-start(bf16[3,128,704]{1,2,0:T(8,128)(2,1)S(1)} %bitcast_add_fusion.3), channel_id=1, source_target_pairs={{0,1},{1,2},{4,5},{5,6},{8,9},{9,10},{12,13},{13,14},{16,17},{17,1... | collective-permute-start | bytes 1622024 | tf_op jit(solution)/shard_map/ppermute | solution.py:1009
  336.3 13.9 %copy-start.7 = (f32[4,128,1024]{2,1,0:T(8,128)S(1)}, f32[4,128,1024]{2,1,0:T(8,128)}, u32[]{:S(2)}) copy-start(f32[4,128,1024]{2,1,0:T(8,128)} %get-tuple-element.56) | copy-start | bytes 6291460
  336.3 12.3 %collective-permute-start.36 = (bf16[128,1024]{1,0:T(8,128)(2,1)S(1)}, bf16[128,1024]{1,0:T(8,128)(2,1)S(1)}, u32[]{:S(2)}, u32[]{:S(2)}) collective-permute-start(bf16[128,1024]{1,0:T(8,128)(2,1)S(1)} %get-tuple-element.135), channel_id=1, source_target_pairs={{3,2},{2,1},{7,6},{6,5},{11,10},{10,9},{15,14},{14,13},{19,18},{18... | collective-permute-start | bytes 786440 | tf_op jit(solution)/shard_map/ppermute | solution.py:1010
  337.1 24.6 %collective-permute-start.34 = (bf16[128,1024]{1,0:T(8,128)(2,1)S(1)}, bf16[128,1024]{1,0:T(8,128)(2,1)S(1)}, u32[]{:S(2)}, u32[]{:S(2)}) collective-permute-start(bf16[128,1024]{1,0:T(8,128)(2,1)S(1)} %get-tuple-element.134), channel_id=1, source_target_pairs={{0,1},{1,2},{2,3},{4,5},{5,6},{6,7},{8,9},{9,10},{10,11},{12,13},{... | collective-permute-start | bytes 786440 | tf_op jit(solution)/shard_map/ppermute | solution.py:1009
  348.0 12.4 %collective-permute-start.43 = (bf16[3,128,704]{1,2,0:T(8,128)(2,1)S(1)}, bf16[3,128,704]{1,2,0:T(8,128)(2,1)S(1)}, u32[]{:S(2)}, u32[]{:S(2)}) collective-permute-start(bf16[3,128,704]{1,2,0:T(8,128)(2,1)S(1)} %get-tuple-element.122), channel_id=1, source_target_pairs={{3,2},{2,1},{7,6},{6,5},{11,10},{10,9},{15,14},{14,13},{19,18},{18... | collective-permute-start | bytes 1622024 | tf_op jit(solution)/shard_map/ppermute | solution.py:1010
  348.7 13.0 %collective-permute-start.37 = (bf16[128,1024]{1,0:T(8,128)(2,1)S(1)}, bf16[128,1024]{1,0:T(8,128)(2,1)S(1)}, u32[]{:S(2)}, u32[]{:S(2)}) collective-permute-start(bf16[128,1024]{1,0:T(8,128)(2,1)S(1)} %bitcast_add_fusion.6), channel_id=1, source_target_pairs={{3,2},{2,1},{1,0},{7,6},{6,5},{5,4},{11,10},{10,9},{9,8},{15,14},{... | collective-permute-start | bytes 786440 | tf_op jit(solution)/shard_map/ppermute | solution.py:1010
  354.0 12.5 %collective-permute-start.41 = (bf16[3,128,704]{1,2,0:T(8,128)(2,1)S(1)}, bf16[3,128,704]{1,2,0:T(8,128)(2,1)}, u32[]{:S(2)}, u32[]{:S(2)}) collective-permute-start(bf16[3,128,704]{1,2,0:T(8,128)(2,1)S(1)} %get-tuple-element.121), channel_id=1, source_target_pairs={{0,1},{1,2},{2,3},{4,5},{5,6},{6,7},{8,9},{9,10},{10,11},{12,13},{... | collective-permute-start | bytes 1622024 | tf_op jit(solution)/shard_map/ppermute | solution.py:1009
  360.4 16.2 %collective-permute-start.44 = (bf16[3,128,704]{1,2,0:T(8,128)(2,1)S(1)}, bf16[3,128,704]{1,2,0:T(8,128)(2,1)}, u32[]{:S(2)}, u32[]{:S(2)}) collective-permute-start(bf16[3,128,704]{1,2,0:T(8,128)(2,1)S(1)} %bitcast_add_fusion.2), channel_id=1, source_target_pairs={{3,2},{2,1},{1,0},{7,6},{6,5},{5,4},{11,10},{10,9},{9,8},{15,14},{... | collective-permute-start | bytes 1622024 | tf_op jit(solution)/shard_map/ppermute | solution.py:1010
  (18 other events, 99.4 us)

commit v3 on v2

--- a/solution.py
+++ b/solution.py
@@ -244,10 +244,11 @@
     return (head_local + mm_nt(query_profile, entering.astype(BF16))) * scale
 
 
-def gate_body(head_local, query_profile, entering, out_gate, gain, gated):
+def gate_body(head_local, query_profile, entering, out_gate, gain, gated, head_out):
     scale = query_profile.shape[-1] ** (-0.5)
     for s in range(head_local.shape[0]):
         head = head_rows(head_local[s], query_profile[s], entering[s], scale)
+        head_out[s] = head.astype(BF16)
         inverse = lax.rsqrt(jnp.mean(head * head, axis=-1, keepdims=True) + EPS_HEAD)
         logits = out_gate[s].astype(F32)
         gated[s] = (head * inverse * gain[...] * (logits * sigmoid(logits))).astype(BF16)
@@ -266,11 +267,11 @@
             rows3(sequences, STEP, dv),
             whole((1, dv)),
         ],
-        rows3(sequences, STEP, dv),
-        shape_of((sequences, length, dv), BF16),
+        [rows3(sequences, STEP, dv)] * 2,
+        [shape_of((sequences, length, dv), BF16)] * 2,
         [],
         2 * sequences * length * dk * dv * 4,
-        sequences * length * (dv * 8 + dk * 2),
+        sequences * length * (dv * 10 + dk * 2),
     )(head_local, query_profile, entering, out_gate, gain)
 
 
@@ -665,283 +666,686 @@
         weight_grads,
         output_grads,
         grad_gated.reshape(sequences, length, dv),
-        own_residual.reshape(sequences, length // 4, width),
-        own_grad.reshape(sequences, length // 4, width),
+        own_residual,
+        own_grad,
         gain_grad,
     )
 
 
-def ungate_body(
-    grad_gated, head_local, query_profile, entering, out_gate, gain,
-    grad_out_gate, grad_head, state_grad, gain_grad,
+SMALL = 48
+
+
+def paired_sum(own, received, order):
+    terms = [own.astype(F32)] + [received[index].astype(F32) for index in order]
+    while len(terms) > 1:
+        half = len(terms) // 2
+        terms = [terms[index] + terms[index + half] for index in range(half)]
+    return terms[0]
+
+
+def mixer_back_body(
+    grad_gated_in, head_in, profile_in, out_gate_in, projected_in, cumulative_in, states_in,
+    normed_in, tok_in, residual_in, grad_residual_in, out_part_in, hidden_grads, output_parts,
+    w_proj_in, w_gate_in, low_rank, halo, taps_in, rank_up, bias, w_rank, before, entering,
+    decays, head_gain, mixer_gain, channel_part, lengths,
+    output, token_grads, hidden_out, mixer_out, small_local, small_shared,
+    grad_gated, head, profile, out_gate, projected, cumulative, states, normed, tok, residual,
+    grad_residual, part, w_proj, w_gate,
+    hidden_kept, hidden_seq, hidden_dp, output_kept, output_seq, output_mp, output_dp,
+    f_via_across, f_via_down, f_across, f_down, g_via_across, g_via_down, g_across, g_down,
+    grad_out_gate, grad_head, grad_projected, grad_low_rank, mixer_grad, mixer_seq, mixer_dp,
+    state_grad, state_seq, upstream, extended, grad_extended, edge_out, edge_in,
+    small, small_low, small_seq, small_dp, small_mp, out_stage,
+    load_sem, seq_send, seq_recv, dp_send, dp_recv, mp_send, mp_recv, f_send, f_recv,
+    g_send, g_recv, store_sem,
 ):
-    step = pl.program_id(0)
-
-    @pl.when(step == 0)
-    def _():
-        state_grad[...] = jnp.zeros_like(state_grad)
-        gain_grad[...] = jnp.zeros_like(gain_grad)
-
-    scale = query_profile.shape[-1] ** (-0.5)
-    for s in range(head_local.shape[0]):
-        upper = grad_gated[s].astype(F32)
-        head = head_rows(head_local[s], query_profile[s], entering[s], scale)
-        inverse = lax.rsqrt(jnp.mean(head * head, axis=-1, keepdims=True) + EPS_HEAD)
-        unit = head * inverse
-        logits = out_gate[s].astype(F32)
-        share = sigmoid(logits)
-        slope = share * (1.0 + logits * (1.0 - share))
-        grad_out_gate[s] = (upper * unit * gain[...] * slope).astype(BF16)
-        grad_normed = upper * (logits * share)
-        gain_grad[...] += jnp.sum(grad_normed * unit, axis=0, keepdims=True)
-        scaled = grad_normed * gain[...]
+    sequences, length, dv = grad_gated.shape
+    width = normed.shape[-1]
+    rank, dk = rank_up.shape
+    c3 = projected.shape[-1]
+    halves = 2
+    turns = sequences * halves
+    MESH = pl.DeviceIdType.MESH
+    me, side, place = lax.axis_index("mp"), lax.axis_index("seq"), lax.axis_index("dp")
+    sides, places = lax.axis_size("seq"), lax.axis_size("dp")
+    across = me + 1 - 2 * (me % 2)
+    down = (me + 2) % 4
+    far = 3 - me
+    share_rows = width // sides
+    shard_rows = share_rows // places
+    steps = length // STEP
+    per_step = STEP // CHUNK
+    first, second = pl.ds(0, HALF), pl.ds(HALF, HALF)
+
+    def remote(source, target, send, recv, axis, device):
+        return pltpu.make_async_remote_copy(
+            src_ref=source,
+            dst_ref=target,
+            send_sem=send,
+            recv_sem=recv,
+            device_id={axis: device},
+            device_id_type=MESH,
+        )
+
+
+    loads = [
+        pltpu.make_async_copy(source, target, load_sem.at[index])
+        for index, (source, target) in enumerate(
+            [
+                (grad_gated_in, grad_gated),
+                (head_in, head),
+                (profile_in, profile),
+                (out_gate_in, out_gate),
+                (out_part_in, part),
+                (hidden_grads.at[:, pl.ds(side * share_rows, share_rows)], hidden_kept),
+                (output_parts.at[:, pl.ds(side * share_rows, share_rows)], output_kept),
+                (normed_in, normed),
+                (projected_in, projected),
+                (cumulative_in, cumulative),
+                (states_in, states),
+                (residual_in, residual),
+                (w_proj_in, w_proj),
+                (w_gate_in, w_gate),
+                (grad_residual_in, grad_residual),
+                (tok_in.at[:, me], tok),
+            ]
+        )
+    ]
+
+    def to_sides(kind, source_of, target):
+        copies = []
+        for hop in range(1, sides):
+            peer = (side + hop) % sides
+            copies.append(
+                remote(
+                    source_of(peer),
+                    target.at[hop - 1],
+                    seq_send.at[kind, hop - 1],
+                    seq_recv.at[kind, hop - 1],
+                    "seq",
+                    peer,
+                )
+            )
+        return copies
+
+    def to_places(kind, source_of, target):
+        copies = []
+        for hop in range(1, places):
+            peer = (place + hop) % places
+            copies.append(
+                remote(
+                    source_of(peer),
+                    target.at[hop - 1],
+                    dp_send.at[kind, hop - 1],
+                    dp_recv.at[kind, hop - 1],
+                    "dp",
+                    peer,
+                )
+            )
+        return copies
+
+    def to_heads(kind, source_of, target):
+        return [
+            remote(
+                source_of(slot),
+                target.at[slot - 1],
+                mp_send.at[kind, slot - 1],
+                mp_recv.at[kind, slot - 1],
+                "mp",
+                (me, across, down, far)[slot],
+            )
+            for slot in range(1, 4)
+        ]
+
+    def share_of(ref):
+        return lambda peer: ref.at[:, pl.ds(peer * share_rows, share_rows)]
+
+    def shard_of(ref):
+        return lambda peer: ref.at[:, pl.ds(peer * shard_rows, shard_rows)]
+
+    hidden_to_sides = to_sides(0, share_of(hidden_grads), hidden_seq)
+    output_to_sides = to_sides(1, share_of(output_parts), output_seq)
+    state_to_sides = to_sides(2, lambda peer: state_grad, state_seq)
+    mixer_to_sides = to_sides(
+        3, lambda peer: mixer_grad.at[pl.ds(peer * share_rows, share_rows)], mixer_seq
+    )
+    small_to_sides = to_sides(4, lambda peer: small_low.at[0], small_seq)
+    edge_copy = remote(
+        edge_out,
+        edge_in,
+        seq_send.at[5, 0],
+        seq_recv.at[5, 0],
+        "seq",
+        (side + sides - 1) % sides,
+    )
+    hidden_to_places = to_places(0, shard_of(hidden_kept), hidden_dp)
+
+    def own_share(peer):
+        return pl.ds(pl.multiple_of(side * share_rows + peer * shard_rows, 16), shard_rows)
+
+    mixer_to_places = to_places(1, lambda peer: mixer_grad.at[own_share(peer)], mixer_dp)
+    output_to_places = to_places(
+        2, lambda peer: output_kept.at[0, pl.ds(peer * shard_rows, shard_rows)], output_dp
+    )
+    small_to_places = to_places(3, lambda peer: small_low.at[1], small_dp)
+    output_to_heads = to_heads(0, lambda slot: output_kept.at[slot], output_mp)
+    small_to_heads = to_heads(1, lambda slot: small_low.at[2], small_mp)
+
+    def scatter(turn, index, forward):
+        if forward:
+            via_across, via_down, from_across, from_down = (
+                f_via_across, f_via_down, f_across, f_down,
+            )
+            send, recv = f_send, f_recv
+        else:
+            via_across, via_down, from_across, from_down = (
+                g_via_across, g_via_down, g_across, g_down,
+            )
+            send, recv = g_send, g_recv
+        s, h = turn // halves, turn % halves
+        low, high = pl.ds(h * PIECE, HALF), pl.ds(h * PIECE + HALF, HALF)
+        source, target, device = (
+            (part.at[s, far, low], via_across.at[turn], across),
+            (part.at[s, far, high], via_down.at[turn], down),
+            (part.at[s, across, low], from_across.at[turn, first], across),
+            (part.at[s, down, high], from_down.at[turn, second], down),
+            (part.at[s, across, high], from_across.at[turn, second], across),
+            (part.at[s, down, low], from_down.at[turn, first], down),
+        )[index]
+        return remote(source, target, send.at[index, turn], recv.at[index, turn], "mp", device)
+
+    def pass_on(turn, forward):
+        via_across, via_down = (
+            (f_via_across, f_via_down) if forward else (g_via_across, g_via_down)
+        )
+        s, h = turn // halves, turn % halves
+        low = pl.ds(h * PIECE, HALF)
+        high = pl.ds(h * PIECE + HALF, HALF)
+        scatter(turn, 0, forward).wait_recv()
+        part[s, down, low] = part[s, down, low] + via_across[turn]
+        scatter(turn, 5, forward).start()
+        scatter(turn, 1, forward).wait_recv()
+        part[s, across, high] = part[s, across, high] + via_down[turn]
+        scatter(turn, 4, forward).start()
+
+    def summed(turn, forward):
+        from_across, from_down = (f_across, f_down) if forward else (g_across, g_down)
+        for index in range(2, 6):
+            scatter(turn, index, forward).wait_recv()
+        s, h = turn // halves, turn % halves
+        total = part[s, me, h * PIECE : (h + 1) * PIECE].astype(F32)
+        return total + from_across[turn].astype(F32) + from_down[turn].astype(F32)
+
+    def store(turn, kind):
+        source, target = ((out_stage, output), (grad_residual, token_grads))[kind]
+        return pltpu.make_async_copy(source.at[turn], target.at[turn], store_sem.at[kind, turn])
+
+
+    barrier = pltpu.get_barrier_semaphore()
+    for copy in loads:
+        copy.start()
+    for axis, peers in (
+        ("seq", [(side + hop) % sides for hop in range(1, sides)]),
+        ("mp", [across, down, far]),
+        ("dp", [(place + hop) % places for hop in range(1, places)]),
+    ):
+        for peer in peers:
+            pl.semaphore_signal(barrier, inc=1, device_id={axis: peer}, device_id_type=MESH)
+    small[...] = jnp.zeros_like(small)
+    state_grad[...] = jnp.zeros_like(state_grad)
+    small[33:34, :] = channel_part[...]
+    pl.semaphore_wait(barrier, sides - 1 + 3 + places - 1)
+    for copy in hidden_to_sides + output_to_sides:
+        copy.start()
+    loads[4].wait()
+    for turn in range(turns):
+        for index in range(2):
+            scatter(turn, index, True).start()
+    for copy in loads[0:4]:
+        copy.wait()
+
+
+    scale = dk ** (-0.5)
+
+    def ungate(index, carry):
+        rows = pl.ds(pl.multiple_of(index * STEP, STEP), STEP)
+        for s in range(sequences):
+            upper = grad_gated[s, rows, :].astype(F32)
+            head_rows_here = head[s, rows, :].astype(F32)
+            inverse = lax.rsqrt(
+                jnp.mean(head_rows_here * head_rows_here, axis=-1, keepdims=True) + EPS_HEAD
+            )
+            unit = head_rows_here * inverse
+            logits = out_gate[s, rows, :].astype(F32)
+            share = sigmoid(logits)
+            slope = share * (1.0 + logits * (1.0 - share))
+            grad_out_gate[s, rows, :] = (upper * unit * head_gain[...] * slope).astype(BF16)
+            grad_normed = upper * (logits * share)
+            small[34:35, :dv] += jnp.sum(grad_normed * unit, axis=0, keepdims=True)
+            scaled = grad_normed * head_gain[...]
+            through = inverse * (scaled - unit * jnp.mean(scaled * unit, axis=-1, keepdims=True))
+            rounded = (through * scale).astype(BF16)
+            grad_head[s, rows, :] = rounded
+            state_grad[s] += mm_tn(rounded, profile[s, rows, :])
+        return carry
+
+    lax.fori_loop(0, steps, ungate, 0)
+    for copy in state_to_sides:
+        copy.start()
+    for turn in range(turns):
+        for index in range(2, 4):
+            scatter(turn, index, True).start()
+    loads[5].wait()
+    for copy in hidden_to_sides:
+        copy.wait_recv()
+    hidden_sum = hidden_kept[...]
+    for hop in range(sides - 1):
+        hidden_sum = hidden_sum + hidden_seq[hop]
+    hidden_kept[...] = hidden_sum
+    for copy in hidden_to_places:
+        copy.start()
+    loads[6].wait()
+    for copy in output_to_sides:
+        copy.wait_recv()
+    output_sum = output_kept[...]
+    for hop in range(sides - 1):
+        output_sum = output_sum + output_seq[hop]
+    output_kept[...] = output_sum
+    for copy in output_to_heads:
+        copy.start()
+    for copy in loads[7:11]:
+        copy.wait()
+    for copy in state_to_sides:
+        copy.wait_recv()
+    total = jnp.zeros_like(upstream)
+    for ahead in range(sides - 1, 0, -1):
+        source = side + ahead
+        decay = decays[source % sides]
+        longer = state_seq[sides - ahead - 1] + jnp.exp(decay) * total
+        total = jnp.where(source < sides, longer, total)
+    upstream[...] = total
+    grad_extended[:, STEP : STEP + 8, :] = jnp.zeros_like(grad_extended[:, STEP : STEP + 8, :])
+
+
+    taps = taps_in[...]
+    causal = triangle(True)
+
+    def backward_step(back, carry):
+        step = steps - 1 - back
+        start = pl.multiple_of(step * STEP, STEP)
+
+        @pl.when(back > 0)
+        def _():
+            grad_extended[:, STEP : STEP + 8, :] = grad_extended[:, 0:8, :]
+
+        @pl.when(step == 0)
+        def _():
+            extended[:, 0:8, :] = halo[...]
+
+        @pl.when(step > 0)
+        def _():
+            earlier = projected[:, pl.ds(pl.multiple_of(jnp.maximum(start - 16, 0), 16), 16), :]
+            extended[:, 0:8, :] = earlier.astype(F32)[:, 8:16, :]
+
+        for s in range(sequences):
+            here = pl.ds(start, STEP)
+            extended[s, 8 : 8 + STEP, :] = projected[s, here, :].astype(F32)
+            filtered = filter_rows(extended.at[s], taps, STEP)
+            share = sigmoid(filtered)
+            convolved = (filtered * share).astype(BF16)
+            slope = share * (1.0 + filtered * (1.0 - share))
+            low_rows = low_rank[s, here, :]
+            logit = mm(low_rows, rank_up[...]) + bias[...]
+            logit_grads = [None] * per_step
+            for piece in reversed(range(per_step)):
+                rows = slice(piece * CHUNK, (piece + 1) * CHUNK)
+                there = pl.ds(start + piece * CHUNK, CHUNK)
+                queries = convolved[rows, :dk].astype(F32)
+                keys = convolved[rows, dk : 2 * dk].astype(F32)
+                values = convolved[rows, 2 * dk :]
+                grad_rows = grad_head[s, there, :]
+                total = cumulative[s, there, :]
+                middle, last = total[CHUNK // 2 - 1 : CHUNK // 2], total[CHUNK - 1 : CHUNK]
+                lift, lower = jnp.exp(total - middle), jnp.exp(middle - total)
+                inner, outer = jnp.exp(total), jnp.exp(last - total)
+                whole_decay = jnp.exp(last)
+                lifted, lowered = (queries * lift).astype(BF16), (keys * lower).astype(BF16)
+                inside, tails = (queries * inner).astype(BF16), (keys * outer).astype(BF16)
+                previous = before[s, pl.ds(step * per_step + piece, 1), :]
+                state = states[s, step * per_step + piece].astype(F32)
+                state = state + entering[s] * jnp.exp(previous)
+                scores = jnp.where(causal, mm_nt(lifted, lowered), 0.0).astype(BF16)
+                grad_scores = jnp.where(causal, mm_nt(grad_rows, values), 0.0).astype(BF16)
+                later = upstream[s]
+                later_low = later.astype(BF16)
+                grad_values = mm_tn(scores, grad_rows) + mm_nt(tails, later_low)
+                grad_lifted = mm(grad_scores, lowered)
+                grad_lowered = mm_tn(grad_scores, lifted)
+                grad_inside = mm(grad_rows, state.astype(BF16))
+                grad_tails = mm(values, later_low)
+                upstream[s] = later * whole_decay + mm_tn(grad_rows, inside)
+                tail_terms = tails.astype(F32) * grad_tails
+                grad_total = (
+                    lifted.astype(F32) * grad_lifted
+                    - lowered.astype(F32) * grad_lowered
+                    + inside.astype(F32) * grad_inside
+                    - tail_terms
+                )
+                grad_last = jnp.sum(tail_terms, axis=0, keepdims=True) + whole_decay * jnp.sum(
+                    later * state, axis=0, keepdims=True
+                )
+                grad_decay = running_sum(grad_total, False) + grad_last
+                logit_grads[piece] = grad_decay / GATE_NORMALIZER * sigmoid(-logit[rows])
+                grad_extended[s, rows, :dk] = (
+                    grad_lifted * lift + grad_inside * inner
+                ) * slope[rows, :dk]
+                grad_extended[s, rows, dk : 2 * dk] = (
+                    grad_lowered * lower + grad_tails * outer
+                ) * slope[rows, dk : 2 * dk]
+                grad_extended[s, rows, 2 * dk :] = grad_values * slope[rows, 2 * dk :]
+            logit_grad = jnp.concatenate(logit_grads, axis=0)
+            logit_low = logit_grad.astype(BF16)
+            small[35:36, :dk] += jnp.sum(logit_grad, axis=0, keepdims=True)
+            small[16 : 16 + rank, :dk] += mm_tn(low_rows, logit_low)
+            grad_low_rank[s, here, :] = mm_nt(logit_low, rank_up[...]).astype(BF16)
+            total_rows = taps[EDGE : EDGE + 1, :] * grad_extended[s, 0:STEP, :]
+            for offset in range(EDGE):
+                total_rows = total_rows + taps[offset : offset + 1, :] * grad_extended[
+                    s, pl.ds(EDGE - offset, STEP), :
+                ]
+            grad_projected[s, here, :] = total_rows.astype(BF16)
+            grad_filtered = grad_extended[s, 0:STEP, :]
+            for offset in range(CONV):
+                small[16 + offset : 17 + offset, dk : dk + c3] += jnp.sum(
+                    grad_filtered * extended[s, pl.ds(8 - EDGE + offset, STEP), :],
+                    axis=0,
+                    keepdims=True,
+                )
+        for turn in range(turns):
+
+            @pl.when(back == turn % steps)
+            def _():
+                pass_on(turn, True)
+
+        return carry
+
+    lax.fori_loop(0, steps, backward_step, 0)
+
+
+    edge_out[...] = jnp.zeros_like(edge_out)
+    for s in range(sequences):
+        rows = grad_extended[s, 0:8, :]
+        for i in range(EDGE):
+            edge_row = taps[0:1] * rows[i : i + 1]
+            for j in range(1, i + 1):
+                edge_row = edge_row + taps[j : j + 1] * rows[i - j : i - j + 1]
+            edge_out[s, 16 - EDGE + i : 17 - EDGE + i, :] = edge_row
+    edge_copy.start()
+
+
+    loads[11].wait()
+    for turn in range(turns):
+        s, h = turn // halves, turn % halves
+        total = residual[turn] + summed(turn, True)
+        position = side * length + me * (length // 4) + h * PIECE
+        position = position + lax.broadcasted_iota(jnp.int32, (PIECE, 1), 0)
+        out_stage[turn] = jnp.where(position < lengths[s : s + 1, 0:1], total, 0.0).astype(BF16)
+        store(turn, 0).start()
+    for turn in range(turns):
+        for index in range(6):
+            scatter(turn, index, True).wait_send()
+    edge_copy.wait_recv()
+    for s in range(sequences):
+        tail = grad_projected[s, length - 16 :, :].astype(F32)
+        tail = tail + jnp.where(side < sides - 1, edge_in[s], 0.0)
+        grad_projected[s, length - 16 :, :] = tail.astype(BF16)
+
+
+    loads[12].wait()
+    loads[13].wait()
+
+    def input_grad(turn):
+        s, h = turn // halves, turn % halves
+        quarter = length // 4
+
+        def rows_of_turn(ref):
+            blocks = [
+                ref[s, q * quarter + h * PIECE : q * quarter + (h + 1) * PIECE, :]
+                for q in range(4)
+            ]
+            return jnp.concatenate(blocks, axis=0)
+
+        total = mm_nt(rows_of_turn(grad_projected), w_proj[...])
+        total = total + mm_nt(rows_of_turn(grad_out_gate), w_gate[...])
+        total = total + mm_nt(rows_of_turn(grad_low_rank), w_rank[...])
+        rounded = total.astype(BF16)
+        for q in range(4):
+            part[s, q, h * PIECE : (h + 1) * PIECE] = rounded[q * PIECE : (q + 1) * PIECE]
+        for index in range(4):
+            scatter(turn, index, False).start()
+        small[32:33, :] += jnp.sum(
+            total * rows_of_turn(normed).astype(F32), axis=0, keepdims=True
+        )
+
+    for turn in range(turns):
+        input_grad(turn)
+
+
+    flat = sequences * length
+    tile = 256
+
+    def weight_tile(index, carry):
+        columns = pl.ds(pl.multiple_of(index * tile, tile), tile)
+        left = normed[:, :, columns].reshape(flat, tile)
+        mixer_grad[columns, :c3] = mm_tn(left, grad_projected[...].reshape(flat, c3)).astype(BF16)
+        mixer_grad[columns, c3:] = mm_tn(left, grad_out_gate[...].reshape(flat, dv)).astype(BF16)
+        small[0:rank, columns] = mm_tn(grad_low_rank[...].reshape(flat, rank), left)
+        return carry
+
+    lax.fori_loop(0, width // tile, weight_tile, 0)
+    small_low[0] = small[...].astype(BF16)
+    for copy in small_to_sides + mixer_to_sides:
+        copy.start()
+    pass_on(0, False)
+    for copy in output_to_heads:
+        copy.wait_recv()
+    output_kept[0] = output_kept[0] + output_mp[0] + output_mp[1] + output_mp[2]
+    for copy in output_to_places:
+        copy.start()
+    for copy in small_to_sides:
+        copy.wait_recv()
+    small_low[1] = paired_sum(small_low[0], small_seq, range(sides - 1)).astype(BF16)
+    for copy in small_to_places:
+        copy.start()
+    for copy in mixer_to_sides:
+        copy.wait_recv()
+    own = pl.ds(pl.multiple_of(side * share_rows, 16), share_rows)
+    mixer_sum = mixer_grad[own, :]
+    for hop in range(sides - 1):
+        mixer_sum = mixer_sum + mixer_seq[hop]
+    mixer_grad[own, :] = mixer_sum
+    for copy in mixer_to_places:
+        copy.start()
+    pass_on(1, False)
+    for copy in small_to_places:
+        copy.wait_recv()
+    summed_here = paired_sum(small_low[1], small_dp, range(places - 1))
+    small_local[...] = summed_here
+    small_low[2] = summed_here.astype(BF16)
+    for copy in small_to_heads:
+        copy.start()
+    pass_on(2, False)
+    for copy in hidden_to_places:
+        copy.wait_recv()
+    own_shard = pl.ds(pl.multiple_of(place * shard_rows, 16), shard_rows)
+    for kind in range(3):
+        total = hidden_kept[kind, own_shard, :].astype(F32)
+        for hop in range(places - 1):
+            total = total + hidden_dp[hop, kind].astype(F32)
+        hidden_out[kind] = total
+    pass_on(3, False)
+
+
+    loads[14].wait()
+    loads[15].wait()
+    for turn in range(turns):
+        s, h = turn // halves, turn % halves
+        grad_normed = summed(turn, False)
+        rows = tok[s, h * PIECE : (h + 1) * PIECE].astype(F32)
+        inverse = lax.rsqrt(jnp.mean(rows * rows, axis=-1, keepdims=True) + EPS_NORM)
+        unit = rows * inverse
+        scaled = grad_normed * mixer_gain[...]
         through = inverse * (scaled - unit * jnp.mean(scaled * unit, axis=-1, keepdims=True))
-        rounded = (through * scale).astype(BF16)
-        grad_head[s] = rounded
-        state_grad[s] += mm_tn(rounded, query_profile[s])
-
-
-def ungate(grad_gated, head_local, query_profile, entering, out_gate, gain):
-    sequences, length, dv = head_local.shape
-    dk = query_profile.shape[-1]
-    return call(
-        ungate_body,
-        (length // STEP,),
-        [
-            rows3(sequences, STEP, dv),
-            rows3(sequences, STEP, dv),
-            rows3(sequences, STEP, dk),
-            whole((sequences, dv, dk)),
-            rows3(sequences, STEP, dv),
-            whole((1, dv)),
+        grad_residual[turn] = grad_residual[turn] + through
+        store(turn, 1).start()
+    for copy in small_to_heads:
+        copy.wait_recv()
+    small_shared[...] = paired_sum(small_low[2], small_mp, (1, 0, 2))
+    for copy in mixer_to_places + output_to_places:
+        copy.wait_recv()
+    total = mixer_grad[own_share(place), :].astype(F32)
+    for hop in range(places - 1):
+        total = total + mixer_dp[hop].astype(F32)
+    mixer_out[:, : c3 + dv] = total
+    total = output_kept[0, own_shard, :].astype(F32)
+    for hop in range(places - 1):
+        total = total + output_dp[hop].astype(F32)
+    mixer_out[:, c3 + dv :] = total
+
+
+    for copies in (
+        hidden_to_sides, output_to_sides, state_to_sides, mixer_to_sides, small_to_sides,
+        [edge_copy], hidden_to_places, mixer_to_places, output_to_places, small_to_places,
+        output_to_heads, small_to_heads,
+    ):
+        for copy in copies:
+            copy.wait_send()
+    for turn in range(turns):
+        for index in range(6):
+            scatter(turn, index, False).wait_send()
+        store(turn, 0).wait()
+        store(turn, 1).wait()
+
+
+def mixer_back(
+    grad_gated, head, profile, out_gate, projected, cumulative, states, normed, tok, residual,
+    grad_residual, out_part, hidden_grads, output_parts, w_proj, w_gate, low_rank, halo, taps,
+    rank_up, bias, w_rank, before, entering, decays, head_gain, mixer_gain, channel_part, lengths,
+    seq_count, dp_count,
+):
+    sequences, length, width = normed.shape
+    dv, c3 = grad_gated.shape[-1], projected.shape[-1]
+    rank, dk = rank_up.shape
+    units = hidden_grads.shape[-1]
+    quarter = length // 4
+    turns = sequences * quarter // PIECE
+    share_rows = width // seq_count
+    shard_rows = share_rows // dp_count
+    peers, others = seq_count - 1, dp_count - 1
+    anywhere = pl.BlockSpec(memory_space=pl.ANY)
+    vmem = pl.BlockSpec(memory_space=pltpu.VMEM)
+    dma = pltpu.SemaphoreType.DMA
+
+    def low(*shape):
+        return pltpu.VMEM(shape, BF16)
+
+    def full(*shape):
+        return pltpu.VMEM(shape, F32)
+
+    hops = [
+        low(turns, HALF, width),
+        low(turns, HALF, width),
+        low(turns, PIECE, width),
+        low(turns, PIECE, width),
+    ]
+    return pl.pallas_call(
+        mixer_back_body,
+        in_specs=[anywhere] * 16 + [vmem] * 13,
+        out_specs=[anywhere] * 2 + [vmem] * 4,
+        out_shape=[
+            shape_of((turns, PIECE, width), BF16),
+            shape_of((turns, PIECE, width), F32),
+            shape_of((3, shard_rows, units), F32),
+            shape_of((shard_rows, c3 + 2 * dv), F32),
+            shape_of((SMALL, width), F32),
+            shape_of((SMALL, width), F32),
         ],
-        [
-            rows3(sequences, STEP, dv),
-            rows3(sequences, STEP, dv),
-            whole((sequences, dv, dk)),
-            whole((1, dv)),
+        scratch_shapes=[
+            low(sequences, length, dv),
+            low(sequences, length, dv),
+            low(sequences, length, dk),
+            low(sequences, length, dv),
+            low(sequences, length, c3),
+            full(sequences, length, dk),
+            low(sequences, length // CHUNK, dv, dk),
+            low(sequences, length, width),
+            low(sequences, quarter, width),
+            full(turns, PIECE, width),
+            full(turns, PIECE, width),
+            low(sequences, 4, quarter, width),
+            low(width, c3),
+            low(width, dv),
+            low(3, share_rows, units),
+            low(peers, 3, share_rows, units),
+            low(others, 3, shard_rows, units),
+            low(4, share_rows, dv),
+            low(peers, 4, share_rows, dv),
+            low(3, share_rows, dv),
+            low(others, shard_rows, dv),
+            *hops,
+            *hops,
+            low(sequences, length, dv),
+            low(sequences, length, dv),
+            low(sequences, length, c3),
+            low(sequences, length, rank),
+            low(width, c3 + dv),
+            low(peers, share_rows, c3 + dv),
+            low(others, shard_rows, c3 + dv),
+            full(sequences, dv, dk),
+            full(peers, sequences, dv, dk),
+            full(sequences, dv, dk),
+            full(sequences, STEP + 8, c3),
+            full(sequences, STEP + 8, c3),
+            full(sequences, 16, c3),
+            full(sequences, 16, c3),
+            full(SMALL, width),
+            low(3, SMALL, width),
+            low(peers, SMALL, width),
+            low(others, SMALL, width),
+            low(3, SMALL, width),
+            low(turns, PIECE, width),
+            dma((16,)),
+            dma((6, peers)),
+            dma((6, peers)),
+            dma((4, others)),
+            dma((4, others)),
+            dma((2, 3)),
+            dma((2, 3)),
+            dma((6, turns)),
+            dma((6, turns)),
+            dma((6, turns)),
+            dma((6, turns)),
+            dma((2, turns)),
         ],
-        [
-            shape_of((sequences, length, dv), BF16),
-            shape_of((sequences, length, dv), BF16),
-            shape_of((sequences, dv, dk), F32),
-            shape_of((1, dv), F32),
-        ],
-        [],
-        2 * sequences * length * dk * dv * 8,
-        sequences * length * (dv * 12 + dk * 2),
-    )(grad_gated, head_local, query_profile, entering, out_gate, gain)
-
-
-def backward_body(
-    projected, earlier, halo, low_rank, taps_in, rank_up, bias, cumulative, states, before,
-    entering, leaving, grad_head,
-    grad_projected, grad_low_rank, first_rows, filter_grad, rank_up_grad, bias_grad,
-    extended, grad_extended, upstream,
-):
-    back = pl.program_id(0)
-    step = pl.num_programs(0) - 1 - back
-    per_step = STEP // CHUNK
-    sequences = projected.shape[0]
-
-    @pl.when(back == 0)
-    def _():
-        upstream[...] = leaving[...]
-        grad_extended[:, STEP : STEP + 8, :] = jnp.zeros_like(grad_extended[:, STEP : STEP + 8, :])
-        filter_grad[...] = jnp.zeros_like(filter_grad)
-        rank_up_grad[...] = jnp.zeros_like(rank_up_grad)
-        bias_grad[...] = jnp.zeros_like(bias_grad)
-
-    @pl.when(back > 0)
-    def _():
-        grad_extended[:, STEP : STEP + 8, :] = grad_extended[:, 0:8, :]
-
-    @pl.when(step == 0)
-    def _():
-        extended[:, 0:8, :] = halo[...]
-
-    @pl.when(step > 0)
-    def _():
-        extended[:, 0:8, :] = earlier[...].astype(F32)[:, 8:16, :]
-
-    taps = taps_in[...]
-    width = rank_up.shape[1]
-    causal = triangle(True)
-    for s in range(sequences):
-        extended[s, 8 : 8 + STEP, :] = projected[s].astype(F32)
-        filtered = filter_rows(extended.at[s], taps, STEP)
-        share = sigmoid(filtered)
-        convolved = (filtered * share).astype(BF16)
-        slope = share * (1.0 + filtered * (1.0 - share))
-        logit = mm(low_rank[s], rank_up[...]) + bias[...]
-        logit_grads = [None] * per_step
-        for part in reversed(range(per_step)):
-            rows = slice(part * CHUNK, (part + 1) * CHUNK)
-            queries = convolved[rows, :width].astype(F32)
-            keys = convolved[rows, width : 2 * width].astype(F32)
-            values = convolved[rows, 2 * width :]
-            grad_rows = grad_head[s, rows, :]
-            total = cumulative[s, rows, :]
-            middle, last = total[CHUNK // 2 - 1 : CHUNK // 2], total[CHUNK - 1 : CHUNK]
-            lift, lower = jnp.exp(total - middle), jnp.exp(middle - total)
-            inner, outer, whole_decay = jnp.exp(total), jnp.exp(last - total), jnp.exp(last)
-            lifted, lowered = (queries * lift).astype(BF16), (keys * lower).astype(BF16)
-            profile, tails = (queries * inner).astype(BF16), (keys * outer).astype(BF16)
-            previous = before[s, pl.ds(step * per_step + part, 1), :]
-            state = states[s, part].astype(F32) + entering[s] * jnp.exp(previous)
-            scores = jnp.where(causal, mm_nt(lifted, lowered), 0.0).astype(BF16)
-            grad_scores = jnp.where(causal, mm_nt(grad_rows, values), 0.0).astype(BF16)
-            later = upstream[s]
-            later_low = later.astype(BF16)
-            grad_values = mm_tn(scores, grad_rows) + mm_nt(tails, later_low)
-            grad_lifted = mm(grad_scores, lowered)
-            grad_lowered = mm_tn(grad_scores, lifted)
-            grad_profile = mm(grad_rows, state.astype(BF16))
-            grad_tails = mm(values, later_low)
-            upstream[s] = later * whole_decay + mm_tn(grad_rows, profile)
-            tail_terms = tails.astype(F32) * grad_tails
-            grad_total = (
-                lifted.astype(F32) * grad_lifted
-                - lowered.astype(F32) * grad_lowered
-                + profile.astype(F32) * grad_profile
-                - tail_terms
-            )
-            grad_last = jnp.sum(tail_terms, axis=0, keepdims=True) + whole_decay * jnp.sum(
-                later * state, axis=0, keepdims=True
-            )
-            grad_decay = running_sum(grad_total, False) + grad_last
-            logit_grads[part] = grad_decay / GATE_NORMALIZER * sigmoid(-logit[rows])
-            grad_extended[s, rows, :width] = (
-                grad_lifted * lift + grad_profile * inner
-            ) * slope[rows, :width]
-            grad_extended[s, rows, width : 2 * width] = (
-                grad_lowered * lower + grad_tails * outer
-            ) * slope[rows, width : 2 * width]
-            grad_extended[s, rows, 2 * width :] = grad_values * slope[rows, 2 * width :]
-        logit_grad = jnp.concatenate(logit_grads, axis=0)
-        logit_low = logit_grad.astype(BF16)
-        bias_grad[...] += jnp.sum(logit_grad, axis=0, keepdims=True)
-        rank_up_grad[...] += mm_tn(low_rank[s], logit_low)
-        grad_low_rank[s] = mm_nt(logit_low, rank_up[...]).astype(BF16)
-        total_rows = taps[EDGE : EDGE + 1, :] * grad_extended[s, 0:STEP, :]
-        for offset in range(EDGE):
-            total_rows = total_rows + taps[offset : offset + 1, :] * grad_extended[
-                s, pl.ds(EDGE - offset, STEP), :
-            ]
-        grad_projected[s] = total_rows.astype(BF16)
-        grad_filtered = grad_extended[s, 0:STEP, :]
-        for offset in range(CONV):
-            filter_grad[offset : offset + 1, :] += jnp.sum(
-                grad_filtered * extended[s, pl.ds(8 - EDGE + offset, STEP), :],
-                axis=0,
-                keepdims=True,
-            )
-        first_rows[s] = grad_extended[s, 0:8, :]
-
-
-def backward_mix(
-    projected, halo, low_rank, taps, rank_up, bias, cumulative, states, before, entering,
-    leaving, grad_head,
-):
-    sequences, length, c3 = projected.shape
-    rank, dk = rank_up.shape
-    dv = grad_head.shape[-1]
-    chunks, per_step, steps = length // CHUNK, STEP // CHUNK, length // STEP
-
-    def reverse(size, width):
-        return pl.BlockSpec((sequences, size, width), lambda i: (0, steps - 1 - i, 0))
-
-    return call(
-        backward_body,
-        (steps,),
-        [
-            reverse(STEP, c3),
-            pl.BlockSpec(
-                (sequences, 16, c3),
-                lambda i: (0, jnp.maximum((steps - 1 - i) * (STEP // 16) - 1, 0), 0),
-            ),
-            whole((sequences, 8, c3)),
-            reverse(STEP, rank),
-            whole(taps.shape),
-            whole((rank, dk)),
-            whole((1, dk)),
-            reverse(STEP, dk),
-            pl.BlockSpec((sequences, per_step, dv, dk), lambda i: (0, steps - 1 - i, 0, 0)),
-            whole((sequences, chunks, dk)),
-            whole((sequences, dv, dk)),
-            whole((sequences, dv, dk)),
-            reverse(STEP, dv),
-        ],
-        [
-            reverse(STEP, c3),
-            reverse(STEP, rank),
-            whole((sequences, 8, c3)),
-            whole(taps.shape),
-            whole((rank, dk)),
-            whole((1, dk)),
-        ],
-        [
-            shape_of((sequences, length, c3), BF16),
-            shape_of((sequences, length, rank), BF16),
-            shape_of((sequences, 8, c3), F32),
-            shape_of(taps.shape, F32),
-            shape_of((rank, dk), F32),
-            shape_of((1, dk), F32),
-        ],
-        [
-            pltpu.VMEM((sequences, STEP + 8, c3), F32),
-            pltpu.VMEM((sequences, STEP + 8, c3), F32),
-            pltpu.VMEM((sequences, dv, dk), F32),
-        ],
-        2 * sequences * length * (12 * dk * dv) * 8,
-        sequences * (length * (c3 * 4 + dk * 4 + dv * 2) + chunks * dv * dk * 2),
+        compiler_params=pltpu.CompilerParams(
+            collective_id=1, has_side_effects=True, vmem_limit_bytes=64 * 2**20
+        ),
+        cost_estimate=pl.CostEstimate(
+            flops=2 * sequences * length * width * 2 * (c3 + dv) * 2,
+            bytes_accessed=sequences * length * width * 16,
+            transcendentals=0,
+        ),
+        name="mixer_back",
     )(
-        projected, projected, halo, low_rank, taps, rank_up, bias, cumulative, states, before,
-        entering, leaving, grad_head,
+        grad_gated, head, profile, out_gate, projected, cumulative, states, normed, tok, residual,
+        grad_residual, out_part, hidden_grads, output_parts, w_proj, w_gate, low_rank, halo, taps,
+        rank_up, bias, w_rank, before, entering, decays, head_gain, mixer_gain, channel_part,
+        lengths,
     )
-
-
-def input_grad_body(
-    grad_projected, grad_out_gate, grad_low_rank, w_proj, w_gate, w_rank, normed,
-    parts, gain_grad,
-):
-    @pl.when(pl.program_id(0) == 0)
-    def _():
-        gain_grad[...] = jnp.zeros_like(gain_grad)
-
-    for s in range(normed.shape[0]):
-        total = mm_nt(grad_projected[s], w_proj[...]) + mm_nt(grad_out_gate[s], w_gate[...])
-        total = total + mm_nt(grad_low_rank[s], w_rank[...])
-        parts[s] = total.astype(BF16)
-        gain_grad[...] += jnp.sum(total * normed[s].astype(F32), axis=0, keepdims=True)
-
-
-def input_grad(grad_projected, grad_out_gate, grad_low_rank, w_proj, w_gate, w_rank, normed):
-    sequences, length, width = normed.shape
-    c3, dv, rank = w_proj.shape[1], w_gate.shape[1], w_rank.shape[1]
-    return call(
-        input_grad_body,
-        (length // STEP,),
-        [
-            rows3(sequences, STEP, c3),
-            rows3(sequences, STEP, dv),
-            rows3(sequences, STEP, rank),
-            whole((width, c3)),
-            whole((width, dv)),
-            whole((width, rank)),
-            rows3(sequences, STEP, width),
-        ],
-        [rows3(sequences, STEP, width), whole((1, width))],
-        [shape_of((sequences, length, width), BF16), shape_of((1, width), F32)],
-        [],
-        2 * sequences * length * width * (c3 + dv + rank),
-        sequences * length * (2 * width + c3 + dv) * 2 + width * (c3 + dv) * 2,
-    )(grad_projected, grad_out_gate, grad_low_rank, w_proj, w_gate, w_rank, normed)
 
 
 ACROSS = [(i, i ^ 1) for i in range(4)]
 DOWN = [(i, i ^ 2) for i in range(4)]
-OPPOSITE = [(i, i ^ 3) for i in range(4)]
 
 
 def gather_relative(block):
@@ -953,24 +1357,6 @@
     return [block, across, down, jnp.concatenate([first, second], axis=0)]
 
 
-def scatter_rows(first, across, down, far):
-    via_across = lax.ppermute(far[:1], "mp", ACROSS)
-    via_down = lax.ppermute(far[1:], "mp", DOWN)
-    across_a = lax.ppermute(across[:1], "mp", ACROSS)
-    down_b = lax.ppermute(down[1:], "mp", DOWN)
-    across_b = lax.ppermute(across[1:] + via_down, "mp", ACROSS)
-    down_a = lax.ppermute(down[:1] + via_across, "mp", DOWN)
-    across = jnp.concatenate([across_a, across_b], axis=0).astype(F32)
-    down = jnp.concatenate([down_a, down_b], axis=0).astype(F32)
-    return first.astype(F32) + across + down
-
-
-def scatter_quarters(parts, me):
-    return scatter_rows(
-        *[lax.dynamic_index_in_dim(parts, me ^ slot, 1, False) for slot in range(4)]
-    )
-
-
 def passed_along(block, axis, distance):
     devices = range(lax.axis_size(axis))
     route = [(i - distance, i) for i in devices if i - distance in devices]
@@ -990,39 +1376,6 @@
         return jnp.where(position < mine, longer, subtotal)
 
     return lax.fori_loop(0, count - 1, hop, jnp.zeros_like(state))
-
-
-def sum_shards(grad):
-    if lax.axis_size("seq") != 2 or lax.axis_size("dp") != 4:
-        total = lax.psum_scatter(grad, ("seq", "dp"), scatter_dimension=0, tiled=True)
-        return total[0].astype(F32)
-    side, place = lax.axis_index("seq"), lax.axis_index("dp")
-    other = lax.dynamic_slice_in_dim(grad, (1 - side) * 4, 4, 0)
-    kept = lax.dynamic_slice_in_dim(grad, side * 4, 4, 0)
-    kept = kept + lax.ppermute(other, "seq", [(0, 1), (1, 0)])
-    upward, downward = None, None
-    for turn in range(1, 4):
-        above = lax.dynamic_index_in_dim(kept, jnp.minimum(place + 4 - turn, 3), 0, False)
-        below = lax.dynamic_index_in_dim(kept, jnp.maximum(place - 4 + turn, 0), 0, False)
-        if turn > 1:
-            above, below = above + upward, below + downward
-        upward = lax.ppermute(above, "dp", [(i, i + 1) for i in range(turn)])
-        downward = lax.ppermute(below, "dp", [(3 - i, 2 - i) for i in range(turn)])
-    mine = lax.dynamic_index_in_dim(kept, place, 0, False)
-    return mine.astype(F32) + upward.astype(F32) + downward.astype(F32)
-
-
-def sum_over(values, axes):
-    for axis in axes:
-        count = lax.axis_size(axis)
-        if count & (count - 1) or count > 4:
-            values = lax.psum(values, axis)
-            continue
-        distance = 1
-        while distance < count:
-            values = values + lax.ppermute(values, axis, [(i, i ^ distance) for i in range(count)])
-            distance *= 2
-    return values
 
 
 def on_device(
@@ -1071,120 +1424,49 @@
         projected, halo, low_rank, taps, rank_up_here, bias, dv
     )
     entering = chain_states(total_decay, end_state, False)
-    gated = gate(head_local, query_profile, entering, out_gate, head_gain_f)
+    gated, head = gate(head_local, query_profile, entering, out_gate, head_gain_f)
     (
         out_part, hidden_grads, output_parts, grad_gated, residual, grad_residual,
         channel_gain_part,
     ) = feed_forward(
         gated, output_weights, tok, channel_gain_f, hidden_gate, hidden_up, hidden_down, upstream
     )
-    grad_out_gate, grad_head, state_grad, head_gain_part = ungate(
-        grad_gated, head_local, query_profile, entering, out_gate, head_gain_f
+    count = lax.axis_size("seq")
+    if count > 2:
+        decays = lax.all_gather(total_decay, "seq")
+    else:
+        decays = jnp.zeros((count, *total_decay.shape), F32)
+    outputs, token_grads, hidden_sums, mixer_sums, small, shared = mixer_back(
+        grad_gated, head, query_profile, out_gate, projected, cumulative, states, normed,
+        tok.reshape(sequences, 4, own_rows, width), residual, grad_residual, out_part,
+        hidden_grads, output_parts, w_proj, gate_weight, low_rank, halo, taps, rank_up_here, bias,
+        rank_down, before, entering, decays, head_gain_f, mixer_gain_f, channel_gain_part,
+        jnp.broadcast_to(lengths.astype(jnp.int32)[:, None], (sequences, 128)),
+        count, lax.axis_size("dp"),
     )
-    leaving = chain_states(total_decay, state_grad, True)
-    (
-        grad_projected, grad_low_rank, first_rows, filter_part, rank_up_part, bias_part,
-    ) = backward_mix(
-        projected, halo, low_rank, taps, rank_up_here, bias, cumulative, states, before,
-        entering, leaving, grad_head,
-    )
-    edge = jnp.concatenate(
-        [
-            sum(taps[j : j + 1] * first_rows[:, i - j : i - j + 1] for j in range(i + 1))
-            for i in range(EDGE)
-        ],
-        axis=1,
-    )
-    edge = passed_along(edge, "seq", -1)
-    tail = grad_projected[:, length - 16 :].astype(F32)
-    tail = tail + jnp.pad(edge, ((0, 0), (16 - EDGE, 0), (0, 0)))
-    grad_projected = lax.dynamic_update_slice_in_dim(
-        grad_projected, tail.astype(BF16), length - 16, 1
-    )
-    normed_parts, mixer_gain_part = input_grad(
-        grad_projected, grad_out_gate, grad_low_rank, w_proj, gate_weight, rank_down, normed
-    )
-
-    def flat(values):
-        return values.reshape(sequences * length, values.shape[-1])
-
-    def in_shards(grad):
-        return grad.astype(BF16).reshape(shards, width // shards, grad.shape[-1])
-
-    hidden_grads = hidden_grads.reshape(3, shards, width // shards, hidden_grads.shape[-1])
-    hidden_grads = sum_shards(hidden_grads.swapaxes(0, 1))
-    halved = output_parts.reshape(4, 2, width // 2, dv)
-    output_grad = scatter_rows(*[halved[slot] for slot in range(4)])
-    mixer_grads = jnp.concatenate(
-        [
-            in_shards(mm_tn(flat(normed), flat(grad_projected))),
-            in_shards(mm_tn(flat(normed), flat(grad_out_gate))),
-            in_shards(output_grad.reshape(width, dv)),
-        ],
-        axis=-1,
-    )
-    mixer_grads = sum_shards(mixer_grads)
-    c3 = w_proj.shape[1]
-
-    shared = [
-        mixer_gain_part[0] / mixer_gain_f[0],
-        channel_gain_part[0],
-        head_gain_part[0],
-        mm_tn(flat(normed), flat(grad_low_rank)).reshape(-1),
-    ]
-    local = [filter_part.reshape(-1), rank_up_part.reshape(-1), bias_part.reshape(-1)]
-    shared_size = sum(part.shape[0] for part in shared)
-    small = sum_over(jnp.concatenate(shared + local), ("seq", "dp"))
-    shared_sum = sum_over(small[:shared_size], ("mp",))
-
-    def take(values, start, shape):
-        count = 1
-        for size in shape:
-            count *= size
-        return lax.slice_in_dim(values, start, start + count).reshape(shape)
+    c3, (rank, _, dk) = w_proj.shape[1], rank_up.shape
 
     def own(values):
-        share = values.shape[-1] // shards
-        return lax.dynamic_slice_in_dim(values, shard * share, share, values.ndim - 1)
-
-    mixer_gain_grad = take(shared_sum, 0, (width,))
-    channel_gain_grad = take(shared_sum, width, (width,))
-    head_gain_grad = take(shared_sum, 2 * width, (dv,))
-    rank_down_grad = take(shared_sum, 2 * width + dv, rank_down.shape)
-    filter_grad = own(take(small, shared_size, filter_weight.shape))
-    start = shared_size + filter_weight.size
-    rank_up_grad = own(take(small, start, rank_up.shape))
-    decay_bias_grad = own(take(small, start + rank_up.size, decay_bias.shape))
-
-    own_shape = (sequences, 4, own_rows, width)
-    ffn_out = scatter_quarters(out_part, me)
-    own_positions = lax.axis_index("seq") * length + me * own_rows
-    own_positions = own_positions + lax.broadcasted_iota(jnp.int32, (1, own_rows, 1), 1)
-    own_mask = own_positions < lengths[:, None, None]
-    outputs = jnp.where(own_mask, residual + ffn_out, 0.0).astype(BF16)
-    grad_normed = scatter_quarters(normed_parts.reshape(own_shape), me)
-    rows = lax.dynamic_index_in_dim(tok.reshape(own_shape), me, 1, False).astype(F32)
-    inverse = lax.rsqrt(jnp.mean(rows * rows, axis=-1, keepdims=True) + EPS_NORM)
-    unit = rows * inverse
-    scaled = grad_normed * mixer_gain_f
-    through = inverse * (scaled - unit * jnp.mean(scaled * unit, axis=-1, keepdims=True))
-    token_grads = grad_residual + through
+        size = values.shape[-1] // shards
+        return lax.dynamic_slice_in_dim(values, shard * size, size, values.ndim - 1)
+
+    own_shape = (sequences, own_rows, width)
     return (
-        outputs.swapaxes(0, 1),
-        token_grads.swapaxes(0, 1),
-        mixer_gain_grad,
-        mixer_grads[:, None, :c3],
-        filter_grad,
-        rank_down_grad,
-        rank_up_grad,
-        decay_bias_grad,
-        mixer_grads[:, c3 : c3 + dv],
-        head_gain_grad,
-        mixer_grads[:, c3 + dv :].T,
-        channel_gain_grad,
-        hidden_grads[0],
-        hidden_grads[1],
-        hidden_grads[2].T,
+        outputs.reshape(own_shape).swapaxes(0, 1),
+        token_grads.reshape(own_shape).swapaxes(0, 1),
+        shared[32] / mixer_gain_f[0],
+        mixer_sums[:, None, :c3],
+        own(small[16 : 16 + CONV, dk : dk + c3])[:, None],
+        shared[:rank].T,
+        own(small[16 : 16 + rank, :dk])[:, None],
+        own(small[35:36, :dk]),
+        mixer_sums[:, c3 : c3 + dv],
+        shared[34, :dv],
+        mixer_sums[:, c3 + dv :].T,
+        shared[33],
+        hidden_sums[0],
+        hidden_sums[1],
+        hidden_sums[2].T,
     )
 
 

time: 385 us -> 292 us (0.76)
  starting transfers between devices: 68.3 us -> 8.25 us
  Pallas kernels: 166 us -> 226 us
  waiting for transfers between devices: 56.4 us -> 0.02 us
  other arithmetic: 25.3 us -> 6.22 us
  matrix products: 8.15 us -> 0.26 us
  local copies, waits for them, and re-layouts: 53.2 us -> 46.3 us
    pallas_call x3 -> x1, Pallas kernels: 36 us -> 94.5 us  [mixer_back(): pl.pallas_call(mixer_back_body, in_specs=[anywhere] * 16 + [vmem] * 13, o...]
    ppermute x37 -> x0, starting transfers between devices: 57.3 us -> none  [the longest x6 26.2 us: sum_shards(): upward = lax.ppermute(above, 'dp', [(i, i + 1) for i in range(turn)])]
    ppermute x37 -> x0, waiting for transfers between devices: 55.6 us -> none  [the longest x6 13.7 us: sum_shards(): upward = lax.ppermute(above, 'dp', [(i, i + 1) for i in range(turn)])]
    add x20 -> x0, other arithmetic: 11.6 us -> none  [the longest x2 3.41 us: scatter_rows(): across_b = lax.ppermute(across[1:] + via_down, 'mp', ACROSS)]
    unnamed x90 -> x36, local copies, waits for them, and re-layouts: 20 us -> 9.16 us
    dot_general x3 -> x0, matrix products: 7.89 us -> none  [mm_tn(): lax.dot_general(left, right, (((0,), (0,)), ((), ())), preferred_element_...]
    reshape x1 -> x2, local copies, waits for them, and re-layouts: 0.19 us -> 6.67 us  [the longest x1 4.62 us: on_device(): token_grads.reshape(own_shape).swapaxes(0, 1)]
    slice x12 -> x5, local copies, waits for them, and re-layouts: 9.44 us -> 4.79 us  [the longest x1 1.43 us: on_device(): shared[33]]
  transfers between devices with their start and end apart: 45 -> 6, of which waited for: 15 -> 0; matrix products, arithmetic and copies ran while one was open for 22% -> 9% of each run, Pallas kernels for 16% -> 11%
where the time goes in v3:
time: 292 us; the launch traced here: 287 us
  Pallas kernels  226 us (77%)
  local copies, waits for them, and re-layouts  46.3 us (16%)
  starting transfers between devices  8.25 us (3%)
  other arithmetic  6.22 us (2%)
    pallas_call x1, Pallas kernels, feed_forward(): pl.pallas_call(ffn_body, in_specs=[vmem] * 5 + [anywhere, vmem] + [anywhe...  98 us
    pallas_call x1, Pallas kernels, mixer_back(): pl.pallas_call(mixer_back_body, in_specs=[anywhere] * 16 + [vmem] * 13, o...  94.5 us
    pallas_call x1, Pallas kernels, project(): call(project_body, (length // CHUNK,), [rows_of(CHUNK * sequences, width)...  15 us
    pallas_call x1, Pallas kernels, forward_mix(): call(forward_body, (length // STEP,), [rows3(sequences, STEP, c3), whole(...  13 us
    unnamed x36, local copies, waits for them, and re-layouts  9.16 us
    reshape x1, local copies, waits for them, and re-layouts, on_device(): tokens.reshape(length * sequences, width)  7.19 us
    reshape x1, local copies, waits for them, and re-layouts, on_device(): cotangent.reshape(length * sequences, width)  7.19 us
  transfers between devices with their start and end apart: 6, of which 0 were waited for; matrix products, arithmetic and copies ran while one was open for 9% of the time, Pallas kernels for 11%

profile of v3, /device:TPU:0, one launch (start us, length us, event | category | flops | bytes accessed | tf_op | source)
XLA Modules:
  0.0 287.4 jit_solution(17841565129770541757)
XLA Ops:
  0.6 3.0 %collective-permute-start.2 = (bf16[256,1024]{1,0:T(8,128)(2,1)}, bf16[256,1024]{1,0:T(8,128)(2,1)}, u32[]{:S(2)}, u32[]{:S(2)}) collective-permute-start(bf16[256,1024]{1,0:T(8,128)(2,1)} %w_own.1), channel_id=1, source_target_pairs={{0,4},{4,0},{8,12},{12,8},{1,5},{5,1},{9,13},{13,9},{2,6},{6,2},{1... | collective-permute-start | bytes 1572872 | tf_op jit(solution)/shard_map/ppermute | solution.py:1353
  3.6 1.5 collective-permute-start.3
  5.2 0.7 slice.48
  5.9 1.3 collective-permute-start
  7.2 0.0 copy-start.8
  7.2 0.0 copy-start.6
  7.2 7.2 %reshape.76.tok_in = bf16[2048,1024]{1,0:T(8,128)(2,1)} reshape(bf16[1024,2,1024]{2,1,0:T(2,128)(2,1)} %param.16) | data formatting | bytes 8388608 | tf_op jit(solution)/shard_map/reshape | solution.py:1415
  14.4 0.0 copy-done.8
  14.4 0.6 convert_element_type.26
  15.0 0.8 copy.31.w_rank
  15.8 7.2 %reshape.77.cot_in = bf16[2048,1024]{1,0:T(8,128)(2,1)} reshape(bf16[1024,2,1024]{2,1,0:T(2,128)(2,1)} %param.31) | data formatting | bytes 8388608 | tf_op jit(solution)/shard_map/reshape | solution.py:1416
  23.0 0.6 pad_add_fusion.places
  23.6 15.0 %shard_map.271 = (bf16[2,1024,1024]{2,1,0:T(8,128)(2,1)}, bf16[2,1024,1024]{2,1,0:T(8,128)(2,1)}, bf16[2,1024,1024]{2,1,0:T(8,128)(2,1)}, bf16[2,1024,512]{2,1,0...) custom-call(s32[3]{0:T(128)} %pad_add_fusion.places, bf16[2048,1024]{1,0:T(8,128)(2,1)} %reshape.76.tok_in, ...), custom_call_target="tpu_custom_call" | custom-call | flops 5435817984 | bytes 25690112 | tf_op jit(solution)/shard_map/pallas_call | solution.py:107
  38.7 0.6 bitcast_convert_fusion.taps_in
  39.3 0.0 collective-permute-done
  39.3 0.1 fusion.2
  39.4 0.1 fusion.4
  39.5 0.3 fusion
  39.8 0.6 pad_convert_fusion.halo
  40.4 13.0 %shard_map.272 = (f32[2,1024,256]{2,1,0:T(8,128)}, bf16[2,1024,128]{2,1,0:T(8,128)(2,1)}, f32[2,1024,128]{2,1,0:T(8,128)}, bf16[2,8,256,128]{3,2,1,0:T(8,128)(2,...) custom-call(bf16[2,1024,512]{2,1,0:T(8,128)(2,1)} %get-tuple-element.42.projected.projected_in, ...), custom_call_target="tpu_custom_call" | custom-call | flops 4831838208 | bytes 6815744 | tf_op jit(solution)/shard_map/pallas_call | solution.py:204
  53.4 0.0 copy-start.1
  53.4 1.6 collective-permute-start.1
  55.0 0.0 collective-permute-done.2.w_across
  55.0 1.0 slice.64
  56.0 0.6 collective-permute-start.4
  56.6 0.0 collective-permute-done.3.w_down_hop
  56.6 1.7 slice.65
  58.3 0.2 collective-permute-start.5
  58.5 0.6 broadcast_in_dim.42
  59.1 1.6 copy.33.w_gate
  60.7 1.6 copy.34.w_up
  62.2 0.0 copy-done.11
  62.2 0.6 broadcast_in_dim.43
  62.8 0.0 collective-permute-done.1.entering
  62.8 0.7 copy-done.5
  63.5 5.0 %shard_map.273 = (bf16[2,1024,256]{2,1,0:T(8,128)(2,1)}, bf16[2,1024,256]{2,1,0:T(8,128)(2,1)}) custom-call(f32[2,1024,256]{2,1,0:T(8,128)} %get-tuple-element.44.head_local, bf16[2,1024,128]{2,1,0:T(8,128)(2,1)} %get-tuple-element.45.query_profile.profile_in, f32[2,256,128]{2,1,0:T(8,128)} %copy-done.5, ...), custom_call_target="tpu_custom_call" | custom-call | flops 536870912 | bytes 5767168 | tf_op jit(solution)/shard_map/pallas_call | solution.py:260
  68.5 0.0 collective-permute-done.4
  68.5 0.0 collective-permute-done.5
  68.5 1.9 pad_maximum_fusion.w_far
  70.4 98.0 %feed_forward.1 = (bf16[2,4,2,128,1024]{4,3,2,1,0:T(8,128)(2,1)}, bf16[3,1024,704]{2,1,0:T(8,128)(2,1)}, bf16[4,1024,256]{2,1,0:T(8,128)(2,1)}, bf16[2,4,2,128,2...) custom-call(bf16[2,4,2,128,256]{4,3,2,1,0:T(8,128)(2,1)} %bitcast.63, ...), custom_call_target="tpu_custom_call" | custom-call | flops 30870077440 | bytes 16777216 | tf_op jit(solution)/shard_map/feed_forward/pallas_call | solution.py:602
  168.4 1.3 broadcast_in_dim.38.lengths
  169.7 0.6 broadcast_in_dim.37.decays
  170.3 94.5 %mixer_back.1 = (bf16[4,128,1024]{2,1,0:T(8,128)(2,1)}, f32[4,128,1024]{2,1,0:T(8,128)}, f32[3,128,704]{2,1,0:T(8,128)}, f32[128,1024]{1,0:T(8,128)}, f32[48,1024]{1,0:T(8,128)}, /*index=5*/f32[48,1024]{1,0:T(8,128)}) custom-call(bf16[2,1024,256]{2,1,0:T(8,128)(2,1)} %bitcast.70, bf16[2,1024,256]{2,1,0:T(8,128)(2,1)} %get-tuple-element.52.head_in, ...), custom_call_target="tpu_custom_call" | custom-call | flops 12884901888 | bytes 33554432 | tf_op jit(solution)/shard_map/mixer_back/pallas_call | solution.py:1261
  264.8 1.0 slice_bitcast_fusion.3
  265.8 1.6 slice_bitcast_fusion.4
  267.4 0.7 slice.55
  268.1 0.7 slice.53
  268.9 0.7 slice.56
  269.5 1.5 slice_bitcast_fusion.5
  271.0 1.4 fusion.6
  272.4 1.3 slice.58
  273.7 4.6 %copy.47 = f32[2,256,1024]{2,0,1:T(2,128)} copy(f32[2,256,1024]{2,1,0:T(8,128)} %bitcast.48) | data formatting | bytes 4194304 | tf_op jit(solution)/shard_map/reshape | solution.py:1456
  278.3 0.1 slice_bitcast_fusion
  278.4 0.9 copy.40
  279.3 0.9 copy.41
  280.2 0.9 copy.42
  281.1 0.0 copy-done.4
  281.1 2.0 copy.48
  283.2 1.0 copy.38
  284.2 0.8 copy.39
  284.9 0.7 constant_dynamic-slice_fusion.1
  285.6 0.6 constant_dynamic-slice_fusion
  286.2 0.6 convert_divide_fusion
  286.8 0.6 constant_dynamic-slice_fusion.2
  (22 shorter events, 0.0 us)
Async XLA Ops:
  0.6 54.4 %collective-permute-start.2 = (bf16[256,1024]{1,0:T(8,128)(2,1)}, bf16[256,1024]{1,0:T(8,128)(2,1)}, u32[]{:S(2)}, u32[]{:S(2)}) collective-permute-start(bf16[256,1024]{1,0:T(8,128)(2,1)} %w_own.1), channel_id=1, source_target_pairs={{0,4},{4,0},{8,12},{12,8},{1,5},{5,1},{9,13},{13,9},{2,6},{6,2},{1... | collective-permute-start | bytes 1572872 | tf_op jit(solution)/shard_map/ppermute | solution.py:1353
  3.6 52.9 %collective-permute-start.3 = (bf16[256,1024]{1,0:T(8,128)(2,1)}, bf16[256,1024]{1,0:T(8,128)(2,1)}, u32[]{:S(2)}, u32[]{:S(2)}) collective-permute-start(bf16[256,1024]{1,0:T(8,128)(2,1)} %w_own.1), channel_id=1, source_target_pairs={{0,8},{4,12},{8,0},{12,4},{1,9},{5,13},{9,1},{13,5},{2,10},{6,14},... | collective-permute-start | bytes 1572872 | tf_op jit(solution)/shard_map/ppermute | solution.py:1354
  5.9 33.4 %collective-permute-start = (bf16[3,2,1024]{2,1,0:T(2,128)(2,1)S(1)}, bf16[3,2,1024]{2,1,0:T(2,128)(2,1)S(1)}, u32[]{:S(2)}, u32[]{:S(2)}) collective-permute-start(bf16[3,2,1024]{2,1,0:T(2,128)(2,1)S(1)} %slice.48), channel_id=1, source_target_pairs={{0,16},{1,17},{2,18},{3,19},{4,20},{5,21},{6,22},{7,23},{8,24},{9,... | collective-permute-start | bytes 36872 | tf_op jit(solution)/shard_map/ppermute | solution.py:1363
  7.2 7.2 %copy-start.8 = (bf16[1024]{0:T(1024)(128)(2,1)S(1)}, bf16[1024]{0:T(1024)(128)(2,1)}, u32[]{:S(2)}) copy-start(bf16[1024]{0:T(1024)(128)(2,1)} %param.18) | copy-start | bytes 6148
  7.2 7.8 %copy-start.6 = (bf16[1024,16]{0,1:T(8,128)(2,1)S(1)}, bf16[1024,16]{0,1:T(8,128)(2,1)}, u32[]{:S(2)}) copy-start(bf16[1024,16]{0,1:T(8,128)(2,1)} %param.21) | copy-start | bytes 98308
  15.8 7.2 %copy-start.13 = (s32[2]{0:T(128)S(1)}, s32[2]{0:T(128)}, u32[]{:S(2)}) copy-start(s32[2]{0:T(128)} %param.17) | copy-start | bytes 28
  23.6 15.0 %copy-start.10 = (bf16[4,1,512]{2,0,1:T(4,128)(2,1)S(1)}, bf16[4,1,512]{2,0,1:T(4,128)(2,1)}, u32[]{:S(2)}) copy-start(bf16[4,1,512]{2,0,1:T(4,128)(2,1)} %param.20) | copy-start | bytes 12292
  23.6 15.8 %copy-start.7 = (f32[1024]{0:T(1024)S(1)}, f32[1024]{0:T(1024)}, u32[]{:S(2)}) copy-start(f32[1024]{0:T(1024)} %convert_element_type.26) | copy-start | bytes 12292
  23.6 15.9 %copy-start.3 = (bf16[1024,1,512]{2,0,1:T(8,128)(2,1)S(1)}, bf16[1024,1,512]{2,0,1:T(8,128)(2,1)}, u32[]{:S(2)}) copy-start(bf16[1024,1,512]{2,0,1:T(8,128)(2,1)} %param.19) | copy-start | bytes 3145732
  40.4 18.1 %copy-start.12 = (bf16[256]{0:T(256)(128)(2,1)S(1)}, bf16[256]{0:T(256)(128)(2,1)}, u32[]{:S(2)}) copy-start(bf16[256]{0:T(256)(128)(2,1)} %param.25) | copy-start | bytes 1540
  40.4 18.7 %copy-start = (bf16[1024,704]{0,1:T(8,128)(2,1)S(1)}, bf16[1024,704]{0,1:T(8,128)(2,1)}, u32[]{:S(2)}) copy-start(bf16[1024,704]{0,1:T(8,128)(2,1)} %param.28) | copy-start | bytes 4325380
  53.4 7.3 %copy-start.1 = (bf16[1024,704]{0,1:T(8,128)(2,1)S(1)}, bf16[1024,704]{0,1:T(8,128)(2,1)}, u32[]{:S(2)}) copy-start(bf16[1024,704]{0,1:T(8,128)(2,1)} %param.29) | copy-start | bytes 4325380
  53.4 9.4 %collective-permute-start.1 = (f32[2,256,128]{2,1,0:T(8,128)}, f32[2,256,128]{2,1,0:T(8,128)S(1)}, u32[]{:S(2)}, u32[]{:S(2)}) collective-permute-start(f32[2,256,128]{2,1,0:T(8,128)} %get-tuple-element.46), channel_id=1, source_target_pairs={{0,16},{1,17},{2,18},{3,19},{4,20},{5,21},{6,22},{7,23},{8,24},{9,... | collective-permute-start | bytes 786440 | tf_op jit(solution)/shard_map/ppermute | solution.py:1363
  56.0 12.5 %collective-permute-start.4 = (bf16[128,1024]{1,0:T(8,128)(2,1)S(1)}, bf16[128,1024]{1,0:T(8,128)(2,1)}, u32[]{:S(2)}, u32[]{:S(2)}) collective-permute-start(bf16[128,1024]{1,0:T(8,128)(2,1)S(1)} %slice.64), channel_id=1, source_target_pairs={{0,8},{4,12},{8,0},{12,4},{1,9},{5,13},{9,1},{13,5},{2,10},{6,14},... | collective-permute-start | bytes 786440 | tf_op jit(solution)/shard_map/ppermute | solution.py:1355
  58.3 10.3 %collective-permute-start.5 = (bf16[128,1024]{1,0:T(8,128)(2,1)}, bf16[128,1024]{1,0:T(8,128)(2,1)}, u32[]{:S(2)}, u32[]{:S(2)}) collective-permute-start(bf16[128,1024]{1,0:T(8,128)(2,1)} %slice.65), channel_id=1, source_target_pairs={{0,4},{4,0},{8,12},{12,8},{1,5},{5,1},{9,13},{13,9},{2,6},{6,2},{1... | collective-permute-start | bytes 786440 | tf_op jit(solution)/shard_map/ppermute | solution.py:1356
  60.7 1.6 copy-start.11
  62.8 0.7 copy-start.5
  273.7 4.6 %copy-start.2 = (f32[3,128,704]{2,1,0:T(8,128)S(1)}, f32[3,128,704]{2,1,0:T(8,128)}, u32[]{:S(2)}) copy-start(f32[3,128,704]{2,1,0:T(8,128)} %get-tuple-element.68) | copy-start | bytes 3244036
  278.3 2.8 copy-start.4
  279.3 6.8 %copy-start.9 = (bf16[1024]{0:T(1024)(128)(2,1)S(1)}, bf16[1024]{0:T(1024)(128)(2,1)}, u32[]{:S(2)}) copy-start(bf16[1024]{0:T(1024)(128)(2,1)} %param.18) | copy-start | bytes 6148

commit v4 on v3

--- a/solution.py
+++ b/solution.py
@@ -1,5 +1,3 @@
-import functools
-
 import jax
 import jax.numpy as jnp
 from jax import lax
@@ -14,7 +12,6 @@
 EPS_NORM = 1e-06
 EPS_HEAD = 1e-05
 GATE_NORMALIZER = 16.0
-HIGHEST = lax.Precision.HIGHEST
 BF16 = jnp.bfloat16
 F32 = jnp.float32
 VMEM_LIMIT = 56 * 2**20
@@ -40,88 +37,11 @@
     return pl.BlockSpec(shape, lambda *_: (0,) * len(shape))
 
 
-def rows_of(size, width):
-    return pl.BlockSpec((size, width), lambda i, *_: (i, 0))
-
-
-def call(body, grid, in_specs, out_specs, out_shape, scratch, flops, moved, prefetch=0):
-    return pl.pallas_call(
-        body,
-        grid_spec=pltpu.PrefetchScalarGridSpec(
-            num_scalar_prefetch=prefetch,
-            grid=grid,
-            in_specs=in_specs,
-            out_specs=out_specs,
-            scratch_shapes=scratch,
-        ),
-        out_shape=out_shape,
-        compiler_params=pltpu.CompilerParams(
-            dimension_semantics=("arbitrary",), vmem_limit_bytes=VMEM_LIMIT
-        ),
-        cost_estimate=pl.CostEstimate(flops=flops, bytes_accessed=moved, transcendentals=0),
-    )
-
-
 def shape_of(shape, dtype):
     return jax.ShapeDtypeStruct(shape, dtype)
 
 
-def project_body(
-    places, tok_in, cot_in, gain, w_proj, w_gate, w_rank,
-    tok, upstream, normed, projected, out_gate, low_rank,
-):
-    step = pl.program_id(0)
-    sequences, count, _ = tok.shape
-    total = sequences * count
-    row = lax.broadcasted_iota(jnp.int32, (total, total), 0)
-    column = lax.broadcasted_iota(jnp.int32, (total, total), 1)
-    source = (row % count) * sequences + row // count
-    order = jnp.where(column == source, 1.0, 0.0).astype(BF16)
-    rows = mm(order, tok_in[...])
-    grads = mm(order, cot_in[...])
-    first = places[sequences] + step * count
-    position = first + lax.broadcasted_iota(jnp.int32, (count, 1), 0)
-    inverse = lax.rsqrt(jnp.mean(rows * rows, axis=-1, keepdims=True) + EPS_NORM)
-    rounded = (rows * inverse * gain[...]).astype(BF16)
-    projected_rows = mm(rounded, w_proj[...]).astype(BF16)
-    gate_rows = mm(rounded, w_gate[...]).astype(BF16)
-    rank_rows = mm(rounded, w_rank[...]).astype(BF16)
-    for s in range(sequences):
-        part = slice(s * count, (s + 1) * count)
-        tok[s] = rows[part].astype(BF16)
-        upstream[s] = jnp.where(position < places[s], grads[part], 0.0).astype(BF16)
-        normed[s] = rounded[part]
-        projected[s] = projected_rows[part]
-        out_gate[s] = gate_rows[part]
-        low_rank[s] = rank_rows[part]
-
-
-def rows3(sequences, size, width):
-    return pl.BlockSpec((sequences, size, width), lambda i, *_: (0, i, 0))
-
-
-def project(places, tok, cot, sequences, gain, w_proj, w_gate, w_rank):
-    length, width = tok.shape[0] // sequences, tok.shape[1]
-    c3, dv, rank = w_proj.shape[1], w_gate.shape[1], w_rank.shape[1]
-    widths = (width, width, width, c3, dv, rank)
-    return call(
-        project_body,
-        (length // CHUNK,),
-        [
-            rows_of(CHUNK * sequences, width),
-            rows_of(CHUNK * sequences, width),
-            whole((1, width)),
-            whole((width, c3)),
-            whole((width, dv)),
-            whole((width, rank)),
-        ],
-        [rows3(sequences, CHUNK, w) for w in widths],
-        [shape_of((sequences, length, w), BF16) for w in widths],
-        [],
-        2 * sequences * length * width * (c3 + dv + rank + 512),
-        sequences * length * (5 * width + c3 + dv) * 2 + width * (c3 + dv) * 2,
-        prefetch=1,
-    )(places, tok, cot, gain, w_proj, w_gate, w_rank)
+MIXER_GAIN, CHANNEL_GAIN, HEAD_GAIN, TAPS, BIAS = 0, 1, 2, 3, 7
 
 
 def triangle(lower):
@@ -130,10 +50,37 @@
     return row >= column if lower else row <= column
 
 
-def running_sum(values, lower):
-    ones = triangle(lower).astype(F32)
-    return lax.dot_general(
-        ones, values, (((1,), (0,)), ((), ())), precision=HIGHEST, preferred_element_type=F32
+def running_sums(blocks, lower):
+    ones = jnp.where(triangle(lower), 1.0, 0.0).astype(BF16)
+    parts = []
+    for block in blocks:
+        high = block.astype(BF16)
+        parts += [high, (block - high.astype(F32)).astype(BF16)]
+    sums = mm(ones, jnp.concatenate(parts, axis=1))
+    width = blocks[0].shape[1]
+    return [
+        sums[:, 2 * i * width : (2 * i + 1) * width]
+        + sums[:, (2 * i + 1) * width : (2 * i + 2) * width]
+        for i in range(len(blocks))
+    ]
+
+
+def causal_pairs(sequences):
+    total = sequences * CHUNK
+    row = lax.broadcasted_iota(jnp.int32, (total, total), 0)
+    column = lax.broadcasted_iota(jnp.int32, (total, total), 1)
+    return jnp.logical_and(row // CHUNK == column // CHUNK, row >= column)
+
+
+def spread(blocks):
+    zeros = jnp.zeros_like(blocks[0])
+    count = len(blocks)
+    return jnp.concatenate(
+        [
+            jnp.concatenate([blocks[s] if t == s else zeros for t in range(count)], axis=1)
+            for s in range(count)
+        ],
+        axis=0,
     )
 
 
@@ -144,135 +91,289 @@
     return total
 
 
-def forward_body(
-    projected, halo, low_rank, taps_in, rank_up, bias,
-    head_local, query_profile, cumulative, states, before, end_state, total_decay,
-    extended, memory, preceding,
+def front_body(
+    tokens, params, w_proj, w_gate, w_rank, rank_up, edge_source, w_own,
+    tok, normed, projected, low_rank, cumulative, states, before, out_gate, profile, gated, head,
+    halo, entering, decays, w_others,
+    extended, memory, preceding, head_local, edge_in, state_out, state_seq, w_here,
+    edge_sem, seq_send, seq_recv, w_send, w_recv, w_store,
 ):
     step = pl.program_id(0)
-    sequences = projected.shape[0]
+    last_step = pl.num_programs(0) - 1
+    sequences, size, width = tok.shape
+    rank, dk = rank_up.shape
+    c3, dv = w_proj.shape[1], w_gate.shape[1]
+    per_step = size // CHUNK
+    MESH = pl.DeviceIdType.MESH
+    me, side, sides = lax.axis_index("mp"), lax.axis_index("seq"), lax.axis_size("seq")
+    across = me + 1 - 2 * (me % 2)
+    down = (me + 2) % 4
+    peers = [(side + hop) % sides for hop in range(1, sides)]
+    half = w_own.shape[0] // 2
+
+    def remote(source, target, send, recv, axis, device):
+        return pltpu.make_async_remote_copy(
+            src_ref=source,
+            dst_ref=target,
+            send_sem=send,
+            recv_sem=recv,
+            device_id={axis: device},
+            device_id_type=MESH,
+        )
+
+    edge_copy = remote(
+        edge_source.at[pl.ds(edge_source.shape[0] - 8, 8)],
+        edge_in,
+        edge_sem.at[0],
+        edge_sem.at[1],
+        "seq",
+        peers[0],
+    )
+    state_copies = [
+        remote(state_out, state_seq.at[i], seq_send.at[i], seq_recv.at[i], "seq", peers[i])
+        for i in range(sides - 1)
+    ]
+    first, second = pl.ds(0, half), pl.ds(half, half)
+    weight_copies = [
+        remote(w_own, w_here.at[0], w_send.at[0], w_recv.at[0], "mp", across),
+        remote(w_own, w_here.at[1], w_send.at[1], w_recv.at[1], "mp", down),
+        remote(
+            w_here.at[0, first], w_here.at[2, first], w_send.at[2], w_recv.at[2], "mp", down
+        ),
+        remote(
+            w_here.at[1, second], w_here.at[2, second], w_send.at[3], w_recv.at[3], "mp", across
+        ),
+    ]
+    weights_out = pltpu.make_async_copy(w_here, w_others, w_store.at[0])
+    barrier = pltpu.get_barrier_semaphore()
 
     @pl.when(step == 0)
     def _():
-        extended[:, 0:8, :] = halo[...]
+        for peer in peers:
+            pl.semaphore_signal(barrier, inc=1, device_id={"seq": peer}, device_id_type=MESH)
+        for peer in (across, down):
+            pl.semaphore_signal(barrier, inc=1, device_id={"mp": peer}, device_id_type=MESH)
         memory[...] = jnp.zeros_like(memory)
         preceding[...] = jnp.zeros_like(preceding)
 
     @pl.when(step > 0)
     def _():
-        extended[:, 0:8, :] = extended[:, STEP : STEP + 8, :]
-
-    width = rank_up.shape[1]
-    causal = triangle(True)
+        extended[:, 0:8, :] = extended[:, size : size + 8, :]
+
+    def first_norm(rows):
+        inverse = lax.rsqrt(jnp.mean(rows * rows, axis=-1, keepdims=True) + EPS_NORM)
+        return (rows * inverse * params[MIXER_GAIN : MIXER_GAIN + 1, :]).astype(BF16)
+
+    here = jnp.swapaxes(tokens[...], 0, 1)
+    tok[...] = here
+    rounded = first_norm(here.reshape(sequences * size, width).astype(F32))
+    normed[...] = rounded.reshape(sequences, size, width)
+    projected_rows = mm(rounded, w_proj[...]).astype(BF16)
+    projected[...] = projected_rows.reshape(sequences, size, c3)
+    rows_here = pl.ds(pl.multiple_of(step * size, size), size)
+    out_gate[:, rows_here, :] = mm(rounded, w_gate[...]).astype(BF16).reshape(sequences, size, dv)
+    low_rows = mm_nt(rounded, w_rank[...]).astype(BF16)
+    low_rank[...] = low_rows.reshape(sequences, size, rank)
+
+    @pl.when(step == 0)
+    def _():
+        pl.semaphore_wait(barrier, sides - 1 + 2)
+        edge_copy.start()
+        for copy in weight_copies[:2]:
+            copy.start()
+        edge_copy.wait()
+        edge = jnp.swapaxes(edge_in[...].astype(F32), 0, 1).reshape(sequences * 8, width)
+        edge_rows = mm(first_norm(edge), w_proj[...]).astype(BF16).astype(F32)
+        edge_rows = jnp.where(side > 0, edge_rows, 0.0).reshape(sequences, 8, c3)
+        extended[:, 0:8, :] = edge_rows
+        halo[...] = edge_rows
+
+    @pl.when(step == 1)
+    def _():
+        for i in range(2):
+            weight_copies[i].wait_recv()
+            weight_copies[2 + i].start()
+
+    taps = params[TAPS : TAPS + CONV, :c3]
+    logit = mm(low_rows, rank_up[...]) + params[BIAS : BIAS + 1, :dk]
+    decay = (jnp.minimum(logit, 0.0) - jnp.log1p(jnp.exp(-jnp.abs(logit)))) / GATE_NORMALIZER
+    blocks = [
+        decay[s * size + p * CHUNK : s * size + (p + 1) * CHUNK]
+        for s in range(sequences)
+        for p in range(per_step)
+    ]
+    totals = running_sums(blocks, True)
+    convolved = []
     for s in range(sequences):
-        extended[s, 8 : 8 + STEP, :] = projected[s].astype(F32)
-        filtered = filter_rows(extended.at[s], taps_in[...], STEP)
-        convolved = (filtered * sigmoid(filtered)).astype(BF16)
-        logit = mm(low_rank[s], rank_up[...]) + bias[...]
-        decay = (jnp.minimum(logit, 0.0) - jnp.log1p(jnp.exp(-jnp.abs(logit)))) / GATE_NORMALIZER
-        for part in range(STEP // CHUNK):
-            rows = slice(part * CHUNK, (part + 1) * CHUNK)
-            queries = convolved[rows, :width].astype(F32)
-            keys = convolved[rows, width : 2 * width].astype(F32)
-            values = convolved[rows, 2 * width :]
-            total = running_sum(decay[rows], True)
+        rows = projected_rows[s * size : (s + 1) * size]
+        extended[s, 8 : 8 + size, :] = rows.astype(F32)
+        filtered = filter_rows(extended.at[s], taps, size)
+        convolved.append((filtered * sigmoid(filtered)).astype(BF16))
+    visible = causal_pairs(sequences)
+    for p in range(per_step):
+        rows = slice(p * CHUNK, (p + 1) * CHUNK)
+        there = pl.ds(pl.multiple_of(step * size + p * CHUNK, CHUNK), CHUNK)
+        lifted, lowered, profiles, tails, lasts = [], [], [], [], []
+        for s in range(sequences):
+            queries = convolved[s][rows, :dk].astype(F32)
+            keys = convolved[s][rows, dk : 2 * dk].astype(F32)
+            total = totals[s * per_step + p]
             middle, last = total[CHUNK // 2 - 1 : CHUNK // 2], total[CHUNK - 1 : CHUNK]
-            lifted = (queries * jnp.exp(total - middle)).astype(BF16)
-            lowered = (keys * jnp.exp(middle - total)).astype(BF16)
-            scores = jnp.where(causal, mm_nt(lifted, lowered), 0.0).astype(BF16)
-            entry = memory[s]
-            entry_low = entry.astype(BF16)
-            states[s, part] = entry_low
-            profile = queries * jnp.exp(total)
-            head_local[s, rows, :] = mm(scores, values) + mm_nt(profile.astype(BF16), entry_low)
-            gone = preceding[s]
-            query_profile[s, rows, :] = (profile * jnp.exp(gone)).astype(BF16)
+            lifted.append((queries * jnp.exp(total - middle)).astype(BF16))
+            lowered.append((keys * jnp.exp(middle - total)).astype(BF16))
+            inside = queries * jnp.exp(total)
+            profiles.append(inside.astype(BF16))
+            tails.append((keys * jnp.exp(last - total)).astype(BF16))
+            lasts.append(last)
+            gone = preceding[:, s * dk : (s + 1) * dk]
+            profile[s, there, :] = (inside * jnp.exp(gone)).astype(BF16)
             cumulative[s, rows, :] = total
-            tails = (keys * jnp.exp(last - total)).astype(BF16)
-            memory[s] = entry * jnp.exp(last) + mm_tn(values, tails)
-            before[s, pl.ds(step * (STEP // CHUNK) + part, 1), :] = gone
-            preceding[s] = gone + last
-    end_state[...] = memory[...]
-    total_decay[...] = preceding[...]
-
-
-def forward_mix(projected, halo, low_rank, taps, rank_up, bias, dv):
-    sequences, length, c3 = projected.shape
+        values = jnp.concatenate([convolved[s][rows, 2 * dk :] for s in range(sequences)], axis=0)
+        scores = mm_nt(jnp.concatenate(lifted, axis=0), jnp.concatenate(lowered, axis=0))
+        scores = jnp.where(visible, scores, 0.0).astype(BF16)
+        entry = memory[...]
+        entry_low = entry.astype(BF16)
+        states[p] = entry_low
+        mixed = mm(scores, values) + mm_nt(spread(profiles), entry_low)
+        for s in range(sequences):
+            head_local[s, there, :] = mixed[s * CHUNK : (s + 1) * CHUNK]
+        last = jnp.concatenate(lasts, axis=1)
+        memory[...] = entry * jnp.exp(last) + mm_tn(values, spread(tails))
+        before[step * per_step + p] = preceding[...]
+        preceding[...] = preceding[...] + last
+
+    @pl.when(step == last_step)
+    def _():
+        state_out[0:dv, :] = memory[...]
+        state_out[dv : dv + 8, :] = jnp.broadcast_to(preceding[...], (8, sequences * dk))
+        for copy in state_copies:
+            copy.start()
+        for copy in weight_copies[2:]:
+            copy.wait_recv()
+        weights_out.start()
+        decays[...] = jnp.zeros_like(decays)
+        for copy in state_copies:
+            copy.wait_recv()
+        total = jnp.zeros_like(memory)
+        for behind in range(sides - 1, 0, -1):
+            source = side - behind
+            gone = state_seq[behind - 1, dv : dv + 1, :]
+            decays[(source + sides) % sides] = gone
+            longer = state_seq[behind - 1, 0:dv, :] + jnp.exp(gone) * total
+            total = jnp.where(source >= 0, longer, total)
+        entering[...] = total
+        entry_low = total.astype(BF16)
+        scale = dk ** (-0.5)
+
+        def gate(index, carry):
+            there = pl.ds(pl.multiple_of(index * size, size), size)
+            for s in range(sequences):
+                rows = head_local[s, there, :]
+                rows = rows + mm_nt(profile[s, there, :], entry_low[:, s * dk : (s + 1) * dk])
+                rows = rows * scale
+                head[s, there, :] = rows.astype(BF16)
+                inverse = lax.rsqrt(jnp.mean(rows * rows, axis=-1, keepdims=True) + EPS_HEAD)
+                logits = out_gate[s, there, :].astype(F32)
+                rows = rows * inverse * params[HEAD_GAIN : HEAD_GAIN + 1, :dv]
+                gated[s, there, :] = (rows * (logits * sigmoid(logits))).astype(BF16)
+            return carry
+
+        lax.fori_loop(0, last_step + 1, gate, 0)
+        edge_sends = state_copies + weight_copies
+        for copy in edge_sends:
+            copy.wait_send()
+        weights_out.wait()
+
+
+def front(tokens, params, w_proj, w_gate, w_rank, rank_up, w_own, seq_count):
+    length, sequences, width = tokens.shape
+    c3, dv = w_proj.shape[1], w_gate.shape[1]
     rank, dk = rank_up.shape
-    chunks = length // CHUNK
-    per_step = STEP // CHUNK
-    return call(
-        forward_body,
-        (length // STEP,),
-        [
-            rows3(sequences, STEP, c3),
+    chunks, per_step = length // CHUNK, STEP // CHUNK
+    both = sequences * dk
+    anywhere = pl.BlockSpec(memory_space=pl.ANY)
+    dma = pltpu.SemaphoreType.DMA
+    peers = seq_count - 1
+
+    def steps(columns):
+        return pl.BlockSpec((sequences, STEP, columns), lambda i: (0, i, 0))
+
+    return pl.pallas_call(
+        front_body,
+        grid=(length // STEP,),
+        in_specs=[
+            pl.BlockSpec((STEP, sequences, width), lambda i: (i, 0, 0)),
+            whole(params.shape),
+            whole(w_proj.shape),
+            whole(w_gate.shape),
+            whole(w_rank.shape),
+            whole(rank_up.shape),
+            anywhere,
+            anywhere,
+        ],
+        out_specs=[
+            steps(width),
+            steps(width),
+            steps(c3),
+            steps(rank),
+            steps(dk),
+            pl.BlockSpec((per_step, dv, both), lambda i: (i, 0, 0)),
+            whole((chunks, 1, both)),
+            whole((sequences, length, dv)),
+            whole((sequences, length, dk)),
+            whole((sequences, length, dv)),
+            whole((sequences, length, dv)),
             whole((sequences, 8, c3)),
-            rows3(sequences, STEP, rank),
-            whole(taps.shape),
-            whole((rank, dk)),
-            whole((1, dk)),
+            whole((dv, both)),
+            whole((seq_count, 1, both)),
+            anywhere,
         ],
-        [
-            rows3(sequences, STEP, dv),
-            rows3(sequences, STEP, dk),
-            rows3(sequences, STEP, dk),
-            pl.BlockSpec((sequences, per_step, dv, dk), lambda i: (0, i, 0, 0)),
-            whole((sequences, chunks, dk)),
-            whole((sequences, dv, dk)),
-            whole((sequences, 1, dk)),
+        out_shape=[
+            shape_of((sequences, length, width), BF16),
+            shape_of((sequences, length, width), BF16),
+            shape_of((sequences, length, c3), BF16),
+            shape_of((sequences, length, rank), BF16),
+            shape_of((sequences, length, dk), F32),
+            shape_of((chunks, dv, both), BF16),
+            shape_of((chunks, 1, both), F32),
+            shape_of((sequences, length, dv), BF16),
+            shape_of((sequences, length, dk), BF16),
+            shape_of((sequences, length, dv), BF16),
+            shape_of((sequences, length, dv), BF16),
+            shape_of((sequences, 8, c3), F32),
+            shape_of((dv, both), F32),
+            shape_of((seq_count, 1, both), F32),
+            shape_of((3, *w_own.shape), BF16),
         ],
-        [
-            shape_of((sequences, length, dv), F32),
-            shape_of((sequences, length, dk), BF16),
-            shape_of((sequences, length, dk), F32),
-            shape_of((sequences, chunks, dv, dk), BF16),
-            shape_of((sequences, chunks, dk), F32),
-            shape_of((sequences, dv, dk), F32),
-            shape_of((sequences, 1, dk), F32),
+        scratch_shapes=[
+            pltpu.VMEM((sequences, STEP + 8, c3), F32),
+            pltpu.VMEM((dv, both), F32),
+            pltpu.VMEM((1, both), F32),
+            pltpu.VMEM((sequences, length, dv), F32),
+            pltpu.VMEM((8, sequences, width), BF16),
+            pltpu.VMEM((dv + 8, both), F32),
+            pltpu.VMEM((peers, dv + 8, both), F32),
+            pltpu.VMEM((3, *w_own.shape), BF16),
+            dma((2,)),
+            dma((peers,)),
+            dma((peers,)),
+            dma((4,)),
+            dma((4,)),
+            dma((1,)),
         ],
-        [
-            pltpu.VMEM((sequences, STEP + 8, c3), F32),
-            pltpu.VMEM((sequences, dv, dk), F32),
-            pltpu.VMEM((sequences, 1, dk), F32),
-        ],
-        2 * sequences * length * (4 * dk * dv + dk * dk) * 8,
-        sequences * (length * (c3 * 2 + dv * 4 + dk * 6) + chunks * dv * dk * 2),
-    )(projected, halo, low_rank, taps, rank_up, bias)
-
-
-def head_rows(head_local, query_profile, entering, scale):
-    return (head_local + mm_nt(query_profile, entering.astype(BF16))) * scale
-
-
-def gate_body(head_local, query_profile, entering, out_gate, gain, gated, head_out):
-    scale = query_profile.shape[-1] ** (-0.5)
-    for s in range(head_local.shape[0]):
-        head = head_rows(head_local[s], query_profile[s], entering[s], scale)
-        head_out[s] = head.astype(BF16)
-        inverse = lax.rsqrt(jnp.mean(head * head, axis=-1, keepdims=True) + EPS_HEAD)
-        logits = out_gate[s].astype(F32)
-        gated[s] = (head * inverse * gain[...] * (logits * sigmoid(logits))).astype(BF16)
-
-
-def gate(head_local, query_profile, entering, out_gate, gain):
-    sequences, length, dv = head_local.shape
-    dk = query_profile.shape[-1]
-    return call(
-        gate_body,
-        (length // STEP,),
-        [
-            rows3(sequences, STEP, dv),
-            rows3(sequences, STEP, dk),
-            whole((sequences, dv, dk)),
-            rows3(sequences, STEP, dv),
-            whole((1, dv)),
-        ],
-        [rows3(sequences, STEP, dv)] * 2,
-        [shape_of((sequences, length, dv), BF16)] * 2,
-        [],
-        2 * sequences * length * dk * dv * 4,
-        sequences * length * (dv * 10 + dk * 2),
-    )(head_local, query_profile, entering, out_gate, gain)
+        compiler_params=pltpu.CompilerParams(
+            dimension_semantics=("arbitrary",),
+            collective_id=2,
+            has_side_effects=True,
+            vmem_limit_bytes=VMEM_LIMIT,
+        ),
+        cost_estimate=pl.CostEstimate(
+            flops=2 * sequences * length * width * (c3 + dv + 128),
+            bytes_accessed=sequences * length * width * 8,
+            transcendentals=0,
+        ),
+        name="front",
+    )(tokens, params, w_proj, w_gate, w_rank, rank_up, tokens, w_own)
 
 
 PIECE = 128
@@ -280,13 +381,14 @@
 
 
 def ffn_body(
-    gated, w_own, w_across, w_down_hop, w_far, tok, gain, w_gate, w_up, w_down, upstream,
+    gated, w_own, w_others, tok, params, w_gate, w_up, w_down, cotangent,
     out_part, weight_grads, output_grads, grad_gated, own_residual, own_grad, gain_grad,
-    g_across, g_down, g_far, tok_here, up_here, wg, wu, wd, normed, hidden, grad_gate, grad_up,
+    g_across, g_down, g_far, tok_here, cot_here, up_here, wg, wu, wd, normed, hidden, grad_gate,
+    grad_up,
     out_stage, part, via_across, via_down, from_across, from_down, residual_here, grad_here,
     mixer_here, pieces, received, weight_stage, output_stage,
-    load_sem, row_sem, ag_send, ag_recv, rs_send, rs_recv, back_send, back_recv, store_sem,
-    stage_sem, last_sem,
+    load_sem, row_sem, cot_sem, ag_send, ag_recv, rs_send, rs_recv, back_send, back_recv,
+    store_sem, stage_sem, last_sem,
 ):
     turns = up_here.shape[0]
     halves = 2
@@ -312,12 +414,13 @@
 
     def load_tok(turn):
         return pltpu.make_async_copy(
-            tok.at[turn // halves, :, turn % halves], tok_here.at[turn % 2], row_sem.at[0, turn]
+            tok.at[turn // halves, :, turn % halves], tok_here.at[turn % 2], row_sem.at[turn]
         )
 
-    def load_up(turn):
+    def load_cot(block):
+        start = pl.multiple_of(block * PIECE, PIECE)
         return pltpu.make_async_copy(
-            upstream.at[turn // halves, :, turn % halves], up_here.at[turn], row_sem.at[1, turn]
+            cotangent.at[pl.ds(start, PIECE)], cot_here.at[block % 2], cot_sem.at[block % 2]
         )
 
     def direct(turn, side):
@@ -372,38 +475,49 @@
     loads = [load(0, w_gate, wg), load(1, w_up, wu), load(2, w_down, wd)]
     for copy in loads:
         copy.start()
-    for turn in range(turns):
-        if turn < 2:
-            load_tok(turn).start()
-        load_up(turn).start()
+    blocks = cotangent.shape[0] // PIECE
+    for turn in range(2):
+        load_tok(turn).start()
+        load_cot(turn).start()
     for device in (across, down, far):
         pl.semaphore_signal(barrier, inc=1, device_id={"mp": device}, device_id_type=MESH)
     pl.semaphore_wait(barrier, 3)
     for side in range(2):
         direct(0, side).start()
-    for side in range(2):
-        direct(1, side).start()
     gain_grad[...] = jnp.zeros_like(gain_grad)
+    gain = params[CHANNEL_GAIN : CHANNEL_GAIN + 1, :]
+    length = cotangent.shape[0]
+    first_position = lax.axis_index("seq") * length
+
+    def take_cotangent(block, carry):
+        load_cot(block).wait()
+        rows = jnp.swapaxes(cot_here[block % 2], 0, 1)
+        position = first_position + block * PIECE
+        position = (position + lax.broadcasted_iota(jnp.int32, (PIECE, 1), 0)).astype(F32)
+        for s in range(turns // halves):
+            column = gated.shape[-1] + s
+            keep = position < params[HEAD_GAIN : HEAD_GAIN + 1, column : column + 1]
+            kept = jnp.where(keep, rows[s].astype(F32), 0.0).astype(BF16)
+            up_here[s * halves + block % halves, block // halves] = kept
+
+        @pl.when(block + 2 < blocks)
+        def _():
+            load_cot(block + 2).start()
+
+        return carry
+
+    lax.fori_loop(0, blocks // 2, take_cotangent, 0)
     for side in range(2):
         direct(0, side).wait_recv()
         relay(0, side).start()
+    for side in range(2):
+        direct(1, side).start()
+    lax.fori_loop(blocks // 2, blocks, take_cotangent, 0)
     for copy in loads:
         copy.wait()
 
     def forward_and_back(turn):
-        for side in range(2):
-
-            @pl.when(turn + 1 < turns)
-            def _():
-                direct(turn + 1, side).wait_recv()
-                relay(turn + 1, side).start()
-
-            @pl.when(turn + 2 < turns)
-            def _():
-                direct(turn + 2, side).start()
-
         load_tok(turn).wait()
-        load_up(turn).wait()
         for side in range(2):
             relay(turn, side).wait_recv()
         rows = 4 * PIECE
@@ -412,9 +526,8 @@
             return values.reshape(rows, values.shape[-1])
 
         mixed = mm(flat(gated[turn // halves, :, turn % halves]), w_own[...])
-        mixed = mixed + mm(flat(g_across[turn]), w_across[...])
-        mixed = mixed + mm(flat(g_down[turn]), w_down_hop[...])
-        mixed = mixed + mm(flat(g_far[turn]), w_far[...])
+        for slot, source in enumerate((g_across, g_down, g_far)):
+            mixed = mixed + mm(flat(source[turn]), w_others[slot])
         residual = flat(tok_here[turn % 2]).astype(F32) + mixed
         for quarter in range(4):
 
@@ -424,21 +537,34 @@
 
         inverse = lax.rsqrt(jnp.mean(residual * residual, axis=-1, keepdims=True) + EPS_NORM)
         unit = residual * inverse
-        rounded = (unit * gain[...]).astype(BF16)
+        rounded = (unit * gain).astype(BF16)
         normed[turn] = rounded
-        gate_rows = mm(rounded, wg[...])
-        up_rows = mm(rounded, wu[...])
+        gate_rows = mm_nt(rounded, wg[...])
+        up_rows = mm_nt(rounded, wu[...])
         share = sigmoid(gate_rows)
         swished = gate_rows * share
         hidden_rows = (swished * up_rows).astype(BF16)
         hidden[turn] = hidden_rows
         grad_hidden = mm_nt(flat(up_here[turn]), wd[...])
+        for side in range(2):
+
+            @pl.when(turn + 1 < turns)
+            def _():
+                direct(turn + 1, side).wait_recv()
+                relay(turn + 1, side).start()
+
+        for side in range(2):
+
+            @pl.when(turn + 2 < turns)
+            def _():
+                direct(turn + 2, side).start()
+
         slope = share * (1.0 + gate_rows * (1.0 - share))
         grad_gate_rows = (grad_hidden * up_rows * slope).astype(BF16)
         grad_up_rows = (grad_hidden * swished).astype(BF16)
         grad_gate[turn] = grad_gate_rows
         grad_up[turn] = grad_up_rows
-        grad_rows = mm_nt(grad_gate_rows, wg[...]) + mm_nt(grad_up_rows, wu[...])
+        grad_rows = mm(grad_gate_rows, wg[...]) + mm(grad_up_rows, wu[...])
         part[turn] = grad_rows.astype(BF16).reshape(4, PIECE, width)
         for index in range(4):
             scatter(turn, index).start()
@@ -471,36 +597,20 @@
         residual = residual_here[turn]
         inverse = lax.rsqrt(jnp.mean(residual * residual, axis=-1, keepdims=True) + EPS_NORM)
         unit = residual * inverse
-        scaled = grad_normed * gain[...]
+        scaled = grad_normed * gain
         through = inverse * (scaled - unit * jnp.mean(scaled * unit, axis=-1, keepdims=True))
         grad_residual = up_here[turn, me].astype(F32) + through
         grad_here[turn] = grad_residual
         grad_mixer = grad_residual.astype(BF16)
         mixer_here[turn] = grad_mixer
-        for slot, weight in enumerate((w_own, w_across, w_down_hop, w_far)):
-            piece = mm_nt(grad_mixer, weight[...]).astype(BF16)
+        for slot in range(4):
+            weight = w_own[...] if slot == 0 else w_others[slot - 1]
+            piece = mm_nt(grad_mixer, weight).astype(BF16)
             if slot == 0:
                 received[turn, 0] = piece
             else:
                 pieces[turn, slot] = piece
                 give_back(turn, slot).start()
-
-    def round_of(index, carry):
-        @pl.when(index < turns)
-        def _():
-            forward_and_back(index)
-
-        @pl.when(jnp.logical_and(index >= 1, index <= turns))
-        def _():
-            pass_on(index - 1)
-
-        @pl.when(index >= 2)
-        def _():
-            collect(index - 2)
-
-        return carry
-
-    lax.fori_loop(0, turns + 2, round_of, 0)
 
     tile = weight_stage.shape[2]
     tiles = width // tile
@@ -533,7 +643,27 @@
             store_weight(kind, index, slot).start()
         return carry
 
-    lax.fori_loop(0, tiles, weight_tile, 0)
+    def round_of(index, carry):
+        @pl.when(index < turns)
+        def _():
+            forward_and_back(index)
+
+        @pl.when(index >= turns)
+        def _():
+            first_tile = (index - turns) * (tiles // 2)
+            lax.fori_loop(first_tile, first_tile + tiles // 2, weight_tile, 0)
+
+        @pl.when(jnp.logical_and(index >= 1, index <= turns))
+        def _():
+            pass_on(index - 1)
+
+        @pl.when(index >= 2)
+        def _():
+            collect(index - 2)
+
+        return carry
+
+    lax.fori_loop(0, turns + 2, round_of, 0)
     mixer_rows = mixer_here[...].reshape(turns * PIECE, width)
     dv = gated.shape[-1]
     for slot in range(4):
@@ -586,9 +716,9 @@
         copy.wait()
 
 
-def feed_forward(gated, weights, tok, gain, w_gate, w_up, w_down, upstream):
+def feed_forward(gated, w_own, w_others, tok, params, w_gate, w_up, w_down, cotangent):
     sequences, length, width = tok.shape
-    dv, units = gated.shape[-1], w_gate.shape[1]
+    dv, units = gated.shape[-1], w_gate.shape[0]
     halves = length // 4 // PIECE
     turns = sequences * halves
 
@@ -601,7 +731,7 @@
     rows = 4 * PIECE
     outs = pl.pallas_call(
         ffn_body,
-        in_specs=[vmem] * 5 + [anywhere, vmem] + [anywhere] * 4,
+        in_specs=[vmem] * 3 + [anywhere, vmem] + [anywhere] * 4,
         out_specs=[anywhere] * 6 + [vmem],
         out_shape=[
             shape_of((sequences, 4, halves, PIECE, width), BF16),
@@ -617,9 +747,10 @@
             pltpu.VMEM((turns, 4, PIECE, dv), BF16),
             pltpu.VMEM((turns, 4, PIECE, dv), BF16),
             pltpu.VMEM((2, 4, PIECE, width), BF16),
+            pltpu.VMEM((2, PIECE, sequences, width), BF16),
             pltpu.VMEM((turns, 4, PIECE, width), BF16),
-            pltpu.VMEM((width, units), BF16),
-            pltpu.VMEM((width, units), BF16),
+            pltpu.VMEM((units, width), BF16),
+            pltpu.VMEM((units, width), BF16),
             pltpu.VMEM((units, width), BF16),
             pltpu.VMEM((turns, rows, width), BF16),
             pltpu.VMEM((turns, rows, units), BF16),
@@ -639,7 +770,8 @@
             pltpu.VMEM((2, 3, 256, units), BF16),
             pltpu.VMEM((4, width, dv), BF16),
             dma((3,)),
-            dma((2, turns)),
+            dma((turns,)),
+            dma((2,)),
             dma((4, turns)),
             dma((4, turns)),
             dma((6, turns)),
@@ -659,7 +791,9 @@
             transcendentals=0,
         ),
         name="feed_forward",
-    )(pieces_of(gated), *weights, pieces_of(tok), gain, w_gate, w_up, w_down, pieces_of(upstream))
+    )(
+        pieces_of(gated), w_own, w_others, pieces_of(tok), params, w_gate, w_up, w_down, cotangent
+    )
     out_part, weight_grads, output_grads, grad_gated, own_residual, own_grad, gain_grad = outs
     return (
         out_part.reshape(sequences, 4, length // 4, width),
@@ -686,8 +820,8 @@
 def mixer_back_body(
     grad_gated_in, head_in, profile_in, out_gate_in, projected_in, cumulative_in, states_in,
     normed_in, tok_in, residual_in, grad_residual_in, out_part_in, hidden_grads, output_parts,
-    w_proj_in, w_gate_in, low_rank, halo, taps_in, rank_up, bias, w_rank, before, entering,
-    decays, head_gain, mixer_gain, channel_part, lengths,
+    w_proj_in, w_gate_in, low_rank, halo, params, rank_up, w_rank, before, entering,
+    decays, channel_part,
     output, token_grads, hidden_out, mixer_out, small_local, small_shared,
     grad_gated, head, profile, out_gate, projected, cumulative, states, normed, tok, residual,
     grad_residual, part, w_proj, w_gate,
@@ -906,6 +1040,8 @@
 
 
     scale = dk ** (-0.5)
+    head_gain = params[HEAD_GAIN : HEAD_GAIN + 1, :dv]
+    mixer_gain = params[MIXER_GAIN : MIXER_GAIN + 1, :]
 
     def ungate(index, carry):
         rows = pl.ds(pl.multiple_of(index * STEP, STEP), STEP)
@@ -919,14 +1055,14 @@
             logits = out_gate[s, rows, :].astype(F32)
             share = sigmoid(logits)
             slope = share * (1.0 + logits * (1.0 - share))
-            grad_out_gate[s, rows, :] = (upper * unit * head_gain[...] * slope).astype(BF16)
+            grad_out_gate[s, rows, :] = (upper * unit * head_gain * slope).astype(BF16)
             grad_normed = upper * (logits * share)
             small[34:35, :dv] += jnp.sum(grad_normed * unit, axis=0, keepdims=True)
-            scaled = grad_normed * head_gain[...]
+            scaled = grad_normed * head_gain
             through = inverse * (scaled - unit * jnp.mean(scaled * unit, axis=-1, keepdims=True))
             rounded = (through * scale).astype(BF16)
             grad_head[s, rows, :] = rounded
-            state_grad[s] += mm_tn(rounded, profile[s, rows, :])
+            state_grad[:, s * dk : (s + 1) * dk] += mm_tn(rounded, profile[s, rows, :])
         return carry
 
     lax.fori_loop(0, steps, ungate, 0)
@@ -967,7 +1103,7 @@
     grad_extended[:, STEP : STEP + 8, :] = jnp.zeros_like(grad_extended[:, STEP : STEP + 8, :])
 
 
-    taps = taps_in[...]
+    taps = params[TAPS : TAPS + CONV, :c3]
     causal = triangle(True)
 
     def backward_step(back, carry):
@@ -995,7 +1131,7 @@
             convolved = (filtered * share).astype(BF16)
             slope = share * (1.0 + filtered * (1.0 - share))
             low_rows = low_rank[s, here, :]
-            logit = mm(low_rows, rank_up[...]) + bias[...]
+            logit = mm(low_rows, rank_up[...]) + params[BIAS : BIAS + 1, :dk]
             logit_grads = [None] * per_step
             for piece in reversed(range(per_step)):
                 rows = slice(piece * CHUNK, (piece + 1) * CHUNK)
@@ -1011,19 +1147,20 @@
                 whole_decay = jnp.exp(last)
                 lifted, lowered = (queries * lift).astype(BF16), (keys * lower).astype(BF16)
                 inside, tails = (queries * inner).astype(BF16), (keys * outer).astype(BF16)
-                previous = before[s, pl.ds(step * per_step + piece, 1), :]
-                state = states[s, step * per_step + piece].astype(F32)
-                state = state + entering[s] * jnp.exp(previous)
+                own = slice(s * dk, (s + 1) * dk)
+                previous = before[step * per_step + piece, :, own]
+                state = states[step * per_step + piece, :, own].astype(F32)
+                state = state + entering[:, own] * jnp.exp(previous)
                 scores = jnp.where(causal, mm_nt(lifted, lowered), 0.0).astype(BF16)
                 grad_scores = jnp.where(causal, mm_nt(grad_rows, values), 0.0).astype(BF16)
-                later = upstream[s]
+                later = upstream[:, own]
                 later_low = later.astype(BF16)
                 grad_values = mm_tn(scores, grad_rows) + mm_nt(tails, later_low)
                 grad_lifted = mm(grad_scores, lowered)
                 grad_lowered = mm_tn(grad_scores, lifted)
                 grad_inside = mm(grad_rows, state.astype(BF16))
                 grad_tails = mm(values, later_low)
-                upstream[s] = later * whole_decay + mm_tn(grad_rows, inside)
+                upstream[:, own] = later * whole_decay + mm_tn(grad_rows, inside)
                 tail_terms = tails.astype(F32) * grad_tails
                 grad_total = (
                     lifted.astype(F32) * grad_lifted
@@ -1034,7 +1171,7 @@
                 grad_last = jnp.sum(tail_terms, axis=0, keepdims=True) + whole_decay * jnp.sum(
                     later * state, axis=0, keepdims=True
                 )
-                grad_decay = running_sum(grad_total, False) + grad_last
+                grad_decay = running_sums([grad_total], False)[0] + grad_last
                 logit_grads[piece] = grad_decay / GATE_NORMALIZER * sigmoid(-logit[rows])
                 grad_extended[s, rows, :dk] = (
                     grad_lifted * lift + grad_inside * inner
@@ -1089,7 +1226,8 @@
         total = residual[turn] + summed(turn, True)
         position = side * length + me * (length // 4) + h * PIECE
         position = position + lax.broadcasted_iota(jnp.int32, (PIECE, 1), 0)
-        out_stage[turn] = jnp.where(position < lengths[s : s + 1, 0:1], total, 0.0).astype(BF16)
+        limit = params[HEAD_GAIN : HEAD_GAIN + 1, dv + s : dv + s + 1]
+        out_stage[turn] = jnp.where(position.astype(F32) < limit, total, 0.0).astype(BF16)
         store(turn, 0).start()
     for turn in range(turns):
         for index in range(6):
@@ -1117,7 +1255,7 @@
 
         total = mm_nt(rows_of_turn(grad_projected), w_proj[...])
         total = total + mm_nt(rows_of_turn(grad_out_gate), w_gate[...])
-        total = total + mm_nt(rows_of_turn(grad_low_rank), w_rank[...])
+        total = total + mm(rows_of_turn(grad_low_rank), w_rank[...])
         rounded = total.astype(BF16)
         for q in range(4):
             part[s, q, h * PIECE : (h + 1) * PIECE] = rounded[q * PIECE : (q + 1) * PIECE]
@@ -1194,7 +1332,7 @@
         rows = tok[s, h * PIECE : (h + 1) * PIECE].astype(F32)
         inverse = lax.rsqrt(jnp.mean(rows * rows, axis=-1, keepdims=True) + EPS_NORM)
         unit = rows * inverse
-        scaled = grad_normed * mixer_gain[...]
+        scaled = grad_normed * mixer_gain
         through = inverse * (scaled - unit * jnp.mean(scaled * unit, axis=-1, keepdims=True))
         grad_residual[turn] = grad_residual[turn] + through
         store(turn, 1).start()
@@ -1229,9 +1367,8 @@
 
 def mixer_back(
     grad_gated, head, profile, out_gate, projected, cumulative, states, normed, tok, residual,
-    grad_residual, out_part, hidden_grads, output_parts, w_proj, w_gate, low_rank, halo, taps,
-    rank_up, bias, w_rank, before, entering, decays, head_gain, mixer_gain, channel_part, lengths,
-    seq_count, dp_count,
+    grad_residual, out_part, hidden_grads, output_parts, w_proj, w_gate, low_rank, halo, params,
+    rank_up, w_rank, before, entering, decays, channel_part, seq_count, dp_count,
 ):
     sequences, length, width = normed.shape
     dv, c3 = grad_gated.shape[-1], projected.shape[-1]
@@ -1260,7 +1397,7 @@
     ]
     return pl.pallas_call(
         mixer_back_body,
-        in_specs=[anywhere] * 16 + [vmem] * 13,
+        in_specs=[anywhere] * 16 + [vmem] * 9,
         out_specs=[anywhere] * 2 + [vmem] * 4,
         out_shape=[
             shape_of((turns, PIECE, width), BF16),
@@ -1277,7 +1414,7 @@
             low(sequences, length, dv),
             low(sequences, length, c3),
             full(sequences, length, dk),
-            low(sequences, length // CHUNK, dv, dk),
+            low(length // CHUNK, dv, sequences * dk),
             low(sequences, length, width),
             low(sequences, quarter, width),
             full(turns, PIECE, width),
@@ -1301,9 +1438,9 @@
             low(width, c3 + dv),
             low(peers, share_rows, c3 + dv),
             low(others, shard_rows, c3 + dv),
-            full(sequences, dv, dk),
-            full(peers, sequences, dv, dk),
-            full(sequences, dv, dk),
+            full(dv, sequences * dk),
+            full(peers, dv, sequences * dk),
+            full(dv, sequences * dk),
             full(sequences, STEP + 8, c3),
             full(sequences, STEP + 8, c3),
             full(sequences, 16, c3),
@@ -1338,44 +1475,9 @@
         name="mixer_back",
     )(
         grad_gated, head, profile, out_gate, projected, cumulative, states, normed, tok, residual,
-        grad_residual, out_part, hidden_grads, output_parts, w_proj, w_gate, low_rank, halo, taps,
-        rank_up, bias, w_rank, before, entering, decays, head_gain, mixer_gain, channel_part,
-        lengths,
+        grad_residual, out_part, hidden_grads, output_parts, w_proj, w_gate, low_rank, halo,
+        params, rank_up, w_rank, before, entering, decays, channel_part,
     )
-
-
-ACROSS = [(i, i ^ 1) for i in range(4)]
-DOWN = [(i, i ^ 2) for i in range(4)]
-
-
-def gather_relative(block):
-    half = block.shape[0] // 2
-    across = lax.ppermute(block, "mp", ACROSS)
-    down = lax.ppermute(block, "mp", DOWN)
-    first = lax.ppermute(across[:half], "mp", DOWN)
-    second = lax.ppermute(down[half:], "mp", ACROSS)
-    return [block, across, down, jnp.concatenate([first, second], axis=0)]
-
-
-def passed_along(block, axis, distance):
-    devices = range(lax.axis_size(axis))
-    route = [(i - distance, i) for i in devices if i - distance in devices]
-    return lax.ppermute(block, axis, route)
-
-
-def chain_states(decay, state, backward):
-    count, mine = lax.axis_size("seq"), lax.axis_index("seq")
-    if count == 2:
-        return passed_along(state, "seq", -1 if backward else 1)
-    decays, states = lax.all_gather(decay, "seq"), lax.all_gather(state, "seq")
-    if backward:
-        decays, states, mine = decays[::-1], states[::-1], count - 1 - mine
-
-    def hop(position, subtotal):
-        longer = subtotal * jnp.exp(decays[position]) + states[position]
-        return jnp.where(position < mine, longer, subtotal)
-
-    return lax.fori_loop(0, count - 1, hop, jnp.zeros_like(state))
 
 
 def on_device(
@@ -1384,67 +1486,47 @@
     cotangent,
 ):
     length, sequences, width = tokens.shape
-    shards = lax.axis_size("seq") * lax.axis_size("dp")
-    shard = lax.axis_index("seq") * lax.axis_size("dp") + lax.axis_index("dp")
-    me = lax.axis_index("mp")
+    seq_count, dp_count = lax.axis_size("seq"), lax.axis_size("dp")
+    shards = seq_count * dp_count
+    shard = lax.axis_index("seq") * dp_count + lax.axis_index("dp")
     own_rows = length // lax.axis_size("mp")
-    w_proj = project_weight[:, 0]
-    taps = filter_weight[:, 0].astype(F32)
-    rank_up_here = rank_up[:, 0]
-    bias = decay_bias.astype(F32)
-    mixer_gain_f = mixer_gain.astype(F32)[None]
-    channel_gain_f = channel_gain.astype(F32)[None]
-    head_gain_f = head_gain.astype(F32)[None]
-    dv = gate_weight.shape[1]
-    places = jnp.concatenate(
-        [lengths.astype(jnp.int32), (lax.axis_index("seq") * length).astype(jnp.int32).reshape(1)]
+    w_proj, rank_up_here = project_weight[:, 0], rank_up[:, 0]
+    c3, dv = w_proj.shape[1], gate_weight.shape[1]
+    rank, dk = rank_up_here.shape
+    w_rank = rank_down.T
+
+    def row(values):
+        values = values.astype(F32).reshape(-1, values.shape[-1])
+        return jnp.pad(values, ((0, 0), (0, width - values.shape[1])))
+
+    params = jnp.concatenate(
+        [
+            row(mixer_gain),
+            row(channel_gain),
+            row(jnp.concatenate([head_gain.astype(F32), lengths.astype(F32)])),
+            row(filter_weight[:, 0]),
+            row(decay_bias),
+        ],
+        axis=0,
     )
-
-    edge_tokens = passed_along(tokens[length - EDGE :], "seq", 1)
-    edge_f = edge_tokens.astype(F32)
-    edge_inverse = lax.rsqrt(jnp.mean(edge_f * edge_f, axis=-1, keepdims=True) + EPS_NORM)
-    edge_normed = (edge_f * edge_inverse * mixer_gain_f).astype(BF16)
-    edge_projected = jnp.einsum(
-        "psd,dc->spc", edge_normed, w_proj, preferred_element_type=F32
-    ).astype(BF16)
-    halo = jnp.pad(edge_projected.astype(F32), ((0, 0), (8 - EDGE, 0), (0, 0)))
-
-    output_weights = gather_relative(output_weight)
-    tok, upstream, normed, projected, out_gate, low_rank = project(
-        places,
-        tokens.reshape(length * sequences, width),
-        cotangent.reshape(length * sequences, width),
-        sequences,
-        mixer_gain_f,
-        w_proj,
-        gate_weight,
-        rank_down,
+    (
+        tok, normed, projected, low_rank, cumulative, states, before, out_gate, profile, gated,
+        head, halo, entering, decays, w_others,
+    ) = front(
+        tokens, params, w_proj, gate_weight, w_rank, rank_up_here, output_weight, seq_count
     )
-    head_local, query_profile, cumulative, states, before, end_state, total_decay = forward_mix(
-        projected, halo, low_rank, taps, rank_up_here, bias, dv
+    (
+        out_part, hidden_grads, output_parts, grad_gated, residual, grad_residual, channel_part,
+    ) = feed_forward(
+        gated, output_weight, w_others, tok, params, hidden_gate.T, hidden_up.T, hidden_down,
+        cotangent,
     )
-    entering = chain_states(total_decay, end_state, False)
-    gated, head = gate(head_local, query_profile, entering, out_gate, head_gain_f)
-    (
-        out_part, hidden_grads, output_parts, grad_gated, residual, grad_residual,
-        channel_gain_part,
-    ) = feed_forward(
-        gated, output_weights, tok, channel_gain_f, hidden_gate, hidden_up, hidden_down, upstream
+    outputs, token_grads, hidden_sums, mixer_sums, small, shared = mixer_back(
+        grad_gated, head, profile, out_gate, projected, cumulative, states, normed,
+        tok.reshape(sequences, 4, own_rows, width), residual, grad_residual, out_part,
+        hidden_grads, output_parts, w_proj, gate_weight, low_rank, halo, params, rank_up_here,
+        w_rank, before, entering, decays, channel_part, seq_count, dp_count,
     )
-    count = lax.axis_size("seq")
-    if count > 2:
-        decays = lax.all_gather(total_decay, "seq")
-    else:
-        decays = jnp.zeros((count, *total_decay.shape), F32)
-    outputs, token_grads, hidden_sums, mixer_sums, small, shared = mixer_back(
-        grad_gated, head, query_profile, out_gate, projected, cumulative, states, normed,
-        tok.reshape(sequences, 4, own_rows, width), residual, grad_residual, out_part,
-        hidden_grads, output_parts, w_proj, gate_weight, low_rank, halo, taps, rank_up_here, bias,
-        rank_down, before, entering, decays, head_gain_f, mixer_gain_f, channel_gain_part,
-        jnp.broadcast_to(lengths.astype(jnp.int32)[:, None], (sequences, 128)),
-        count, lax.axis_size("dp"),
-    )
-    c3, (rank, _, dk) = w_proj.shape[1], rank_up.shape
 
     def own(values):
         size = values.shape[-1] // shards
@@ -1454,7 +1536,7 @@
     return (
         outputs.reshape(own_shape).swapaxes(0, 1),
         token_grads.reshape(own_shape).swapaxes(0, 1),
-        shared[32] / mixer_gain_f[0],
+        shared[32] / mixer_gain.astype(F32),
         mixer_sums[:, None, :c3],
         own(small[16 : 16 + CONV, dk : dk + c3])[:, None],
         shared[:rank].T,

time: 292 us -> 252 us (0.86)
  local copies, waits for them, and re-layouts: 46.3 us -> 21.4 us
  starting transfers between devices: 8.25 us -> 0 us
  Pallas kernels: 226 us -> 222 us
    reshape x2 -> x1, local copies, waits for them, and re-layouts: 14.4 us -> 0.01 us  [row(): values = values.astype(F32).reshape(-1, values.shape[-1])]
    ppermute x6 -> x0, starting transfers between devices: 8.25 us -> none  [the longest x1 3 us: gather_relative(): across = lax.ppermute(block, 'mp', ACROSS)]
    unnamed x36 -> x13, local copies, waits for them, and re-layouts: 9.16 us -> 4.45 us
    pallas_call x5 -> x3, Pallas kernels: 226 us -> 222 us  [the longest x1 93.8 us: feed_forward(): pl.pallas_call(ffn_body, in_specs=[vmem] * 3 + [anywhere, vmem] + [anywhe...]
    slice x3 -> x0, local copies, waits for them, and re-layouts: 3.35 us -> none  [the longest x1 1.67 us: gather_relative(): second = lax.ppermute(down[half:], 'mp', ACROSS)]
  transfers between devices with their start and end apart: 6 -> 0, of which waited for: 0 -> 0; matrix products, arithmetic and copies ran while one was open for 9% -> 0% of each run, Pallas kernels for 11% -> 0%
where the time goes in v4:
time: 252 us; the launch traced here: 248 us
  Pallas kernels  222 us (88%)
  local copies, waits for them, and re-layouts  21.4 us (8%)
  other arithmetic  3.99 us (2%)
    pallas_call x1, Pallas kernels, feed_forward(): pl.pallas_call(ffn_body, in_specs=[vmem] * 3 + [anywhere, vmem] + [anywhe...  93.8 us
    pallas_call x1, Pallas kernels, mixer_back(): pl.pallas_call(mixer_back_body, in_specs=[anywhere] * 16 + [vmem] * 9, ou...  93.7 us
    pallas_call x1, Pallas kernels, front(): pl.pallas_call(front_body, grid=(length // STEP,), in_specs=[pl.BlockSpec...  34.2 us

profile of v4, /device:TPU:0, one launch (start us, length us, event | category | flops | bytes accessed | tf_op | source)
XLA Modules:
  0.0 247.8 jit_solution(16583893250775784286)
XLA Ops:
  0.6 0.7 pad_convert_fusion
  1.3 0.7 convert_element_type.22
  2.0 0.7 convert_element_type.23
  2.7 0.7 convert_element_type.21
  3.4 0.7 reshape.76
  4.0 0.7 pad.18
  4.7 0.6 concatenate.7.params
  5.4 34.2 %front.1 = (bf16[2,1024,1024]{2,1,0:T(8,128)(2,1)}, bf16[2,1024,1024]{2,1,0:T(8,128)(2,1)}, bf16[2,1024,512]{2,1,0:T(8,128)(2,1)}, bf16[2,1024,16]{2,1,0:T(8,128...) custom-call(bf16[1024,2,1024]{2,1,0:T(2,128)(2,1)} %edge_source.1, ...), custom_call_target="tpu_custom_call" | custom-call | flops 3758096384 | bytes 16777216 | tf_op jit(solution)/shard_map/front/pallas_call | solution.py:301
  39.5 93.8 %feed_forward.1 = (bf16[2,4,2,128,1024]{4,3,2,1,0:T(8,128)(2,1)}, bf16[3,1024,704]{2,1,0:T(8,128)(2,1)}, bf16[4,1024,256]{2,1,0:T(8,128)(2,1)}, bf16[2,4,2,128,2...) custom-call(bf16[2,4,2,128,256]{4,3,2,1,0:T(8,128)(2,1)} %bitcast.64, ...), custom_call_target="tpu_custom_call" | custom-call | flops 30870077440 | bytes 16777216 | tf_op jit(solution)/shard_map/feed_forward/pallas_call | solution.py:732
  133.4 93.7 %mixer_back.1 = (bf16[4,128,1024]{2,1,0:T(8,128)(2,1)}, f32[4,128,1024]{2,1,0:T(8,128)}, f32[3,128,704]{2,1,0:T(8,128)}, f32[128,1024]{1,0:T(8,128)}, f32[48,1024]{1,0:T(8,128)}, /*index=5*/f32[48,1024]{1,0:T(8,128)}) custom-call(bf16[2,1024,256]{2,1,0:T(8,128)(2,1)} %bitcast.63, bf16[2,1024,256]{2,1,0:T(8,128)(2,1)} %get-tuple-element.47.head_in, ...), custom_call_target="tpu_custom_call" | custom-call | flops 12884901888 | bytes 33554432 | tf_op jit(solution)/shard_map/mixer_back/pallas_call | solution.py:1398
  227.1 0.0 copy-start
  227.1 4.6 %copy.40 = f32[2,256,1024]{2,0,1:T(2,128)} copy(f32[2,256,1024]{2,1,0:T(8,128)} %bitcast.41) | data formatting | bytes 4194304 | tf_op jit(solution)/shard_map/reshape | solution.py:1538
  231.7 0.0 copy-done
  231.7 0.0 copy-start.1
  231.7 0.1 slice_bitcast_fusion
  231.8 0.0 copy-start.2
  231.8 0.9 copy.35
  232.7 0.9 copy.36
  233.6 0.9 copy.37
  234.5 0.0 copy-start.3
  234.5 0.0 copy-done.1
  234.5 2.0 copy.41
  236.6 0.0 copy-done.2
  236.6 1.0 copy.33
  237.6 0.7 slice_bitcast_fusion.4
  238.3 0.8 copy.34
  239.0 1.5 slice_bitcast_fusion.5
  240.5 0.7 slice.43
  241.2 0.7 constant_dynamic-slice_fusion.1
  241.9 0.7 slice.41
  242.6 0.6 constant_dynamic-slice_fusion.2
  243.2 0.7 slice.44
  243.9 0.6 constant_dynamic-slice_fusion
  244.5 1.4 fusion
  245.9 0.0 copy-done.3
  245.9 0.6 convert_divide_fusion
  246.5 1.3 slice.46
  (4 shorter events, 0.0 us)
Async XLA Ops:
  227.1 4.6 %copy-start = (f32[3,128,704]{2,1,0:T(8,128)S(1)}, f32[3,128,704]{2,1,0:T(8,128)}, u32[]{:S(2)}) copy-start(f32[3,128,704]{2,1,0:T(8,128)} %get-tuple-element.70) | copy-start | bytes 3244036
  231.7 2.8 %copy-start.1 = (bf16[4,128,1024]{2,1,0:T(8,128)(2,1)S(1)}, bf16[4,128,1024]{2,1,0:T(8,128)(2,1)}, u32[]{:S(2)}) copy-start(bf16[4,128,1024]{2,1,0:T(8,128)(2,1)} %get-tuple-element.65) | copy-start | bytes 3145732
  231.8 4.8 %copy-start.2 = (f32[128,1024]{1,0:T(8,128)S(1)}, f32[128,1024]{1,0:T(8,128)}, u32[]{:S(2)}) copy-start(f32[128,1024]{1,0:T(8,128)} %get-tuple-element.68) | copy-start | bytes 1572868
  234.5 11.4 %copy-start.3 = (bf16[1024]{0:T(1024)(128)(2,1)S(1)}, bf16[1024]{0:T(1024)(128)(2,1)}, u32[]{:S(2)}) copy-start(bf16[1024]{0:T(1024)(128)(2,1)} %param.18) | copy-start | bytes 6148

commit v5 on v4

--- a/solution.py
+++ b/solution.py
@@ -92,8 +92,9 @@
 
 
 def front_body(
-    tokens, params, w_proj, w_gate, w_rank, rank_up, edge_source, w_own,
-    tok, normed, projected, low_rank, cumulative, states, before, out_gate, profile, gated, head,
+    tokens, mixer_gain, channel_gain, head_gain, filter_weight, decay_bias, lengths, w_proj,
+    w_gate, w_rank, rank_up, edge_source, w_own,
+    params, tok, normed, projected, low_rank, cumulative, states, before, out_gate, profile, gated, head,
     halo, entering, decays, w_others,
     extended, memory, preceding, head_local, edge_in, state_out, state_seq, w_here,
     edge_sem, seq_send, seq_recv, w_send, w_recv, w_store,
@@ -155,6 +156,17 @@
             pl.semaphore_signal(barrier, inc=1, device_id={"mp": peer}, device_id_type=MESH)
         memory[...] = jnp.zeros_like(memory)
         preceding[...] = jnp.zeros_like(preceding)
+        params[...] = jnp.zeros_like(params)
+        params[MIXER_GAIN : MIXER_GAIN + 1, :] = mixer_gain[...].astype(F32).reshape(1, width)
+        params[CHANNEL_GAIN : CHANNEL_GAIN + 1, :] = channel_gain[...].astype(F32).reshape(1, width)
+        params[HEAD_GAIN : HEAD_GAIN + 1, :dv] = head_gain[...].astype(F32).reshape(1, dv)
+        column = lax.broadcasted_iota(jnp.int32, (1, 128), 1)
+        limits = jnp.zeros((1, 128), F32)
+        for s in range(sequences):
+            limits = jnp.where(column == s, lengths[s].astype(F32), limits)
+        params[HEAD_GAIN : HEAD_GAIN + 1, dv : dv + 128] = limits
+        params[TAPS : TAPS + CONV, :c3] = filter_weight[...].astype(F32)
+        params[BIAS : BIAS + 1, :dk] = decay_bias[...]
 
     @pl.when(step > 0)
     def _():
@@ -285,7 +297,10 @@
         weights_out.wait()
 
 
-def front(tokens, params, w_proj, w_gate, w_rank, rank_up, w_own, seq_count):
+def front(
+    tokens, mixer_gain, channel_gain, head_gain, filter_weight, decay_bias, lengths, w_proj,
+    w_gate, w_rank, rank_up, w_own, seq_count,
+):
     length, sequences, width = tokens.shape
     c3, dv = w_proj.shape[1], w_gate.shape[1]
     rank, dk = rank_up.shape
@@ -303,7 +318,12 @@
         grid=(length // STEP,),
         in_specs=[
             pl.BlockSpec((STEP, sequences, width), lambda i: (i, 0, 0)),
-            whole(params.shape),
+            whole(mixer_gain.shape),
+            whole(channel_gain.shape),
+            whole(head_gain.shape),
+            whole(filter_weight.shape),
+            whole(decay_bias.shape),
+            pl.BlockSpec(memory_space=pltpu.SMEM),
             whole(w_proj.shape),
             whole(w_gate.shape),
             whole(w_rank.shape),
@@ -312,6 +332,7 @@
             anywhere,
         ],
         out_specs=[
+            whole((8, width)),
             steps(width),
             steps(width),
             steps(c3),
@@ -329,6 +350,7 @@
             anywhere,
         ],
         out_shape=[
+            shape_of((8, width), F32),
             shape_of((sequences, length, width), BF16),
             shape_of((sequences, length, width), BF16),
             shape_of((sequences, length, c3), BF16),
@@ -373,7 +395,10 @@
             transcendentals=0,
         ),
         name="front",
-    )(tokens, params, w_proj, w_gate, w_rank, rank_up, tokens, w_own)
+    )(
+        tokens, mixer_gain, channel_gain, head_gain, filter_weight, decay_bias, lengths, w_proj,
+        w_gate, w_rank, rank_up, tokens, w_own,
+    )
 
 
 PIECE = 128
@@ -822,7 +847,7 @@
     normed_in, tok_in, residual_in, grad_residual_in, out_part_in, hidden_grads, output_parts,
     w_proj_in, w_gate_in, low_rank, halo, params, rank_up, w_rank, before, entering,
     decays, channel_part,
-    output, token_grads, hidden_out, mixer_out, small_local, small_shared,
+    output, token_grads, hidden_out, mixer_out, small_out, shared_out,
     grad_gated, head, profile, out_gate, projected, cumulative, states, normed, tok, residual,
     grad_residual, part, w_proj, w_gate,
     hidden_kept, hidden_seq, hidden_dp, output_kept, output_seq, output_mp, output_dp,
@@ -1308,8 +1333,19 @@
     for copy in small_to_places:
         copy.wait_recv()
     summed_here = paired_sum(small_low[1], small_dp, range(places - 1))
-    small_local[...] = summed_here
     small_low[2] = summed_here.astype(BF16)
+    shard, shards = side * places + place, sides * places
+
+    def own_columns(values):
+        size = values.shape[1] // shards
+        total = values[:, 0:size]
+        for index in range(1, shards):
+            total = jnp.where(shard == index, values[:, index * size : (index + 1) * size], total)
+        return total
+
+    small_out[0:CONV, : c3 // shards] = own_columns(summed_here[16 : 16 + CONV, dk : dk + c3])
+    small_out[8 : 8 + rank, : dk // shards] = own_columns(summed_here[16 : 16 + rank, :dk])
+    small_out[24:25, : dk // shards] = own_columns(summed_here[35:36, :dk])
     for copy in small_to_heads:
         copy.start()
     pass_on(2, False)
@@ -1338,7 +1374,9 @@
         store(turn, 1).start()
     for copy in small_to_heads:
         copy.wait_recv()
-    small_shared[...] = paired_sum(small_low[2], small_mp, (1, 0, 2))
+    shared = paired_sum(small_low[2], small_mp, (1, 0, 2))
+    shared_out[...] = shared
+    shared_out[32:33, :] = shared[32:33, :] / mixer_gain
     for copy in mixer_to_places + output_to_places:
         copy.wait_recv()
     total = mixer_grad[own_share(place), :].astype(F32)
@@ -1404,7 +1442,7 @@
             shape_of((turns, PIECE, width), F32),
             shape_of((3, shard_rows, units), F32),
             shape_of((shard_rows, c3 + 2 * dv), F32),
-            shape_of((SMALL, width), F32),
+            shape_of((32, 128), F32),
             shape_of((SMALL, width), F32),
         ],
         scratch_shapes=[
@@ -1480,6 +1518,75 @@
     )
 
 
+def finish_body(
+    outputs, token_grads, hidden, mixer, small, shared,
+    output, tokens_grad, mixer_gain, project, filters, rank_down, rank_up, bias, w_gate,
+    head_gain, w_out, channel_gain, hidden_gate, hidden_up, hidden_down,
+):
+    output[...] = jnp.swapaxes(outputs[:, 0], 0, 1)
+    tokens_grad[...] = jnp.swapaxes(token_grads[:, 0], 0, 1)
+
+    @pl.when(pl.program_id(0) == 0)
+    def _():
+        c3, dv = project.shape[-1], w_gate.shape[-1]
+        project[:, 0, :] = mixer[:, :c3]
+        w_gate[...] = mixer[:, c3 : c3 + dv]
+        w_out[...] = mixer[:, c3 + dv :].T
+        for s in range(filters.shape[0]):
+            filters[s] = small[s : s + 1, : filters.shape[-1]]
+        for s in range(rank_up.shape[0]):
+            rank_up[s] = small[8 + s : 9 + s, : rank_up.shape[-1]]
+        bias[...] = small[24:25, : bias.shape[-1]]
+        rank_down[...] = shared[: rank_down.shape[0], :]
+        mixer_gain[...] = shared[32:33, :]
+        channel_gain[...] = shared[33:34, :]
+        head_gain[...] = shared[34:35, :dv]
+        for target, kind in ((hidden_gate, 0), (hidden_up, 1), (hidden_down, 2)):
+            target[...] = hidden[kind].T
+
+
+def finish(outputs, token_grads, hidden, mixer, small, shared, sequences, c3, dv, dk, rank, shards):
+    turns, piece, width = outputs.shape
+    halves = turns // sequences
+    rows, units = hidden.shape[1:]
+
+    def by_half(values):
+        return values.reshape(sequences, halves, piece, width)
+
+    half = pl.BlockSpec((sequences, 1, piece, width), lambda i: (0, i, 0, 0))
+    placed = pl.BlockSpec((piece, sequences, width), lambda i: (i, 0, 0))
+    shapes = [
+        (1, width),
+        (rows, 1, c3),
+        (CONV, 1, c3 // shards),
+        (rank, width),
+        (rank, 1, dk // shards),
+        (1, dk // shards),
+        (rows, dv),
+        (1, dv),
+        (dv, rows),
+        (1, width),
+        (units, rows),
+        (units, rows),
+        (units, rows),
+    ]
+    return pl.pallas_call(
+        finish_body,
+        grid=(halves,),
+        in_specs=[half, half] + [whole(v.shape) for v in (hidden, mixer, small, shared)],
+        out_specs=[placed, placed] + [whole(shape) for shape in shapes],
+        out_shape=[
+            shape_of((halves * piece, sequences, width), BF16),
+            shape_of((halves * piece, sequences, width), F32),
+        ]
+        + [shape_of(shape, F32) for shape in shapes],
+        compiler_params=pltpu.CompilerParams(
+            dimension_semantics=("arbitrary",), vmem_limit_bytes=VMEM_LIMIT
+        ),
+        name="finish",
+    )(by_half(outputs), by_half(token_grads), hidden, mixer, small, shared)
+
+
 def on_device(
     tokens, lengths, mixer_gain, project_weight, filter_weight, rank_down, rank_up, decay_bias,
     gate_weight, head_gain, output_weight, channel_gain, hidden_gate, hidden_up, hidden_down,
@@ -1488,32 +1595,17 @@
     length, sequences, width = tokens.shape
     seq_count, dp_count = lax.axis_size("seq"), lax.axis_size("dp")
     shards = seq_count * dp_count
-    shard = lax.axis_index("seq") * dp_count + lax.axis_index("dp")
     own_rows = length // lax.axis_size("mp")
     w_proj, rank_up_here = project_weight[:, 0], rank_up[:, 0]
     c3, dv = w_proj.shape[1], gate_weight.shape[1]
     rank, dk = rank_up_here.shape
     w_rank = rank_down.T
-
-    def row(values):
-        values = values.astype(F32).reshape(-1, values.shape[-1])
-        return jnp.pad(values, ((0, 0), (0, width - values.shape[1])))
-
-    params = jnp.concatenate(
-        [
-            row(mixer_gain),
-            row(channel_gain),
-            row(jnp.concatenate([head_gain.astype(F32), lengths.astype(F32)])),
-            row(filter_weight[:, 0]),
-            row(decay_bias),
-        ],
-        axis=0,
-    )
     (
-        tok, normed, projected, low_rank, cumulative, states, before, out_gate, profile, gated,
-        head, halo, entering, decays, w_others,
+        params, tok, normed, projected, low_rank, cumulative, states, before, out_gate, profile,
+        gated, head, halo, entering, decays, w_others,
     ) = front(
-        tokens, params, w_proj, gate_weight, w_rank, rank_up_here, output_weight, seq_count
+        tokens, mixer_gain, channel_gain, head_gain, filter_weight[:, 0], decay_bias, lengths,
+        w_proj, gate_weight, w_rank, rank_up_here, output_weight, seq_count,
     )
     (
         out_part, hidden_grads, output_parts, grad_gated, residual, grad_residual, channel_part,
@@ -1521,34 +1613,33 @@
         gated, output_weight, w_others, tok, params, hidden_gate.T, hidden_up.T, hidden_down,
         cotangent,
     )
-    outputs, token_grads, hidden_sums, mixer_sums, small, shared = mixer_back(
+    results = mixer_back(
         grad_gated, head, profile, out_gate, projected, cumulative, states, normed,
         tok.reshape(sequences, 4, own_rows, width), residual, grad_residual, out_part,
         hidden_grads, output_parts, w_proj, gate_weight, low_rank, halo, params, rank_up_here,
         w_rank, before, entering, decays, channel_part, seq_count, dp_count,
     )
-
-    def own(values):
-        size = values.shape[-1] // shards
-        return lax.dynamic_slice_in_dim(values, shard * size, size, values.ndim - 1)
-
-    own_shape = (sequences, own_rows, width)
+    (
+        output, tokens_grad, mixer_gain_grad, project_grad, filter_grad, rank_down_grad,
+        rank_up_grad, decay_bias_grad, gate_grad, head_gain_grad, output_weight_grad,
+        channel_gain_grad, hidden_gate_grad, hidden_up_grad, hidden_down_grad,
+    ) = finish(*results, sequences, c3, dv, dk, rank, shards)
     return (
-        outputs.reshape(own_shape).swapaxes(0, 1),
-        token_grads.reshape(own_shape).swapaxes(0, 1),
-        shared[32] / mixer_gain.astype(F32),
-        mixer_sums[:, None, :c3],
-        own(small[16 : 16 + CONV, dk : dk + c3])[:, None],
-        shared[:rank].T,
-        own(small[16 : 16 + rank, :dk])[:, None],
-        own(small[35:36, :dk]),
-        mixer_sums[:, c3 : c3 + dv],
-        shared[34, :dv],
-        mixer_sums[:, c3 + dv :].T,
-        shared[33],
-        hidden_sums[0],
-        hidden_sums[1],
-        hidden_sums[2].T,
+        output,
+        tokens_grad,
+        mixer_gain_grad[0],
+        project_grad,
+        filter_grad,
+        rank_down_grad.T,
+        rank_up_grad,
+        decay_bias_grad,
+        gate_grad,
+        head_gain_grad[0],
+        output_weight_grad,
+        channel_gain_grad[0],
+        hidden_gate_grad.T,
+        hidden_up_grad.T,
+        hidden_down_grad,
     )
 
 

time: 252 us -> 231 us (0.917)
  local copies, waits for them, and re-layouts: 21.4 us -> 0 us
  Pallas kernels: 222 us -> 227 us
  other arithmetic: 3.99 us -> 0 us
    reshape x3 -> x0, local copies, waits for them, and re-layouts: 6.68 us -> none  [the longest x1 4.62 us: on_device(): token_grads.reshape(own_shape).swapaxes(0, 1)]
    pallas_call x0 -> x1, Pallas kernels: none -> 4.87 us  [finish(): pl.pallas_call(finish_body, grid=(halves,), in_specs=[half, half] + [whol...]
    slice x5 -> x0, local copies, waits for them, and re-layouts: 4.79 us -> none  [the longest x1 1.43 us: on_device(): shared[33]]
    unnamed x13 -> x0, local copies, waits for them, and re-layouts: 4.45 us -> none
where the time goes in v5:
time: 231 us; the launch traced here: 228 us
  Pallas kernels  227 us (98%)
    pallas_call x1, Pallas kernels, mixer_back(): pl.pallas_call(mixer_back_body, in_specs=[anywhere] * 16 + [vmem] * 9, ou...  94.3 us
    pallas_call x1, Pallas kernels, feed_forward(): pl.pallas_call(ffn_body, in_specs=[vmem] * 3 + [anywhere, vmem] + [anywhe...  93.8 us
    pallas_call x1, Pallas kernels, front(): pl.pallas_call(front_body, grid=(length // STEP,), in_specs=[pl.BlockSpec...  34.3 us
    pallas_call x1, Pallas kernels, finish(): pl.pallas_call(finish_body, grid=(halves,), in_specs=[half, half] + [whol...  4.87 us

profile of v5, /device:TPU:0, one launch (start us, length us, event | category | flops | bytes accessed | tf_op | source)
XLA Modules:
  0.0 228.2 jit_solution(13871194752625536376)
XLA Ops:
  0.6 34.3 %front.1 = (f32[8,1024]{1,0:T(8,128)}, bf16[2,1024,1024]{2,1,0:T(8,128)(2,1)}, bf16[2,1024,1024]{2,1,0:T(8,128)(2,1)}, bf16[2,1024,512]{2,1,0:T(8,128)(2,1)}, bf...) custom-call(bf16[1024,2,1024]{2,1,0:T(2,128)(2,1)} %edge_source.1, ...), custom_call_target="tpu_custom_call" | custom-call | flops 3758096384 | bytes 16777216 | tf_op jit(solution)/shard_map/front/pallas_call | solution.py:316
  35.0 93.8 %feed_forward.1 = (bf16[2,4,2,128,1024]{4,3,2,1,0:T(8,128)(2,1)}, bf16[3,1024,704]{2,1,0:T(8,128)(2,1)}, bf16[4,1024,256]{2,1,0:T(8,128)(2,1)}, bf16[2,4,2,128,2...) custom-call(bf16[2,4,2,128,256]{4,3,2,1,0:T(8,128)(2,1)} %bitcast.40, ...), custom_call_target="tpu_custom_call" | custom-call | flops 30870077440 | bytes 16777216 | tf_op jit(solution)/shard_map/feed_forward/pallas_call | solution.py:757
  128.8 94.3 %mixer_back.1 = (bf16[4,128,1024]{2,1,0:T(8,128)(2,1)}, f32[4,128,1024]{2,1,0:T(8,128)}, f32[3,128,704]{2,1,0:T(8,128)}, f32[128,1024]{1,0:T(8,128)}, f32[32,128]{1,0:T(8,128)}, /*index=5*/f32[48,1024]{1,0:T(8,128)}) custom-call(bf16[2,1024,256]{2,1,0:T(8,128)(2,1)} %bitcast.39, bf16[2,1024,256]{2,1,0:T(8,128)(2,1)} %get-tuple-element.64.head_in, ...), custom_call_target="tpu_custom_call" | custom-call | flops 12884901888 | bytes 33554432 | tf_op jit(solution)/shard_map/mixer_back/pallas_call | solution.py:1436
  223.1 4.9 %finish.1 = (bf16[256,2,1024]{2,1,0:T(2,128)(2,1)}, f32[256,2,1024]{2,1,0:T(2,128)}, f32[1,1024]{1,0:T(1,128)}, f32[128,1,512]{2,1,0:T(1,128)}, f32[4,1,64]{2,1,...) custom-call(bf16[2,2,128,1024]{3,2,1,0:T(8,128)(2,1)} %bitcast.20, ...), custom_call_target="tpu_custom_call" | custom-call | tf_op jit(solution)/shard_map/finish/pallas_call | solution.py:1573

commit v6 on v5

--- a/solution.py
+++ b/solution.py
@@ -180,6 +180,14 @@
     tok[...] = here
     rounded = first_norm(here.reshape(sequences * size, width).astype(F32))
     normed[...] = rounded.reshape(sequences, size, width)
+
+    @pl.when(step == 0)
+    def _():
+        pl.semaphore_wait(barrier, sides - 1 + 2)
+        edge_copy.start()
+        for copy in weight_copies[:2]:
+            copy.start()
+
     projected_rows = mm(rounded, w_proj[...]).astype(BF16)
     projected[...] = projected_rows.reshape(sequences, size, c3)
     rows_here = pl.ds(pl.multiple_of(step * size, size), size)
@@ -187,26 +195,6 @@
     low_rows = mm_nt(rounded, w_rank[...]).astype(BF16)
     low_rank[...] = low_rows.reshape(sequences, size, rank)
 
-    @pl.when(step == 0)
-    def _():
-        pl.semaphore_wait(barrier, sides - 1 + 2)
-        edge_copy.start()
-        for copy in weight_copies[:2]:
-            copy.start()
-        edge_copy.wait()
-        edge = jnp.swapaxes(edge_in[...].astype(F32), 0, 1).reshape(sequences * 8, width)
-        edge_rows = mm(first_norm(edge), w_proj[...]).astype(BF16).astype(F32)
-        edge_rows = jnp.where(side > 0, edge_rows, 0.0).reshape(sequences, 8, c3)
-        extended[:, 0:8, :] = edge_rows
-        halo[...] = edge_rows
-
-    @pl.when(step == 1)
-    def _():
-        for i in range(2):
-            weight_copies[i].wait_recv()
-            weight_copies[2 + i].start()
-
-    taps = params[TAPS : TAPS + CONV, :c3]
     logit = mm(low_rows, rank_up[...]) + params[BIAS : BIAS + 1, :dk]
     decay = (jnp.minimum(logit, 0.0) - jnp.log1p(jnp.exp(-jnp.abs(logit)))) / GATE_NORMALIZER
     blocks = [
@@ -215,6 +203,17 @@
         for p in range(per_step)
     ]
     totals = running_sums(blocks, True)
+
+    @pl.when(step == 0)
+    def _():
+        edge_copy.wait()
+        edge = jnp.swapaxes(edge_in[...].astype(F32), 0, 1).reshape(sequences * 8, width)
+        edge_rows = mm(first_norm(edge), w_proj[...]).astype(BF16).astype(F32)
+        edge_rows = jnp.where(side > 0, edge_rows, 0.0).reshape(sequences, 8, c3)
+        extended[:, 0:8, :] = edge_rows
+        halo[...] = edge_rows
+
+    taps = params[TAPS : TAPS + CONV, :c3]
     convolved = []
     for s in range(sequences):
         rows = projected_rows[s * size : (s + 1) * size]
@@ -253,6 +252,12 @@
         memory[...] = entry * jnp.exp(last) + mm_tn(values, spread(tails))
         before[step * per_step + p] = preceding[...]
         preceding[...] = preceding[...] + last
+
+    @pl.when(step == last_step - 1)
+    def _():
+        for i in range(2):
+            weight_copies[i].wait_recv()
+            weight_copies[2 + i].start()
 
     @pl.when(step == last_step)
     def _():
@@ -831,7 +836,7 @@
     )
 
 
-SMALL = 48
+SMALL, PACKED = 48, 32
 
 
 def paired_sum(own, received, order):
@@ -849,12 +854,12 @@
     decays, channel_part,
     output, token_grads, hidden_out, mixer_out, small_out, shared_out,
     grad_gated, head, profile, out_gate, projected, cumulative, states, normed, tok, residual,
-    grad_residual, part, w_proj, w_gate,
+    grad_residual, part_f, part_g, w_proj, w_gate,
     hidden_kept, hidden_seq, hidden_dp, output_kept, output_seq, output_mp, output_dp,
     f_via_across, f_via_down, f_across, f_down, g_via_across, g_via_down, g_across, g_down,
     grad_out_gate, grad_head, grad_projected, grad_low_rank, mixer_grad, mixer_seq, mixer_dp,
     state_grad, state_seq, upstream, extended, grad_extended, edge_out, edge_in,
-    small, small_low, small_seq, small_dp, small_mp, out_stage,
+    small, packed, small_low, small_seq, small_dp, small_mp, out_stage,
     load_sem, seq_send, seq_recv, dp_send, dp_recv, mp_send, mp_recv, f_send, f_recv,
     g_send, g_recv, store_sem,
 ):
@@ -895,7 +900,7 @@
                 (head_in, head),
                 (profile_in, profile),
                 (out_gate_in, out_gate),
-                (out_part_in, part),
+                (out_part_in, part_f),
                 (hidden_grads.at[:, pl.ds(side * share_rows, share_rows)], hidden_kept),
                 (output_parts.at[:, pl.ds(side * share_rows, share_rows)], output_kept),
                 (normed_in, normed),
@@ -991,6 +996,7 @@
     small_to_heads = to_heads(1, lambda slot: small_low.at[2], small_mp)
 
     def scatter(turn, index, forward):
+        part = part_f if forward else part_g
         if forward:
             via_across, via_down, from_across, from_down = (
                 f_via_across, f_via_down, f_across, f_down,
@@ -1014,6 +1020,7 @@
         return remote(source, target, send.at[index, turn], recv.at[index, turn], "mp", device)
 
     def pass_on(turn, forward):
+        part = part_f if forward else part_g
         via_across, via_down = (
             (f_via_across, f_via_down) if forward else (g_via_across, g_via_down)
         )
@@ -1028,6 +1035,7 @@
         scatter(turn, 4, forward).start()
 
     def summed(turn, forward):
+        part = part_f if forward else part_g
         from_across, from_down = (f_across, f_down) if forward else (g_across, g_down)
         for index in range(2, 6):
             scatter(turn, index, forward).wait_recv()
@@ -1060,6 +1068,15 @@
     for turn in range(turns):
         for index in range(2):
             scatter(turn, index, True).start()
+    loads[5].wait()
+    for copy in hidden_to_sides:
+        copy.wait_recv()
+    hidden_sum = hidden_kept[...]
+    for hop in range(sides - 1):
+        hidden_sum = hidden_sum + hidden_seq[hop]
+    hidden_kept[...] = hidden_sum
+    for copy in hidden_to_places:
+        copy.start()
     for copy in loads[0:4]:
         copy.wait()
 
@@ -1096,15 +1113,6 @@
     for turn in range(turns):
         for index in range(2, 4):
             scatter(turn, index, True).start()
-    loads[5].wait()
-    for copy in hidden_to_sides:
-        copy.wait_recv()
-    hidden_sum = hidden_kept[...]
-    for hop in range(sides - 1):
-        hidden_sum = hidden_sum + hidden_seq[hop]
-    hidden_kept[...] = hidden_sum
-    for copy in hidden_to_places:
-        copy.start()
     loads[6].wait()
     for copy in output_to_sides:
         copy.wait_recv()
@@ -1244,54 +1252,11 @@
             edge_out[s, 16 - EDGE + i : 17 - EDGE + i, :] = edge_row
     edge_copy.start()
 
-
-    loads[11].wait()
-    for turn in range(turns):
-        s, h = turn // halves, turn % halves
-        total = residual[turn] + summed(turn, True)
-        position = side * length + me * (length // 4) + h * PIECE
-        position = position + lax.broadcasted_iota(jnp.int32, (PIECE, 1), 0)
-        limit = params[HEAD_GAIN : HEAD_GAIN + 1, dv + s : dv + s + 1]
-        out_stage[turn] = jnp.where(position.astype(F32) < limit, total, 0.0).astype(BF16)
-        store(turn, 0).start()
-    for turn in range(turns):
-        for index in range(6):
-            scatter(turn, index, True).wait_send()
     edge_copy.wait_recv()
     for s in range(sequences):
         tail = grad_projected[s, length - 16 :, :].astype(F32)
         tail = tail + jnp.where(side < sides - 1, edge_in[s], 0.0)
         grad_projected[s, length - 16 :, :] = tail.astype(BF16)
-
-
-    loads[12].wait()
-    loads[13].wait()
-
-    def input_grad(turn):
-        s, h = turn // halves, turn % halves
-        quarter = length // 4
-
-        def rows_of_turn(ref):
-            blocks = [
-                ref[s, q * quarter + h * PIECE : q * quarter + (h + 1) * PIECE, :]
-                for q in range(4)
-            ]
-            return jnp.concatenate(blocks, axis=0)
-
-        total = mm_nt(rows_of_turn(grad_projected), w_proj[...])
-        total = total + mm_nt(rows_of_turn(grad_out_gate), w_gate[...])
-        total = total + mm(rows_of_turn(grad_low_rank), w_rank[...])
-        rounded = total.astype(BF16)
-        for q in range(4):
-            part[s, q, h * PIECE : (h + 1) * PIECE] = rounded[q * PIECE : (q + 1) * PIECE]
-        for index in range(4):
-            scatter(turn, index, False).start()
-        small[32:33, :] += jnp.sum(
-            total * rows_of_turn(normed).astype(F32), axis=0, keepdims=True
-        )
-
-    for turn in range(turns):
-        input_grad(turn)
 
 
     flat = sequences * length
@@ -1306,14 +1271,58 @@
         return carry
 
     lax.fori_loop(0, width // tile, weight_tile, 0)
-    small_low[0] = small[...].astype(BF16)
-    for copy in small_to_sides + mixer_to_sides:
+    for copy in mixer_to_sides:
         copy.start()
-    pass_on(0, False)
-    for copy in output_to_heads:
-        copy.wait_recv()
-    output_kept[0] = output_kept[0] + output_mp[0] + output_mp[1] + output_mp[2]
-    for copy in output_to_places:
+
+
+    loads[12].wait()
+    loads[13].wait()
+
+    def input_grad(turn):
+        s, h = turn // halves, turn % halves
+        quarter = length // 4
+
+        def rows_of_turn(ref):
+            blocks = [
+                ref[s, q * quarter + h * PIECE : q * quarter + (h + 1) * PIECE, :]
+                for q in range(4)
+            ]
+            return jnp.concatenate(blocks, axis=0)
+
+        total = mm_nt(rows_of_turn(grad_projected), w_proj[...])
+        total = total + mm_nt(rows_of_turn(grad_out_gate), w_gate[...])
+        total = total + mm(rows_of_turn(grad_low_rank), w_rank[...])
+        rounded = total.astype(BF16)
+        for q in range(4):
+            part_g[s, q, h * PIECE : (h + 1) * PIECE] = rounded[q * PIECE : (q + 1) * PIECE]
+        for index in range(2):
+            scatter(turn, index, False).start()
+        small[32:33, :] += jnp.sum(
+            total * rows_of_turn(normed).astype(F32), axis=0, keepdims=True
+        )
+
+    for turn in range(turns):
+        input_grad(turn)
+    for turn in range(turns):
+        for index in range(2, 4):
+            scatter(turn, index, False).start()
+
+
+    packed[...] = jnp.zeros_like(packed)
+    packed[0:rank, :] = small[0:rank, :]
+    packed[16:17, :] = small[32:33, :]
+    packed[17:18, :] = small[33:34, :]
+    packed[18:19, :dv] = small[34:35, :dv]
+    packed[18:19, dv : dv + dk] = small[35:36, :dk]
+    taps_in_row, ranks_in_row = width // c3, width // dk
+    for j in range(CONV):
+        row, column = 19 + j // taps_in_row, (j % taps_in_row) * c3
+        packed[row : row + 1, column : column + c3] = small[16 + j : 17 + j, dk : dk + c3]
+    for j in range(rank):
+        row, column = 22 + j // ranks_in_row, (j % ranks_in_row) * dk
+        packed[row : row + 1, column : column + dk] = small[16 + j : 17 + j, :dk]
+    small_low[0] = packed[...].astype(BF16)
+    for copy in small_to_sides:
         copy.start()
     for copy in small_to_sides:
         copy.wait_recv()
@@ -1329,11 +1338,29 @@
     mixer_grad[own, :] = mixer_sum
     for copy in mixer_to_places:
         copy.start()
-    pass_on(1, False)
+    for copy in output_to_heads:
+        copy.wait_recv()
+    output_kept[0] = output_kept[0] + output_mp[0] + output_mp[1] + output_mp[2]
+    for copy in output_to_places:
+        copy.start()
+
+    loads[11].wait()
+    for turn in range(turns):
+        s, h = turn // halves, turn % halves
+        total = residual[turn] + summed(turn, True)
+        position = side * length + me * (length // 4) + h * PIECE
+        position = position + lax.broadcasted_iota(jnp.int32, (PIECE, 1), 0)
+        limit = params[HEAD_GAIN : HEAD_GAIN + 1, dv + s : dv + s + 1]
+        out_stage[turn] = jnp.where(position.astype(F32) < limit, total, 0.0).astype(BF16)
+        store(turn, 0).start()
+    for turn in range(turns):
+        pass_on(turn, False)
     for copy in small_to_places:
         copy.wait_recv()
     summed_here = paired_sum(small_low[1], small_dp, range(places - 1))
     small_low[2] = summed_here.astype(BF16)
+    for copy in small_to_heads:
+        copy.start()
     shard, shards = side * places + place, sides * places
 
     def own_columns(values):
@@ -1343,12 +1370,17 @@
             total = jnp.where(shard == index, values[:, index * size : (index + 1) * size], total)
         return total
 
-    small_out[0:CONV, : c3 // shards] = own_columns(summed_here[16 : 16 + CONV, dk : dk + c3])
-    small_out[8 : 8 + rank, : dk // shards] = own_columns(summed_here[16 : 16 + rank, :dk])
-    small_out[24:25, : dk // shards] = own_columns(summed_here[35:36, :dk])
-    for copy in small_to_heads:
-        copy.start()
-    pass_on(2, False)
+    for j in range(CONV):
+        row, column = 19 + j // taps_in_row, (j % taps_in_row) * c3
+        small_out[j : j + 1, : c3 // shards] = own_columns(
+            summed_here[row : row + 1, column : column + c3]
+        )
+    for j in range(rank):
+        row, column = 22 + j // ranks_in_row, (j % ranks_in_row) * dk
+        small_out[8 + j : 9 + j, : dk // shards] = own_columns(
+            summed_here[row : row + 1, column : column + dk]
+        )
+    small_out[24:25, : dk // shards] = own_columns(summed_here[18:19, dv : dv + dk])
     for copy in hidden_to_places:
         copy.wait_recv()
     own_shard = pl.ds(pl.multiple_of(place * shard_rows, 16), shard_rows)
@@ -1357,7 +1389,6 @@
         for hop in range(places - 1):
             total = total + hidden_dp[hop, kind].astype(F32)
         hidden_out[kind] = total
-    pass_on(3, False)
 
 
     loads[14].wait()
@@ -1376,7 +1407,7 @@
         copy.wait_recv()
     shared = paired_sum(small_low[2], small_mp, (1, 0, 2))
     shared_out[...] = shared
-    shared_out[32:33, :] = shared[32:33, :] / mixer_gain
+    shared_out[16:17, :] = shared[16:17, :] / mixer_gain
     for copy in mixer_to_places + output_to_places:
         copy.wait_recv()
     total = mixer_grad[own_share(place), :].astype(F32)
@@ -1398,6 +1429,7 @@
             copy.wait_send()
     for turn in range(turns):
         for index in range(6):
+            scatter(turn, index, True).wait_send()
             scatter(turn, index, False).wait_send()
         store(turn, 0).wait()
         store(turn, 1).wait()
@@ -1443,7 +1475,7 @@
             shape_of((3, shard_rows, units), F32),
             shape_of((shard_rows, c3 + 2 * dv), F32),
             shape_of((32, 128), F32),
-            shape_of((SMALL, width), F32),
+            shape_of((PACKED, width), F32),
         ],
         scratch_shapes=[
             low(sequences, length, dv),
@@ -1457,6 +1489,7 @@
             low(sequences, quarter, width),
             full(turns, PIECE, width),
             full(turns, PIECE, width),
+            low(sequences, 4, quarter, width),
             low(sequences, 4, quarter, width),
             low(width, c3),
             low(width, dv),
@@ -1484,10 +1517,11 @@
             full(sequences, 16, c3),
             full(sequences, 16, c3),
             full(SMALL, width),
-            low(3, SMALL, width),
-            low(peers, SMALL, width),
-            low(others, SMALL, width),
-            low(3, SMALL, width),
+            full(PACKED, width),
+            low(3, PACKED, width),
+            low(peers, PACKED, width),
+            low(others, PACKED, width),
+            low(3, PACKED, width),
             low(turns, PIECE, width),
             dma((16,)),
             dma((6, peers)),
@@ -1538,9 +1572,9 @@
             rank_up[s] = small[8 + s : 9 + s, : rank_up.shape[-1]]
         bias[...] = small[24:25, : bias.shape[-1]]
         rank_down[...] = shared[: rank_down.shape[0], :]
-        mixer_gain[...] = shared[32:33, :]
-        channel_gain[...] = shared[33:34, :]
-        head_gain[...] = shared[34:35, :dv]
+        mixer_gain[...] = shared[16:17, :]
+        channel_gain[...] = shared[17:18, :]
+        head_gain[...] = shared[18:19, :dv]
         for target, kind in ((hidden_gate, 0), (hidden_up, 1), (hidden_down, 2)):
             target[...] = hidden[kind].T
 

time: 231 us -> 219 us (0.948)
  Pallas kernels: 227 us -> 217 us
    pallas_call x1, Pallas kernels: 94.3 us -> 89.8 us  [mixer_back(): pl.pallas_call(mixer_back_body, in_specs=[anywhere] * 16 + [vmem] * 9, ou...]
    pallas_call x1, Pallas kernels: 34.3 us -> 30.9 us  [front(): pl.pallas_call(front_body, grid=(length // STEP,), in_specs=[pl.BlockSpec...]
    pallas_call x1, Pallas kernels: 93.8 us -> 91.4 us  [feed_forward(): pl.pallas_call(ffn_body, in_specs=[vmem] * 3 + [anywhere, vmem] + [anywhe...]
where the time goes in v6:
time: 219 us; the launch traced here: 218 us
  Pallas kernels  217 us (99%)
    pallas_call x1, Pallas kernels, feed_forward(): pl.pallas_call(ffn_body, in_specs=[vmem] * 3 + [anywhere, vmem] + [anywhe...  91.4 us
    pallas_call x1, Pallas kernels, mixer_back(): pl.pallas_call(mixer_back_body, in_specs=[anywhere] * 16 + [vmem] * 9, ou...  89.8 us
    pallas_call x1, Pallas kernels, front(): pl.pallas_call(front_body, grid=(length // STEP,), in_specs=[pl.BlockSpec...  30.9 us
    pallas_call x1, Pallas kernels, finish(): pl.pallas_call(finish_body, grid=(halves,), in_specs=[half, half] + [whol...  4.87 us

profile of v6, /device:TPU:0, one launch (start us, length us, event | category | flops | bytes accessed | tf_op | source)
XLA Modules:
  0.0 217.8 jit_solution(3519545971248738691)
XLA Ops:
  0.6 30.9 %front.1 = (f32[8,1024]{1,0:T(8,128)}, bf16[2,1024,1024]{2,1,0:T(8,128)(2,1)}, bf16[2,1024,1024]{2,1,0:T(8,128)(2,1)}, bf16[2,1024,512]{2,1,0:T(8,128)(2,1)}, bf...) custom-call(bf16[1024,2,1024]{2,1,0:T(2,128)(2,1)} %edge_source.1, ...), custom_call_target="tpu_custom_call" | custom-call | flops 3758096384 | bytes 16777216 | tf_op jit(solution)/shard_map/front/pallas_call | solution.py:321
  31.6 91.4 %feed_forward.1 = (bf16[2,4,2,128,1024]{4,3,2,1,0:T(8,128)(2,1)}, bf16[3,1024,704]{2,1,0:T(8,128)(2,1)}, bf16[4,1024,256]{2,1,0:T(8,128)(2,1)}, bf16[2,4,2,128,2...) custom-call(bf16[2,4,2,128,256]{4,3,2,1,0:T(8,128)(2,1)} %bitcast.40, ...), custom_call_target="tpu_custom_call" | custom-call | flops 30870077440 | bytes 16777216 | tf_op jit(solution)/shard_map/feed_forward/pallas_call | solution.py:762
  123.0 89.8 %mixer_back.1 = (bf16[4,128,1024]{2,1,0:T(8,128)(2,1)}, f32[4,128,1024]{2,1,0:T(8,128)}, f32[3,128,704]{2,1,0:T(8,128)}, f32[128,1024]{1,0:T(8,128)}, f32[32,128]{1,0:T(8,128)}, /*index=5*/f32[32,1024]{1,0:T(8,128)}) custom-call(bf16[2,1024,256]{2,1,0:T(8,128)(2,1)} %bitcast.39, bf16[2,1024,256]{2,1,0:T(8,128)(2,1)} %get-tuple-element.64.head_in, ...), custom_call_target="tpu_custom_call" | custom-call | flops 12884901888 | bytes 33554432 | tf_op jit(solution)/shard_map/mixer_back/pallas_call | solution.py:1468
  212.8 4.9 %finish.1 = (bf16[256,2,1024]{2,1,0:T(2,128)(2,1)}, f32[256,2,1024]{2,1,0:T(2,128)}, f32[1,1024]{1,0:T(1,128)}, f32[128,1,512]{2,1,0:T(1,128)}, f32[4,1,64]{2,1,...) custom-call(bf16[2,2,128,1024]{3,2,1,0:T(8,128)(2,1)} %bitcast.20, ...), custom_call_target="tpu_custom_call" | custom-call | tf_op jit(solution)/shard_map/finish/pallas_call | solution.py:1607
